TPU v7x, 256 devices: a whole 4x4x8 slice. The times are simulated.
256 devices in a mesh: seq: 64 (over y, z, core), head: 4 (over x).
Axes of the slice: x: 4, y: 4, z: 8, core: 2. Of those that a mesh axis runs over, the one named last changes fastest.
Arguments:
- lin_query: bfloat16 [16384, 4096], P('seq', 'head'), may hold values from -6 to 6
- lin_key: bfloat16 [16384, 4096], P('seq', 'head'), may hold values from -6 to 6
- lin_value: bfloat16 [16384, 4096], P('seq', 'head'), may hold values from -6 to 6
- out_gate: bfloat16 [16384, 4096], P('seq', 'head'), may hold values from -6 to 6
- norm_gain: float32 [4096], P('head'), may hold values from 0.25 to 1.75
- decay_rate: float32 [32], P('head'), may hold values from 0 to 0.04, as said below
- soft_query: bfloat16 [16384, 4096], P('seq', 'head'), may hold values from -130 to 130
- soft_key: bfloat16 [16384, 4096], P('seq', 'head'), may hold values from -130 to 130
- soft_value: bfloat16 [16384, 4096], P('seq', 'head'), may hold values from -6 to 6
- doc_ids: int32 [128], replicated, may hold values from 0 to 31, never falling along the last dimension, each value on 1 to 8 neighbouring positions
- block_mask: int32 [128, 128], P('seq'), may hold values 0 or 1
Outputs:
- lin_output: bfloat16 [16384, 4096], P('seq', 'head')
- soft_output: bfloat16 [16384, 4096], P('seq', 'head')
Inputs may be any that keep to these rules, and one draw needn't show every extreme that they name: `decay_rate`: each head's rate is positive. `doc_ids`: never falls; each document covers 1 to 8 blocks, one exactly 8.
All inputs are finite; a program needn't handle non-finite values. No bound on the sum of `block_mask` on one device may be relied on, other than what follows from the above.
Results may differ from a plain program's by a relative error of at most 0.0055.
Values may be sent and summed in bfloat16 or wider, within the bound.
No kernel may reach another device: no remote copies, remote signals or barrier semaphores. Data moves between devices by JAX's collectives and lax.ppermute only.
A program may use at most 128 MiB of HBM per device.

v0:
```python
import jax
import jax.numpy as jnp
from jax import lax
from jax.sharding import PartitionSpec as P

D = 4096
BLK = 128
SPAN = 4


masked_fill = -1e30


def entering(value, axis, join, neutral):
    count, mine = (lax.axis_size(axis), lax.axis_index(axis))
    pieces = jax.tree.map(lambda part: lax.all_gather(part, axis), value)
    so_far = jax.tree.map(
        lambda part, zero: jnp.full_like(part, 0) + jnp.asarray(zero, part.dtype), value, neutral
    )

    def lap(position, so_far):
        longer = join(so_far, jax.tree.map(lambda part: part[position], pieces))
        return jax.tree.map(lambda new, old: jnp.where(position < mine, new, old), longer, so_far)

    return lax.fori_loop(0, count - 1, lap, so_far)


def passed_along(block, axis, distance):
    devices = range(lax.axis_size(axis))
    route = [(i - distance, i) for i in devices if i - distance in devices]
    return lax.ppermute(block, axis, route)


def combine_states(earlier, later):
    return (earlier[0] * later[0], later[0][:, None, None] * earlier[1] + later[1])


def per_device(
    lin_query,
    lin_key,
    lin_value,
    out_gate,
    norm_gain,
    decay_rate,
    soft_query,
    soft_key,
    soft_value,
    doc_ids,
    block_mask,
):
    rows_dev = lin_query.shape[0]
    width_local = lin_query.shape[1]
    heads_local = decay_rate.shape[0]
    head_size = width_local // heads_local
    blocks_dev = rows_dev // BLK
    block_count = doc_ids.shape[0]
    offsets = jnp.arange(BLK, dtype=jnp.float32)
    distance = offsets[:, None] - offsets[None, :]
    intra_decay = jnp.where(
        distance[None] >= 0,
        jnp.exp(-decay_rate[:, None, None] * jnp.maximum(distance, 0.0)[None]),
        0.0,
    )
    query_decay = jnp.exp(-decay_rate[None, :] * (offsets[:, None] + 1.0))
    key_decay = jnp.exp(-decay_rate[None, :] * (BLK - 1.0 - offsets[:, None]))
    block_decay = jnp.exp(-decay_rate * BLK)

    def lin_block(kv_state, inputs):
        query_part, key_part, value_part = inputs
        scores = jnp.einsum(
            "ihd,jhd->hij", query_part, key_part, preferred_element_type=jnp.float32
        )
        weights = (scores * intra_decay).astype(jnp.bfloat16)
        local_part = jnp.einsum(
            "hij,jhd->ihd", weights, value_part, preferred_element_type=jnp.float32
        )
        decayed_keys = (key_part.astype(jnp.float32) * key_decay[:, :, None]).astype(jnp.bfloat16)
        updated = block_decay[:, None, None] * kv_state + jnp.einsum(
            "jhd,jhe->hde", decayed_keys, value_part, preferred_element_type=jnp.float32
        )
        return (updated, (local_part, kv_state))

    def split_blocks(array):
        return array.reshape(blocks_dev, BLK, heads_local, head_size)

    query_blocks = split_blocks(lin_query)
    zero_state = jnp.zeros((heads_local, head_size, head_size), jnp.float32)
    local_end, scanned = lax.scan(
        lin_block, zero_state, (query_blocks, split_blocks(lin_key), split_blocks(lin_value))
    )
    local_out, prior_states = scanned
    incoming = entering(
        (jnp.exp(-decay_rate * rows_dev), local_end),
        "seq",
        combine_states,
        (jnp.ones_like(decay_rate), jnp.zeros_like(local_end)),
    )
    block_starts = jnp.arange(blocks_dev, dtype=jnp.float32) * BLK
    start_decay = jnp.exp(-decay_rate[None, :] * block_starts[:, None])
    full_states = (prior_states + start_decay[:, :, None, None] * incoming[1][None]).astype(
        jnp.bfloat16
    )
    carried = (
        jnp.einsum("bihd,bhde->bihe", query_blocks, full_states, preferred_element_type=jnp.float32)
        * query_decay[None, :, :, None]
    )
    lin_heads = (local_out + carried).reshape(rows_dev, width_local)
    square_sum = lax.psum(jnp.sum(lin_heads * lin_heads, axis=1), "head")
    inverse_rms = lax.rsqrt(square_sum / D + 1e-06)
    lin_output = (
        lin_heads
        * inverse_rms[:, None]
        * norm_gain[None, :]
        * jax.nn.sigmoid(out_gate.astype(jnp.float32))
    ).astype(jnp.bfloat16)
    device_index = lax.axis_index("seq")
    my_blocks = device_index * blocks_dev + jnp.arange(blocks_dev, dtype=jnp.int32)
    table_ids = jnp.arange(block_count, dtype=jnp.int32)
    query_matches = table_ids[None, :] == my_blocks[:, None]
    query_docs = jnp.sum(jnp.where(query_matches, doc_ids[None, :], 0), axis=1)
    local_rows = jnp.arange(rows_dev, dtype=jnp.int32)
    causal = local_rows[None, :] <= local_rows[:, None]
    soft_heads = soft_query.reshape(rows_dev, heads_local, head_size)
    score_scale = head_size ** (-0.5)

    def attend(running, packed, source):
        key_blocks = source * blocks_dev + jnp.arange(blocks_dev, dtype=jnp.int32)
        matches = table_ids[None, :] == key_blocks[:, None]
        picked = jnp.sum(jnp.where(matches[None, :, :], block_mask[:, None, :], 0), axis=2)
        key_docs = jnp.sum(jnp.where(matches, doc_ids[None, :], 0), axis=1)
        block_ok = (
            (key_blocks[None, :] < my_blocks[:, None])
            & (key_blocks[None, :] >= 0)
            & (picked == 1)
            & (key_docs[None, :] == query_docs[:, None])
        )
        same_block = key_blocks[None, :] == my_blocks[:, None]
        token_ok = (
            jnp.repeat(jnp.repeat(block_ok, BLK, axis=0), BLK, axis=1)
            | jnp.repeat(jnp.repeat(same_block, BLK, axis=0), BLK, axis=1) & causal
        )
        key_heads = packed[0].reshape(rows_dev, heads_local, head_size)
        value_heads = packed[1].reshape(rows_dev, heads_local, head_size)
        scores = (
            jnp.einsum("ihd,jhd->hij", soft_heads, key_heads, preferred_element_type=jnp.float32)
            * score_scale
        )
        masked = jnp.where(token_ok[None], scores, masked_fill)
        row_max, row_sum, accumulated = running
        new_max = jnp.maximum(row_max, jnp.max(masked, axis=2))
        weights_raw = jnp.where(token_ok[None], jnp.exp(masked - new_max[:, :, None]), 0.0)
        rescale = jnp.exp(row_max - new_max)
        row_sum = row_sum * rescale + jnp.sum(weights_raw, axis=2)
        accumulated = accumulated * rescale.T[:, :, None] + jnp.einsum(
            "hij,jhd->ihd",
            weights_raw.astype(jnp.bfloat16),
            value_heads,
            preferred_element_type=jnp.float32,
        )
        return (new_max, row_sum, accumulated)

    initial = (
        jnp.full((heads_local, rows_dev), masked_fill, jnp.float32),
        jnp.zeros((heads_local, rows_dev), jnp.float32),
        jnp.zeros((rows_dev, heads_local, head_size), jnp.float32),
    )
    own_pair = jnp.stack([soft_key, soft_value])
    running = attend(initial, own_pair, device_index)
    moving = own_pair
    for shift_count in range(1, SPAN + 1):
        moving = passed_along(moving, "seq", 1)
        running = attend(running, moving, device_index - shift_count)
    row_max, row_sum, accumulated = running
    soft_output = (
        (accumulated / row_sum.T[:, :, None]).reshape(rows_dev, width_local).astype(jnp.bfloat16)
    )
    return (lin_output, soft_output)


def solution(mesh):
    return jax.shard_map(
        per_device,
        mesh=mesh,
        in_specs=(
            P("seq", "head"),
            P("seq", "head"),
            P("seq", "head"),
            P("seq", "head"),
            P("head"),
            P("head"),
            P("seq", "head"),
            P("seq", "head"),
            P("seq", "head"),
            P(),
            P("seq", None),
        ),
        out_specs=(P("seq", "head"), P("seq", "head")),
        check_vma=False,
    )
```

profile of v0, /device:TPU:1, one launch (start us, length us, event | category | flops | bytes accessed | tf_op | source)
XLA Modules:
  0.0 323.1 jit_solution(15980316952122723341)
XLA Ops:
  7.4 1.2 copy.169
  12.2 7.4 %while.32 = (s32[]{:T(128)}, f32[8,128,128]{2,1,0:T(8,128)S(1)}, f32[2,128,8,128]{1,3,2,0:T(8,128)}, f32[2,8,128,128]{3,2,1,0:T(8,128)}, f32[8]{0:T(128)S(1)}, /...) while((s32[]{:T(128)}, f32[8,128,128]{2,1,0:T(8,128)S(1)}, ...), condition=%wide.region_1.2_spmd.clone.clone.clone, body=%wide.region_0.1_spmd.clone.clone.clone.sunk | while | flops 102106112 | bytes 5072640 | solution.py:88
  13.7 2.3 fusion.166
  17.4 2.3 fusion.166
  20.5 1.3 copy.164
  21.7 1.2 copy.131
  24.1 4.9 %collective-permute-start = (bf16[2,256,1024]{1,2,0:T(8,128)(2,1)}, bf16[2,256,1024]{1,2,0:T(8,128)(2,1)S(1)}, u32[]{:S(2)}, u32[]{:S(2)}) collective-permute-start(bf16[2,256,1024]{1,2,0:T(8,128)(2,1)} %pad_maximum_fusion), channel_id=1, source_target_pairs={{0,4},{4,8},{8,12},{12,16},{16,20},{20,24},{24,28},{28,32},{32,36}... | collective-permute-start | bytes 3145736 | tf_op jit(solution)/shard_map/ppermute | solution.py:31
  29.0 141.6 %all-reduce = f32[512]{0:T(512)S(1)} all-reduce(f32[512]{0:T(512)S(1)} %get-tuple-element.414), channel_id=2, replica_groups=mesh['seq'=64,'head'=4] {'seq'}, use_global_device_ids=true, to_apply=%add | all-reduce | flops 512 | bytes 4096
  173.2 1.9 collective-permute-start.1
  176.0 10.9 %collective-permute-done.1 = bf16[2,256,1024]{1,2,0:T(8,128)(2,1)} collective-permute-done((bf16[2,256,1024]{1,2,0:T(8,128)(2,1)S(1)}, bf16[2,256,1024]{1,2,0:T(8,128)(2,1)}, u32[]{:S(2)}, u32[]{:S(2)}) %collective-permute-start.1) | collective-permute-done | bytes 1048608 | tf_op jit(solution)/shard_map/ppermute | solution.py:31
  186.9 4.5 %collective-permute-start.2 = (bf16[2,256,1024]{1,2,0:T(8,128)(2,1)}, bf16[2,256,1024]{1,2,0:T(8,128)(2,1)S(1)}, u32[]{:S(2)}, u32[]{:S(2)}) collective-permute-start(bf16[2,256,1024]{1,2,0:T(8,128)(2,1)} %collective-permute-done.1), channel_id=1, source_target_pairs={{0,4},{4,8},{8,12},{12,16},{16,20},{20,24},{24,28},{28,32},{32,36}... | collective-permute-start | bytes 3145736 | tf_op jit(solution)/shard_map/ppermute | solution.py:31
  191.5 1.6 fusion.22
  193.7 9.8 %collective-permute-done.2 = bf16[2,256,1024]{1,2,0:T(8,128)(2,1)S(1)} collective-permute-done((bf16[2,256,1024]{1,2,0:T(8,128)(2,1)}, bf16[2,256,1024]{1,2,0:T(8,128)(2,1)S(1)}, u32[]{:S(2)}, u32[]{:S(2)}) %collective-permute-start.2) | collective-permute-done | bytes 1048608 | tf_op jit(solution)/shard_map/ppermute | solution.py:31
  203.4 4.5 %collective-permute-start.3 = (bf16[2,256,1024]{1,2,0:T(8,128)(2,1)S(1)}, bf16[2,256,1024]{1,2,0:T(8,128)(2,1)S(1)}, u32[]{:S(2)}, u32[]{:S(2)}) collective-permute-start(bf16[2,256,1024]{1,2,0:T(8,128)(2,1)S(1)} %collective-permute-done.2), channel_id=1, source_target_pairs={{0,4},{4,8},{8,12},{12,16},{16,20},{20,24},{24,28},{28,32},{32,36}... | collective-permute-start | bytes 3145736 | tf_op jit(solution)/shard_map/ppermute | solution.py:31
  207.9 1.3 fusion.144
  210.4 9.1 %collective-permute-done.3 = bf16[2,256,1024]{1,2,0:T(8,128)(2,1)S(1)} collective-permute-done((bf16[2,256,1024]{1,2,0:T(8,128)(2,1)S(1)}, bf16[2,256,1024]{1,2,0:T(8,128)(2,1)S(1)}, u32[]{:S(2)}, u32[]{:S(2)}) %collective-permute-start.3) | collective-permute-done | bytes 1048608 | tf_op jit(solution)/shard_map/ppermute | solution.py:31
  227.2 76.6 %while.31 = (s32[]{:T(128)}, f32[8,128,128]{2,1,0:T(8,128)S(1)}, s32[]{:T(128)}, f32[64,8]{1,0:T(8,128)S(1)}, f32[64,8,128,128]{3,2,1,0:T(8,128)}, /*index=5*/s32[]{:T(128)}, s32[]{:T(128)}) while((s32[]{:T(128)}, f32[8,128,128]{2,1,0:T(8,128)S(1)}, s32[]{:T(128)}, f32[64,8]{1,0:T(8,128)S(1)}, f32[64,8,128,128]{3,2,1,0:T(8,128)}, ...), condition=%wide.region_3.4_spmd.clone, body=%wide.region_2.3_spmd.clone.sunk | while | flops 524292 | bytes 1573073 | solution.py:25
  228.4 1.2 fusion.164
  234.5 1.2 fusion.164
  235.7 1.2 fusion.164
  237.0 1.2 fusion.164
  238.2 1.2 fusion.164
  239.4 1.2 fusion.164
  240.6 1.2 fusion.164
  246.7 1.2 fusion.164
  247.9 1.2 fusion.164
  249.1 1.2 fusion.164
  250.3 1.2 fusion.164
  251.6 1.2 fusion.164
  257.6 1.2 fusion.164
  258.9 1.2 fusion.164
  260.1 1.2 fusion.164
  261.3 1.2 fusion.164
  262.5 1.2 fusion.164
  263.7 1.2 fusion.164
  269.8 1.2 fusion.164
  271.0 1.2 fusion.164
  272.3 1.2 fusion.164
  273.5 1.2 fusion.164
  274.7 1.2 fusion.164
  280.8 1.2 fusion.164
  282.0 1.2 fusion.164
  283.2 1.2 fusion.164
  284.4 1.2 fusion.164
  285.6 1.2 fusion.164
  303.9 2.2 multiply_reduce_fusion
  306.5 8.6 %psum.7 = f32[256]{0:T(256)S(1)} all-reduce(f32[256]{0:T(256)S(1)} %bitcast.435), channel_id=1, replica_groups=mesh['seq'=64,'head'=4] {'head'}, use_global_device_ids=true, to_apply=%region_5.6 | all-reduce | flops 256 | bytes 2048 | tf_op jit(solution)/shard_map/psum | solution.py:108
  315.0 1.2 fusion.57
  (221 shorter events, 62.7 us)
Async XLA Ops:
  7.2 184.3 %copy-start = (bf16[256,1024]{1,0:T(8,128)(2,1)S(1)}, bf16[256,1024]{1,0:T(8,128)(2,1)}, u32[]{:S(2)}) copy-start(bf16[256,1024]{1,0:T(8,128)(2,1)} %param.21) | copy-start | bytes 1572868
  7.2 2.5 copy-start.3
  7.2 220.0 %all-gather.4.cloned.1.call-start = ((), (), s32[]{:S(2)}) async-start(), calls=%async_computation | async-start | bytes 34078720 | tf_op jit(solution)/shard_map/all_gather | solution.py:16
  7.4 3.4 %copy-start.9 = (u32[256]{0:T(256)S(1)}, u32[256]{0:T(256)}, u32[]{:S(2)}) copy-start(u32[256]{0:T(256)} %constant.93) | copy-start | bytes 3076
  7.4 4.7 %copy-start.7 = (f32[8]{0:T(128)S(1)}, f32[8]{0:T(128)}, u32[]{:S(2)}) copy-start(f32[8]{0:T(128)} %param.20) | copy-start | bytes 100
  19.6 0.8 copy-start.2
  20.4 150.6 %copy-start.6 = (s32[2,128]{1,0:T(2,128)S(1)}, s32[2,128]{1,0:T(2,128)}, u32[]{:S(2)}) copy-start(s32[2,128]{1,0:T(2,128)} %param.25) | copy-start | bytes 3076
  20.5 150.9 %copy-start.8 = (s32[128]{0:T(128)S(1)}, s32[128]{0:T(128)}, u32[]{:S(2)}) copy-start(s32[128]{0:T(128)} %param.24) | copy-start | bytes 1540
  24.1 149.2 %collective-permute-start = (bf16[2,256,1024]{1,2,0:T(8,128)(2,1)}, bf16[2,256,1024]{1,2,0:T(8,128)(2,1)S(1)}, u32[]{:S(2)}, u32[]{:S(2)}) collective-permute-start(bf16[2,256,1024]{1,2,0:T(8,128)(2,1)} %pad_maximum_fusion), channel_id=1, source_target_pairs={{0,4},{4,8},{8,12},{12,16},{16,20},{20,24},{24,28},{28,32},{32,36}... | collective-permute-start | bytes 3145736 | tf_op jit(solution)/shard_map/ppermute | solution.py:31
  173.2 13.6 %collective-permute-start.1 = (bf16[2,256,1024]{1,2,0:T(8,128)(2,1)S(1)}, bf16[2,256,1024]{1,2,0:T(8,128)(2,1)}, u32[]{:S(2)}, u32[]{:S(2)}) collective-permute-start(bf16[2,256,1024]{1,2,0:T(8,128)(2,1)S(1)} %collective-permute-done), channel_id=1, source_target_pairs={{0,4},{4,8},{8,12},{12,16},{16,20},{20,24},{24,28},{28,32},{32,36}... | collective-permute-start | bytes 3145736 | tf_op jit(solution)/shard_map/ppermute | solution.py:31
  186.9 16.5 %collective-permute-start.2 = (bf16[2,256,1024]{1,2,0:T(8,128)(2,1)}, bf16[2,256,1024]{1,2,0:T(8,128)(2,1)S(1)}, u32[]{:S(2)}, u32[]{:S(2)}) collective-permute-start(bf16[2,256,1024]{1,2,0:T(8,128)(2,1)} %collective-permute-done.1), channel_id=1, source_target_pairs={{0,4},{4,8},{8,12},{12,16},{16,20},{20,24},{24,28},{28,32},{32,36}... | collective-permute-start | bytes 3145736 | tf_op jit(solution)/shard_map/ppermute | solution.py:31
  203.4 16.0 %collective-permute-start.3 = (bf16[2,256,1024]{1,2,0:T(8,128)(2,1)S(1)}, bf16[2,256,1024]{1,2,0:T(8,128)(2,1)S(1)}, u32[]{:S(2)}, u32[]{:S(2)}) collective-permute-start(bf16[2,256,1024]{1,2,0:T(8,128)(2,1)S(1)} %collective-permute-done.2), channel_id=1, source_target_pairs={{0,4},{4,8},{8,12},{12,16},{16,20},{20,24},{24,28},{28,32},{32,36}... | collective-permute-start | bytes 3145736 | tf_op jit(solution)/shard_map/ppermute | solution.py:31
  306.0 9.0 %copy-start.4 = (bf16[256,1024]{1,0:T(8,128)(2,1)S(1)}, bf16[256,1024]{1,0:T(8,128)(2,1)}, u32[]{:S(2)}) copy-start(bf16[256,1024]{1,0:T(8,128)(2,1)} %param.18) | copy-start | bytes 1572868
  306.1 9.0 %copy-start.5 = (f32[1024]{0:T(1024)S(1)}, f32[1024]{0:T(1024)}, u32[]{:S(2)}) copy-start(f32[1024]{0:T(1024)} %param.19) | copy-start | bytes 12292
  306.1 10.2 %copy-start.1 = (bf16[256,1024]{1,0:T(8,128)(2,1)S(1)}, bf16[256,1024]{1,0:T(8,128)(2,1)}, u32[]{:S(2)}) copy-start(bf16[256,1024]{1,0:T(8,128)(2,1)} %param.21) | copy-start | bytes 1572868
Sparse Core Ops, SparseCore 0:
  20.6 151.5 all-gather.3
where the time goes:
time: 328 us; the launch traced here: 323 us
  blocking collectives  150 us (46%)
  other arithmetic  82.1 us (25%)
  waiting for transfers between devices  29.8 us (9%)
  starting transfers between devices  15.8 us (5%)
  between operations  15.3 us (5%)
  matrix products  15 us (5%)
  local copies, waits for them, and re-layouts  12.9 us (4%)
    unnamed x1, blocking collectives  142 us
    select_n x63, other arithmetic, lap(): jnp.where(position < mine, new, old)  73.9 us
    ppermute x4, waiting for transfers between devices, passed_along(): return lax.ppermute(block, axis, route)  29.7 us
    ppermute x4, starting transfers between devices, passed_along(): return lax.ppermute(block, axis, route)  15.8 us
    psum x1, blocking collectives, per_device(): square_sum = lax.psum(jnp.sum(lin_heads * lin_heads, axis=1), 'head')  8.55 us
    unnamed x48, local copies, waits for them, and re-layouts  7.93 us
  transfers between devices with their start and end apart: 5, of which 3 were waited for; matrix products, arithmetic and copies ran while one was open for 6% of the time, Pallas kernels for 0%

commit v1 on v0

v1 whole, which is shorter than its diff:
```python
import math

import jax
import jax.numpy as jnp
from jax import lax
from jax.experimental import pallas as pl
from jax.experimental.pallas import tpu as pltpu
from jax.sharding import PartitionSpec as P

HD = 128
BLK = 128
NBLK = 128
ROWS = 256
LOCAL = 8
WIDTH = LOCAL * HD
D = 4096
SHARDS = 64
FILL = -1e30
EXP2_SCALE = HD ** (-0.5) * math.log2(math.e)

f32 = jnp.float32
bf16 = jnp.bfloat16

SMEM = pl.BlockSpec(memory_space=pltpu.SMEM)
VMEM = pl.BlockSpec(memory_space=pltpu.VMEM)


def call(body, outs, ins, specs, flops, scratch=()):
    moved = sum(math.prod(x.shape) * x.dtype.itemsize for x in (*ins, *outs))
    return pl.pallas_call(
        body,
        out_shape=outs,
        in_specs=specs,
        out_specs=[VMEM] * len(outs),
        scratch_shapes=list(scratch),
        compiler_params=pltpu.CompilerParams(vmem_limit_bytes=32 * 1024 * 1024),
        cost_estimate=pl.CostEstimate(flops=flops, bytes_accessed=moved, transcendentals=0),
    )(*ins)


def cols(h):
    return slice(h * HD, (h + 1) * HD)


def dot(a, b, dims):
    return lax.dot_general(a, b, (dims, ((), ())), preferred_element_type=f32)


def exact_dot(a, b, dims):
    return lax.dot_general(
        a, b, (dims, ((), ())), precision=lax.Precision.HIGHEST, preferred_element_type=f32
    )


def state_body(rate, k, v, out):
    back = (ROWS - 1.0) - lax.broadcasted_iota(jnp.int32, (ROWS, HD), 0).astype(f32)
    for h in range(LOCAL):
        decayed = (k[:, cols(h)].astype(f32) * jnp.exp(-rate[h] * back)).astype(bf16)
        out[cols(h), :] = dot(decayed, v[:, cols(h)], ((0,), (0,))).astype(bf16)


def prefix_body(index, rate, parts, out):
    step = jnp.exp(jnp.full((16, HD), -rate[index[0] // 8] * ROWS, f32))
    state = jnp.zeros((16, HD), f32)
    for i in range(SHARDS):
        out[i] = state.astype(bf16)
        if i + 1 < SHARDS:
            state = step * state + parts[i].astype(f32)


def inner_body(rate, q, k, v, out):
    row = lax.broadcasted_iota(jnp.int32, (ROWS, ROWS), 0)
    col = lax.broadcasted_iota(jnp.int32, (ROWS, ROWS), 1)
    gap = (row - col).astype(f32)
    for h in range(LOCAL):
        decay = jnp.where(row >= col, jnp.exp(-rate[h] * jnp.maximum(gap, 0.0)), 0.0)
        scores = dot(q[:, cols(h)], k[:, cols(h)], ((1,), (1,)))
        out[:, cols(h)] = dot((scores * decay).astype(bf16), v[:, cols(h)], ((1,), (0,)))


def carry_body(rate, inner, q, state, heads, squares):
    ahead = lax.broadcasted_iota(jnp.int32, (ROWS, HD), 0).astype(f32) + 1.0
    total = jnp.zeros((ROWS, HD), f32)
    for h in range(LOCAL):
        carried = dot(q[:, cols(h)], state[cols(h), :], ((1,), (0,)))
        value = inner[:, cols(h)] + carried * jnp.exp(-rate[h] * ahead)
        heads[:, cols(h)] = value
        total = total + value * value
    squares[...] = exact_dot(jnp.ones((8, HD), f32), total, ((1,), (1,)))


def norm_body(heads, gate, gain, s0, s1, s2, s3, out):
    total = s0[...] + s1[...] + s2[...] + s3[...]
    first = (lax.broadcasted_iota(jnp.int32, (8, HD), 0) == 0).astype(f32)
    spread = exact_dot(total, first, ((0,), (0,)))
    inverse = lax.rsqrt(spread / D + 1e-06)
    for h in range(LOCAL):
        scale = gain[:, cols(h)] * jax.nn.sigmoid(gate[:, cols(h)].astype(f32))
        out[:, cols(h)] = (heads[:, cols(h)] * inverse * scale).astype(bf16)


def block_ok(docs, mask, i, query, key):
    q_at = jnp.clip(query, 0, NBLK - 1)
    k_at = jnp.clip(key, 0, NBLK - 1)
    inside = (key >= 0) & (key < query) & (query < NBLK)
    return inside & (mask[i, k_at] == 1) & (docs[k_at] == docs[q_at])


def fill_bias(bias, at, docs, mask, query, key, own):
    for i in range(2):
        for j in range(2):
            rows = slice(i * BLK, (i + 1) * BLK)
            columns = slice(at + j * BLK, at + (j + 1) * BLK)
            if own and i == j:
                row = lax.broadcasted_iota(jnp.int32, (BLK, BLK), 0)
                col = lax.broadcasted_iota(jnp.int32, (BLK, BLK), 1)
                bias[rows, columns] = jnp.where(col <= row, 0.0, FILL)
            else:
                ok = block_ok(docs, mask, i, query + i, key + j)
                bias[rows, columns] = jnp.full((BLK, BLK), jnp.where(ok, 0.0, FILL), f32)


def attend_head(q, keys, values, bias):
    scores = dot(q, keys, ((1,), (1,))) + bias
    top = jnp.max(scores, axis=1, keepdims=True)
    weights = jnp.exp2((scores - top) * EXP2_SCALE).astype(bf16)
    ones = jnp.ones(values.shape, bf16)
    both = dot(weights, jnp.concatenate([values, ones], axis=1), ((1,), (0,)))
    return both[:, :HD], top, both[:, HD:]


def joined(refs, h):
    return jnp.concatenate([ref[:, cols(h)] for ref in refs], axis=0)


def far_body(index, docs, mask, q, k1, k2, v1, v2, out, stats, bias):
    me = index[0]
    query = 2 * (me + 2)
    fill_bias(bias, 0, docs, mask, query, 2 * (me - 2), False)
    fill_bias(bias, ROWS, docs, mask, query, 2 * ((me ^ 1) - 2), False)
    lane = lax.broadcasted_iota(jnp.int32, (ROWS, HD), 1)
    table = jnp.zeros((ROWS, HD), f32)
    for h in range(LOCAL):
        acc, top, total = attend_head(
            q[:, cols(h)], joined((k1, k2), h), joined((v1, v2), h), bias[...]
        )
        out[:, cols(h)] = (acc / total).astype(bf16)
        table = jnp.where(lane == h, top, table)
        table = jnp.where(lane == LOCAL + h, total, table)
    stats[...] = table.T[: 2 * LOCAL, :]


def near_body(
    index, docs, mask, q, k0, k1, k2, k3, v0, v1, v2, v3, out, tops, sums, bias
):
    me = index[0]
    query = 2 * me
    for at, source in enumerate((me, me ^ 1, me - 2, (me ^ 1) - 2)):
        fill_bias(bias, at * ROWS, docs, mask, query, 2 * source, at == 0)
    lane = lax.broadcasted_iota(jnp.int32, (ROWS, HD), 1)
    top_table = jnp.zeros((ROWS, HD), f32)
    sum_table = jnp.zeros((ROWS, HD), f32)
    for h in range(LOCAL):
        acc, top, total = attend_head(
            q[:, cols(h)], joined((k0, k1, k2, k3), h), joined((v0, v1, v2, v3), h), bias[...]
        )
        out[:, cols(h)] = acc
        top_table = jnp.where(lane == h, top, top_table)
        sum_table = jnp.where(lane == h, total, sum_table)
    tops[...] = top_table
    sums[...] = sum_table


def merge_body(near, tops, sums, far, stats, out):
    table = jnp.concatenate([stats[...], jnp.zeros((HD - 2 * LOCAL, ROWS), f32)], axis=0).T
    for h in range(LOCAL):
        top1 = tops[:, h : h + 1]
        sum1 = sums[:, h : h + 1]
        top2 = table[:, h : h + 1]
        sum2 = table[:, LOCAL + h : LOCAL + h + 1]
        top = jnp.maximum(top1, top2)
        scale1 = jnp.exp2((top1 - top) * EXP2_SCALE)
        scale2 = jnp.exp2((top2 - top) * EXP2_SCALE) * sum2
        total = scale1 * sum1 + scale2
        value = near[:, cols(h)] * (scale1 / total) + far[:, cols(h)].astype(f32) * (scale2 / total)
        out[:, cols(h)] = value.astype(bf16)


def shifted(x, distance):
    return lax.ppermute(x, "seq", [(i, (i + distance) % SHARDS) for i in range(SHARDS)])


def swapped(x):
    return lax.ppermute(x, "seq", [(i, i ^ 1) for i in range(SHARDS)])


def turned(x, distance):
    return lax.ppermute(x, "head", [(i, (i + distance) % 4) for i in range(4)])


def per_device(
    lin_query,
    lin_key,
    lin_value,
    out_gate,
    norm_gain,
    decay_rate,
    soft_query,
    soft_key,
    soft_value,
    doc_ids,
    block_mask,
):
    like = jax.ShapeDtypeStruct
    index = lax.axis_index("seq").astype(jnp.int32).reshape(1)
    wide = like((ROWS, WIDTH), f32)
    narrow = like((ROWS, WIDTH), bf16)

    key1 = shifted(soft_key, 2)
    value1 = shifted(soft_value, 2)
    query1 = shifted(soft_query, -2)
    mask1 = shifted(block_mask, -2)
    key_other = swapped(soft_key)
    value_other = swapped(soft_value)
    key2 = swapped(key1)
    value2 = swapped(value1)

    (state,) = call(
        state_body,
        [like((WIDTH, HD), bf16)],
        (decay_rate, lin_key, lin_value),
        [SMEM, VMEM, VMEM],
        2 * ROWS * WIDTH * HD,
    )
    parts = lax.all_to_all(state.reshape(SHARDS, 16, HD), "seq", 0, 0)
    (prefix,) = call(
        prefix_body,
        [like((SHARDS, 16, HD), bf16)],
        (index, decay_rate, parts),
        [SMEM, SMEM, VMEM],
        4 * SHARDS * 16 * HD,
    )
    entering = lax.all_to_all(prefix, "seq", 0, 0).reshape(WIDTH, HD)
    (inner,) = call(
        inner_body,
        [wide],
        (decay_rate, lin_query, lin_key, lin_value),
        [SMEM, VMEM, VMEM, VMEM],
        4 * ROWS * ROWS * WIDTH,
    )
    heads, squares = call(
        carry_body,
        [wide, like((8, ROWS), f32)],
        (decay_rate, inner, lin_query, entering),
        [SMEM, VMEM, VMEM, VMEM],
        2 * ROWS * WIDTH * HD,
    )
    others = [turned(squares, d) for d in (1, 2, 3)]
    (lin_output,) = call(
        norm_body,
        [narrow],
        (heads, out_gate, norm_gain.reshape(1, WIDTH), squares, *others),
        [VMEM] * 7,
        8 * ROWS * WIDTH,
    )

    far, far_stats = call(
        far_body,
        [narrow, like((2 * LOCAL, ROWS), f32)],
        (index, doc_ids, mask1, query1, key1, key2, value1, value2),
        [SMEM] * 3 + [VMEM] * 5,
        4 * ROWS * 2 * ROWS * WIDTH,
        [pltpu.VMEM((ROWS, 2 * ROWS), f32)],
    )
    far = shifted(far, 2)
    far_stats = shifted(far_stats, 2)
    near, tops, sums = call(
        near_body,
        [wide, like((ROWS, HD), f32), like((ROWS, HD), f32)],
        (
            index, doc_ids, block_mask, soft_query,
            soft_key, key_other, key1, key2,
            soft_value, value_other, value1, value2,
        ),
        [SMEM] * 3 + [VMEM] * 9,
        4 * ROWS * 4 * ROWS * WIDTH,
        [pltpu.VMEM((ROWS, 4 * ROWS), f32)],
    )
    (soft_output,) = call(
        merge_body,
        [narrow],
        (near, tops, sums, far, far_stats),
        [VMEM] * 5,
        8 * ROWS * WIDTH,
    )
    return (lin_output, soft_output)


def solution(mesh):
    rows = P("seq", "head")
    return jax.shard_map(
        per_device,
        mesh=mesh,
        in_specs=(
            rows, rows, rows, rows, P("head"), P("head"), rows, rows, rows, P(), P("seq", None),
        ),
        out_specs=(rows, rows),
        check_vma=False,
    )
```

time: 328 us -> 83.5 us (0.25)
  the two profiles are of different devices: /device:TPU:1 before, /device:TPU:38 now
where the time goes in v1:
time: 83.5 us; the launch traced here: 83 us
  starting transfers between devices  30.4 us (36%)
  waiting for transfers between devices  30.2 us (36%)
  Pallas kernels  17.8 us (21%)
  local copies, waits for them, and re-layouts  3.83 us (5%)
    pallas_call x8, Pallas kernels, call(): pl.pallas_call(body, out_shape=outs, in_specs=specs, out_specs=[VMEM] * l...  17.8 us
    ppermute x6, waiting for transfers between devices, shifted(): lax.ppermute(x, 'seq', [(i, (i + distance) % SHARDS) for i in range(SHARD...  15.3 us
    all_to_all x1, waiting for transfers between devices, per_device(): parts = lax.all_to_all(state.reshape(SHARDS, 16, HD), 'seq', 0, 0)  10.1 us
    all_to_all x1, starting transfers between devices, per_device(): parts = lax.all_to_all(state.reshape(SHARDS, 16, HD), 'seq', 0, 0)  10.1 us
    ppermute x6, starting transfers between devices, shifted(): lax.ppermute(x, 'seq', [(i, (i + distance) % SHARDS) for i in range(SHARD...  10 us
    all_to_all x1, starting transfers between devices, per_device(): entering = lax.all_to_all(prefix, 'seq', 0, 0).reshape(WIDTH, HD)  6.36 us
    ppermute x3, waiting for transfers between devices, turned(): return lax.ppermute(x, 'head', [(i, (i + distance) % 4) for i in range(4)])  4.78 us
    ppermute x3, starting transfers between devices, turned(): return lax.ppermute(x, 'head', [(i, (i + distance) % 4) for i in range(4)])  3.9 us
  transfers between devices with their start and end apart: 15, of which 6 were waited for; matrix products, arithmetic and copies ran while one was open for 0% of the time, Pallas kernels for 18%

profile of v1, /device:TPU:38, one launch (start us, length us, event | category | flops | bytes accessed | tf_op | source)
XLA Modules:
  0.0 83.0 jit_solution(230035024823989554)
XLA Ops:
  0.6 2.0 %collective-permute-start.4 = (bf16[256,1024]{1,0:T(8,128)(2,1)}, bf16[256,1024]{1,0:T(8,128)(2,1)S(1)}, u32[]{:S(2)}, u32[]{:S(2)}) collective-permute-start(bf16[256,1024]{1,0:T(8,128)(2,1)} %k0.1), channel_id=1, source_target_pairs={{0,8},{4,12},{8,16},{12,20},{16,24},{20,28},{24,32},{28,36},{32,40... | collective-permute-start | bytes 1572872 | tf_op jit(solution)/shard_map/ppermute | solution.py:190
  2.6 1.9 %collective-permute-start.7 = (bf16[256,1024]{1,0:T(8,128)(2,1)}, bf16[256,1024]{1,0:T(8,128)(2,1)S(1)}, u32[]{:S(2)}, u32[]{:S(2)}) collective-permute-start(bf16[256,1024]{1,0:T(8,128)(2,1)} %v0.1), channel_id=1, source_target_pairs={{0,8},{4,12},{8,16},{12,20},{16,24},{20,28},{24,32},{28,36},{32,40... | collective-permute-start | bytes 1572872 | tf_op jit(solution)/shard_map/ppermute | solution.py:190
  4.5 1.0 %copy-done = bf16[256,1024]{1,0:T(8,128)(2,1)S(1)} copy-done((bf16[256,1024]{1,0:T(8,128)(2,1)S(1)}, bf16[256,1024]{1,0:T(8,128)(2,1)}, u32[]{:S(2)}) %copy-start) | copy-done | bytes 524312
  5.6 1.0 %copy-done.2 = bf16[256,1024]{1,0:T(8,128)(2,1)S(1)} copy-done((bf16[256,1024]{1,0:T(8,128)(2,1)S(1)}, bf16[256,1024]{1,0:T(8,128)(2,1)}, u32[]{:S(2)}) %copy-start.2) | copy-done | bytes 524312
  6.6 0.7 copy-done.11
  7.3 1.7 %shard_map.123 = bf16[1024,128]{1,0:T(8,128)(2,1)} custom-call(f32[8]{0:T(128)S(1)} %copy-done.11, bf16[256,1024]{1,0:T(8,128)(2,1)S(1)} %copy-done, bf16[256,1024]{1,0:T(8,128)(2,1)S(1)} %copy-done.2), custom_call_target="tpu_custom_call" | custom-call | flops 67108864 | bytes 1310752 | tf_op jit(solution)/shard_map/pallas_call | solution.py:30
  9.0 10.1 %all-to-all-start = ((bf16[64,16,128]{2,1,0:T(8,128)(2,1)}), bf16[64,16,128]{2,1,0:T(8,128)(2,1)S(1)}, u32[]{:S(2)}, u32[]{:S(2)}) async-start(bf16[64,16,128]{2,1,0:T(8,128)(2,1)} %bitcast.1), calls=%async_computation | async-start | bytes 524288 | tf_op jit(solution)/shard_map/all_to_all | solution.py:235
  19.1 0.5 collective-permute-start.10
  19.6 0.0 collective-permute-done.4.k2.k1
  19.6 0.0 collective-permute-start.5
  19.7 8.9 %collective-permute-done.7.v2.v1 = bf16[256,1024]{1,0:T(8,128)(2,1)S(1)} collective-permute-done((bf16[256,1024]{1,0:T(8,128)(2,1)}, bf16[256,1024]{1,0:T(8,128)(2,1)S(1)}, u32[]{:S(2)}, u32[]{:S(2)}) %collective-permute-start.7) | collective-permute-done | bytes 524320 | tf_op jit(solution)/shard_map/ppermute | solution.py:190
  28.5 0.0 collective-permute-start.8
  28.5 10.1 %all-to-all-done.parts = bf16[64,16,128]{2,1,0:T(8,128)(2,1)S(1)} async-done(((bf16[64,16,128]{2,1,0:T(8,128)(2,1)}), bf16[64,16,128]{2,1,0:T(8,128)(2,1)S(1)}, u32[]{:S(2)}, u32[]{:S(2)}) %all-to-all-start) | async-done | bytes 262176 | tf_op jit(solution)/shard_map/all_to_all | solution.py:235
  38.6 0.0 copy-done.12
  38.6 1.4 %shard_map.124 = bf16[64,16,128]{2,1,0:T(8,128)(2,1)} custom-call(s32[1]{0:T(128)} %bitcast.index, f32[8]{0:T(128)S(1)} %copy-done.12, bf16[64,16,128]{2,1,0:T(8,128)(2,1)S(1)} %all-to-all-done.parts), custom_call_target="tpu_custom_call" | custom-call | flops 524288 | bytes 524324 | tf_op jit(solution)/shard_map/pallas_call | solution.py:30
  40.0 6.4 %all-to-all-start.1 = ((bf16[64,16,128]{2,1,0:T(8,128)(2,1)}), bf16[64,16,128]{2,1,0:T(8,128)(2,1)S(1)}, u32[]{:S(2)}, u32[]{:S(2)}) async-start(bf16[64,16,128]{2,1,0:T(8,128)(2,1)} %shard_map.124), calls=%async_computation.1 | async-start | bytes 524288 | tf_op jit(solution)/shard_map/all_to_all | solution.py:243
  46.4 0.0 copy-start.1
  46.4 0.0 copy-start.3
  46.4 0.0 copy-start.4
  46.4 0.5 collective-permute-start.9
  47.0 0.0 collective-permute-start.3
  47.0 6.4 %collective-permute-done.9.mask = s32[2,128]{1,0:T(2,128)S(1)} collective-permute-done((s32[2,128]{1,0:T(2,128)S(1)}, s32[2,128]{1,0:T(2,128)S(1)}, u32[]{:S(2)}, u32[]{:S(2)}) %collective-permute-start.9) | collective-permute-done | bytes 1056 | tf_op jit(solution)/shard_map/ppermute | solution.py:190
  53.4 0.0 collective-permute-start.6
  53.4 0.0 collective-permute-done.10.q
  53.4 0.0 collective-permute-done.5.k3.k2
  53.4 0.0 collective-permute-done.8.v3.v2
  53.5 3.5 %shard_map.128 = (bf16[256,1024]{1,0:T(8,128)(2,1)}, f32[16,256]{1,0:T(8,128)S(1)}) custom-call(s32[1]{0:T(128)} %bitcast.index, s32[128]{0:T(128)S(1)} %copy-done.14, s32[2,128]{1,0:T(2,128)S(1)} %collective-permute-done.9.mask, bf16[256,1024]{1,0:T(8,128)(2,1)} %collective-permute-done.10.q, bf16[256,1024]{1,0:T(8,128)(2,1)S(1)} %collective-permute-done.4.k2.k1, ...), custom_call_target="tpu_custom_call" | custom-call | flops 536870912 | bytes 3163652 | tf_op jit(solution)/shard_map/pallas_call | solution.py:30
  56.9 0.4 collective-permute-start.11
  57.4 1.5 %shard_map.122.inner = f32[256,1024]{1,0:T(8,128)S(1)} custom-call(f32[8]{0:T(128)S(1)} %copy-done.12, bf16[256,1024]{1,0:T(8,128)(2,1)S(1)} %copy-done.4, bf16[256,1024]{1,0:T(8,128)(2,1)S(1)} %copy-done.1, bf16[256,1024]{1,0:T(8,128)(2,1)S(1)} %copy-done.3), custom_call_target="tpu_custom_call" | custom-call | flops 268435456 | bytes 2621472 | tf_op jit(solution)/shard_map/pallas_call | solution.py:30
  58.9 0.0 all-to-all-done.1
  58.9 0.0 copy-start.5
  58.9 1.0 %copy-done.5 = bf16[256,1024]{1,0:T(8,128)(2,1)S(1)} copy-done((bf16[256,1024]{1,0:T(8,128)(2,1)S(1)}, bf16[256,1024]{1,0:T(8,128)(2,1)}, u32[]{:S(2)}) %copy-start.5) | copy-done | bytes 524312
  59.9 1.2 %shard_map.125 = (f32[256,1024]{1,0:T(8,128)S(1)}, f32[8,256]{1,0:T(8,128)S(1)}) custom-call(f32[8]{0:T(128)S(1)} %copy-done.12, f32[256,1024]{1,0:T(8,128)S(1)} %shard_map.122.inner, bf16[256,1024]{1,0:T(8,128)(2,1)S(1)} %copy-done.5, bf16[1024,128]{1,0:T(8,128)(2,1)S(1)} %bitcast.4), custom_call_target="tpu_custom_call" | custom-call | flops 67108864 | bytes 2891808 | tf_op jit(solution)/shard_map/pallas_call | solution.py:30
  61.1 0.6 collective-permute-start
  61.8 2.4 %collective-permute-start.1 = (f32[8,256]{1,0:T(8,128)S(1)}, f32[8,256]{1,0:T(8,128)S(1)}, u32[]{:S(2)}, u32[]{:S(2)}) collective-permute-start(f32[8,256]{1,0:T(8,128)S(1)} %get-tuple-element.10.s0), channel_id=1, source_target_pairs={{0,2},{1,3},{2,0},{3,1},{4,6},{5,7},{6,4},{7,5},{8,10},{9,11},{10,... | collective-permute-start | bytes 24584 | tf_op jit(solution)/shard_map/ppermute | solution.py:198
  64.2 0.8 collective-permute-done.s1
  65.0 0.8 collective-permute-start.2
  65.8 1.2 %collective-permute-done.1.s2 = f32[8,256]{1,0:T(8,128)S(1)} collective-permute-done((f32[8,256]{1,0:T(8,128)S(1)}, f32[8,256]{1,0:T(8,128)S(1)}, u32[]{:S(2)}, u32[]{:S(2)}) %collective-permute-start.1) | collective-permute-done | bytes 8224 | tf_op jit(solution)/shard_map/ppermute | solution.py:198
  67.0 2.9 %collective-permute-done.2.s3 = f32[8,256]{1,0:T(8,128)S(1)} collective-permute-done((f32[8,256]{1,0:T(8,128)S(1)}, f32[8,256]{1,0:T(8,128)S(1)}, u32[]{:S(2)}, u32[]{:S(2)}) %collective-permute-start.2) | collective-permute-done | bytes 8224 | tf_op jit(solution)/shard_map/ppermute | solution.py:198
  69.8 0.0 copy-start.9
  69.9 1.3 %shard_map.126 = bf16[256,1024]{1,0:T(8,128)(2,1)} custom-call(f32[256,1024]{1,0:T(8,128)S(1)} %get-tuple-element.9.heads, bf16[256,1024]{1,0:T(8,128)(2,1)S(1)} %copy-done.10, f32[1,1024]{1,0:T(1,128)S(1)} %bitcast.5, f32[8,256]{1,0:T(8,128)S(1)} %get-tuple-element.10.s0, f32[8,256]{1,0:T(8,128)S(1)} %collective-permute-done.s1, ...), custom_call_target="tpu_custom_call" | custom-call | flops 2097152 | bytes 2134016 | tf_op jit(solution)/shard_map/pallas_call | solution.py:30
  71.2 4.6 %collective-permute-start.12 = (f32[16,256]{1,0:T(8,128)S(1)}, f32[16,256]{1,0:T(8,128)S(1)}, u32[]{:S(2)}, u32[]{:S(2)}) collective-permute-start(f32[16,256]{1,0:T(8,128)S(1)} %get-tuple-element.15), channel_id=1, source_target_pairs={{0,8},{4,12},{8,16},{12,20},{16,24},{20,28},{24,32},{28,36},{32,40... | collective-permute-start | bytes 49160 | tf_op jit(solution)/shard_map/ppermute | solution.py:190
  75.8 0.0 collective-permute-done.3.k1
  75.8 0.0 collective-permute-done.6.v1
  75.8 4.4 %shard_map.127 = (f32[256,1024]{1,0:T(8,128)S(1)}, f32[256,128]{1,0:T(8,128)S(1)}, f32[256,128]{1,0:T(8,128)S(1)}) custom-call(s32[1]{0:T(128)} %bitcast.index, s32[128]{0:T(128)S(1)} %copy-done.14, s32[2,128]{1,0:T(2,128)S(1)} %copy-done.15, bf16[256,1024]{1,0:T(8,128)(2,1)S(1)} %copy-done.7, bf16[256,1024]{1,0:T(8,128)(2,1)S(1)} %copy-done.8, ...), custom_call_target="tpu_custom_call" | custom-call | flops 1073741824 | bytes 6030852 | tf_op jit(solution)/shard_map/pallas_call | solution.py:30
  80.2 0.0 collective-permute-done.12.stats
  80.2 0.0 collective-permute-done.11.far
  80.2 2.8 %shard_map.129 = bf16[256,1024]{1,0:T(8,128)(2,1)} custom-call(f32[256,1024]{1,0:T(8,128)S(1)} %get-tuple-element.11.near, f32[256,128]{1,0:T(8,128)S(1)} %get-tuple-element.12.tops, f32[256,128]{1,0:T(8,128)S(1)} %get-tuple-element.13.sums, bf16[256,1024]{1,0:T(8,128)(2,1)} %collective-permute-done.11.far, f32[16,256]{1,0:T(8,128)S(1)} %collective-permute-done.12.stats), custom_call_target="tpu_custom_call" | custom-call | flops 2097152 | bytes 2375680 | tf_op jit(solution)/shard_map/pallas_call | solution.py:30
  (22 shorter events, 0.0 us)
Async XLA Ops:
  0.6 19.0 %collective-permute-start.4 = (bf16[256,1024]{1,0:T(8,128)(2,1)}, bf16[256,1024]{1,0:T(8,128)(2,1)S(1)}, u32[]{:S(2)}, u32[]{:S(2)}) collective-permute-start(bf16[256,1024]{1,0:T(8,128)(2,1)} %k0.1), channel_id=1, source_target_pairs={{0,8},{4,12},{8,16},{12,20},{16,24},{20,28},{24,32},{28,36},{32,40... | collective-permute-start | bytes 1572872 | tf_op jit(solution)/shard_map/ppermute | solution.py:190
  2.6 25.9 %collective-permute-start.7 = (bf16[256,1024]{1,0:T(8,128)(2,1)}, bf16[256,1024]{1,0:T(8,128)(2,1)S(1)}, u32[]{:S(2)}, u32[]{:S(2)}) collective-permute-start(bf16[256,1024]{1,0:T(8,128)(2,1)} %v0.1), channel_id=1, source_target_pairs={{0,8},{4,12},{8,16},{12,20},{16,24},{20,28},{24,32},{28,36},{32,40... | collective-permute-start | bytes 1572872 | tf_op jit(solution)/shard_map/ppermute | solution.py:190
  4.5 1.0 %copy-start = (bf16[256,1024]{1,0:T(8,128)(2,1)S(1)}, bf16[256,1024]{1,0:T(8,128)(2,1)}, u32[]{:S(2)}) copy-start(bf16[256,1024]{1,0:T(8,128)(2,1)} %k.3) | copy-start | bytes 1572868
  5.6 1.0 %copy-start.2 = (bf16[256,1024]{1,0:T(8,128)(2,1)S(1)}, bf16[256,1024]{1,0:T(8,128)(2,1)}, u32[]{:S(2)}) copy-start(bf16[256,1024]{1,0:T(8,128)(2,1)} %v.3) | copy-start | bytes 1572868
  6.6 0.7 copy-start.11
  9.0 10.1 %copy-start.6 = (bf16[256,1024]{1,0:T(8,128)(2,1)S(1)}, bf16[256,1024]{1,0:T(8,128)(2,1)}, u32[]{:S(2)}) copy-start(bf16[256,1024]{1,0:T(8,128)(2,1)} %q.5) | copy-start | bytes 1572868
  9.0 29.6 %all-to-all-start = ((bf16[64,16,128]{2,1,0:T(8,128)(2,1)}), bf16[64,16,128]{2,1,0:T(8,128)(2,1)S(1)}, u32[]{:S(2)}, u32[]{:S(2)}) async-start(bf16[64,16,128]{2,1,0:T(8,128)(2,1)} %bitcast.1), calls=%async_computation | async-start | bytes 524288 | tf_op jit(solution)/shard_map/all_to_all | solution.py:235
  19.1 34.3 %collective-permute-start.10 = (bf16[256,1024]{1,0:T(8,128)(2,1)S(1)}, bf16[256,1024]{1,0:T(8,128)(2,1)}, u32[]{:S(2)}, u32[]{:S(2)}) collective-permute-start(bf16[256,1024]{1,0:T(8,128)(2,1)S(1)} %copy-done.6), channel_id=1, source_target_pairs={{0,248},{4,252},{8,0},{12,4},{16,8},{20,12},{24,16},{28,20},{32,24... | collective-permute-start | bytes 1572872 | tf_op jit(solution)/shard_map/ppermute | solution.py:190
  19.6 33.8 %collective-permute-start.5 = (bf16[256,1024]{1,0:T(8,128)(2,1)S(1)}, bf16[256,1024]{1,0:T(8,128)(2,1)S(1)}, u32[]{:S(2)}, u32[]{:S(2)}) collective-permute-start(bf16[256,1024]{1,0:T(8,128)(2,1)S(1)} %collective-permute-done.4.k2.k1), channel_id=1, source_target_pairs={{0,4},{4,0},{8,12},{12,8},{16,20},{20,16},{24,28},{28,24},{32,36},... | collective-permute-start | bytes 1572872 | tf_op jit(solution)/shard_map/ppermute | solution.py:194
  28.5 24.9 %collective-permute-start.8 = (bf16[256,1024]{1,0:T(8,128)(2,1)S(1)}, bf16[256,1024]{1,0:T(8,128)(2,1)S(1)}, u32[]{:S(2)}, u32[]{:S(2)}) collective-permute-start(bf16[256,1024]{1,0:T(8,128)(2,1)S(1)} %collective-permute-done.7.v2.v1), channel_id=1, source_target_pairs={{0,4},{4,0},{8,12},{12,8},{16,20},{20,16},{24,28},{28,24},{32,36},... | collective-permute-start | bytes 1572872 | tf_op jit(solution)/shard_map/ppermute | solution.py:194
  28.5 10.1 %copy-start.12 = (f32[8]{0:T(128)S(1)}, f32[8]{0:T(128)}, u32[]{:S(2)}) copy-start(f32[8]{0:T(128)} %rate.7) | copy-start | bytes 100
  40.0 6.4 %copy-start.15 = (s32[2,128]{1,0:T(2,128)S(1)}, s32[2,128]{1,0:T(2,128)}, u32[]{:S(2)}) copy-start(s32[2,128]{1,0:T(2,128)} %mask.1) | copy-start | bytes 3076
  40.0 13.4 %copy-start.14 = (s32[128]{0:T(128)S(1)}, s32[128]{0:T(128)}, u32[]{:S(2)}) copy-start(s32[128]{0:T(128)} %docs.3) | copy-start | bytes 1540
  40.0 18.8 %all-to-all-start.1 = ((bf16[64,16,128]{2,1,0:T(8,128)(2,1)}), bf16[64,16,128]{2,1,0:T(8,128)(2,1)S(1)}, u32[]{:S(2)}, u32[]{:S(2)}) async-start(bf16[64,16,128]{2,1,0:T(8,128)(2,1)} %shard_map.124), calls=%async_computation.1 | async-start | bytes 524288 | tf_op jit(solution)/shard_map/all_to_all | solution.py:243
  46.4 11.0 %copy-start.1 = (bf16[256,1024]{1,0:T(8,128)(2,1)S(1)}, bf16[256,1024]{1,0:T(8,128)(2,1)}, u32[]{:S(2)}) copy-start(bf16[256,1024]{1,0:T(8,128)(2,1)} %k.3) | copy-start | bytes 1572868
  46.4 10.9 %copy-start.3 = (bf16[256,1024]{1,0:T(8,128)(2,1)S(1)}, bf16[256,1024]{1,0:T(8,128)(2,1)}, u32[]{:S(2)}) copy-start(bf16[256,1024]{1,0:T(8,128)(2,1)} %v.3) | copy-start | bytes 1572868
  46.4 10.9 %copy-start.4 = (bf16[256,1024]{1,0:T(8,128)(2,1)S(1)}, bf16[256,1024]{1,0:T(8,128)(2,1)}, u32[]{:S(2)}) copy-start(bf16[256,1024]{1,0:T(8,128)(2,1)} %q.4) | copy-start | bytes 1572868
  46.4 7.0 %collective-permute-start.9 = (s32[2,128]{1,0:T(2,128)S(1)}, s32[2,128]{1,0:T(2,128)S(1)}, u32[]{:S(2)}, u32[]{:S(2)}) collective-permute-start(s32[2,128]{1,0:T(2,128)S(1)} %copy-done.15), channel_id=1, source_target_pairs={{0,248},{4,252},{8,0},{12,4},{16,8},{20,12},{24,16},{28,20},{32,24... | collective-permute-start | bytes 3080 | tf_op jit(solution)/shard_map/ppermute | solution.py:190
  47.0 28.8 %collective-permute-start.3 = (bf16[256,1024]{1,0:T(8,128)(2,1)}, bf16[256,1024]{1,0:T(8,128)(2,1)}, u32[]{:S(2)}, u32[]{:S(2)}) collective-permute-start(bf16[256,1024]{1,0:T(8,128)(2,1)} %k0.1), channel_id=1, source_target_pairs={{0,4},{4,0},{8,12},{12,8},{16,20},{20,16},{24,28},{28,24},{32,36},... | collective-permute-start | bytes 1572872 | tf_op jit(solution)/shard_map/ppermute | solution.py:194
  53.4 22.4 %collective-permute-start.6 = (bf16[256,1024]{1,0:T(8,128)(2,1)}, bf16[256,1024]{1,0:T(8,128)(2,1)}, u32[]{:S(2)}, u32[]{:S(2)}) collective-permute-start(bf16[256,1024]{1,0:T(8,128)(2,1)} %v0.1), channel_id=1, source_target_pairs={{0,4},{4,0},{8,12},{12,8},{16,20},{20,16},{24,28},{28,24},{32,36},... | collective-permute-start | bytes 1572872 | tf_op jit(solution)/shard_map/ppermute | solution.py:194
  56.9 23.3 %collective-permute-start.11 = (bf16[256,1024]{1,0:T(8,128)(2,1)}, bf16[256,1024]{1,0:T(8,128)(2,1)}, u32[]{:S(2)}, u32[]{:S(2)}) collective-permute-start(bf16[256,1024]{1,0:T(8,128)(2,1)} %get-tuple-element.14), channel_id=1, source_target_pairs={{0,8},{4,12},{8,16},{12,20},{16,24},{20,28},{24,32},{28,36},{32,40... | collective-permute-start | bytes 1572872 | tf_op jit(solution)/shard_map/ppermute | solution.py:190
  58.9 1.0 %copy-start.5 = (bf16[256,1024]{1,0:T(8,128)(2,1)S(1)}, bf16[256,1024]{1,0:T(8,128)(2,1)}, u32[]{:S(2)}) copy-start(bf16[256,1024]{1,0:T(8,128)(2,1)} %q.4) | copy-start | bytes 1572868
  59.9 9.9 %copy-start.10 = (bf16[256,1024]{1,0:T(8,128)(2,1)S(1)}, bf16[256,1024]{1,0:T(8,128)(2,1)}, u32[]{:S(2)}) copy-start(bf16[256,1024]{1,0:T(8,128)(2,1)} %gate.1) | copy-start | bytes 1572868
  61.1 8.7 %copy-start.13 = (f32[1024]{0:T(1024)S(1)}, f32[1024]{0:T(1024)}, u32[]{:S(2)}) copy-start(f32[1024]{0:T(1024)} %param.15) | copy-start | bytes 12292
  61.1 3.8 %collective-permute-start = (f32[8,256]{1,0:T(8,128)S(1)}, f32[8,256]{1,0:T(8,128)S(1)}, u32[]{:S(2)}, u32[]{:S(2)}) collective-permute-start(f32[8,256]{1,0:T(8,128)S(1)} %get-tuple-element.10.s0), channel_id=1, source_target_pairs={{0,1},{1,2},{2,3},{3,0},{4,5},{5,6},{6,7},{7,4},{8,9},{9,10},{10,1... | collective-permute-start | bytes 24584 | tf_op jit(solution)/shard_map/ppermute | solution.py:198
  61.8 5.2 %collective-permute-start.1 = (f32[8,256]{1,0:T(8,128)S(1)}, f32[8,256]{1,0:T(8,128)S(1)}, u32[]{:S(2)}, u32[]{:S(2)}) collective-permute-start(f32[8,256]{1,0:T(8,128)S(1)} %get-tuple-element.10.s0), channel_id=1, source_target_pairs={{0,2},{1,3},{2,0},{3,1},{4,6},{5,7},{6,4},{7,5},{8,10},{9,11},{10,... | collective-permute-start | bytes 24584 | tf_op jit(solution)/shard_map/ppermute | solution.py:198
  65.0 4.9 %collective-permute-start.2 = (f32[8,256]{1,0:T(8,128)S(1)}, f32[8,256]{1,0:T(8,128)S(1)}, u32[]{:S(2)}, u32[]{:S(2)}) collective-permute-start(f32[8,256]{1,0:T(8,128)S(1)} %get-tuple-element.10.s0), channel_id=1, source_target_pairs={{0,3},{1,0},{2,1},{3,2},{4,7},{5,4},{6,5},{7,6},{8,11},{9,8},{10,9... | collective-permute-start | bytes 24584 | tf_op jit(solution)/shard_map/ppermute | solution.py:198
  69.8 5.9 %copy-start.7 = (bf16[256,1024]{1,0:T(8,128)(2,1)S(1)}, bf16[256,1024]{1,0:T(8,128)(2,1)}, u32[]{:S(2)}) copy-start(bf16[256,1024]{1,0:T(8,128)(2,1)} %q.5) | copy-start | bytes 1572868
  69.8 6.0 %copy-start.8 = (bf16[256,1024]{1,0:T(8,128)(2,1)S(1)}, bf16[256,1024]{1,0:T(8,128)(2,1)}, u32[]{:S(2)}) copy-start(bf16[256,1024]{1,0:T(8,128)(2,1)} %k0.1) | copy-start | bytes 1572868
  69.8 6.0 %copy-start.9 = (bf16[256,1024]{1,0:T(8,128)(2,1)S(1)}, bf16[256,1024]{1,0:T(8,128)(2,1)}, u32[]{:S(2)}) copy-start(bf16[256,1024]{1,0:T(8,128)(2,1)} %v0.1) | copy-start | bytes 1572868
  71.2 9.0 %collective-permute-start.12 = (f32[16,256]{1,0:T(8,128)S(1)}, f32[16,256]{1,0:T(8,128)S(1)}, u32[]{:S(2)}, u32[]{:S(2)}) collective-permute-start(f32[16,256]{1,0:T(8,128)S(1)} %get-tuple-element.15), channel_id=1, source_target_pairs={{0,8},{4,12},{8,16},{12,20},{16,24},{20,28},{24,32},{28,36},{32,40... | collective-permute-start | bytes 49160 | tf_op jit(solution)/shard_map/ppermute | solution.py:190

commit v2 on v1

v2 whole, which is shorter than its diff:
```python
import math

import jax
import jax.numpy as jnp
from jax import lax
from jax.experimental import pallas as pl
from jax.experimental.pallas import tpu as pltpu
from jax.sharding import PartitionSpec as P

HD = 128
BLK = 128
NBLK = 128
ROWS = 256
LOCAL = 8
WIDTH = LOCAL * HD
HALF = WIDTH // 2
D = 4096
SHARDS = 64
FILL = -1e30
PREFIX_COST = 5_000_000_000
CARRY_COST = 10_000_000_000
EXP2_SCALE = HD ** (-0.5) * math.log2(math.e)

f32 = jnp.float32
bf16 = jnp.bfloat16

SMEM = pl.BlockSpec(memory_space=pltpu.SMEM)
VMEM = pl.BlockSpec(memory_space=pltpu.VMEM)


def call(body, outs, ins, specs, scratch=(), flops=1, room=16):
    return pl.pallas_call(
        body,
        out_shape=outs,
        in_specs=specs,
        out_specs=[VMEM] * len(outs),
        scratch_shapes=list(scratch),
        compiler_params=pltpu.CompilerParams(vmem_limit_bytes=room * 1024 * 1024),
        cost_estimate=pl.CostEstimate(flops=flops, bytes_accessed=1, transcendentals=0),
    )(*ins)


def cols(h):
    return slice(h * HD, (h + 1) * HD)


def dot(a, b, dims):
    return lax.dot_general(a, b, (dims, ((), ())), preferred_element_type=f32)


def exact_dot(a, b, dims):
    return lax.dot_general(
        a, b, (dims, ((), ())), precision=lax.Precision.HIGHEST, preferred_element_type=f32
    )


def state_body(rate_hbm, k_hbm, v_hbm, first, out, rate, k, v, rate_sem, k_sem, v_sem):
    def chunk(g):
        return slice(g * 2 * HD, (g + 1) * 2 * HD)

    copies = [pltpu.make_async_copy(rate_hbm, rate, rate_sem)]
    for g in range(LOCAL // 2):
        at = chunk(g)
        copies.append(pltpu.make_async_copy(k_hbm.at[:, at], k.at[:, at], k_sem.at[g]))
        copies.append(pltpu.make_async_copy(v_hbm.at[:, at], v.at[:, at], v_sem.at[g]))
    for copy in copies:
        copy.start()
    copies[0].wait()
    back = (BLK - 1.0) - lax.broadcasted_iota(jnp.int32, (BLK, HD), 0).astype(f32)
    for g in range(LOCAL // 2):
        copies[2 * g + 1].wait()
        copies[2 * g + 2].wait()
        for h in (2 * g, 2 * g + 1):
            decay = jnp.exp(-rate[h] * back)
            parts = []
            for b in range(2):
                rows = slice(b * BLK, (b + 1) * BLK)
                decayed = (k[rows, cols(h)].astype(f32) * decay).astype(bf16)
                parts.append(dot(decayed, v[rows, cols(h)], ((0,), (0,))))
            step = jnp.exp(jnp.full((HD, HD), -rate[h] * BLK, f32))
            first[cols(h), :] = parts[0]
            out[cols(h), :] = (step * parts[0] + parts[1]).astype(bf16)


def prefix_body(index, rate, parts, out):
    step = jnp.exp(jnp.full((16, HD), -rate[index[0] // 8] * ROWS, f32))
    state = jnp.zeros((16, HD), f32)
    for i in range(SHARDS):
        out[i] = state.astype(bf16)
        if i + 1 < SHARDS:
            state = step * state + parts[i].astype(f32)


def inner_body(rate, q, k, v, out):
    row = lax.broadcasted_iota(jnp.int32, (BLK, BLK), 0)
    col = lax.broadcasted_iota(jnp.int32, (BLK, BLK), 1)
    gap = jnp.maximum(row - col, 0).astype(f32)
    for h in range(LOCAL):
        decay = jnp.where(row >= col, jnp.exp(-rate[h] * gap), 0.0)
        for b in range(2):
            rows = slice(b * BLK, (b + 1) * BLK)
            scores = dot(q[rows, cols(h)], k[rows, cols(h)], ((1,), (1,)))
            out[rows, cols(h)] = dot(
                (scores * decay).astype(bf16), v[rows, cols(h)], ((1,), (0,))
            )


def carry_body(rate, inner, q, first, state, heads, squares):
    ahead = lax.broadcasted_iota(jnp.int32, (BLK, HD), 0).astype(f32) + 1.0
    totals = [jnp.zeros((BLK, HD), f32)] * 2
    for h in range(LOCAL):
        step = jnp.exp(jnp.full((HD, HD), -rate[h] * BLK, f32))
        decay = jnp.exp(-rate[h] * ahead)
        entering = state[cols(h), :]
        middle = (step * entering.astype(f32) + first[cols(h), :]).astype(bf16)
        for b, block_state in enumerate((entering, middle)):
            rows = slice(b * BLK, (b + 1) * BLK)
            carried = dot(q[rows, cols(h)], block_state, ((1,), (0,)))
            value = inner[rows, cols(h)] + carried * decay
            heads[rows, cols(h)] = value
            totals[b] = totals[b] + value * value
    total = jnp.concatenate(totals, axis=0)
    squares[...] = exact_dot(jnp.ones((8, HD), f32), total, ((1,), (1,)))


def norm_body(heads, gate, gain, s0, s1, s2, s3, out):
    total = s0[...] + s1[...] + s2[...] + s3[...]
    first = (lax.broadcasted_iota(jnp.int32, (8, HD), 0) == 0).astype(f32)
    spread = exact_dot(total, first, ((0,), (0,)))
    inverse = lax.rsqrt(spread / D + 1e-06)
    for h in range(LOCAL):
        scale = gain[:, cols(h)] * jax.nn.sigmoid(gate[:, cols(h)].astype(f32))
        out[:, cols(h)] = (heads[:, cols(h)] * inverse * scale).astype(bf16)


def half(c):
    return pl.ds(pl.multiple_of(c * HALF, HALF), HALF)


def split_body(index, mask, q, k, v, out, sem):
    other = 1 - index[0] % 2
    copies = [
        pltpu.make_async_copy(
            ref.at[:, half(other)], out.at[at * ROWS : (at + 1) * ROWS, :], sem.at[at]
        )
        for at, ref in enumerate((q, k, v))
    ]
    for copy in copies:
        copy.start()
    flags = mask[...].astype(f32)
    flags = jnp.concatenate([flags, jnp.zeros((14, NBLK), f32)], axis=0).astype(bf16)
    out[3 * ROWS :, :] = jnp.concatenate([flags] * 4, axis=1)
    for copy in copies:
        copy.wait()


def gather_body(index, mask, q, k, v, other, near_q, far_q, pair, flags):
    core = index[0] % 2

    def lay(own, at, mine):
        theirs = other[at * ROWS : (at + 1) * ROWS, :]
        first = jnp.where(core == 0, mine, theirs)
        second = jnp.where(core == 0, theirs, mine)
        return first, second

    q0, q1 = lay(q, 0, q[:, half(core)])
    near_q[:ROWS, :] = q0
    near_q[ROWS:, :] = q1
    far_q[:ROWS, :] = q0
    far_q[ROWS : 3 * BLK, :] = q1[:BLK]
    for at, ref in ((1, k), (2, v)):
        low, high = lay(ref, at, ref[:, half(core)])
        base = (at - 1) * 2 * ROWS
        pair[base : base + ROWS, :] = low
        pair[base + ROWS : base + 2 * ROWS, :] = high
    own = mask[...].astype(f32)
    theirs = other[3 * ROWS :, :NBLK].astype(f32)[:2]
    first = jnp.where(core == 0, own, theirs)
    second = jnp.where(core == 0, theirs, own)
    rows = jnp.concatenate([first, second, jnp.zeros((12, NBLK), f32)], axis=0)
    flags[...] = rows
    far_q[3 * BLK :, :] = jnp.concatenate([rows.astype(bf16)] * 4, axis=1)


def allowed(docs, flags, i, query, key):
    q_at = jnp.clip(query, 0, NBLK - 1)
    k_at = jnp.clip(key, 0, NBLK - 1)
    inside = (key >= 0) & (key < query) & (query < NBLK) & (docs[k_at] == docs[q_at])
    lane = lax.broadcasted_iota(jnp.int32, (1, NBLK), 1)
    wanted = jnp.where(inside, k_at, -1)
    ok = jnp.sum(jnp.where(lane == wanted, flags[i : i + 1, :], 0.0), axis=1, keepdims=True)
    return jnp.broadcast_to(jnp.where(ok > 0.5, 0.0, FILL), (BLK, BLK))


def block(i):
    return slice(i * BLK, (i + 1) * BLK)


def attend_head(q, keys, values, bias):
    scores = dot(q, keys, ((1,), (1,))) + bias
    top = jnp.max(scores, axis=1, keepdims=True)
    weights = jnp.exp2((scores - top) * EXP2_SCALE).astype(bf16)
    ones = jnp.ones(values.shape, bf16)
    both = dot(weights, jnp.concatenate([values, ones], axis=1), ((1,), (0,)))
    return both[:, :HD], top, both[:, HD:]


def far_body(index, docs, q, pair, out, bias):
    chip = index[0] // 2
    flags = q[3 * BLK :, :NBLK].astype(f32)
    for i in range(3):
        for j in range(3):
            bias[block(i), block(j)] = allowed(
                docs, flags, i, 4 * (chip + 1) + i, 4 * (chip - 1) + 1 + j
            )
    lane = lax.broadcasted_iota(jnp.int32, (3 * BLK, HD), 1)
    table = jnp.zeros((3 * BLK, HD), f32)
    for h in range(LOCAL // 2):
        acc, top, total = attend_head(
            q[: 3 * BLK, cols(h)],
            pair[BLK : 4 * BLK, cols(h)],
            pair[5 * BLK :, cols(h)],
            bias[...],
        )
        out[: 3 * BLK, cols(h)] = (acc / total).astype(bf16)
        table = jnp.where(lane == h, top, table)
        table = jnp.where(lane == LOCAL // 2 + h, total, table)
    rest = table.T[:LOCAL, :]
    rest = jnp.concatenate([rest, jnp.zeros((LOCAL, 3 * BLK), f32)], axis=0)
    rest = jnp.concatenate([rest, jnp.zeros((2 * LOCAL, BLK), f32)], axis=1)
    for piece in range(3):
        part = rest.astype(bf16)
        out[3 * BLK + piece * 2 * LOCAL : 3 * BLK + (piece + 1) * 2 * LOCAL, :] = part
        rest = rest - part.astype(f32)


def near_body(
    index, docs, flags, q, own, pair, out, tops, sums, bias
):
    chip = index[0] // 2
    rows = flags[...]
    for i in range(4):
        for j in range(4):
            if j == i:
                row = lax.broadcasted_iota(jnp.int32, (BLK, BLK), 0)
                col = lax.broadcasted_iota(jnp.int32, (BLK, BLK), 1)
                bias[block(i), block(j)] = jnp.where(col <= row, 0.0, FILL)
            elif j > i:
                bias[block(i), block(j)] = jnp.full((BLK, BLK), FILL, f32)
            else:
                bias[block(i), block(j)] = allowed(docs, rows, i, 4 * chip + i, 4 * chip + j)
            bias[block(i), block(4 + j)] = allowed(
                docs, rows, i, 4 * chip + i, 4 * (chip - 1) + j
            )
    lane = lax.broadcasted_iota(jnp.int32, (4 * BLK, HD), 1)
    top_table = jnp.zeros((4 * BLK, HD), f32)
    sum_table = jnp.zeros((4 * BLK, HD), f32)
    for h in range(LOCAL // 2):
        keys = jnp.concatenate([own[: 4 * BLK, cols(h)], pair[: 4 * BLK, cols(h)]], axis=0)
        values = jnp.concatenate([own[4 * BLK :, cols(h)], pair[4 * BLK :, cols(h)]], axis=0)
        acc, top, total = attend_head(q[:, cols(h)], keys, values, bias[...])
        out[:, cols(h)] = acc / total
        top_table = jnp.where(lane == h, top, top_table)
        sum_table = jnp.where(lane == h, total, sum_table)
    tops[...] = top_table
    sums[...] = sum_table


def merge_body(near, tops, sums, far, out):
    stats = jnp.zeros((2 * LOCAL, HALF), f32)
    for p in range(3):
        at = 3 * BLK + p * 2 * LOCAL
        stats = stats + far[at : at + 2 * LOCAL, :].astype(f32)
    heads = LOCAL // 2
    pad = jnp.zeros((HD - heads, 3 * BLK), f32)
    far_tops = jnp.concatenate([stats[:heads, : 3 * BLK], pad], axis=0).T
    far_sums = jnp.concatenate([stats[heads:LOCAL, : 3 * BLK], pad], axis=0).T
    rows = slice(0, 3 * BLK)
    top = jnp.maximum(tops[rows, :], far_tops)
    near_part = jnp.exp2((tops[rows, :] - top) * EXP2_SCALE) * sums[rows, :]
    far_part = jnp.exp2((far_tops - top) * EXP2_SCALE) * far_sums
    lane = lax.broadcasted_iota(jnp.int32, (3 * BLK, HD), 1)
    share = jnp.where(lane < heads, far_part / (near_part + far_part), 0.0)
    for h in range(heads):
        own = near[rows, cols(h)]
        there = far[rows, cols(h)].astype(f32)
        out[rows, cols(h)] = (own + (there - own) * share[:, h : h + 1]).astype(bf16)
        out[3 * BLK :, cols(h)] = near[3 * BLK :, cols(h)].astype(bf16)


def part_body(index, merged, mine, send):
    core = index[0] % 2
    mine[...] = merged[pl.ds(pl.multiple_of(core * ROWS, ROWS), ROWS), :]
    send[...] = merged[pl.ds(pl.multiple_of((1 - core) * ROWS, ROWS), ROWS), :]


def place_body(index, mine, other, out):
    core = index[0] % 2
    out[:, half(core)] = mine[...]
    out[:, half(1 - core)] = other[...]


def shifted(x, distance):
    return lax.ppermute(x, "seq", [(i, (i + distance) % SHARDS) for i in range(SHARDS)])


def swapped(x):
    return lax.ppermute(x, "seq", [(i, i ^ 1) for i in range(SHARDS)])


def turned(x, distance):
    return lax.ppermute(x, "head", [(i, (i + distance) % 4) for i in range(4)])


def per_device(
    lin_query,
    lin_key,
    lin_value,
    out_gate,
    norm_gain,
    decay_rate,
    soft_query,
    soft_key,
    soft_value,
    doc_ids,
    block_mask,
):
    like = jax.ShapeDtypeStruct
    index = lax.axis_index("seq").astype(jnp.int32).reshape(1)
    wide = like((ROWS, WIDTH), f32)
    narrow = like((ROWS, WIDTH), bf16)

    (sent,) = call(
        split_body,
        [like((3 * ROWS + 16, HALF), bf16)],
        (index, block_mask, soft_query, soft_key, soft_value),
        [SMEM, VMEM] + [pl.BlockSpec(memory_space=pl.ANY)] * 3,
        [pltpu.SemaphoreType.DMA((3,))],
        room=56,
    )
    other = swapped(sent)
    first, state = pl.pallas_call(
        state_body,
        out_shape=[like((WIDTH, HD), f32), like((WIDTH, HD), bf16)],
        in_specs=[pl.BlockSpec(memory_space=pl.ANY)] * 3,
        out_specs=[VMEM] * 2,
        scratch_shapes=[
            pltpu.SMEM((LOCAL,), f32),
            pltpu.VMEM((ROWS, WIDTH), bf16),
            pltpu.VMEM((ROWS, WIDTH), bf16),
            pltpu.SemaphoreType.DMA,
            pltpu.SemaphoreType.DMA((LOCAL // 2,)),
            pltpu.SemaphoreType.DMA((LOCAL // 2,)),
        ],
        compiler_params=pltpu.CompilerParams(vmem_limit_bytes=56 * 1024 * 1024),
        cost_estimate=pl.CostEstimate(
            flops=1, bytes_accessed=1, transcendentals=0
        ),
    )(decay_rate, lin_key, lin_value)
    parts = lax.all_to_all(state.reshape(SHARDS, 16, HD), "seq", 0, 0)
    near_q, far_q, own_pair, flags = call(
        gather_body,
        [
            like((2 * ROWS, HALF), bf16),
            like((3 * BLK + 16, HALF), bf16),
            like((8 * BLK, HALF), bf16),
            like((16, NBLK), f32),
        ],
        (index, block_mask, soft_query, soft_key, soft_value, other),
        [SMEM] + [VMEM] * 5,
        room=56,
    )
    pair = shifted(own_pair, 2)
    next_q = shifted(far_q, -2)

    (prefix,) = call(
        prefix_body,
        [like((SHARDS, 16, HD), bf16)],
        (index, decay_rate, parts),
        [SMEM, SMEM, VMEM],
        flops=PREFIX_COST,
    )
    prefix, next_q = lax.optimization_barrier((prefix, next_q))
    entering = lax.all_to_all(prefix, "seq", 0, 0).reshape(WIDTH, HD)
    (inner,) = call(
        inner_body,
        [wide],
        (decay_rate, lin_query, lin_key, lin_value),
        [SMEM, VMEM, VMEM, VMEM],
    )
    (far,) = call(
        far_body,
        [like((3 * BLK + 48, HALF), bf16)],
        (index, doc_ids, next_q, pair),
        [SMEM] * 2 + [VMEM] * 2,
        [pltpu.VMEM((3 * BLK, 3 * BLK), f32)],
    )
    far = shifted(far, 2)
    near, tops, sums = call(
        near_body,
        [like((4 * BLK, HALF), f32), like((4 * BLK, HD), f32), like((4 * BLK, HD), f32)],
        (index, doc_ids, flags, near_q, own_pair, pair),
        [SMEM] * 2 + [VMEM] * 4,
        [pltpu.VMEM((4 * BLK, 8 * BLK), f32)],
    )
    near, inner = lax.optimization_barrier((near, inner))
    heads, squares = call(
        carry_body,
        [wide, like((8, ROWS), f32)],
        (decay_rate, inner, lin_query, first, entering),
        [SMEM] + [VMEM] * 4,
        flops=CARRY_COST,
    )
    others = [turned(squares, d) for d in (1, 2, 3)]
    far, heads = lax.optimization_barrier((far, heads))
    (merged,) = call(
        merge_body, [like((4 * BLK, HALF), bf16)], (near, tops, sums, far), [VMEM] * 4
    )
    merged, *others = lax.optimization_barrier((merged, *others))
    (lin_output,) = call(
        norm_body,
        [narrow],
        (heads, out_gate, norm_gain.reshape(1, WIDTH), squares, *others),
        [VMEM] * 7,
    )

    mine, send = call(
        part_body, [like((ROWS, HALF), bf16)] * 2, (index, merged), [SMEM, VMEM]
    )
    (soft_output,) = call(
        place_body, [narrow], (index, mine, swapped(send)), [SMEM, VMEM, VMEM]
    )
    return (lin_output, soft_output)


def solution(mesh):
    rows = P("seq", "head")
    return jax.shard_map(
        per_device,
        mesh=mesh,
        in_specs=(
            rows, rows, rows, rows, P("head"), P("head"), rows, rows, rows, P(), P("seq", None),
        ),
        out_specs=(rows, rows),
        check_vma=False,
    )
```

time: 83.5 us -> 77.5 us (0.928)
  the two profiles are of different devices: /device:TPU:38 before, /device:TPU:1 now
where the time goes in v2:
time: 77.5 us; the launch traced here: 76.3 us
  starting transfers between devices  35.5 us (46%)
  Pallas kernels  24.7 us (32%)
  waiting for transfers between devices  9.23 us (12%)
  local copies, waits for them, and re-layouts  6.06 us (8%)
  between operations  0.82 us (1%)
    pallas_call x11, Pallas kernels, call(): pl.pallas_call(body, out_shape=outs, in_specs=specs, out_specs=[VMEM] * l...  21.9 us
    all_to_all x1, starting transfers between devices, per_device(): parts = lax.all_to_all(state.reshape(SHARDS, 16, HD), 'seq', 0, 0)  10 us
    all_to_all x1, starting transfers between devices, per_device(): entering = lax.all_to_all(prefix, 'seq', 0, 0).reshape(WIDTH, HD)  9.91 us
    ppermute x3, waiting for transfers between devices, shifted(): lax.ppermute(x, 'seq', [(i, (i + distance) % SHARDS) for i in range(SHARD...  6.16 us
    unnamed x34, local copies, waits for them, and re-layouts  6.06 us
    ppermute x2, starting transfers between devices, swapped(): return lax.ppermute(x, 'seq', [(i, i ^ 1) for i in range(SHARDS)])  5.45 us
    ppermute x3, starting transfers between devices, shifted(): lax.ppermute(x, 'seq', [(i, (i + distance) % SHARDS) for i in range(SHARD...  5.09 us
    ppermute x3, starting transfers between devices, turned(): return lax.ppermute(x, 'head', [(i, (i + distance) % 4) for i in range(4)])  4.99 us
  transfers between devices with their start and end apart: 10, of which 4 were waited for; matrix products, arithmetic and copies ran while one was open for 0% of the time, Pallas kernels for 28%

profile of v2, /device:TPU:1, one launch (start us, length us, event | category | flops | bytes accessed | tf_op | source)
XLA Modules:
  0.0 76.3 jit_solution(15374609478646253473)
XLA Ops:
  0.6 2.7 %shard_map.124 = bf16[784,512]{1,0:T(8,128)(2,1)} custom-call(s32[1]{0:T(128)} %bitcast.index, s32[2,128]{1,0:T(2,128)} %mask.3, bf16[256,1024]{1,0:T(8,128)(2,1)} %q.5, bf16[256,1024]{1,0:T(8,128)(2,1)} %k.4, bf16[256,1024]{1,0:T(8,128)(2,1)} %v.4), custom_call_target="tpu_custom_call" | custom-call | flops 1 | bytes 1 | tf_op jit(solution)/shard_map/pallas_call | solution.py:32
  3.4 3.3 %collective-permute-start = (bf16[784,512]{1,0:T(8,128)(2,1)}, bf16[784,512]{1,0:T(8,128)(2,1)S(1)}, u32[]{:S(2)}, u32[]{:S(2)}) collective-permute-start(bf16[784,512]{1,0:T(8,128)(2,1)} %shard_map.124), channel_id=1, source_target_pairs={{0,4},{4,0},{8,12},{12,8},{16,20},{20,16},{24,28},{28,24},{32,36},... | collective-permute-start | bytes 2408456 | tf_op jit(solution)/shard_map/ppermute | solution.py:308
  6.7 2.9 %shard_map.122 = (f32[1024,128]{1,0:T(8,128)}, bf16[1024,128]{1,0:T(8,128)(2,1)}) custom-call(f32[8]{0:T(128)} %rate.5, bf16[256,1024]{1,0:T(8,128)(2,1)} %k.5, bf16[256,1024]{1,0:T(8,128)(2,1)} %v.5), custom_call_target="tpu_custom_call" | custom-call | flops 1 | bytes 1 | tf_op jit(solution)/shard_map/pallas_call | solution.py:342
  9.6 10.0 %all-to-all-start = ((bf16[64,16,128]{2,1,0:T(8,128)(2,1)}), bf16[64,16,128]{2,1,0:T(8,128)(2,1)S(1)}, u32[]{:S(2)}, u32[]{:S(2)}) async-start(bf16[64,16,128]{2,1,0:T(8,128)(2,1)} %bitcast.5), calls=%async_computation | async-start | bytes 524288 | tf_op jit(solution)/shard_map/all_to_all | solution.py:360
  19.6 0.0 collective-permute-done.other
  19.6 0.0 copy-start.16
  19.6 0.9 %copy-done.16 = bf16[784,512]{1,0:T(8,128)(2,1)} copy-done((bf16[784,512]{1,0:T(8,128)(2,1)}, bf16[784,512]{1,0:T(8,128)(2,1)S(1)}, u32[]{:S(2)}) %copy-start.16) | copy-done | bytes 802840
  20.5 3.0 %shard_map.125 = (bf16[512,512]{1,0:T(8,128)(2,1)}, bf16[400,512]{1,0:T(8,128)(2,1)}, bf16[1024,512]{1,0:T(8,128)(2,1)}, f32[16,128]{1,0:T(8,128)}) custom-call(s32[1]{0:T(128)} %bitcast.index, s32[2,128]{1,0:T(2,128)} %mask.3, bf16[256,1024]{1,0:T(8,128)(2,1)} %q.5, bf16[256,1024]{1,0:T(8,128)(2,1)} %k.4, bf16[256,1024]{1,0:T(8,128)(2,1)} %v.4, ...), custom_call_target="tpu_custom_call" | custom-call | flops 1 | bytes 1 | tf_op jit(solution)/shard_map/pallas_call | solution.py:32
  23.5 1.4 %collective-permute-start.2 = (bf16[1024,512]{1,0:T(8,128)(2,1)}, bf16[1024,512]{1,0:T(8,128)(2,1)S(1)}, u32[]{:S(2)}, u32[]{:S(2)}) collective-permute-start(bf16[1024,512]{1,0:T(8,128)(2,1)} %get-tuple-element.28.own), channel_id=1, source_target_pairs={{0,8},{4,12},{8,16},{12,20},{16,24},{20,28},{24,32},{28,36},{32,40... | collective-permute-start | bytes 3145736 | tf_op jit(solution)/shard_map/ppermute | solution.py:304
  24.9 3.7 %collective-permute-start.1 = (bf16[400,512]{1,0:T(8,128)(2,1)}, bf16[400,512]{1,0:T(8,128)(2,1)S(1)}, u32[]{:S(2)}, u32[]{:S(2)}) collective-permute-start(bf16[400,512]{1,0:T(8,128)(2,1)} %get-tuple-element.26), channel_id=1, source_target_pairs={{0,248},{4,252},{8,0},{12,4},{16,8},{20,12},{24,16},{28,20},{32,24... | collective-permute-start | bytes 1228808 | tf_op jit(solution)/shard_map/ppermute | solution.py:304
  28.6 3.1 %all-to-all-done.parts = bf16[64,16,128]{2,1,0:T(8,128)(2,1)S(1)} async-done(((bf16[64,16,128]{2,1,0:T(8,128)(2,1)}), bf16[64,16,128]{2,1,0:T(8,128)(2,1)S(1)}, u32[]{:S(2)}, u32[]{:S(2)}) %all-to-all-start) | async-done | bytes 262176 | tf_op jit(solution)/shard_map/all_to_all | solution.py:360
  31.7 0.0 copy-done.12
  31.7 1.4 %shard_map.123 = bf16[64,16,128]{2,1,0:T(8,128)(2,1)} custom-call(s32[1]{0:T(128)} %bitcast.index, f32[8]{0:T(128)S(1)} %copy-done.12, bf16[64,16,128]{2,1,0:T(8,128)(2,1)S(1)} %all-to-all-done.parts), custom_call_target="tpu_custom_call" | custom-call | flops 5000000000 | bytes 1 | tf_op jit(solution)/shard_map/pallas_call | solution.py:32
  33.1 4.3 %collective-permute-done.1.q = bf16[400,512]{1,0:T(8,128)(2,1)S(1)} collective-permute-done((bf16[400,512]{1,0:T(8,128)(2,1)}, bf16[400,512]{1,0:T(8,128)(2,1)S(1)}, u32[]{:S(2)}, u32[]{:S(2)}) %collective-permute-start.1) | collective-permute-done | bytes 409632 | tf_op jit(solution)/shard_map/ppermute | solution.py:304
  37.3 9.9 %all-to-all-start.1 = ((bf16[64,16,128]{2,1,0:T(8,128)(2,1)}), bf16[64,16,128]{2,1,0:T(8,128)(2,1)}, u32[]{:S(2)}, u32[]{:S(2)}) async-start(bf16[64,16,128]{2,1,0:T(8,128)(2,1)} %shard_map.123), calls=%async_computation.1 | async-start | bytes 524288 | tf_op jit(solution)/shard_map/all_to_all | solution.py:384
  47.3 0.0 copy-done.1
  47.3 0.0 copy-start.4
  47.3 1.0 %copy-done.4 = bf16[256,1024]{1,0:T(8,128)(2,1)S(1)} copy-done((bf16[256,1024]{1,0:T(8,128)(2,1)S(1)}, bf16[256,1024]{1,0:T(8,128)(2,1)}, u32[]{:S(2)}) %copy-start.4) | copy-done | bytes 524312
  48.3 0.7 copy-done.13
  49.0 3.1 %shard_map.128.inner = f32[256,1024]{1,0:T(8,128)S(1)} custom-call(f32[8]{0:T(128)S(1)} %copy-done.13, bf16[256,1024]{1,0:T(8,128)(2,1)S(1)} %copy-done.4, bf16[256,1024]{1,0:T(8,128)(2,1)S(1)} %copy-done, bf16[256,1024]{1,0:T(8,128)(2,1)S(1)} %copy-done.1), custom_call_target="tpu_custom_call" | custom-call | flops 1 | bytes 1 | tf_op jit(solution)/shard_map/pallas_call | solution.py:32
  52.1 0.0 copy-start.3
  52.1 1.4 %collective-permute-done.2.pair = bf16[1024,512]{1,0:T(8,128)(2,1)S(1)} collective-permute-done((bf16[1024,512]{1,0:T(8,128)(2,1)}, bf16[1024,512]{1,0:T(8,128)(2,1)S(1)}, u32[]{:S(2)}, u32[]{:S(2)}) %collective-permute-start.2) | collective-permute-done | bytes 1048608 | tf_op jit(solution)/shard_map/ppermute | solution.py:304
  53.6 2.6 %shard_map.126 = bf16[432,512]{1,0:T(8,128)(2,1)} custom-call(s32[1]{0:T(128)} %bitcast.index, s32[128]{0:T(128)S(1)} %copy-done.11, bf16[400,512]{1,0:T(8,128)(2,1)S(1)} %collective-permute-done.1.q, bf16[1024,512]{1,0:T(8,128)(2,1)S(1)} %collective-permute-done.2.pair), custom_call_target="tpu_custom_call" | custom-call | flops 1 | bytes 1 | tf_op jit(solution)/shard_map/pallas_call | solution.py:32
  56.2 0.0 collective-permute-start.3
  56.2 0.0 copy-done.2
  56.2 3.8 %shard_map.127 = (f32[512,512]{1,0:T(8,128)S(1)}, f32[512,128]{1,0:T(8,128)S(1)}, f32[512,128]{1,0:T(8,128)S(1)}) custom-call(s32[1]{0:T(128)} %bitcast.index, s32[128]{0:T(128)S(1)} %copy-done.11, f32[16,128]{1,0:T(8,128)S(1)} %copy-done.9, bf16[512,512]{1,0:T(8,128)(2,1)S(1)} %copy-done.3, bf16[1024,512]{1,0:T(8,128)(2,1)S(1)} %copy-done.2, ...), custom_call_target="tpu_custom_call" | custom-call | flops 1 | bytes 1 | tf_op jit(solution)/shard_map/pallas_call | solution.py:32
  60.0 0.0 copy-start.7
  60.0 0.7 copy-done.7
  60.7 0.0 all-to-all-done.1
  60.7 0.7 copy-done.14
  61.4 1.0 %copy-done.5 = bf16[256,1024]{1,0:T(8,128)(2,1)S(1)} copy-done((bf16[256,1024]{1,0:T(8,128)(2,1)S(1)}, bf16[256,1024]{1,0:T(8,128)(2,1)}, u32[]{:S(2)}) %copy-start.5) | copy-done | bytes 524312
  62.4 1.0 %copy-done.15 = f32[1024,128]{1,0:T(8,128)S(1)} copy-done((f32[1024,128]{1,0:T(8,128)S(1)}, f32[1024,128]{1,0:T(8,128)}, u32[]{:S(2)}) %copy-start.15) | copy-done | bytes 524312
  63.4 1.6 %shard_map.129 = (f32[256,1024]{1,0:T(8,128)S(1)}, f32[8,256]{1,0:T(8,128)S(1)}) custom-call(f32[8]{0:T(128)S(1)} %copy-done.14, f32[256,1024]{1,0:T(8,128)S(1)} %shard_map.128.inner, bf16[256,1024]{1,0:T(8,128)(2,1)S(1)} %copy-done.5, f32[1024,128]{1,0:T(8,128)S(1)} %copy-done.15, bf16[1024,128]{1,0:T(8,128)(2,1)} %bitcast.2.state), custom_call_target="tpu_custom_call" | custom-call | flops 10000000000 | bytes 1 | tf_op jit(solution)/shard_map/pallas_call | solution.py:32
  65.0 1.4 %collective-permute-start.4 = (f32[8,256]{1,0:T(8,128)S(1)}, f32[8,256]{1,0:T(8,128)S(1)}, u32[]{:S(2)}, u32[]{:S(2)}) collective-permute-start(f32[8,256]{1,0:T(8,128)S(1)} %get-tuple-element.37.s0), channel_id=1, source_target_pairs={{0,1},{1,2},{2,3},{3,0},{4,5},{5,6},{6,7},{7,4},{8,9},{9,10},{10,1... | collective-permute-start | bytes 24584 | tf_op jit(solution)/shard_map/ppermute | solution.py:312
  66.4 2.5 %collective-permute-start.5 = (f32[8,256]{1,0:T(8,128)S(1)}, f32[8,256]{1,0:T(8,128)S(1)}, u32[]{:S(2)}, u32[]{:S(2)}) collective-permute-start(f32[8,256]{1,0:T(8,128)S(1)} %get-tuple-element.37.s0), channel_id=1, source_target_pairs={{0,2},{1,3},{2,0},{3,1},{4,6},{5,7},{6,4},{7,5},{8,10},{9,11},{10,... | collective-permute-start | bytes 24584 | tf_op jit(solution)/shard_map/ppermute | solution.py:312
  68.8 1.2 %collective-permute-start.6 = (f32[8,256]{1,0:T(8,128)S(1)}, f32[8,256]{1,0:T(8,128)S(1)}, u32[]{:S(2)}, u32[]{:S(2)}) collective-permute-start(f32[8,256]{1,0:T(8,128)S(1)} %get-tuple-element.37.s0), channel_id=1, source_target_pairs={{0,3},{1,0},{2,1},{3,2},{4,7},{5,4},{6,5},{7,6},{8,11},{9,8},{10,9... | collective-permute-start | bytes 24584 | tf_op jit(solution)/shard_map/ppermute | solution.py:312
  70.0 0.5 collective-permute-done.3.far
  70.5 1.5 %shard_map.130.merged = bf16[512,512]{1,0:T(8,128)(2,1)S(1)} custom-call(f32[512,512]{1,0:T(8,128)S(1)} %get-tuple-element.38.near, f32[512,128]{1,0:T(8,128)S(1)} %get-tuple-element.39.tops, f32[512,128]{1,0:T(8,128)S(1)} %copy-done.8, bf16[432,512]{1,0:T(8,128)(2,1)} %collective-permute-done.3.far), custom_call_target="tpu_custom_call" | custom-call | flops 1 | bytes 1 | tf_op jit(solution)/shard_map/pallas_call | solution.py:32
  72.0 0.0 copy-start.6
  72.0 0.0 collective-permute-done.4.s1
  72.0 0.0 collective-permute-done.5.s2
  72.0 0.0 collective-permute-done.6.s3
  72.0 0.0 copy-start.10
  72.1 2.1 %collective-permute-start.7 = (bf16[256,512]{1,0:T(8,128)(2,1)S(1)}, bf16[256,512]{1,0:T(8,128)(2,1)S(1)}, u32[]{:S(2)}, u32[]{:S(2)}) collective-permute-start(bf16[256,512]{1,0:T(8,128)(2,1)S(1)} %get-tuple-element.47), channel_id=1, source_target_pairs={{0,4},{4,0},{8,12},{12,8},{16,20},{20,16},{24,28},{28,24},{32,36},... | collective-permute-start | bytes 786440 | tf_op jit(solution)/shard_map/ppermute | solution.py:308
  74.2 0.0 copy-done.10
  74.2 1.3 %shard_map.131 = bf16[256,1024]{1,0:T(8,128)(2,1)} custom-call(f32[256,1024]{1,0:T(8,128)S(1)} %get-tuple-element.36.heads, bf16[256,1024]{1,0:T(8,128)(2,1)S(1)} %copy-done.6, f32[1,1024]{1,0:T(1,128)S(1)} %bitcast.4, f32[8,256]{1,0:T(8,128)S(1)} %get-tuple-element.37.s0, f32[8,256]{1,0:T(8,128)S(1)} %collective-permute-done.4.s1, ...), custom_call_target="tpu_custom_call" | custom-call | flops 1 | bytes 1 | tf_op jit(solution)/shard_map/pallas_call | solution.py:32
  75.5 0.0 collective-permute-done.7.other
  75.5 0.8 %shard_map.133 = bf16[256,1024]{1,0:T(8,128)(2,1)} custom-call(s32[1]{0:T(128)} %bitcast.index, bf16[256,512]{1,0:T(8,128)(2,1)S(1)} %get-tuple-element.46.mine, bf16[256,512]{1,0:T(8,128)(2,1)S(1)} %collective-permute-done.7.other), custom_call_target="tpu_custom_call" | custom-call | flops 1 | bytes 1 | tf_op jit(solution)/shard_map/pallas_call | solution.py:32
  (18 shorter events, 0.1 us)
Async XLA Ops:
  3.4 16.2 %collective-permute-start = (bf16[784,512]{1,0:T(8,128)(2,1)}, bf16[784,512]{1,0:T(8,128)(2,1)S(1)}, u32[]{:S(2)}, u32[]{:S(2)}) collective-permute-start(bf16[784,512]{1,0:T(8,128)(2,1)} %shard_map.124), channel_id=1, source_target_pairs={{0,4},{4,0},{8,12},{12,8},{16,20},{20,16},{24,28},{28,24},{32,36},... | collective-permute-start | bytes 2408456 | tf_op jit(solution)/shard_map/ppermute | solution.py:308
  9.6 22.1 %all-to-all-start = ((bf16[64,16,128]{2,1,0:T(8,128)(2,1)}), bf16[64,16,128]{2,1,0:T(8,128)(2,1)S(1)}, u32[]{:S(2)}, u32[]{:S(2)}) async-start(bf16[64,16,128]{2,1,0:T(8,128)(2,1)} %bitcast.5), calls=%async_computation | async-start | bytes 524288 | tf_op jit(solution)/shard_map/all_to_all | solution.py:360
  19.6 0.9 %copy-start.16 = (bf16[784,512]{1,0:T(8,128)(2,1)}, bf16[784,512]{1,0:T(8,128)(2,1)S(1)}, u32[]{:S(2)}) copy-start(bf16[784,512]{1,0:T(8,128)(2,1)S(1)} %collective-permute-done.other) | copy-start | bytes 2408452
  23.5 8.2 %copy-start.12 = (f32[8]{0:T(128)S(1)}, f32[8]{0:T(128)}, u32[]{:S(2)}) copy-start(f32[8]{0:T(128)} %rate.5) | copy-start | bytes 100
  23.5 30.0 %collective-permute-start.2 = (bf16[1024,512]{1,0:T(8,128)(2,1)}, bf16[1024,512]{1,0:T(8,128)(2,1)S(1)}, u32[]{:S(2)}, u32[]{:S(2)}) collective-permute-start(bf16[1024,512]{1,0:T(8,128)(2,1)} %get-tuple-element.28.own), channel_id=1, source_target_pairs={{0,8},{4,12},{8,16},{12,20},{16,24},{20,28},{24,32},{28,36},{32,40... | collective-permute-start | bytes 3145736 | tf_op jit(solution)/shard_map/ppermute | solution.py:304
  24.9 12.4 %collective-permute-start.1 = (bf16[400,512]{1,0:T(8,128)(2,1)}, bf16[400,512]{1,0:T(8,128)(2,1)S(1)}, u32[]{:S(2)}, u32[]{:S(2)}) collective-permute-start(bf16[400,512]{1,0:T(8,128)(2,1)} %get-tuple-element.26), channel_id=1, source_target_pairs={{0,248},{4,252},{8,0},{12,4},{16,8},{20,12},{24,16},{28,20},{32,24... | collective-permute-start | bytes 1228808 | tf_op jit(solution)/shard_map/ppermute | solution.py:304
  31.7 15.6 %copy-start.1 = (bf16[256,1024]{1,0:T(8,128)(2,1)S(1)}, bf16[256,1024]{1,0:T(8,128)(2,1)}, u32[]{:S(2)}) copy-start(bf16[256,1024]{1,0:T(8,128)(2,1)} %v.5) | copy-start | bytes 1572868
  33.1 14.2 %copy-start = (bf16[256,1024]{1,0:T(8,128)(2,1)S(1)}, bf16[256,1024]{1,0:T(8,128)(2,1)}, u32[]{:S(2)}) copy-start(bf16[256,1024]{1,0:T(8,128)(2,1)} %k.5) | copy-start | bytes 1572868
  37.3 23.4 %all-to-all-start.1 = ((bf16[64,16,128]{2,1,0:T(8,128)(2,1)}), bf16[64,16,128]{2,1,0:T(8,128)(2,1)}, u32[]{:S(2)}, u32[]{:S(2)}) async-start(bf16[64,16,128]{2,1,0:T(8,128)(2,1)} %shard_map.123), calls=%async_computation.1 | async-start | bytes 524288 | tf_op jit(solution)/shard_map/all_to_all | solution.py:384
  47.3 1.0 %copy-start.4 = (bf16[256,1024]{1,0:T(8,128)(2,1)S(1)}, bf16[256,1024]{1,0:T(8,128)(2,1)}, u32[]{:S(2)}) copy-start(bf16[256,1024]{1,0:T(8,128)(2,1)} %q.7) | copy-start | bytes 1572868
  48.3 0.7 copy-start.13
  49.0 4.6 %copy-start.11 = (s32[128]{0:T(128)S(1)}, s32[128]{0:T(128)}, u32[]{:S(2)}) copy-start(s32[128]{0:T(128)} %docs.3) | copy-start | bytes 1540
  52.1 4.1 %copy-start.2 = (bf16[1024,512]{1,0:T(8,128)(2,1)S(1)}, bf16[1024,512]{1,0:T(8,128)(2,1)}, u32[]{:S(2)}) copy-start(bf16[1024,512]{1,0:T(8,128)(2,1)} %get-tuple-element.28.own) | copy-start | bytes 3145732
  52.1 4.1 %copy-start.3 = (bf16[512,512]{1,0:T(8,128)(2,1)S(1)}, bf16[512,512]{1,0:T(8,128)(2,1)}, u32[]{:S(2)}) copy-start(bf16[512,512]{1,0:T(8,128)(2,1)} %get-tuple-element.30.q) | copy-start | bytes 1572868
  53.6 2.7 %copy-start.9 = (f32[16,128]{1,0:T(8,128)S(1)}, f32[16,128]{1,0:T(8,128)}, u32[]{:S(2)}) copy-start(f32[16,128]{1,0:T(8,128)} %get-tuple-element.29.flags) | copy-start | bytes 24580
  56.2 14.3 %collective-permute-start.3 = (bf16[432,512]{1,0:T(8,128)(2,1)}, bf16[432,512]{1,0:T(8,128)(2,1)}, u32[]{:S(2)}, u32[]{:S(2)}) collective-permute-start(bf16[432,512]{1,0:T(8,128)(2,1)} %shard_map.126), channel_id=1, source_target_pairs={{0,8},{4,12},{8,16},{12,20},{16,24},{20,28},{24,32},{28,36},{32,40... | collective-permute-start | bytes 1327112 | tf_op jit(solution)/shard_map/ppermute | solution.py:304
  60.0 0.7 copy-start.7
  60.7 0.7 copy-start.14
  61.4 1.0 %copy-start.5 = (bf16[256,1024]{1,0:T(8,128)(2,1)S(1)}, bf16[256,1024]{1,0:T(8,128)(2,1)}, u32[]{:S(2)}) copy-start(bf16[256,1024]{1,0:T(8,128)(2,1)} %q.7) | copy-start | bytes 1572868
  62.4 1.0 %copy-start.15 = (f32[1024,128]{1,0:T(8,128)S(1)}, f32[1024,128]{1,0:T(8,128)}, u32[]{:S(2)}) copy-start(f32[1024,128]{1,0:T(8,128)} %get-tuple-element.33.first) | copy-start | bytes 1572868
  63.4 7.0 %copy-start.8 = (f32[512,128]{1,0:T(8,128)S(1)}, f32[512,128]{1,0:T(8,128)}, u32[]{:S(2)}) copy-start(f32[512,128]{1,0:T(8,128)} %copy-done.7) | copy-start | bytes 786436
  65.0 7.0 %collective-permute-start.4 = (f32[8,256]{1,0:T(8,128)S(1)}, f32[8,256]{1,0:T(8,128)S(1)}, u32[]{:S(2)}, u32[]{:S(2)}) collective-permute-start(f32[8,256]{1,0:T(8,128)S(1)} %get-tuple-element.37.s0), channel_id=1, source_target_pairs={{0,1},{1,2},{2,3},{3,0},{4,5},{5,6},{6,7},{7,4},{8,9},{9,10},{10,1... | collective-permute-start | bytes 24584 | tf_op jit(solution)/shard_map/ppermute | solution.py:312
  66.4 5.6 %collective-permute-start.5 = (f32[8,256]{1,0:T(8,128)S(1)}, f32[8,256]{1,0:T(8,128)S(1)}, u32[]{:S(2)}, u32[]{:S(2)}) collective-permute-start(f32[8,256]{1,0:T(8,128)S(1)} %get-tuple-element.37.s0), channel_id=1, source_target_pairs={{0,2},{1,3},{2,0},{3,1},{4,6},{5,7},{6,4},{7,5},{8,10},{9,11},{10,... | collective-permute-start | bytes 24584 | tf_op jit(solution)/shard_map/ppermute | solution.py:312
  68.8 3.2 %collective-permute-start.6 = (f32[8,256]{1,0:T(8,128)S(1)}, f32[8,256]{1,0:T(8,128)S(1)}, u32[]{:S(2)}, u32[]{:S(2)}) collective-permute-start(f32[8,256]{1,0:T(8,128)S(1)} %get-tuple-element.37.s0), channel_id=1, source_target_pairs={{0,3},{1,0},{2,1},{3,2},{4,7},{5,4},{6,5},{7,6},{8,11},{9,8},{10,9... | collective-permute-start | bytes 24584 | tf_op jit(solution)/shard_map/ppermute | solution.py:312
  72.0 2.2 %copy-start.6 = (bf16[256,1024]{1,0:T(8,128)(2,1)S(1)}, bf16[256,1024]{1,0:T(8,128)(2,1)}, u32[]{:S(2)}) copy-start(bf16[256,1024]{1,0:T(8,128)(2,1)} %gate.1) | copy-start | bytes 1572868
  72.0 2.2 %copy-start.10 = (f32[1024]{0:T(1024)S(1)}, f32[1024]{0:T(1024)}, u32[]{:S(2)}) copy-start(f32[1024]{0:T(1024)} %param.15) | copy-start | bytes 12292
  72.1 3.4 %collective-permute-start.7 = (bf16[256,512]{1,0:T(8,128)(2,1)S(1)}, bf16[256,512]{1,0:T(8,128)(2,1)S(1)}, u32[]{:S(2)}, u32[]{:S(2)}) collective-permute-start(bf16[256,512]{1,0:T(8,128)(2,1)S(1)} %get-tuple-element.47), channel_id=1, source_target_pairs={{0,4},{4,0},{8,12},{12,8},{16,20},{20,16},{24,28},{28,24},{32,36},... | collective-permute-start | bytes 786440 | tf_op jit(solution)/shard_map/ppermute | solution.py:308

commit v3 on v2

v3 whole, which is shorter than its diff:
```python
import math

import jax
import jax.numpy as jnp
from jax import lax
from jax.experimental import pallas as pl
from jax.experimental.pallas import tpu as pltpu
from jax.sharding import PartitionSpec as P

HD = 128
BLK = 128
NBLK = 128
ROWS = 256
LOCAL = 8
WIDTH = LOCAL * HD
HALF = WIDTH // 2
HEADS = LOCAL // 2
D = 4096
SHARDS = 64
FILL = -1e30
PREFIX_COST = 5_000_000_000
CARRY_COST = 10_000_000_000
EXP2_SCALE = HD ** (-0.5) * math.log2(math.e)

f32 = jnp.float32
bf16 = jnp.bfloat16

SMEM = pl.BlockSpec(memory_space=pltpu.SMEM)
VMEM = pl.BlockSpec(memory_space=pltpu.VMEM)


def call(body, outs, ins, specs, scratch=(), flops=1, room=16):
    return pl.pallas_call(
        body,
        out_shape=outs,
        in_specs=specs,
        out_specs=[VMEM] * len(outs),
        scratch_shapes=list(scratch),
        compiler_params=pltpu.CompilerParams(vmem_limit_bytes=room * 1024 * 1024),
        cost_estimate=pl.CostEstimate(flops=flops, bytes_accessed=1, transcendentals=0),
    )(*ins)


def cols(h):
    return slice(h * HD, (h + 1) * HD)


def dot(a, b, dims):
    return lax.dot_general(a, b, (dims, ((), ())), preferred_element_type=f32)


def exact_dot(a, b, dims):
    return lax.dot_general(
        a, b, (dims, ((), ())), precision=lax.Precision.HIGHEST, preferred_element_type=f32
    )


def start_body(
    index, rate_hbm, mask, k_hbm, v_hbm, sq, sk, sv, first, out, sent, rate, k, v, rate_sem, sems
):
    other = 1 - index[0] % 2
    copies = [pltpu.make_async_copy(rate_hbm, rate, rate_sem)]
    for g in range(LOCAL // 2):
        at = slice(g * 2 * HD, (g + 1) * 2 * HD)
        copies.append(pltpu.make_async_copy(k_hbm.at[:, at], k.at[:, at], sems.at[2 * g]))
        copies.append(pltpu.make_async_copy(v_hbm.at[:, at], v.at[:, at], sems.at[2 * g + 1]))
    for at, ref in enumerate((sq, sk, sv)):
        rows = slice(at * ROWS, (at + 1) * ROWS)
        copies.append(
            pltpu.make_async_copy(ref.at[:, half(other)], sent.at[rows, :], sems.at[LOCAL + at])
        )
    for copy in copies:
        copy.start()
    flags = mask[...].astype(f32)
    flags = jnp.concatenate([flags, jnp.zeros((14, NBLK), f32)], axis=0).astype(bf16)
    sent[3 * ROWS :, :] = jnp.concatenate([flags] * 4, axis=1)
    copies[0].wait()
    back = (BLK - 1.0) - lax.broadcasted_iota(jnp.int32, (BLK, HD), 0).astype(f32)
    for g in range(LOCAL // 2):
        copies[2 * g + 1].wait()
        copies[2 * g + 2].wait()
        for h in (2 * g, 2 * g + 1):
            decay = jnp.exp(-rate[h] * back)
            parts = []
            for b in range(2):
                rows = slice(b * BLK, (b + 1) * BLK)
                decayed = (k[rows, cols(h)].astype(f32) * decay).astype(bf16)
                parts.append(dot(decayed, v[rows, cols(h)], ((0,), (0,))))
            step = jnp.exp(jnp.full((HD, HD), -rate[h] * BLK, f32))
            first[cols(h), :] = parts[0]
            out[cols(h), :] = (step * parts[0] + parts[1]).astype(bf16)
    for copy in copies[LOCAL + 1 :]:
        copy.wait()


def prefix_body(index, rate, parts, out):
    step = jnp.exp(jnp.full((16, HD), -rate[index[0] // 8] * ROWS, f32))
    state = jnp.zeros((16, HD), f32)
    for i in range(SHARDS):
        out[i] = state.astype(bf16)
        if i + 1 < SHARDS:
            state = step * state + parts[i].astype(f32)


def inner_body(rate, q, k, v, out):
    row = lax.broadcasted_iota(jnp.int32, (BLK, BLK), 0)
    col = lax.broadcasted_iota(jnp.int32, (BLK, BLK), 1)
    gap = jnp.maximum(row - col, 0).astype(f32)
    for h in range(LOCAL):
        decay = jnp.where(row >= col, jnp.exp(-rate[h] * gap), 0.0)
        for b in range(2):
            rows = slice(b * BLK, (b + 1) * BLK)
            scores = dot(q[rows, cols(h)], k[rows, cols(h)], ((1,), (1,)))
            out[rows, cols(h)] = dot(
                (scores * decay).astype(bf16), v[rows, cols(h)], ((1,), (0,))
            )


def carry_body(
    rate_hbm, inner_hbm, q_hbm, first_hbm, state, heads, squares, rate, inner, q, first, rate_sem, sems
):
    copies = [pltpu.make_async_copy(rate_hbm, rate, rate_sem)]
    for g in range(LOCAL // 2):
        at = slice(g * 2 * HD, (g + 1) * 2 * HD)
        copies.append(pltpu.make_async_copy(q_hbm.at[:, at], q.at[:, at], sems.at[3 * g]))
        copies.append(pltpu.make_async_copy(first_hbm.at[at, :], first.at[at, :], sems.at[3 * g + 1]))
        copies.append(pltpu.make_async_copy(inner_hbm.at[:, at], inner.at[:, at], sems.at[3 * g + 2]))
    for copy in copies:
        copy.start()
    copies[0].wait()
    ahead = lax.broadcasted_iota(jnp.int32, (BLK, HD), 0).astype(f32) + 1.0
    totals = [jnp.zeros((BLK, HD), f32)] * 2
    for h in range(LOCAL):
        if h % 2 == 0:
            for copy in copies[3 * (h // 2) + 1 : 3 * (h // 2) + 4]:
                copy.wait()
        step = jnp.exp(jnp.full((HD, HD), -rate[h] * BLK, f32))
        decay = jnp.exp(-rate[h] * ahead)
        entering = state[cols(h), :]
        middle = (step * entering.astype(f32) + first[cols(h), :]).astype(bf16)
        for b, block_state in enumerate((entering, middle)):
            rows = slice(b * BLK, (b + 1) * BLK)
            carried = dot(q[rows, cols(h)], block_state, ((1,), (0,)))
            value = inner[rows, cols(h)] + carried * decay
            heads[rows, cols(h)] = value
            totals[b] = totals[b] + value * value
    total = jnp.concatenate(totals, axis=0)
    squares[...] = exact_dot(jnp.ones((8, HD), f32), total, ((1,), (1,)))


def norm_body(heads, gate, gain, s0, s1, s2, s3, out):
    total = s0[...] + s1[...] + s2[...] + s3[...]
    first = (lax.broadcasted_iota(jnp.int32, (8, HD), 0) == 0).astype(f32)
    spread = exact_dot(total, first, ((0,), (0,)))
    inverse = lax.rsqrt(spread / D + 1e-06)
    for h in range(LOCAL):
        scale = gain[:, cols(h)] * jax.nn.sigmoid(gate[:, cols(h)].astype(f32))
        out[:, cols(h)] = (heads[:, cols(h)] * inverse * scale).astype(bf16)


def half(c):
    return pl.ds(pl.multiple_of(c * HALF, HALF), HALF)


def gather_body(index, mask, q, k, v, other, near_q, far_q, pair, tail, flags):
    core = index[0] % 2

    def lay(at, mine):
        theirs = other[at * ROWS : (at + 1) * ROWS, :]
        first = jnp.where(core == 0, mine, theirs)
        second = jnp.where(core == 0, theirs, mine)
        return first, second

    for at, ref in enumerate((q, k, v)):
        low, high = lay(at, ref[:, half(core)])
        if at == 0:
            for out in (near_q, far_q):
                out[:ROWS, :] = low
                out[ROWS : 2 * ROWS, :] = high
        else:
            base = (at - 1) * 2 * ROWS
            pair[base : base + ROWS, :] = low
            pair[base + ROWS : base + 2 * ROWS, :] = high
            base = (at - 1) * 3 * BLK
            tail[base : base + BLK, :] = low[BLK:]
            tail[base + BLK : base + 3 * BLK, :] = high
    own = mask[...].astype(f32)
    theirs = other[3 * ROWS :, :NBLK].astype(f32)[:2]
    first = jnp.where(core == 0, own, theirs)
    second = jnp.where(core == 0, theirs, own)
    rows = jnp.concatenate([first, second, jnp.zeros((12, NBLK), f32)], axis=0)
    flags[...] = rows
    far_q[4 * BLK :, :] = jnp.concatenate([rows.astype(bf16)] * 4, axis=1)


def allowed(docs, flags, i, query, key):
    q_at = jnp.clip(query, 0, NBLK - 1)
    k_at = jnp.clip(key, 0, NBLK - 1)
    inside = (key >= 0) & (key < query) & (query < NBLK) & (docs[k_at] == docs[q_at])
    lane = lax.broadcasted_iota(jnp.int32, (1, NBLK), 1)
    wanted = jnp.where(inside, k_at, -1)
    ok = jnp.sum(jnp.where(lane == wanted, flags[i : i + 1, :], 0.0), axis=1, keepdims=True)
    return jnp.broadcast_to(jnp.where(ok > 0.5, 0.0, FILL), (BLK, BLK))


def block(i):
    return slice(i * BLK, (i + 1) * BLK)


def attend_head(q, keys, values, bias):
    scores = dot(q, keys, ((1,), (1,))) + bias
    top = jnp.max(scores, axis=1, keepdims=True)
    weights = jnp.exp2((scores - top) * EXP2_SCALE).astype(bf16)
    ones = jnp.ones(values.shape, bf16)
    both = dot(weights, jnp.concatenate([values, ones], axis=1), ((1,), (0,)))
    return both[:, :HD], top, both[:, HD:]


def attend_chip(index, docs, rows, ahead, q, pair, out, tops, sums, bias):
    chip = index[0] // 2
    for i in range(4):
        for j in range(4):
            if ahead == 0 and j == i:
                row = lax.broadcasted_iota(jnp.int32, (BLK, BLK), 0)
                col = lax.broadcasted_iota(jnp.int32, (BLK, BLK), 1)
                bias[block(i), block(j)] = jnp.where(col <= row, 0.0, FILL)
            elif ahead == 0 and j > i:
                bias[block(i), block(j)] = jnp.full((BLK, BLK), FILL, f32)
            else:
                bias[block(i), block(j)] = allowed(
                    docs, rows, i, 4 * (chip + ahead) + i, 4 * chip + j
                )
    lane = lax.broadcasted_iota(jnp.int32, (2 * BLK, HD), 1)
    for r in range(2):
        part = slice(r * 2 * BLK, (r + 1) * 2 * BLK)
        count = 4 * BLK if ahead or r else 2 * BLK
        top_table = jnp.zeros((2 * BLK, HD), f32)
        sum_table = jnp.zeros((2 * BLK, HD), f32)
        for h in range(HEADS):
            acc, top, total = attend_head(
                q[part, cols(h)],
                pair[:count, cols(h)],
                pair[4 * BLK : 4 * BLK + count, cols(h)],
                bias[part, :count],
            )
            out[part, cols(h)] = acc / total
            top_table = jnp.where(lane == h, top, top_table)
            sum_table = jnp.where(lane == h, total, sum_table)
        tops[part, :] = top_table
        sums[part, :] = sum_table


def near_body(index, docs, flags, q, pair, out, tops, sums, bias):
    attend_chip(index, docs, flags[...], 0, q, pair, out, tops, sums, bias)


def next_body(index, docs, q, pair, out, tops, sums, bias):
    rows = q[4 * BLK :, :NBLK].astype(f32)
    attend_chip(index, docs, rows, 1, q, pair, out, tops, sums, bias)


def weighed(top1, sum1, top2, sum2):
    top = jnp.maximum(top1, top2)
    part1 = jnp.exp2((top1 - top) * EXP2_SCALE) * sum1
    part2 = jnp.exp2((top2 - top) * EXP2_SCALE) * sum2
    return top, part1 + part2, part2 / (part1 + part2)


def far_body(index, docs, q, tail, done, tops, sums, out, bias):
    chip = index[0] // 2
    flags = q[4 * BLK :, :NBLK].astype(f32)
    for i in range(3):
        for j in range(3):
            bias[block(i), block(j)] = allowed(
                docs, flags, i, 4 * (chip + 1) + i, 4 * (chip - 1) + 1 + j
            )
    rows = slice(0, 3 * BLK)
    rest = slice(3 * BLK, 4 * BLK)
    lane = lax.broadcasted_iota(jnp.int32, (3 * BLK, HD), 1)
    top_table = jnp.zeros((3 * BLK, HD), f32)
    sum_table = jnp.ones((3 * BLK, HD), f32)
    for h in range(HEADS):
        acc, top, total = attend_head(
            q[rows, cols(h)], tail[rows, cols(h)], tail[3 * BLK :, cols(h)], bias[...]
        )
        top_table = jnp.where(lane == h, top, top_table)
        sum_table = jnp.where(lane == h, total, sum_table)
        top1 = tops[rows, h : h + 1]
        _, _, share = weighed(top1, sums[rows, h : h + 1], top, total)
        here = done[rows, cols(h)]
        out[rows, cols(h)] = (here + (acc / total - here) * share).astype(bf16)
        out[rest, cols(h)] = done[rest, cols(h)].astype(bf16)
    top, total, _ = weighed(tops[rows, :], jnp.where(lane < HEADS, sums[rows, :], 1.0), top_table, sum_table)
    top = jnp.concatenate([top, tops[rest, :]], axis=0)
    total = jnp.concatenate([total, sums[rest, :]], axis=0)
    filler = jnp.zeros((LOCAL, 4 * BLK), f32)
    left = jnp.concatenate([top.T[:HEADS], total.T[:HEADS], filler], axis=0)
    for piece in range(3):
        part = left.astype(bf16)
        at = 4 * BLK + piece * 2 * LOCAL
        out[at : at + 2 * LOCAL, :] = part
        left = left - part.astype(f32)


def merge_body(index, near, tops, sums, far, mine, send, share):
    stats = jnp.zeros((2 * LOCAL, HALF), f32)
    for p in range(3):
        at = 4 * BLK + p * 2 * LOCAL
        stats = stats + far[at : at + 2 * LOCAL, :].astype(f32)
    pad = jnp.ones((HD - HEADS, 4 * BLK), f32)
    far_tops = jnp.concatenate([stats[:HEADS], pad], axis=0).T
    far_sums = jnp.concatenate([stats[HEADS : 2 * HEADS], pad], axis=0).T
    lane = lax.broadcasted_iota(jnp.int32, (4 * BLK, HD), 1)
    near_sums = jnp.where(lane < HEADS, sums[...], 1.0)
    share[...] = weighed(tops[...], near_sums, far_tops, far_sums)[2]
    core = index[0] % 2
    for out, which in ((send, 1 - core), (mine, core)):
        rows = pl.ds(pl.multiple_of(which * ROWS, ROWS), ROWS)
        part = share[rows, :]
        for h in range(HEADS):
            own = near[rows, cols(h)]
            there = far[rows, cols(h)].astype(f32)
            out[:, cols(h)] = (own + (there - own) * part[:, h : h + 1]).astype(bf16)


def place_body(index, mine, other, out):
    core = index[0] % 2
    out[:, half(core)] = mine[...]
    out[:, half(1 - core)] = other[...]


def shifted(x, distance):
    return lax.ppermute(x, "seq", [(i, (i + distance) % SHARDS) for i in range(SHARDS)])


def swapped(x):
    return lax.ppermute(x, "seq", [(i, i ^ 1) for i in range(SHARDS)])


def turned(x, distance):
    return lax.ppermute(x, "head", [(i, (i + distance) % 4) for i in range(4)])


def per_device(
    lin_query,
    lin_key,
    lin_value,
    out_gate,
    norm_gain,
    decay_rate,
    soft_query,
    soft_key,
    soft_value,
    doc_ids,
    block_mask,
):
    like = jax.ShapeDtypeStruct
    index = lax.axis_index("seq").astype(jnp.int32).reshape(1)
    wide = like((ROWS, WIDTH), f32)
    narrow = like((ROWS, WIDTH), bf16)

    anywhere = pl.BlockSpec(memory_space=pl.ANY)
    first, state, sent = call(
        start_body,
        [like((WIDTH, HD), f32), like((WIDTH, HD), bf16), like((3 * ROWS + 16, HALF), bf16)],
        (index, decay_rate, block_mask, lin_key, lin_value, soft_query, soft_key, soft_value),
        [SMEM, anywhere, VMEM] + [anywhere] * 5,
        [
            pltpu.SMEM((LOCAL,), f32),
            pltpu.VMEM((ROWS, WIDTH), bf16),
            pltpu.VMEM((ROWS, WIDTH), bf16),
            pltpu.SemaphoreType.DMA,
            pltpu.SemaphoreType.DMA((LOCAL + 3,)),
        ],
        room=56,
    )
    other = swapped(sent)
    parts = lax.all_to_all(state.reshape(SHARDS, 16, HD), "seq", 0, 0)
    near_q, far_q, own_pair, own_tail, flags = call(
        gather_body,
        [
            like((2 * ROWS, HALF), bf16),
            like((2 * ROWS + 16, HALF), bf16),
            like((8 * BLK, HALF), bf16),
            like((6 * BLK, HALF), bf16),
            like((16, NBLK), f32),
        ],
        (index, block_mask, soft_query, soft_key, soft_value, other),
        [SMEM] + [VMEM] * 5,
        room=56,
    )
    tail = shifted(own_tail, 2)
    next_q = shifted(far_q, -2)

    (prefix,) = call(
        prefix_body,
        [like((SHARDS, 16, HD), bf16)],
        (index, decay_rate, parts),
        [SMEM, SMEM, VMEM],
        flops=PREFIX_COST,
    )
    prefix, doc_ids = lax.optimization_barrier((prefix, doc_ids))
    entering = lax.all_to_all(prefix, "seq", 0, 0).reshape(WIDTH, HD)
    (inner,) = call(
        inner_body,
        [wide],
        (decay_rate, lin_query, lin_key, lin_value),
        [SMEM, VMEM, VMEM, VMEM],
    )
    tables = [like((4 * BLK, HALF), f32), like((4 * BLK, HD), f32), like((4 * BLK, HD), f32)]
    near, tops, sums = call(
        near_body,
        tables,
        (index, doc_ids, flags, near_q, own_pair),
        [SMEM] * 2 + [VMEM] * 3,
        [pltpu.VMEM((4 * BLK, 4 * BLK), f32)],
    )
    done, done_tops, done_sums = call(
        next_body,
        tables,
        (index, doc_ids, next_q, own_pair),
        [SMEM] * 2 + [VMEM] * 2,
        [pltpu.VMEM((4 * BLK, 4 * BLK), f32)],
    )
    (far,) = call(
        far_body,
        [like((4 * BLK + 48, HALF), bf16)],
        (index, doc_ids, next_q, tail, done, done_tops, done_sums),
        [SMEM] * 2 + [VMEM] * 5,
        [pltpu.VMEM((3 * BLK, 3 * BLK), f32)],
    )
    far = shifted(far, 2)
    heads, squares = call(
        carry_body,
        [wide, like((8, ROWS), f32)],
        (decay_rate, inner, lin_query, first, entering),
        [anywhere] * 4 + [VMEM],
        [
            pltpu.SMEM((LOCAL,), f32),
            pltpu.VMEM((ROWS, WIDTH), f32),
            pltpu.VMEM((ROWS, WIDTH), bf16),
            pltpu.VMEM((WIDTH, HD), f32),
            pltpu.SemaphoreType.DMA,
            pltpu.SemaphoreType.DMA((3 * LOCAL // 2,)),
        ],
        flops=CARRY_COST,
        room=56,
    )
    others = [turned(squares, d) for d in (1, 2, 3)]
    far, heads = lax.optimization_barrier((far, heads))
    mine, send = call(
        merge_body,
        [like((ROWS, HALF), bf16)] * 2,
        (index, near, tops, sums, far),
        [SMEM] + [VMEM] * 4,
        [pltpu.VMEM((4 * BLK, HD), f32)],
    )
    send, *others = lax.optimization_barrier((send, *others))
    (lin_output,) = call(
        norm_body,
        [narrow],
        (heads, out_gate, norm_gain.reshape(1, WIDTH), squares, *others),
        [VMEM] * 7,
    )

    (soft_output,) = call(
        place_body, [narrow], (index, mine, swapped(send)), [SMEM, VMEM, VMEM]
    )
    return (lin_output, soft_output)


def solution(mesh):
    rows = P("seq", "head")
    return jax.shard_map(
        per_device,
        mesh=mesh,
        in_specs=(
            rows, rows, rows, rows, P("head"), P("head"), rows, rows, rows, P(), P("seq", None),
        ),
        out_specs=(rows, rows),
        check_vma=False,
    )
```

time: 77.5 us -> 76.4 us (0.986); the launches traced: 76.3 us -> 76 us
  waiting for transfers between devices: 9.23 us -> 12.3 us
  local copies, waits for them, and re-layouts: 6.06 us -> 3.58 us
  starting transfers between devices: 35.5 us -> 34.5 us
    all_to_all x1, starting transfers between devices: 9.91 us -> 6.61 us  [per_device(): entering = lax.all_to_all(prefix, 'seq', 0, 0).reshape(WIDTH, HD)]
    pallas_call x11, Pallas kernels: 21.9 us -> 24.9 us  [call(): pl.pallas_call(body, out_shape=outs, in_specs=specs, out_specs=[VMEM] * l...]
    pallas_call x1 -> x0, Pallas kernels: 2.85 us -> none  [per_device(): pl.pallas_call(state_body, out_shape=[like((WIDTH, HD), f32), like((WIDTH...]
    unnamed x34 -> x28, local copies, waits for them, and re-layouts: 6.06 us -> 3.58 us
    ppermute x2, starting transfers between devices: 5.45 us -> 7.83 us  [swapped(): return lax.ppermute(x, 'seq', [(i, i ^ 1) for i in range(SHARDS)])]
    ppermute x3, waiting for transfers between devices: 6.16 us -> 8.07 us  [shifted(): lax.ppermute(x, 'seq', [(i, (i + distance) % SHARDS) for i in range(SHARD...]
    all_to_all x1, waiting for transfers between devices: 0.01 us -> 1.5 us  [per_device(): entering = lax.all_to_all(prefix, 'seq', 0, 0).reshape(WIDTH, HD)]
  transfers between devices with their start and end apart: 10 -> 10, of which waited for: 4 -> 4; matrix products, arithmetic and copies ran while one was open for 0% -> 0% of each run, Pallas kernels for 28% -> 27%
where the time goes in v3:
time: 76.4 us; the launch traced here: 76 us
  starting transfers between devices  34.5 us (45%)
  Pallas kernels  24.9 us (33%)
  waiting for transfers between devices  12.3 us (16%)
  local copies, waits for them, and re-layouts  3.58 us (5%)
  between operations  0.8 us (1%)
    pallas_call x11, Pallas kernels, call(): pl.pallas_call(body, out_shape=outs, in_specs=specs, out_specs=[VMEM] * l...  24.9 us
    all_to_all x1, starting transfers between devices, per_device(): parts = lax.all_to_all(state.reshape(SHARDS, 16, HD), 'seq', 0, 0)  10 us
    ppermute x3, waiting for transfers between devices, shifted(): lax.ppermute(x, 'seq', [(i, (i + distance) % SHARDS) for i in range(SHARD...  8.07 us
    ppermute x2, starting transfers between devices, swapped(): return lax.ppermute(x, 'seq', [(i, i ^ 1) for i in range(SHARDS)])  7.83 us
    all_to_all x1, starting transfers between devices, per_device(): entering = lax.all_to_all(prefix, 'seq', 0, 0).reshape(WIDTH, HD)  6.61 us
    ppermute x3, starting transfers between devices, shifted(): lax.ppermute(x, 'seq', [(i, (i + distance) % SHARDS) for i in range(SHARD...  5.1 us
    ppermute x3, starting transfers between devices, turned(): return lax.ppermute(x, 'head', [(i, (i + distance) % 4) for i in range(4)])  4.89 us
    unnamed x28, local copies, waits for them, and re-layouts  3.58 us
  transfers between devices with their start and end apart: 10, of which 4 were waited for; matrix products, arithmetic and copies ran while one was open for 0% of the time, Pallas kernels for 27%

profile of v3, /device:TPU:1, one launch (start us, length us, event | category | flops | bytes accessed | tf_op | source)
XLA Modules:
  0.0 76.0 jit_solution(12477903378262344642)
XLA Ops:
  0.6 3.9 %shard_map.122 = (f32[1024,128]{1,0:T(8,128)}, bf16[1024,128]{1,0:T(8,128)(2,1)}, bf16[784,512]{1,0:T(8,128)(2,1)}) custom-call(s32[1]{0:T(128)} %bitcast.index, f32[8]{0:T(128)} %rate_hbm.3, s32[2,128]{1,0:T(2,128)} %mask.3, bf16[256,1024]{1,0:T(8,128)(2,1)} %k.3, bf16[256,1024]{1,0:T(8,128)(2,1)} %v.3, bf16[256,1024]{1,0:T(8,128)(2,1)} %q.2, ...), custom_call_target="tpu_custom_call" | custom-call | flops 1 | bytes 1 | tf_op jit(solution)/shard_map/pallas_call | solution.py:33
  4.5 3.3 %collective-permute-start = (bf16[784,512]{1,0:T(8,128)(2,1)}, bf16[784,512]{1,0:T(8,128)(2,1)S(1)}, u32[]{:S(2)}, u32[]{:S(2)}) collective-permute-start(bf16[784,512]{1,0:T(8,128)(2,1)} %get-tuple-element.30), channel_id=1, source_target_pairs={{0,4},{4,0},{8,12},{12,8},{16,20},{20,16},{24,28},{28,24},{32,36},... | collective-permute-start | bytes 2408456 | tf_op jit(solution)/shard_map/ppermute | solution.py:337
  7.8 10.0 %all-to-all-start = ((bf16[64,16,128]{2,1,0:T(8,128)(2,1)}), bf16[64,16,128]{2,1,0:T(8,128)(2,1)S(1)}, u32[]{:S(2)}, u32[]{:S(2)}) async-start(bf16[64,16,128]{2,1,0:T(8,128)(2,1)} %bitcast.5), calls=%async_computation | async-start | bytes 524288 | tf_op jit(solution)/shard_map/all_to_all | solution.py:378
  17.9 0.0 collective-permute-done.other
  17.9 0.0 copy-start.13
  17.9 0.9 %copy-done.13 = bf16[784,512]{1,0:T(8,128)(2,1)} copy-done((bf16[784,512]{1,0:T(8,128)(2,1)}, bf16[784,512]{1,0:T(8,128)(2,1)S(1)}, u32[]{:S(2)}) %copy-start.13) | copy-done | bytes 802840
  18.8 3.3 %shard_map.124 = (bf16[512,512]{1,0:T(8,128)(2,1)}, bf16[528,512]{1,0:T(8,128)(2,1)}, bf16[1024,512]{1,0:T(8,128)(2,1)}, bf16[768,512]{1,0:T(8,128)(2,1)}, f32[16,128]{1,0:T(8,128)}) custom-call(s32[1]{0:T(128)} %bitcast.index, s32[2,128]{1,0:T(2,128)} %mask.3, bf16[256,1024]{1,0:T(8,128)(2,1)} %q.2, bf16[256,1024]{1,0:T(8,128)(2,1)} %k.2, ...), custom_call_target="tpu_custom_call" | custom-call | flops 1 | bytes 1 | tf_op jit(solution)/shard_map/pallas_call | solution.py:33
  22.1 5.0 %collective-permute-start.1 = (bf16[528,512]{1,0:T(8,128)(2,1)}, bf16[528,512]{1,0:T(8,128)(2,1)S(1)}, u32[]{:S(2)}, u32[]{:S(2)}) collective-permute-start(bf16[528,512]{1,0:T(8,128)(2,1)} %get-tuple-element.31), channel_id=1, source_target_pairs={{0,248},{4,252},{8,0},{12,4},{16,8},{20,12},{24,16},{28,20},{32,24... | collective-permute-start | bytes 1622024 | tf_op jit(solution)/shard_map/ppermute | solution.py:333
  27.1 0.0 collective-permute-start.2
  27.1 2.8 %all-to-all-done.parts = bf16[64,16,128]{2,1,0:T(8,128)(2,1)S(1)} async-done(((bf16[64,16,128]{2,1,0:T(8,128)(2,1)}), bf16[64,16,128]{2,1,0:T(8,128)(2,1)S(1)}, u32[]{:S(2)}, u32[]{:S(2)}) %all-to-all-start) | async-done | bytes 262176 | tf_op jit(solution)/shard_map/all_to_all | solution.py:378
  29.9 0.0 copy-done.12
  29.9 1.4 %shard_map.123 = bf16[64,16,128]{2,1,0:T(8,128)(2,1)} custom-call(s32[1]{0:T(128)} %bitcast.index, f32[8]{0:T(128)S(1)} %copy-done.12, bf16[64,16,128]{2,1,0:T(8,128)(2,1)S(1)} %all-to-all-done.parts), custom_call_target="tpu_custom_call" | custom-call | flops 5000000000 | bytes 1 | tf_op jit(solution)/shard_map/pallas_call | solution.py:33
  31.2 6.6 %all-to-all-start.1 = ((bf16[64,16,128]{2,1,0:T(8,128)(2,1)}), bf16[64,16,128]{2,1,0:T(8,128)(2,1)}, u32[]{:S(2)}, u32[]{:S(2)}) async-start(bf16[64,16,128]{2,1,0:T(8,128)(2,1)} %shard_map.123), calls=%async_computation.1 | async-start | bytes 524288 | tf_op jit(solution)/shard_map/all_to_all | solution.py:403
  37.9 0.0 copy-done.2
  37.9 0.0 copy-done.1
  37.9 0.0 copy-start.5
  37.9 1.0 %copy-done.5 = bf16[256,1024]{1,0:T(8,128)(2,1)S(1)} copy-done((bf16[256,1024]{1,0:T(8,128)(2,1)S(1)}, bf16[256,1024]{1,0:T(8,128)(2,1)}, u32[]{:S(2)}) %copy-start.5) | copy-done | bytes 524312
  38.9 3.1 %shard_map.127.inner_hbm = f32[256,1024]{1,0:T(8,128)S(1)} custom-call(f32[8]{0:T(128)S(1)} %copy-done.12, bf16[256,1024]{1,0:T(8,128)(2,1)S(1)} %copy-done.5, bf16[256,1024]{1,0:T(8,128)(2,1)S(1)} %copy-done.1, bf16[256,1024]{1,0:T(8,128)(2,1)S(1)} %copy-done.2), custom_call_target="tpu_custom_call" | custom-call | flops 1 | bytes 1 | tf_op jit(solution)/shard_map/pallas_call | solution.py:33
  42.1 0.0 copy-start.4
  42.1 1.0 %copy-done.4 = f32[256,1024]{1,0:T(8,128)} copy-done((f32[256,1024]{1,0:T(8,128)}, f32[256,1024]{1,0:T(8,128)S(1)}, u32[]{:S(2)}) %copy-start.4) | copy-done | bytes 1048600
  43.0 0.0 collective-permute-done.1.q
  43.0 0.0 copy-done
  43.0 0.6 copy-done.10
  43.7 2.2 %shard_map.125 = (f32[512,512]{1,0:T(8,128)S(1)}, f32[512,128]{1,0:T(8,128)S(1)}, f32[512,128]{1,0:T(8,128)S(1)}) custom-call(s32[1]{0:T(128)} %bitcast.index, s32[128]{0:T(128)S(1)} %copy-done.10, bf16[528,512]{1,0:T(8,128)(2,1)S(1)} %collective-permute-done.1.q, bf16[1024,512]{1,0:T(8,128)(2,1)S(1)} %copy-done), custom_call_target="tpu_custom_call" | custom-call | flops 1 | bytes 1 | tf_op jit(solution)/shard_map/pallas_call | solution.py:33
  45.9 6.2 %collective-permute-done.2.tail = bf16[768,512]{1,0:T(8,128)(2,1)S(1)} collective-permute-done((bf16[768,512]{1,0:T(8,128)(2,1)}, bf16[768,512]{1,0:T(8,128)(2,1)S(1)}, u32[]{:S(2)}, u32[]{:S(2)}) %collective-permute-start.2) | collective-permute-done | bytes 786464 | tf_op jit(solution)/shard_map/ppermute | solution.py:333
  52.1 2.2 %shard_map.126 = bf16[560,512]{1,0:T(8,128)(2,1)S(1)} custom-call(s32[1]{0:T(128)} %bitcast.index, s32[128]{0:T(128)S(1)} %copy-done.10, bf16[528,512]{1,0:T(8,128)(2,1)S(1)} %collective-permute-done.1.q, bf16[768,512]{1,0:T(8,128)(2,1)S(1)} %collective-permute-done.2.tail, f32[512,512]{1,0:T(8,128)S(1)} %get-tuple-element.34.done, ...), custom_call_target="tpu_custom_call" | custom-call | flops 1 | bytes 1 | tf_op jit(solution)/shard_map/pallas_call | solution.py:33
  54.3 0.1 collective-permute-start.3
  54.4 1.5 %all-to-all-done.1 = bf16[64,16,128]{2,1,0:T(8,128)(2,1)} async-done(((bf16[64,16,128]{2,1,0:T(8,128)(2,1)}), bf16[64,16,128]{2,1,0:T(8,128)(2,1)}, u32[]{:S(2)}, u32[]{:S(2)}) %all-to-all-start.1) | async-done | bytes 262176 | tf_op jit(solution)/shard_map/all_to_all | solution.py:403
  55.9 4.0 %shard_map.128 = (f32[256,1024]{1,0:T(8,128)}, f32[8,256]{1,0:T(8,128)}) custom-call(f32[8]{0:T(128)} %rate_hbm.3, f32[256,1024]{1,0:T(8,128)} %copy-done.4, bf16[256,1024]{1,0:T(8,128)(2,1)} %q_hbm.1, f32[1024,128]{1,0:T(8,128)} %get-tuple-element.37.first_hbm, bf16[1024,128]{1,0:T(8,128)(2,1)} %bitcast.2.state), custom_call_target="tpu_custom_call" | custom-call | flops 10000000000 | bytes 1 | tf_op jit(solution)/shard_map/pallas_call | solution.py:33
  59.9 1.3 %collective-permute-start.4 = (f32[8,256]{1,0:T(8,128)}, f32[8,256]{1,0:T(8,128)S(1)}, u32[]{:S(2)}, u32[]{:S(2)}) collective-permute-start(f32[8,256]{1,0:T(8,128)} %get-tuple-element.41.s0), channel_id=1, source_target_pairs={{0,1},{1,2},{2,3},{3,0},{4,5},{5,6},{6,7},{7,4},{8,9},{9,10},{10,1... | collective-permute-start | bytes 24584 | tf_op jit(solution)/shard_map/ppermute | solution.py:341
  61.2 2.5 %collective-permute-start.5 = (f32[8,256]{1,0:T(8,128)}, f32[8,256]{1,0:T(8,128)S(1)}, u32[]{:S(2)}, u32[]{:S(2)}) collective-permute-start(f32[8,256]{1,0:T(8,128)} %get-tuple-element.41.s0), channel_id=1, source_target_pairs={{0,2},{1,3},{2,0},{3,1},{4,6},{5,7},{6,4},{7,5},{8,10},{9,11},{10,... | collective-permute-start | bytes 24584 | tf_op jit(solution)/shard_map/ppermute | solution.py:341
  63.7 1.2 %collective-permute-start.6 = (f32[8,256]{1,0:T(8,128)}, f32[8,256]{1,0:T(8,128)S(1)}, u32[]{:S(2)}, u32[]{:S(2)}) collective-permute-start(f32[8,256]{1,0:T(8,128)} %get-tuple-element.41.s0), channel_id=1, source_target_pairs={{0,3},{1,0},{2,1},{3,2},{4,7},{5,4},{6,5},{7,6},{8,11},{9,8},{10,9... | collective-permute-start | bytes 24584 | tf_op jit(solution)/shard_map/ppermute | solution.py:341
  64.8 0.0 copy-done.7
  64.8 0.0 copy-done.8
  64.8 2.0 %shard_map.129 = (f32[512,512]{1,0:T(8,128)S(1)}, f32[512,128]{1,0:T(8,128)S(1)}, f32[512,128]{1,0:T(8,128)S(1)}) custom-call(s32[1]{0:T(128)} %bitcast.index, s32[128]{0:T(128)S(1)} %copy-done.10, f32[16,128]{1,0:T(8,128)S(1)} %copy-done.8, bf16[512,512]{1,0:T(8,128)(2,1)S(1)} %copy-done.7, bf16[1024,512]{1,0:T(8,128)(2,1)S(1)} %copy-done), custom_call_target="tpu_custom_call" | custom-call | flops 1 | bytes 1 | tf_op jit(solution)/shard_map/pallas_call | solution.py:33
  66.8 1.9 %collective-permute-done.3.far = bf16[560,512]{1,0:T(8,128)(2,1)S(1)} collective-permute-done((bf16[560,512]{1,0:T(8,128)(2,1)S(1)}, bf16[560,512]{1,0:T(8,128)(2,1)S(1)}, u32[]{:S(2)}, u32[]{:S(2)}) %collective-permute-start.3) | collective-permute-done | bytes 573472 | tf_op jit(solution)/shard_map/ppermute | solution.py:333
  68.7 0.6 shard_map.130
  69.3 0.0 collective-permute-done.4.s1
  69.3 0.0 collective-permute-done.5.s2
  69.4 0.0 collective-permute-done.6.s3
  69.4 4.5 %collective-permute-start.7 = (bf16[256,512]{1,0:T(8,128)(2,1)S(1)}, bf16[256,512]{1,0:T(8,128)(2,1)S(1)}, u32[]{:S(2)}, u32[]{:S(2)}) collective-permute-start(bf16[256,512]{1,0:T(8,128)(2,1)S(1)} %get-tuple-element.53), channel_id=1, source_target_pairs={{0,4},{4,0},{8,12},{12,8},{16,20},{20,16},{24,28},{28,24},{32,36},... | collective-permute-start | bytes 786440 | tf_op jit(solution)/shard_map/ppermute | solution.py:337
  73.9 0.0 copy-done.3
  73.9 0.0 copy-done.6
  73.9 0.0 copy-done.9
  73.9 0.0 copy-done.11
  73.9 1.3 %shard_map.131 = bf16[256,1024]{1,0:T(8,128)(2,1)} custom-call(f32[256,1024]{1,0:T(8,128)S(1)} %copy-done.3, bf16[256,1024]{1,0:T(8,128)(2,1)S(1)} %copy-done.6, f32[1,1024]{1,0:T(1,128)S(1)} %bitcast.4, f32[8,256]{1,0:T(8,128)S(1)} %copy-done.9, f32[8,256]{1,0:T(8,128)S(1)} %collective-permute-done.4.s1, f32[8,256]{1,0:T(8,128)S(1)} %collective-permute-done.5.s2, ...), custom_call_target="tpu_custom_call" | custom-call | flops 1 | bytes 1 | tf_op jit(solution)/shard_map/pallas_call | solution.py:33
  75.2 0.0 collective-permute-done.7.other
  75.2 0.8 %shard_map.132 = bf16[256,1024]{1,0:T(8,128)(2,1)} custom-call(s32[1]{0:T(128)} %bitcast.index, bf16[256,512]{1,0:T(8,128)(2,1)S(1)} %get-tuple-element.52.mine, bf16[256,512]{1,0:T(8,128)(2,1)S(1)} %collective-permute-done.7.other), custom_call_target="tpu_custom_call" | custom-call | flops 1 | bytes 1 | tf_op jit(solution)/shard_map/pallas_call | solution.py:33
  (11 shorter events, 0.0 us)
Async XLA Ops:
  4.5 13.4 %collective-permute-start = (bf16[784,512]{1,0:T(8,128)(2,1)}, bf16[784,512]{1,0:T(8,128)(2,1)S(1)}, u32[]{:S(2)}, u32[]{:S(2)}) collective-permute-start(bf16[784,512]{1,0:T(8,128)(2,1)} %get-tuple-element.30), channel_id=1, source_target_pairs={{0,4},{4,0},{8,12},{12,8},{16,20},{20,16},{24,28},{28,24},{32,36},... | collective-permute-start | bytes 2408456 | tf_op jit(solution)/shard_map/ppermute | solution.py:337
  7.8 22.0 %all-to-all-start = ((bf16[64,16,128]{2,1,0:T(8,128)(2,1)}), bf16[64,16,128]{2,1,0:T(8,128)(2,1)S(1)}, u32[]{:S(2)}, u32[]{:S(2)}) async-start(bf16[64,16,128]{2,1,0:T(8,128)(2,1)} %bitcast.5), calls=%async_computation | async-start | bytes 524288 | tf_op jit(solution)/shard_map/all_to_all | solution.py:378
  17.9 0.9 %copy-start.13 = (bf16[784,512]{1,0:T(8,128)(2,1)}, bf16[784,512]{1,0:T(8,128)(2,1)S(1)}, u32[]{:S(2)}) copy-start(bf16[784,512]{1,0:T(8,128)(2,1)S(1)} %collective-permute-done.other) | copy-start | bytes 2408452
  22.1 7.8 %copy-start.12 = (f32[8]{0:T(128)S(1)}, f32[8]{0:T(128)}, u32[]{:S(2)}) copy-start(f32[8]{0:T(128)} %rate_hbm.3) | copy-start | bytes 100
  22.1 20.9 %collective-permute-start.1 = (bf16[528,512]{1,0:T(8,128)(2,1)}, bf16[528,512]{1,0:T(8,128)(2,1)S(1)}, u32[]{:S(2)}, u32[]{:S(2)}) collective-permute-start(bf16[528,512]{1,0:T(8,128)(2,1)} %get-tuple-element.31), channel_id=1, source_target_pairs={{0,248},{4,252},{8,0},{12,4},{16,8},{20,12},{24,16},{28,20},{32,24... | collective-permute-start | bytes 1622024 | tf_op jit(solution)/shard_map/ppermute | solution.py:333
  27.1 25.0 %collective-permute-start.2 = (bf16[768,512]{1,0:T(8,128)(2,1)}, bf16[768,512]{1,0:T(8,128)(2,1)S(1)}, u32[]{:S(2)}, u32[]{:S(2)}) collective-permute-start(bf16[768,512]{1,0:T(8,128)(2,1)} %get-tuple-element.32), channel_id=1, source_target_pairs={{0,8},{4,12},{8,16},{12,20},{16,24},{20,28},{24,32},{28,36},{32,40... | collective-permute-start | bytes 2359304 | tf_op jit(solution)/shard_map/ppermute | solution.py:333
  29.9 8.0 %copy-start.2 = (bf16[256,1024]{1,0:T(8,128)(2,1)S(1)}, bf16[256,1024]{1,0:T(8,128)(2,1)}, u32[]{:S(2)}) copy-start(bf16[256,1024]{1,0:T(8,128)(2,1)} %v.3) | copy-start | bytes 1572868
  31.2 6.6 %copy-start.1 = (bf16[256,1024]{1,0:T(8,128)(2,1)S(1)}, bf16[256,1024]{1,0:T(8,128)(2,1)}, u32[]{:S(2)}) copy-start(bf16[256,1024]{1,0:T(8,128)(2,1)} %k.3) | copy-start | bytes 1572868
  31.2 24.7 %all-to-all-start.1 = ((bf16[64,16,128]{2,1,0:T(8,128)(2,1)}), bf16[64,16,128]{2,1,0:T(8,128)(2,1)}, u32[]{:S(2)}, u32[]{:S(2)}) async-start(bf16[64,16,128]{2,1,0:T(8,128)(2,1)} %shard_map.123), calls=%async_computation.1 | async-start | bytes 524288 | tf_op jit(solution)/shard_map/all_to_all | solution.py:403
  37.9 1.0 %copy-start.5 = (bf16[256,1024]{1,0:T(8,128)(2,1)S(1)}, bf16[256,1024]{1,0:T(8,128)(2,1)}, u32[]{:S(2)}) copy-start(bf16[256,1024]{1,0:T(8,128)(2,1)} %q_hbm.1) | copy-start | bytes 1572868
  38.9 4.1 %copy-start = (bf16[1024,512]{1,0:T(8,128)(2,1)S(1)}, bf16[1024,512]{1,0:T(8,128)(2,1)}, u32[]{:S(2)}) copy-start(bf16[1024,512]{1,0:T(8,128)(2,1)} %get-tuple-element.33.pair) | copy-start | bytes 3145732
  42.1 1.0 %copy-start.4 = (f32[256,1024]{1,0:T(8,128)}, f32[256,1024]{1,0:T(8,128)S(1)}, u32[]{:S(2)}) copy-start(f32[256,1024]{1,0:T(8,128)S(1)} %shard_map.127.inner_hbm) | copy-start | bytes 3145732
  43.0 0.7 copy-start.10
  54.3 14.4 %collective-permute-start.3 = (bf16[560,512]{1,0:T(8,128)(2,1)S(1)}, bf16[560,512]{1,0:T(8,128)(2,1)S(1)}, u32[]{:S(2)}, u32[]{:S(2)}) collective-permute-start(bf16[560,512]{1,0:T(8,128)(2,1)S(1)} %shard_map.126), channel_id=1, source_target_pairs={{0,8},{4,12},{8,16},{12,20},{16,24},{20,28},{24,32},{28,36},{32,40... | collective-permute-start | bytes 1720328 | tf_op jit(solution)/shard_map/ppermute | solution.py:333
  55.9 8.9 %copy-start.7 = (bf16[512,512]{1,0:T(8,128)(2,1)S(1)}, bf16[512,512]{1,0:T(8,128)(2,1)}, u32[]{:S(2)}) copy-start(bf16[512,512]{1,0:T(8,128)(2,1)} %get-tuple-element.43.q) | copy-start | bytes 1572868
  55.9 8.9 %copy-start.8 = (f32[16,128]{1,0:T(8,128)S(1)}, f32[16,128]{1,0:T(8,128)}, u32[]{:S(2)}) copy-start(f32[16,128]{1,0:T(8,128)} %get-tuple-element.42.flags) | copy-start | bytes 24580
  59.9 9.4 %collective-permute-start.4 = (f32[8,256]{1,0:T(8,128)}, f32[8,256]{1,0:T(8,128)S(1)}, u32[]{:S(2)}, u32[]{:S(2)}) collective-permute-start(f32[8,256]{1,0:T(8,128)} %get-tuple-element.41.s0), channel_id=1, source_target_pairs={{0,1},{1,2},{2,3},{3,0},{4,5},{5,6},{6,7},{7,4},{8,9},{9,10},{10,1... | collective-permute-start | bytes 24584 | tf_op jit(solution)/shard_map/ppermute | solution.py:341
  61.2 8.1 %collective-permute-start.5 = (f32[8,256]{1,0:T(8,128)}, f32[8,256]{1,0:T(8,128)S(1)}, u32[]{:S(2)}, u32[]{:S(2)}) collective-permute-start(f32[8,256]{1,0:T(8,128)} %get-tuple-element.41.s0), channel_id=1, source_target_pairs={{0,2},{1,3},{2,0},{3,1},{4,6},{5,7},{6,4},{7,5},{8,10},{9,11},{10,... | collective-permute-start | bytes 24584 | tf_op jit(solution)/shard_map/ppermute | solution.py:341
  63.7 5.7 %collective-permute-start.6 = (f32[8,256]{1,0:T(8,128)}, f32[8,256]{1,0:T(8,128)S(1)}, u32[]{:S(2)}, u32[]{:S(2)}) collective-permute-start(f32[8,256]{1,0:T(8,128)} %get-tuple-element.41.s0), channel_id=1, source_target_pairs={{0,3},{1,0},{2,1},{3,2},{4,7},{5,4},{6,5},{7,6},{8,11},{9,8},{10,9... | collective-permute-start | bytes 24584 | tf_op jit(solution)/shard_map/ppermute | solution.py:341
  68.7 5.2 %copy-start.3 = (f32[256,1024]{1,0:T(8,128)S(1)}, f32[256,1024]{1,0:T(8,128)}, u32[]{:S(2)}) copy-start(f32[256,1024]{1,0:T(8,128)} %get-tuple-element.40.heads) | copy-start | bytes 3145732
  68.7 5.2 %copy-start.6 = (bf16[256,1024]{1,0:T(8,128)(2,1)S(1)}, bf16[256,1024]{1,0:T(8,128)(2,1)}, u32[]{:S(2)}) copy-start(bf16[256,1024]{1,0:T(8,128)(2,1)} %gate.1) | copy-start | bytes 1572868
  68.7 5.2 %copy-start.9 = (f32[8,256]{1,0:T(8,128)S(1)}, f32[8,256]{1,0:T(8,128)}, u32[]{:S(2)}) copy-start(f32[8,256]{1,0:T(8,128)} %get-tuple-element.41.s0) | copy-start | bytes 24580
  68.7 5.2 %copy-start.11 = (f32[1024]{0:T(1024)S(1)}, f32[1024]{0:T(1024)}, u32[]{:S(2)}) copy-start(f32[1024]{0:T(1024)} %param.15) | copy-start | bytes 12292
  69.4 5.8 %collective-permute-start.7 = (bf16[256,512]{1,0:T(8,128)(2,1)S(1)}, bf16[256,512]{1,0:T(8,128)(2,1)S(1)}, u32[]{:S(2)}, u32[]{:S(2)}) collective-permute-start(bf16[256,512]{1,0:T(8,128)(2,1)S(1)} %get-tuple-element.53), channel_id=1, source_target_pairs={{0,4},{4,0},{8,12},{12,8},{16,20},{20,16},{24,28},{28,24},{32,36},... | collective-permute-start | bytes 786440 | tf_op jit(solution)/shard_map/ppermute | solution.py:337

commit v4 on v3

--- a/solution.py
+++ b/solution.py
@@ -29,14 +29,14 @@
 VMEM = pl.BlockSpec(memory_space=pltpu.VMEM)
 
 
-def call(body, outs, ins, specs, scratch=(), flops=1, room=16):
+def call(body, outs, ins, specs, scratch=(), flops=1, outs_at=None):
     return pl.pallas_call(
         body,
         out_shape=outs,
         in_specs=specs,
-        out_specs=[VMEM] * len(outs),
+        out_specs=outs_at or [VMEM] * len(outs),
         scratch_shapes=list(scratch),
-        compiler_params=pltpu.CompilerParams(vmem_limit_bytes=room * 1024 * 1024),
+        compiler_params=pltpu.CompilerParams(vmem_limit_bytes=(16 if body in SMALL else 60) * 1024 * 1024),
         cost_estimate=pl.CostEstimate(flops=flops, bytes_accessed=1, transcendentals=0),
     )(*ins)
 
@@ -55,8 +55,15 @@
     )
 
 
+def block_state(rate, k, v, h, b):
+    rows = slice(b * BLK, (b + 1) * BLK)
+    back = (BLK - 1.0) - lax.broadcasted_iota(jnp.int32, (BLK, HD), 0).astype(f32)
+    decayed = (k[rows, cols(h)].astype(f32) * jnp.exp(-rate[h] * back)).astype(bf16)
+    return dot(decayed, v[rows, cols(h)], ((0,), (0,)))
+
+
 def start_body(
-    index, rate_hbm, mask, k_hbm, v_hbm, sq, sk, sv, first, out, sent, rate, k, v, rate_sem, sems
+    index, rate_hbm, mask, k_hbm, v_hbm, sq, sk, sv, out, sent, rate, k, v, packed, rate_sem, sems
 ):
     other = 1 - index[0] % 2
     copies = [pltpu.make_async_copy(rate_hbm, rate, rate_sem)]
@@ -73,22 +80,17 @@
         copy.start()
     flags = mask[...].astype(f32)
     flags = jnp.concatenate([flags, jnp.zeros((14, NBLK), f32)], axis=0).astype(bf16)
-    sent[3 * ROWS :, :] = jnp.concatenate([flags] * 4, axis=1)
+    packed[...] = jnp.concatenate([flags] * 4, axis=1)
+    copies.append(pltpu.make_async_copy(packed, sent.at[3 * ROWS :, :], sems.at[LOCAL + 3]))
+    copies[-1].start()
     copies[0].wait()
-    back = (BLK - 1.0) - lax.broadcasted_iota(jnp.int32, (BLK, HD), 0).astype(f32)
     for g in range(LOCAL // 2):
         copies[2 * g + 1].wait()
         copies[2 * g + 2].wait()
         for h in (2 * g, 2 * g + 1):
-            decay = jnp.exp(-rate[h] * back)
-            parts = []
-            for b in range(2):
-                rows = slice(b * BLK, (b + 1) * BLK)
-                decayed = (k[rows, cols(h)].astype(f32) * decay).astype(bf16)
-                parts.append(dot(decayed, v[rows, cols(h)], ((0,), (0,))))
             step = jnp.exp(jnp.full((HD, HD), -rate[h] * BLK, f32))
-            first[cols(h), :] = parts[0]
-            out[cols(h), :] = (step * parts[0] + parts[1]).astype(bf16)
+            state = step * block_state(rate, k, v, h, 0) + block_state(rate, k, v, h, 1)
+            out[cols(h), :] = state.astype(bf16)
     for copy in copies[LOCAL + 1 :]:
         copy.wait()
 
@@ -102,11 +104,14 @@
             state = step * state + parts[i].astype(f32)
 
 
-def inner_body(rate, q, k, v, out):
+def inner_body(rate, q, k, v, out, q_out, first, rates):
     row = lax.broadcasted_iota(jnp.int32, (BLK, BLK), 0)
     col = lax.broadcasted_iota(jnp.int32, (BLK, BLK), 1)
     gap = jnp.maximum(row - col, 0).astype(f32)
+    q_out[...] = q[...]
     for h in range(LOCAL):
+        rates[h : h + 1, :] = jnp.full((1, HD), rate[h], f32)
+        first[cols(h), :] = block_state(rate, k, v, h, 0)
         decay = jnp.where(row >= col, jnp.exp(-rate[h] * gap), 0.0)
         for b in range(2):
             rows = slice(b * BLK, (b + 1) * BLK)
@@ -116,31 +121,17 @@
             )
 
 
-def carry_body(
-    rate_hbm, inner_hbm, q_hbm, first_hbm, state, heads, squares, rate, inner, q, first, rate_sem, sems
-):
-    copies = [pltpu.make_async_copy(rate_hbm, rate, rate_sem)]
-    for g in range(LOCAL // 2):
-        at = slice(g * 2 * HD, (g + 1) * 2 * HD)
-        copies.append(pltpu.make_async_copy(q_hbm.at[:, at], q.at[:, at], sems.at[3 * g]))
-        copies.append(pltpu.make_async_copy(first_hbm.at[at, :], first.at[at, :], sems.at[3 * g + 1]))
-        copies.append(pltpu.make_async_copy(inner_hbm.at[:, at], inner.at[:, at], sems.at[3 * g + 2]))
-    for copy in copies:
-        copy.start()
-    copies[0].wait()
+def carry_body(rates, inner, q, first, state, heads, squares):
     ahead = lax.broadcasted_iota(jnp.int32, (BLK, HD), 0).astype(f32) + 1.0
     totals = [jnp.zeros((BLK, HD), f32)] * 2
     for h in range(LOCAL):
-        if h % 2 == 0:
-            for copy in copies[3 * (h // 2) + 1 : 3 * (h // 2) + 4]:
-                copy.wait()
-        step = jnp.exp(jnp.full((HD, HD), -rate[h] * BLK, f32))
-        decay = jnp.exp(-rate[h] * ahead)
+        rate = rates[h : h + 1, :]
+        decay = jnp.exp(-rate * ahead)
         entering = state[cols(h), :]
-        middle = (step * entering.astype(f32) + first[cols(h), :]).astype(bf16)
-        for b, block_state in enumerate((entering, middle)):
+        middle = (jnp.exp(-rate * BLK) * entering.astype(f32) + first[cols(h), :]).astype(bf16)
+        for b, block_start in enumerate((entering, middle)):
             rows = slice(b * BLK, (b + 1) * BLK)
-            carried = dot(q[rows, cols(h)], block_state, ((1,), (0,)))
+            carried = dot(q[rows, cols(h)], block_start, ((1,), (0,)))
             value = inner[rows, cols(h)] + carried * decay
             heads[rows, cols(h)] = value
             totals[b] = totals[b] + value * value
@@ -162,35 +153,59 @@
     return pl.ds(pl.multiple_of(c * HALF, HALF), HALF)
 
 
-def gather_body(index, mask, q, k, v, other, near_q, far_q, pair, tail, flags):
+def gather_body(index, mask, q, k, v, other, far_q, head, tail, theirs, packed, sems):
     core = index[0] % 2
 
-    def lay(at, mine):
-        theirs = other[at * ROWS : (at + 1) * ROWS, :]
-        first = jnp.where(core == 0, mine, theirs)
-        second = jnp.where(core == 0, theirs, mine)
-        return first, second
-
-    for at, ref in enumerate((q, k, v)):
-        low, high = lay(at, ref[:, half(core)])
-        if at == 0:
-            for out in (near_q, far_q):
-                out[:ROWS, :] = low
-                out[ROWS : 2 * ROWS, :] = high
-        else:
-            base = (at - 1) * 2 * ROWS
-            pair[base : base + ROWS, :] = low
-            pair[base + ROWS : base + 2 * ROWS, :] = high
+    def put(source, target, at):
+        return pltpu.make_async_copy(source, target, sems.at[at])
+
+    def layout(mine):
+        def part(at, ref, owner, rows):
+            if owner == mine:
+                return ref.at[rows, half(core)]
+            return other.at[slice(at * ROWS + rows.start, at * ROWS + rows.stop), :]
+
+        low, high, whole = slice(0, BLK), slice(BLK, ROWS), slice(0, ROWS)
+        copies = [
+            put(part(0, q, 0, whole), far_q.at[:ROWS, :], 0),
+            put(part(0, q, 1, whole), far_q.at[ROWS : 2 * ROWS, :], 1),
+        ]
+        for at, ref in ((1, k), (2, v)):
             base = (at - 1) * 3 * BLK
-            tail[base : base + BLK, :] = low[BLK:]
-            tail[base + BLK : base + 3 * BLK, :] = high
+            sem = 3 * at - 1
+            copies += [
+                put(part(at, ref, 0, low), head.at[(at - 1) * BLK : at * BLK, :], sem),
+                put(part(at, ref, 0, high), tail.at[base : base + BLK, :], sem + 1),
+                put(part(at, ref, 1, whole), tail.at[base + BLK : base + 3 * BLK, :], sem + 2),
+            ]
+        return copies
+
+    for mine in range(2):
+
+        @pl.when(core == mine)
+        def _():
+            for copy in layout(mine):
+                copy.start()
+
+    fetch = put(other.at[3 * ROWS :, :NBLK], theirs, 8)
+    fetch.start()
+    fetch.wait()
     own = mask[...].astype(f32)
-    theirs = other[3 * ROWS :, :NBLK].astype(f32)[:2]
-    first = jnp.where(core == 0, own, theirs)
-    second = jnp.where(core == 0, theirs, own)
+    arrived = theirs[...].astype(f32)[:2]
+    first = jnp.where(core == 0, own, arrived)
+    second = jnp.where(core == 0, arrived, own)
     rows = jnp.concatenate([first, second, jnp.zeros((12, NBLK), f32)], axis=0)
-    flags[...] = rows
-    far_q[4 * BLK :, :] = jnp.concatenate([rows.astype(bf16)] * 4, axis=1)
+    packed[...] = jnp.concatenate([rows.astype(bf16)] * 4, axis=1)
+    flags = put(packed, far_q.at[4 * BLK :, :], 9)
+    flags.start()
+    for mine in range(2):
+
+        @pl.when(core == mine)
+        def _():
+            for copy in layout(mine):
+                copy.wait()
+
+    flags.wait()
 
 
 def allowed(docs, flags, i, query, key):
@@ -216,8 +231,9 @@
     return both[:, :HD], top, both[:, HD:]
 
 
-def attend_chip(index, docs, rows, ahead, q, pair, out, tops, sums, bias):
+def attend_chip(index, docs, ahead, q, head, tail, out, tops, sums, bias):
     chip = index[0] // 2
+    rows = q[4 * BLK :, :NBLK].astype(f32)
     for i in range(4):
         for j in range(4):
             if ahead == 0 and j == i:
@@ -239,8 +255,10 @@
         for h in range(HEADS):
             acc, top, total = attend_head(
                 q[part, cols(h)],
-                pair[:count, cols(h)],
-                pair[4 * BLK : 4 * BLK + count, cols(h)],
+                jnp.concatenate([head[:BLK, cols(h)], tail[: count - BLK, cols(h)]], axis=0),
+                jnp.concatenate(
+                    [head[BLK:, cols(h)], tail[3 * BLK : 2 * BLK + count, cols(h)]], axis=0
+                ),
                 bias[part, :count],
             )
             out[part, cols(h)] = acc / total
@@ -250,13 +268,12 @@
         sums[part, :] = sum_table
 
 
-def near_body(index, docs, flags, q, pair, out, tops, sums, bias):
-    attend_chip(index, docs, flags[...], 0, q, pair, out, tops, sums, bias)
-
-
-def next_body(index, docs, q, pair, out, tops, sums, bias):
-    rows = q[4 * BLK :, :NBLK].astype(f32)
-    attend_chip(index, docs, rows, 1, q, pair, out, tops, sums, bias)
+def near_body(index, docs, q, head, tail, out, tops, sums, bias):
+    attend_chip(index, docs, 0, q, head, tail, out, tops, sums, bias)
+
+
+def next_body(index, docs, q, head, tail, out, tops, sums, bias):
+    attend_chip(index, docs, 1, q, head, tail, out, tops, sums, bias)
 
 
 def weighed(top1, sum1, top2, sum2):
@@ -308,8 +325,10 @@
         at = 4 * BLK + p * 2 * LOCAL
         stats = stats + far[at : at + 2 * LOCAL, :].astype(f32)
     pad = jnp.ones((HD - HEADS, 4 * BLK), f32)
+    far_sums = jnp.concatenate([stats[HEADS : 2 * HEADS], pad], axis=0).T
     far_tops = jnp.concatenate([stats[:HEADS], pad], axis=0).T
-    far_sums = jnp.concatenate([stats[HEADS : 2 * HEADS], pad], axis=0).T
+    far_tops = jnp.where(far_sums > 0.0, far_tops, FILL)
+    far_sums = jnp.where(far_sums > 0.0, far_sums, 1.0)
     lane = lax.broadcasted_iota(jnp.int32, (4 * BLK, HD), 1)
     near_sums = jnp.where(lane < HEADS, sums[...], 1.0)
     share[...] = weighed(tops[...], near_sums, far_tops, far_sums)[2]
@@ -329,8 +348,11 @@
     out[:, half(1 - core)] = other[...]
 
 
+SMALL = (prefix_body, next_body, far_body, merge_body, norm_body, place_body)
+
+
 def shifted(x, distance):
-    return lax.ppermute(x, "seq", [(i, (i + distance) % SHARDS) for i in range(SHARDS)])
+    return lax.ppermute(x, "seq", [(i, i + distance) for i in range(SHARDS) if 0 <= i + distance < SHARDS])
 
 
 def swapped(x):
@@ -360,38 +382,51 @@
     narrow = like((ROWS, WIDTH), bf16)
 
     anywhere = pl.BlockSpec(memory_space=pl.ANY)
-    first, state, sent = call(
+    state, sent = call(
         start_body,
-        [like((WIDTH, HD), f32), like((WIDTH, HD), bf16), like((3 * ROWS + 16, HALF), bf16)],
+        [like((WIDTH, HD), bf16), like((3 * ROWS + 16, HALF), bf16)],
         (index, decay_rate, block_mask, lin_key, lin_value, soft_query, soft_key, soft_value),
         [SMEM, anywhere, VMEM] + [anywhere] * 5,
         [
             pltpu.SMEM((LOCAL,), f32),
             pltpu.VMEM((ROWS, WIDTH), bf16),
             pltpu.VMEM((ROWS, WIDTH), bf16),
+            pltpu.VMEM((16, HALF), bf16),
             pltpu.SemaphoreType.DMA,
-            pltpu.SemaphoreType.DMA((LOCAL + 3,)),
+            pltpu.SemaphoreType.DMA((LOCAL + 4,)),
         ],
-        room=56,
+        outs_at=[VMEM, anywhere],
     )
     other = swapped(sent)
     parts = lax.all_to_all(state.reshape(SHARDS, 16, HD), "seq", 0, 0)
-    near_q, far_q, own_pair, own_tail, flags = call(
+    far_q, own_head, own_tail = call(
         gather_body,
         [
-            like((2 * ROWS, HALF), bf16),
             like((2 * ROWS + 16, HALF), bf16),
-            like((8 * BLK, HALF), bf16),
+            like((2 * BLK, HALF), bf16),
             like((6 * BLK, HALF), bf16),
-            like((16, NBLK), f32),
         ],
         (index, block_mask, soft_query, soft_key, soft_value, other),
-        [SMEM] + [VMEM] * 5,
-        room=56,
+        [SMEM, VMEM] + [anywhere] * 4,
+        [
+            pltpu.VMEM((16, NBLK), bf16),
+            pltpu.VMEM((16, HALF), bf16),
+            pltpu.SemaphoreType.DMA((10,)),
+        ],
+        outs_at=[anywhere] * 3,
     )
     tail = shifted(own_tail, 2)
     next_q = shifted(far_q, -2)
 
+    tables = [like((4 * BLK, HALF), f32), like((4 * BLK, HD), f32), like((4 * BLK, HD), f32)]
+    near, tops, sums = call(
+        near_body,
+        tables,
+        (index, doc_ids, far_q, own_head, own_tail),
+        [SMEM] * 2 + [VMEM] * 3,
+        [pltpu.VMEM((4 * BLK, 4 * BLK), f32)],
+    )
+    near, parts = lax.optimization_barrier((near, parts))
     (prefix,) = call(
         prefix_body,
         [like((SHARDS, 16, HD), bf16)],
@@ -401,25 +436,17 @@
     )
     prefix, doc_ids = lax.optimization_barrier((prefix, doc_ids))
     entering = lax.all_to_all(prefix, "seq", 0, 0).reshape(WIDTH, HD)
-    (inner,) = call(
+    inner, q_held, first, rates = call(
         inner_body,
-        [wide],
+        [wide, narrow, like((WIDTH, HD), f32), like((LOCAL, HD), f32)],
         (decay_rate, lin_query, lin_key, lin_value),
         [SMEM, VMEM, VMEM, VMEM],
-    )
-    tables = [like((4 * BLK, HALF), f32), like((4 * BLK, HD), f32), like((4 * BLK, HD), f32)]
-    near, tops, sums = call(
-        near_body,
-        tables,
-        (index, doc_ids, flags, near_q, own_pair),
-        [SMEM] * 2 + [VMEM] * 3,
-        [pltpu.VMEM((4 * BLK, 4 * BLK), f32)],
     )
     done, done_tops, done_sums = call(
         next_body,
         tables,
-        (index, doc_ids, next_q, own_pair),
-        [SMEM] * 2 + [VMEM] * 2,
+        (index, doc_ids, next_q, own_head, own_tail),
+        [SMEM] * 2 + [VMEM] * 3,
         [pltpu.VMEM((4 * BLK, 4 * BLK), f32)],
     )
     (far,) = call(
@@ -433,18 +460,9 @@
     heads, squares = call(
         carry_body,
         [wide, like((8, ROWS), f32)],
-        (decay_rate, inner, lin_query, first, entering),
-        [anywhere] * 4 + [VMEM],
-        [
-            pltpu.SMEM((LOCAL,), f32),
-            pltpu.VMEM((ROWS, WIDTH), f32),
-            pltpu.VMEM((ROWS, WIDTH), bf16),
-            pltpu.VMEM((WIDTH, HD), f32),
-            pltpu.SemaphoreType.DMA,
-            pltpu.SemaphoreType.DMA((3 * LOCAL // 2,)),
-        ],
+        (rates, inner, q_held, first, entering),
+        [VMEM] * 5,
         flops=CARRY_COST,
-        room=56,
     )
     others = [turned(squares, d) for d in (1, 2, 3)]
     far, heads = lax.optimization_barrier((far, heads))

time: 76.4 us -> 144 us (1.88)
  Pallas kernels: 24.9 us -> 96 us
  waiting for transfers between devices: 12.3 us -> 4.64 us
  starting transfers between devices: 34.5 us -> 38.5 us
    pallas_call x11, Pallas kernels: 24.9 us -> 96 us  [call(): pl.pallas_call(body, out_shape=outs, in_specs=specs, out_specs=outs_at or...]
    ppermute x3, waiting for transfers between devices: 8.07 us -> 2.55 us  [shifted(): lax.ppermute(x, 'seq', [(i, i + distance) for i in range(SHARDS) if 0 <=...]
    all_to_all x1, starting transfers between devices: 6.61 us -> 10.8 us  [per_device(): entering = lax.all_to_all(prefix, 'seq', 0, 0).reshape(WIDTH, HD)]
    ppermute x3, starting transfers between devices: 5.1 us -> 8.65 us  [shifted(): lax.ppermute(x, 'seq', [(i, i + distance) for i in range(SHARDS) if 0 <=...]
    all_to_all x1, waiting for transfers between devices: 2.76 us -> 0.01 us  [per_device(): parts = lax.all_to_all(state.reshape(SHARDS, 16, HD), 'seq', 0, 0)]
    ppermute x2, starting transfers between devices: 7.83 us -> 5.43 us  [swapped(): return lax.ppermute(x, 'seq', [(i, i ^ 1) for i in range(SHARDS)])]
    unnamed x28 -> x26, local copies, waits for them, and re-layouts: 3.58 us -> 2.28 us
  transfers between devices with their start and end apart: 10 -> 10, of which waited for: 4 -> 3; matrix products, arithmetic and copies ran while one was open for 0% -> 0% of each run, Pallas kernels for 27% -> 48%
where the time goes in v4:
time: 144 us; the launch traced here: 142 us
  Pallas kernels  96 us (67%)
  starting transfers between devices  38.5 us (27%)
  waiting for transfers between devices  4.64 us (3%)
  local copies, waits for them, and re-layouts  2.28 us (2%)
    pallas_call x11, Pallas kernels, call(): pl.pallas_call(body, out_shape=outs, in_specs=specs, out_specs=outs_at or...  96 us
    all_to_all x1, starting transfers between devices, per_device(): entering = lax.all_to_all(prefix, 'seq', 0, 0).reshape(WIDTH, HD)  10.8 us
    all_to_all x1, starting transfers between devices, per_device(): parts = lax.all_to_all(state.reshape(SHARDS, 16, HD), 'seq', 0, 0)  10 us
    ppermute x3, starting transfers between devices, shifted(): lax.ppermute(x, 'seq', [(i, i + distance) for i in range(SHARDS) if 0 <=...  8.65 us
    ppermute x2, starting transfers between devices, swapped(): return lax.ppermute(x, 'seq', [(i, i ^ 1) for i in range(SHARDS)])  5.43 us
    ppermute x3, starting transfers between devices, turned(): return lax.ppermute(x, 'head', [(i, (i + distance) % 4) for i in range(4)])  3.6 us
  transfers between devices with their start and end apart: 10, of which 3 were waited for; matrix products, arithmetic and copies ran while one was open for 0% of the time, Pallas kernels for 48%

profile of v4, /device:TPU:1, one launch (start us, length us, event | category | flops | bytes accessed | tf_op | source)
XLA Modules:
  0.0 142.3 jit_solution(17241550836003669558)
XLA Ops:
  0.6 26.4 %shard_map.122 = (bf16[1024,128]{1,0:T(8,128)(2,1)}, bf16[784,512]{1,0:T(8,128)(2,1)}) custom-call(s32[1]{0:T(128)} %bitcast.index, f32[8]{0:T(128)} %rate.3, s32[2,128]{1,0:T(2,128)} %mask.3, bf16[256,1024]{1,0:T(8,128)(2,1)} %k.3, bf16[256,1024]{1,0:T(8,128)(2,1)} %v.3, bf16[256,1024]{1,0:T(8,128)(2,1)} %q.2, bf16[256,1024]{1,0:T(8,128)(2,1)} %k.2, ...), custom_call_target="tpu_custom_call" | custom-call | flops 1 | bytes 1 | tf_op jit(solution)/shard_map/pallas_call | solution.py:33
  27.1 3.3 %collective-permute-start = (bf16[784,512]{1,0:T(8,128)(2,1)}, bf16[784,512]{1,0:T(8,128)(2,1)S(1)}, u32[]{:S(2)}, u32[]{:S(2)}) collective-permute-start(bf16[784,512]{1,0:T(8,128)(2,1)} %get-tuple-element.31), channel_id=1, source_target_pairs={{0,4},{4,0},{8,12},{12,8},{16,20},{20,16},{24,28},{28,24},{32,36},... | collective-permute-start | bytes 2408456 | tf_op jit(solution)/shard_map/ppermute | solution.py:359
  30.4 10.0 %all-to-all-start = ((bf16[64,16,128]{2,1,0:T(8,128)(2,1)}), bf16[64,16,128]{2,1,0:T(8,128)(2,1)S(1)}, u32[]{:S(2)}, u32[]{:S(2)}) async-start(bf16[64,16,128]{2,1,0:T(8,128)(2,1)} %bitcast.6), calls=%async_computation | async-start | bytes 524288 | tf_op jit(solution)/shard_map/all_to_all | solution.py:401
  40.4 0.0 collective-permute-done.other
  40.4 0.0 copy-start.11
  40.5 0.9 copy-done.11
  41.3 49.5 %shard_map.123 = (bf16[528,512]{1,0:T(8,128)(2,1)}, bf16[256,512]{1,0:T(8,128)(2,1)}, bf16[768,512]{1,0:T(8,128)(2,1)}) custom-call(s32[1]{0:T(128)} %bitcast.index, s32[2,128]{1,0:T(2,128)} %mask.3, bf16[256,1024]{1,0:T(8,128)(2,1)} %q.2, bf16[256,1024]{1,0:T(8,128)(2,1)} %k.2, bf16[256,1024]{1,0:T(8,128)(2,1)} %v.2, bf16[784,512]{1,0:T(8,128)(2,1)} %copy-done.11), custom_call_target="tpu_custom_call" | custom-call | flops 1 | bytes 1 | tf_op jit(solution)/shard_map/pallas_call | solution.py:33
  90.9 1.3 collective-permute-start.1
  92.2 4.0 %collective-permute-start.2 = (bf16[768,512]{1,0:T(8,128)(2,1)}, bf16[768,512]{1,0:T(8,128)(2,1)S(1)}, u32[]{:S(2)}, u32[]{:S(2)}) collective-permute-start(bf16[768,512]{1,0:T(8,128)(2,1)} %get-tuple-element.34.tail), channel_id=1, source_target_pairs={{0,8},{4,12},{8,16},{12,20},{16,24},{20,28},{24,32},{28,36},{32,40... | collective-permute-start | bytes 2359304 | tf_op jit(solution)/shard_map/ppermute | solution.py:355
  96.2 3.9 %shard_map.124 = (f32[512,512]{1,0:T(8,128)}, f32[512,128]{1,0:T(8,128)}, f32[512,128]{1,0:T(8,128)}) custom-call(s32[1]{0:T(128)} %bitcast.index, s32[128]{0:T(128)} %docs.3, bf16[528,512]{1,0:T(8,128)(2,1)} %get-tuple-element.32.q, bf16[256,512]{1,0:T(8,128)(2,1)} %get-tuple-element.33.head, bf16[768,512]{1,0:T(8,128)(2,1)} %get-tuple-element.34.tail), custom_call_target="tpu_custom_call" | custom-call | flops 1 | bytes 1 | tf_op jit(solution)/shard_map/pallas_call | solution.py:33
  100.1 0.0 all-to-all-done.parts
  100.1 0.6 copy-done.10
  100.8 1.4 shard_map.125
  102.2 10.8 %all-to-all-start.1 = ((bf16[64,16,128]{2,1,0:T(8,128)(2,1)}), bf16[64,16,128]{2,1,0:T(8,128)(2,1)S(1)}, u32[]{:S(2)}, u32[]{:S(2)}) async-start(bf16[64,16,128]{2,1,0:T(8,128)(2,1)} %shard_map.125), calls=%async_computation.1 | async-start | bytes 524288 | tf_op jit(solution)/shard_map/all_to_all | solution.py:438
  113.0 0.0 copy-start
  113.0 0.0 copy-start.3
  113.0 0.0 copy-start.8
  113.0 4.4 %shard_map.128 = (f32[256,1024]{1,0:T(8,128)}, bf16[256,1024]{1,0:T(8,128)(2,1)}, f32[1024,128]{1,0:T(8,128)}, f32[8,128]{1,0:T(8,128)}) custom-call(f32[8]{0:T(128)} %rate.3, bf16[256,1024]{1,0:T(8,128)(2,1)} %q.3, bf16[256,1024]{1,0:T(8,128)(2,1)} %k.3, bf16[256,1024]{1,0:T(8,128)(2,1)} %v.3), custom_call_target="tpu_custom_call" | custom-call | flops 1 | bytes 1 | tf_op jit(solution)/shard_map/pallas_call | solution.py:33
  117.5 0.0 collective-permute-done.1.q
  117.5 0.0 copy-done
  117.5 0.0 copy-done.3
  117.5 0.0 copy-done.8
  117.5 2.2 %shard_map.126 = (f32[512,512]{1,0:T(8,128)S(1)}, f32[512,128]{1,0:T(8,128)S(1)}, f32[512,128]{1,0:T(8,128)S(1)}) custom-call(s32[1]{0:T(128)} %bitcast.index, s32[128]{0:T(128)S(1)} %copy-done.8, bf16[528,512]{1,0:T(8,128)(2,1)S(1)} %collective-permute-done.1.q, bf16[256,512]{1,0:T(8,128)(2,1)S(1)} %copy-done.3, bf16[768,512]{1,0:T(8,128)(2,1)S(1)} %copy-done), custom_call_target="tpu_custom_call" | custom-call | flops 1 | bytes 1 | tf_op jit(solution)/shard_map/pallas_call | solution.py:33
  119.7 0.0 collective-permute-done.2.tail
  119.7 2.3 %shard_map.127 = bf16[560,512]{1,0:T(8,128)(2,1)S(1)} custom-call(s32[1]{0:T(128)} %bitcast.index, s32[128]{0:T(128)S(1)} %copy-done.8, bf16[528,512]{1,0:T(8,128)(2,1)S(1)} %collective-permute-done.1.q, bf16[768,512]{1,0:T(8,128)(2,1)S(1)} %collective-permute-done.2.tail, f32[512,512]{1,0:T(8,128)S(1)} %get-tuple-element.39.done, ...), custom_call_target="tpu_custom_call" | custom-call | flops 1 | bytes 1 | tf_op jit(solution)/shard_map/pallas_call | solution.py:33
  122.0 3.3 %collective-permute-start.3 = (bf16[560,512]{1,0:T(8,128)(2,1)S(1)}, bf16[560,512]{1,0:T(8,128)(2,1)S(1)}, u32[]{:S(2)}, u32[]{:S(2)}) collective-permute-start(bf16[560,512]{1,0:T(8,128)(2,1)S(1)} %shard_map.127), channel_id=1, source_target_pairs={{0,8},{4,12},{8,16},{12,20},{16,24},{20,28},{24,32},{28,36},{32,40... | collective-permute-start | bytes 1720328 | tf_op jit(solution)/shard_map/ppermute | solution.py:355
  125.3 2.0 %all-to-all-done.1 = bf16[64,16,128]{2,1,0:T(8,128)(2,1)S(1)} async-done(((bf16[64,16,128]{2,1,0:T(8,128)(2,1)}), bf16[64,16,128]{2,1,0:T(8,128)(2,1)S(1)}, u32[]{:S(2)}, u32[]{:S(2)}) %all-to-all-start.1) | async-done | bytes 262176 | tf_op jit(solution)/shard_map/all_to_all | solution.py:438
  127.3 0.7 copy-done.12
  128.0 3.1 %shard_map.129 = (f32[256,1024]{1,0:T(8,128)}, f32[8,256]{1,0:T(8,128)}) custom-call(f32[8,128]{1,0:T(8,128)} %get-tuple-element.42.rates, f32[256,1024]{1,0:T(8,128)} %get-tuple-element.43.inner, bf16[256,1024]{1,0:T(8,128)(2,1)} %get-tuple-element.44.q, f32[1024,128]{1,0:T(8,128)} %get-tuple-element.45.first, bf16[1024,128]{1,0:T(8,128)(2,1)} %bitcast.5), custom_call_target="tpu_custom_call" | custom-call | flops 10000000000 | bytes 1 | tf_op jit(solution)/shard_map/pallas_call | solution.py:33
  131.1 2.5 %collective-permute-start.6 = (f32[8,256]{1,0:T(8,128)}, f32[8,256]{1,0:T(8,128)S(1)}, u32[]{:S(2)}, u32[]{:S(2)}) collective-permute-start(f32[8,256]{1,0:T(8,128)} %get-tuple-element.49.s0), channel_id=1, source_target_pairs={{0,3},{1,0},{2,1},{3,2},{4,7},{5,4},{6,5},{7,6},{8,11},{9,8},{10,9... | collective-permute-start | bytes 24584 | tf_op jit(solution)/shard_map/ppermute | solution.py:363
  133.6 0.5 collective-permute-start.5
  134.1 0.6 collective-permute-start.4
  134.7 2.5 %collective-permute-done.3.far = bf16[560,512]{1,0:T(8,128)(2,1)S(1)} collective-permute-done((bf16[560,512]{1,0:T(8,128)(2,1)S(1)}, bf16[560,512]{1,0:T(8,128)(2,1)S(1)}, u32[]{:S(2)}, u32[]{:S(2)}) %collective-permute-start.3) | collective-permute-done | bytes 573472 | tf_op jit(solution)/shard_map/ppermute | solution.py:355
  137.2 0.0 copy-done.1
  137.2 0.0 copy-done.5
  137.3 0.0 copy-done.6
  137.3 0.0 copy-start.4
  137.3 0.0 copy-start.7
  137.3 0.0 copy-start.9
  137.3 0.6 shard_map.130
  137.9 0.0 collective-permute-done.6.s3
  137.9 0.0 collective-permute-done.5.s2
  137.9 0.1 collective-permute-done.4.s1
  138.0 2.1 %collective-permute-start.7 = (bf16[256,512]{1,0:T(8,128)(2,1)S(1)}, bf16[256,512]{1,0:T(8,128)(2,1)S(1)}, u32[]{:S(2)}, u32[]{:S(2)}) collective-permute-start(bf16[256,512]{1,0:T(8,128)(2,1)S(1)} %get-tuple-element.59), channel_id=1, source_target_pairs={{0,4},{4,0},{8,12},{12,8},{16,20},{20,16},{24,28},{28,24},{32,36},... | collective-permute-start | bytes 786440 | tf_op jit(solution)/shard_map/ppermute | solution.py:359
  140.1 0.0 copy-done.2
  140.1 1.3 shard_map.131
  141.4 0.0 collective-permute-done.7.other
  141.5 0.8 shard_map.132
  (9 shorter events, 0.0 us)
Async XLA Ops:
  27.1 13.4 %collective-permute-start = (bf16[784,512]{1,0:T(8,128)(2,1)}, bf16[784,512]{1,0:T(8,128)(2,1)S(1)}, u32[]{:S(2)}, u32[]{:S(2)}) collective-permute-start(bf16[784,512]{1,0:T(8,128)(2,1)} %get-tuple-element.31), channel_id=1, source_target_pairs={{0,4},{4,0},{8,12},{12,8},{16,20},{20,16},{24,28},{28,24},{32,36},... | collective-permute-start | bytes 2408456 | tf_op jit(solution)/shard_map/ppermute | solution.py:359
  30.4 69.7 %all-to-all-start = ((bf16[64,16,128]{2,1,0:T(8,128)(2,1)}), bf16[64,16,128]{2,1,0:T(8,128)(2,1)S(1)}, u32[]{:S(2)}, u32[]{:S(2)}) async-start(bf16[64,16,128]{2,1,0:T(8,128)(2,1)} %bitcast.6), calls=%async_computation | async-start | bytes 524288 | tf_op jit(solution)/shard_map/all_to_all | solution.py:401
  40.4 0.9 copy-start.11
  90.9 26.6 %collective-permute-start.1 = (bf16[528,512]{1,0:T(8,128)(2,1)}, bf16[528,512]{1,0:T(8,128)(2,1)S(1)}, u32[]{:S(2)}, u32[]{:S(2)}) collective-permute-start(bf16[528,512]{1,0:T(8,128)(2,1)} %get-tuple-element.32.q), channel_id=1, source_target_pairs={{8,0},{12,4},{16,8},{20,12},{24,16},{28,20},{32,24},{36,28},{40,32... | collective-permute-start | bytes 1622024 | tf_op jit(solution)/shard_map/ppermute | solution.py:355
  92.2 27.5 %collective-permute-start.2 = (bf16[768,512]{1,0:T(8,128)(2,1)}, bf16[768,512]{1,0:T(8,128)(2,1)S(1)}, u32[]{:S(2)}, u32[]{:S(2)}) collective-permute-start(bf16[768,512]{1,0:T(8,128)(2,1)} %get-tuple-element.34.tail), channel_id=1, source_target_pairs={{0,8},{4,12},{8,16},{12,20},{16,24},{20,28},{24,32},{28,36},{32,40... | collective-permute-start | bytes 2359304 | tf_op jit(solution)/shard_map/ppermute | solution.py:355
  100.1 0.7 copy-start.10
  102.2 25.1 %all-to-all-start.1 = ((bf16[64,16,128]{2,1,0:T(8,128)(2,1)}), bf16[64,16,128]{2,1,0:T(8,128)(2,1)S(1)}, u32[]{:S(2)}, u32[]{:S(2)}) async-start(bf16[64,16,128]{2,1,0:T(8,128)(2,1)} %shard_map.125), calls=%async_computation.1 | async-start | bytes 524288 | tf_op jit(solution)/shard_map/all_to_all | solution.py:438
  113.0 4.5 %copy-start = (bf16[768,512]{1,0:T(8,128)(2,1)S(1)}, bf16[768,512]{1,0:T(8,128)(2,1)}, u32[]{:S(2)}) copy-start(bf16[768,512]{1,0:T(8,128)(2,1)} %get-tuple-element.34.tail) | copy-start | bytes 2359300
  113.0 4.5 %copy-start.3 = (bf16[256,512]{1,0:T(8,128)(2,1)S(1)}, bf16[256,512]{1,0:T(8,128)(2,1)}, u32[]{:S(2)}) copy-start(bf16[256,512]{1,0:T(8,128)(2,1)} %get-tuple-element.33.head) | copy-start | bytes 786436
  113.0 4.5 %copy-start.8 = (s32[128]{0:T(128)S(1)}, s32[128]{0:T(128)}, u32[]{:S(2)}) copy-start(s32[128]{0:T(128)} %docs.3) | copy-start | bytes 1540
  122.0 15.3 %collective-permute-start.3 = (bf16[560,512]{1,0:T(8,128)(2,1)S(1)}, bf16[560,512]{1,0:T(8,128)(2,1)S(1)}, u32[]{:S(2)}, u32[]{:S(2)}) collective-permute-start(bf16[560,512]{1,0:T(8,128)(2,1)S(1)} %shard_map.127), channel_id=1, source_target_pairs={{0,8},{4,12},{8,16},{12,20},{16,24},{20,28},{24,32},{28,36},{32,40... | collective-permute-start | bytes 1720328 | tf_op jit(solution)/shard_map/ppermute | solution.py:355
  127.3 0.7 copy-start.12
  128.0 9.2 %copy-start.1 = (f32[512,512]{1,0:T(8,128)S(1)}, f32[512,512]{1,0:T(8,128)}, u32[]{:S(2)}) copy-start(f32[512,512]{1,0:T(8,128)} %get-tuple-element.50.near) | copy-start | bytes 3145732
  128.0 9.2 %copy-start.5 = (f32[512,128]{1,0:T(8,128)S(1)}, f32[512,128]{1,0:T(8,128)}, u32[]{:S(2)}) copy-start(f32[512,128]{1,0:T(8,128)} %get-tuple-element.51.tops) | copy-start | bytes 786436
  128.0 9.2 %copy-start.6 = (f32[512,128]{1,0:T(8,128)S(1)}, f32[512,128]{1,0:T(8,128)}, u32[]{:S(2)}) copy-start(f32[512,128]{1,0:T(8,128)} %get-tuple-element.52.sums) | copy-start | bytes 786436
  131.1 6.8 %collective-permute-start.6 = (f32[8,256]{1,0:T(8,128)}, f32[8,256]{1,0:T(8,128)S(1)}, u32[]{:S(2)}, u32[]{:S(2)}) collective-permute-start(f32[8,256]{1,0:T(8,128)} %get-tuple-element.49.s0), channel_id=1, source_target_pairs={{0,3},{1,0},{2,1},{3,2},{4,7},{5,4},{6,5},{7,6},{8,11},{9,8},{10,9... | collective-permute-start | bytes 24584 | tf_op jit(solution)/shard_map/ppermute | solution.py:363
  133.6 4.4 %collective-permute-start.5 = (f32[8,256]{1,0:T(8,128)}, f32[8,256]{1,0:T(8,128)S(1)}, u32[]{:S(2)}, u32[]{:S(2)}) collective-permute-start(f32[8,256]{1,0:T(8,128)} %get-tuple-element.49.s0), channel_id=1, source_target_pairs={{0,2},{1,3},{2,0},{3,1},{4,6},{5,7},{6,4},{7,5},{8,10},{9,11},{10,... | collective-permute-start | bytes 24584 | tf_op jit(solution)/shard_map/ppermute | solution.py:363
  134.1 3.9 %collective-permute-start.4 = (f32[8,256]{1,0:T(8,128)}, f32[8,256]{1,0:T(8,128)S(1)}, u32[]{:S(2)}, u32[]{:S(2)}) collective-permute-start(f32[8,256]{1,0:T(8,128)} %get-tuple-element.49.s0), channel_id=1, source_target_pairs={{0,1},{1,2},{2,3},{3,0},{4,5},{5,6},{6,7},{7,4},{8,9},{9,10},{10,1... | collective-permute-start | bytes 24584 | tf_op jit(solution)/shard_map/ppermute | solution.py:363
  137.3 2.9 %copy-start.2 = (f32[256,1024]{1,0:T(8,128)S(1)}, f32[256,1024]{1,0:T(8,128)}, u32[]{:S(2)}) copy-start(f32[256,1024]{1,0:T(8,128)} %get-tuple-element.48.heads) | copy-start | bytes 3145732
  137.3 2.9 %copy-start.4 = (bf16[256,1024]{1,0:T(8,128)(2,1)S(1)}, bf16[256,1024]{1,0:T(8,128)(2,1)}, u32[]{:S(2)}) copy-start(bf16[256,1024]{1,0:T(8,128)(2,1)} %gate.1) | copy-start | bytes 1572868
  137.3 2.9 %copy-start.7 = (f32[8,256]{1,0:T(8,128)S(1)}, f32[8,256]{1,0:T(8,128)}, u32[]{:S(2)}) copy-start(f32[8,256]{1,0:T(8,128)} %get-tuple-element.49.s0) | copy-start | bytes 24580
  137.3 2.9 %copy-start.9 = (f32[1024]{0:T(1024)S(1)}, f32[1024]{0:T(1024)}, u32[]{:S(2)}) copy-start(f32[1024]{0:T(1024)} %param.15) | copy-start | bytes 12292
  138.0 3.4 %collective-permute-start.7 = (bf16[256,512]{1,0:T(8,128)(2,1)S(1)}, bf16[256,512]{1,0:T(8,128)(2,1)S(1)}, u32[]{:S(2)}, u32[]{:S(2)}) collective-permute-start(bf16[256,512]{1,0:T(8,128)(2,1)S(1)} %get-tuple-element.59), channel_id=1, source_target_pairs={{0,4},{4,0},{8,12},{12,8},{16,20},{20,16},{24,28},{28,24},{32,36},... | collective-permute-start | bytes 786440 | tf_op jit(solution)/shard_map/ppermute | solution.py:359

commit v5 on v4

--- a/solution.py
+++ b/solution.py
@@ -348,7 +348,7 @@
     out[:, half(1 - core)] = other[...]
 
 
-SMALL = (prefix_body, next_body, far_body, merge_body, norm_body, place_body)
+SMALL = (gather_body, near_body, prefix_body, next_body, far_body, merge_body, norm_body, place_body)
 
 
 def shifted(x, distance):
@@ -395,7 +395,6 @@
             pltpu.SemaphoreType.DMA,
             pltpu.SemaphoreType.DMA((LOCAL + 4,)),
         ],
-        outs_at=[VMEM, anywhere],
     )
     other = swapped(sent)
     parts = lax.all_to_all(state.reshape(SHARDS, 16, HD), "seq", 0, 0)
@@ -413,7 +412,6 @@
             pltpu.VMEM((16, HALF), bf16),
             pltpu.SemaphoreType.DMA((10,)),
         ],
-        outs_at=[anywhere] * 3,
     )
     tail = shifted(own_tail, 2)
     next_q = shifted(far_q, -2)

time: 144 us -> 74.6 us (0.52)
  the two profiles are of different devices: /device:TPU:1 before, /device:TPU:27 now
where the time goes in v5:
time: 74.6 us; the launch traced here: 74.1 us
  starting transfers between devices  38.6 us (52%)
  Pallas kernels  24.5 us (33%)
  waiting for transfers between devices  7.25 us (10%)
  local copies, waits for them, and re-layouts  2.82 us (4%)
  between operations  0.89 us (1%)
    pallas_call x11, Pallas kernels, call(): pl.pallas_call(body, out_shape=outs, in_specs=specs, out_specs=outs_at or...  24.5 us
    all_to_all x1, starting transfers between devices, per_device(): parts = lax.all_to_all(state.reshape(SHARDS, 16, HD), 'seq', 0, 0)  12.2 us
    all_to_all x1, starting transfers between devices, per_device(): entering = lax.all_to_all(prefix, 'seq', 0, 0).reshape(WIDTH, HD)  9.25 us
    ppermute x3, starting transfers between devices, shifted(): lax.ppermute(x, 'seq', [(i, i + distance) for i in range(SHARDS) if 0 <=...  9.09 us
    ppermute x3, waiting for transfers between devices, shifted(): lax.ppermute(x, 'seq', [(i, i + distance) for i in range(SHARDS) if 0 <=...  7.23 us
    ppermute x2, starting transfers between devices, swapped(): return lax.ppermute(x, 'seq', [(i, i ^ 1) for i in range(SHARDS)])  4.19 us
    ppermute x3, starting transfers between devices, turned(): return lax.ppermute(x, 'head', [(i, (i + distance) % 4) for i in range(4)])  3.91 us
    unnamed x30, local copies, waits for them, and re-layouts  2.82 us
  transfers between devices with their start and end apart: 10, of which 2 were waited for; matrix products, arithmetic and copies ran while one was open for 0% of the time, Pallas kernels for 27%

profile of v5, /device:TPU:27, one launch (start us, length us, event | category | flops | bytes accessed | tf_op | source)
XLA Modules:
  0.0 74.1 jit_solution(2273230552484739296)
XLA Ops:
  0.7 3.8 %shard_map.122 = (bf16[1024,128]{1,0:T(8,128)(2,1)}, bf16[784,512]{1,0:T(8,128)(2,1)}) custom-call(s32[1]{0:T(128)} %bitcast.index, f32[8]{0:T(128)} %rate.3, s32[2,128]{1,0:T(2,128)} %mask.3, bf16[256,1024]{1,0:T(8,128)(2,1)} %k.3, bf16[256,1024]{1,0:T(8,128)(2,1)} %v.3, bf16[256,1024]{1,0:T(8,128)(2,1)} %q.2, bf16[256,1024]{1,0:T(8,128)(2,1)} %k.2, ...), custom_call_target="tpu_custom_call" | custom-call | flops 1 | bytes 1 | tf_op jit(solution)/shard_map/pallas_call | solution.py:33
  4.4 0.0 copy-start
  4.5 0.8 %collective-permute-start = (bf16[784,512]{1,0:T(8,128)(2,1)}, bf16[784,512]{1,0:T(8,128)(2,1)S(1)}, u32[]{:S(2)}, u32[]{:S(2)}) collective-permute-start(bf16[784,512]{1,0:T(8,128)(2,1)} %get-tuple-element.31), channel_id=1, source_target_pairs={{0,4},{4,0},{8,12},{12,8},{16,20},{20,16},{24,28},{28,24},{32,36},... | collective-permute-start | bytes 2408456 | tf_op jit(solution)/shard_map/ppermute | solution.py:359
  5.2 12.2 %all-to-all-start = ((bf16[64,16,128]{2,1,0:T(8,128)(2,1)}), bf16[64,16,128]{2,1,0:T(8,128)(2,1)}, u32[]{:S(2)}, u32[]{:S(2)}) async-start(bf16[64,16,128]{2,1,0:T(8,128)(2,1)} %bitcast.5), calls=%async_computation | async-start | bytes 524288 | tf_op jit(solution)/shard_map/all_to_all | solution.py:400
  17.4 0.0 collective-permute-done.other
  17.4 0.0 copy-done.1
  17.4 0.0 copy-done.2
  17.4 0.0 copy-done
  17.4 0.0 copy-done.12
  17.4 1.7 %shard_map.123 = (bf16[528,512]{1,0:T(8,128)(2,1)}, bf16[256,512]{1,0:T(8,128)(2,1)S(1)}, bf16[768,512]{1,0:T(8,128)(2,1)S(1)}) custom-call(s32[1]{0:T(128)} %bitcast.index, s32[2,128]{1,0:T(2,128)S(1)} %copy-done.12, bf16[256,1024]{1,0:T(8,128)(2,1)S(1)} %copy-done, bf16[256,1024]{1,0:T(8,128)(2,1)S(1)} %copy-done.1, bf16[256,1024]{1,0:T(8,128)(2,1)S(1)} %copy-done.2, ...), custom_call_target="tpu_custom_call" | custom-call | flops 1 | bytes 1 | tf_op jit(solution)/shard_map/pallas_call | solution.py:33
  19.2 4.6 %collective-permute-start.1 = (bf16[528,512]{1,0:T(8,128)(2,1)}, bf16[528,512]{1,0:T(8,128)(2,1)S(1)}, u32[]{:S(2)}, u32[]{:S(2)}) collective-permute-start(bf16[528,512]{1,0:T(8,128)(2,1)} %get-tuple-element.32.q), channel_id=1, source_target_pairs={{8,0},{12,4},{16,8},{20,12},{24,16},{28,20},{32,24},{36,28},{40,32... | collective-permute-start | bytes 1622024 | tf_op jit(solution)/shard_map/ppermute | solution.py:355
  23.7 0.0 copy-start.11
  23.8 1.9 %collective-permute-start.2 = (bf16[768,512]{1,0:T(8,128)(2,1)S(1)}, bf16[768,512]{1,0:T(8,128)(2,1)S(1)}, u32[]{:S(2)}, u32[]{:S(2)}) collective-permute-start(bf16[768,512]{1,0:T(8,128)(2,1)S(1)} %get-tuple-element.34.tail), channel_id=1, source_target_pairs={{0,8},{4,12},{8,16},{12,20},{16,24},{20,28},{24,32},{28,36},{32,40... | collective-permute-start | bytes 2359304 | tf_op jit(solution)/shard_map/ppermute | solution.py:355
  25.7 0.0 copy-done.11
  25.7 2.5 %shard_map.124 = (f32[512,512]{1,0:T(8,128)S(1)}, f32[512,128]{1,0:T(8,128)S(1)}, f32[512,128]{1,0:T(8,128)S(1)}) custom-call(s32[1]{0:T(128)} %bitcast.index, s32[128]{0:T(128)S(1)} %copy-done.11, bf16[528,512]{1,0:T(8,128)(2,1)} %get-tuple-element.32.q, bf16[256,512]{1,0:T(8,128)(2,1)S(1)} %get-tuple-element.33.head, ...), custom_call_target="tpu_custom_call" | custom-call | flops 1 | bytes 1 | tf_op jit(solution)/shard_map/pallas_call | solution.py:33
  28.2 0.7 copy-done.5
  28.9 0.7 copy-done.7
  29.6 0.0 all-to-all-done.parts
  29.6 0.7 copy-done.14
  30.3 1.1 %shard_map.125 = bf16[64,16,128]{2,1,0:T(8,128)(2,1)S(1)} custom-call(s32[1]{0:T(128)} %bitcast.index, f32[8]{0:T(128)S(1)} %copy-done.14, bf16[64,16,128]{2,1,0:T(8,128)(2,1)} %all-to-all-done.parts), custom_call_target="tpu_custom_call" | custom-call | flops 5000000000 | bytes 1 | tf_op jit(solution)/shard_map/pallas_call | solution.py:33
  31.4 0.7 copy-done.9
  32.1 9.2 %all-to-all-start.1 = ((bf16[64,16,128]{2,1,0:T(8,128)(2,1)}), bf16[64,16,128]{2,1,0:T(8,128)(2,1)}, u32[]{:S(2)}, u32[]{:S(2)}) async-start(bf16[64,16,128]{2,1,0:T(8,128)(2,1)} %copy-done.9), calls=%async_computation.1 | async-start | bytes 524288 | tf_op jit(solution)/shard_map/all_to_all | solution.py:436
  41.4 4.4 %shard_map.128 = (f32[256,1024]{1,0:T(8,128)}, bf16[256,1024]{1,0:T(8,128)(2,1)}, f32[1024,128]{1,0:T(8,128)}, f32[8,128]{1,0:T(8,128)}) custom-call(f32[8]{0:T(128)} %rate.3, bf16[256,1024]{1,0:T(8,128)(2,1)} %q.3, bf16[256,1024]{1,0:T(8,128)(2,1)} %k.3, bf16[256,1024]{1,0:T(8,128)(2,1)} %v.3), custom_call_target="tpu_custom_call" | custom-call | flops 1 | bytes 1 | tf_op jit(solution)/shard_map/pallas_call | solution.py:33
  45.7 0.0 collective-permute-done.1.q
  45.7 2.2 %shard_map.126 = (f32[512,512]{1,0:T(8,128)S(1)}, f32[512,128]{1,0:T(8,128)S(1)}, f32[512,128]{1,0:T(8,128)S(1)}) custom-call(s32[1]{0:T(128)} %bitcast.index, s32[128]{0:T(128)S(1)} %copy-done.11, bf16[528,512]{1,0:T(8,128)(2,1)S(1)} %collective-permute-done.1.q, bf16[256,512]{1,0:T(8,128)(2,1)S(1)} %get-tuple-element.33.head, ...), custom_call_target="tpu_custom_call" | custom-call | flops 1 | bytes 1 | tf_op jit(solution)/shard_map/pallas_call | solution.py:33
  47.9 0.5 collective-permute-done.2.tail
  48.4 3.1 %shard_map.127 = bf16[560,512]{1,0:T(8,128)(2,1)} custom-call(s32[1]{0:T(128)} %bitcast.index, s32[128]{0:T(128)S(1)} %copy-done.11, bf16[528,512]{1,0:T(8,128)(2,1)S(1)} %collective-permute-done.1.q, bf16[768,512]{1,0:T(8,128)(2,1)S(1)} %collective-permute-done.2.tail, f32[512,512]{1,0:T(8,128)S(1)} %get-tuple-element.39.done, ...), custom_call_target="tpu_custom_call" | custom-call | flops 1 | bytes 1 | tf_op jit(solution)/shard_map/pallas_call | solution.py:33
  51.5 2.6 %collective-permute-start.3 = (bf16[560,512]{1,0:T(8,128)(2,1)}, bf16[560,512]{1,0:T(8,128)(2,1)S(1)}, u32[]{:S(2)}, u32[]{:S(2)}) collective-permute-start(bf16[560,512]{1,0:T(8,128)(2,1)} %shard_map.127), channel_id=1, source_target_pairs={{0,8},{4,12},{8,16},{12,20},{16,24},{20,28},{24,32},{28,36},{32,40... | collective-permute-start | bytes 1720328 | tf_op jit(solution)/shard_map/ppermute | solution.py:355
  54.1 0.0 all-to-all-done.1
  54.2 0.0 copy-start.6
  54.2 0.0 copy-start.8
  54.2 3.0 %shard_map.129 = (f32[256,1024]{1,0:T(8,128)}, f32[8,256]{1,0:T(8,128)}) custom-call(f32[8,128]{1,0:T(8,128)} %get-tuple-element.42.rates, f32[256,1024]{1,0:T(8,128)} %get-tuple-element.43.inner, bf16[256,1024]{1,0:T(8,128)(2,1)} %get-tuple-element.44.q, f32[1024,128]{1,0:T(8,128)} %get-tuple-element.45.first, bf16[1024,128]{1,0:T(8,128)(2,1)} %bitcast.2.state), custom_call_target="tpu_custom_call" | custom-call | flops 10000000000 | bytes 1 | tf_op jit(solution)/shard_map/pallas_call | solution.py:33
  57.2 0.3 collective-permute-start.6
  57.4 2.1 %collective-permute-start.5 = (f32[8,256]{1,0:T(8,128)}, f32[8,256]{1,0:T(8,128)S(1)}, u32[]{:S(2)}, u32[]{:S(2)}) collective-permute-start(f32[8,256]{1,0:T(8,128)} %get-tuple-element.49.s0), channel_id=1, source_target_pairs={{0,2},{1,3},{2,0},{3,1},{4,6},{5,7},{6,4},{7,5},{8,10},{9,11},{10,... | collective-permute-start | bytes 24584 | tf_op jit(solution)/shard_map/ppermute | solution.py:363
  59.6 1.5 %collective-permute-start.4 = (f32[8,256]{1,0:T(8,128)}, f32[8,256]{1,0:T(8,128)S(1)}, u32[]{:S(2)}, u32[]{:S(2)}) collective-permute-start(f32[8,256]{1,0:T(8,128)} %get-tuple-element.49.s0), channel_id=1, source_target_pairs={{0,1},{1,2},{2,3},{3,0},{4,5},{5,6},{6,7},{7,4},{8,9},{9,10},{10,1... | collective-permute-start | bytes 24584 | tf_op jit(solution)/shard_map/ppermute | solution.py:363
  61.1 6.7 %collective-permute-done.3.far = bf16[560,512]{1,0:T(8,128)(2,1)S(1)} collective-permute-done((bf16[560,512]{1,0:T(8,128)(2,1)}, bf16[560,512]{1,0:T(8,128)(2,1)S(1)}, u32[]{:S(2)}, u32[]{:S(2)}) %collective-permute-start.3) | collective-permute-done | bytes 573472 | tf_op jit(solution)/shard_map/ppermute | solution.py:355
  67.8 0.0 copy-done.6
  67.8 0.0 copy-start.10
  67.8 0.0 copy-start.13
  67.8 0.6 shard_map.130
  68.5 0.0 collective-permute-done.6.s3
  68.5 0.0 collective-permute-done.5.s2
  68.5 0.0 collective-permute-done.4.s1
  68.5 3.4 %collective-permute-start.7 = (bf16[256,512]{1,0:T(8,128)(2,1)S(1)}, bf16[256,512]{1,0:T(8,128)(2,1)S(1)}, u32[]{:S(2)}, u32[]{:S(2)}) collective-permute-start(bf16[256,512]{1,0:T(8,128)(2,1)S(1)} %get-tuple-element.59), channel_id=1, source_target_pairs={{0,4},{4,0},{8,12},{12,8},{16,20},{20,16},{24,28},{28,24},{32,36},... | collective-permute-start | bytes 786440 | tf_op jit(solution)/shard_map/ppermute | solution.py:359
  71.9 0.0 copy-done.13
  71.9 1.3 %shard_map.131 = bf16[256,1024]{1,0:T(8,128)(2,1)} custom-call(f32[256,1024]{1,0:T(8,128)S(1)} %copy-done.3, bf16[256,1024]{1,0:T(8,128)(2,1)S(1)} %copy-done.4, f32[1,1024]{1,0:T(1,128)S(1)} %bitcast.4, f32[8,256]{1,0:T(8,128)S(1)} %copy-done.10, f32[8,256]{1,0:T(8,128)S(1)} %collective-permute-done.4.s1, f32[8,256]{1,0:T(8,128)S(1)} %collective-permute-done.5.s2, ...), custom_call_target="tpu_custom_call" | custom-call | flops 1 | bytes 1 | tf_op jit(solution)/shard_map/pallas_call | solution.py:33
  73.3 0.0 collective-permute-done.7.other
  73.3 0.8 %shard_map.132 = bf16[256,1024]{1,0:T(8,128)(2,1)} custom-call(s32[1]{0:T(128)} %bitcast.index, bf16[256,512]{1,0:T(8,128)(2,1)S(1)} %get-tuple-element.58.mine, bf16[256,512]{1,0:T(8,128)(2,1)S(1)} %collective-permute-done.7.other), custom_call_target="tpu_custom_call" | custom-call | flops 1 | bytes 1 | tf_op jit(solution)/shard_map/pallas_call | solution.py:33
  (13 shorter events, 0.0 us)
Async XLA Ops:
  0.6 16.8 %copy-start.1 = (bf16[256,1024]{1,0:T(8,128)(2,1)S(1)}, bf16[256,1024]{1,0:T(8,128)(2,1)}, u32[]{:S(2)}) copy-start(bf16[256,1024]{1,0:T(8,128)(2,1)} %k.2) | copy-start | bytes 1572868
  0.6 16.8 %copy-start.2 = (bf16[256,1024]{1,0:T(8,128)(2,1)S(1)}, bf16[256,1024]{1,0:T(8,128)(2,1)}, u32[]{:S(2)}) copy-start(bf16[256,1024]{1,0:T(8,128)(2,1)} %v.2) | copy-start | bytes 1572868
  4.4 13.0 %copy-start = (bf16[256,1024]{1,0:T(8,128)(2,1)S(1)}, bf16[256,1024]{1,0:T(8,128)(2,1)}, u32[]{:S(2)}) copy-start(bf16[256,1024]{1,0:T(8,128)(2,1)} %q.2) | copy-start | bytes 1572868
  4.5 12.9 %collective-permute-start = (bf16[784,512]{1,0:T(8,128)(2,1)}, bf16[784,512]{1,0:T(8,128)(2,1)S(1)}, u32[]{:S(2)}, u32[]{:S(2)}) collective-permute-start(bf16[784,512]{1,0:T(8,128)(2,1)} %get-tuple-element.31), channel_id=1, source_target_pairs={{0,4},{4,0},{8,12},{12,8},{16,20},{20,16},{24,28},{28,24},{32,36},... | collective-permute-start | bytes 2408456 | tf_op jit(solution)/shard_map/ppermute | solution.py:359
  5.2 12.2 %copy-start.12 = (s32[2,128]{1,0:T(2,128)S(1)}, s32[2,128]{1,0:T(2,128)}, u32[]{:S(2)}) copy-start(s32[2,128]{1,0:T(2,128)} %mask.3) | copy-start | bytes 3076
  5.2 24.4 %all-to-all-start = ((bf16[64,16,128]{2,1,0:T(8,128)(2,1)}), bf16[64,16,128]{2,1,0:T(8,128)(2,1)}, u32[]{:S(2)}, u32[]{:S(2)}) async-start(bf16[64,16,128]{2,1,0:T(8,128)(2,1)} %bitcast.5), calls=%async_computation | async-start | bytes 524288 | tf_op jit(solution)/shard_map/all_to_all | solution.py:400
  19.2 26.6 %collective-permute-start.1 = (bf16[528,512]{1,0:T(8,128)(2,1)}, bf16[528,512]{1,0:T(8,128)(2,1)S(1)}, u32[]{:S(2)}, u32[]{:S(2)}) collective-permute-start(bf16[528,512]{1,0:T(8,128)(2,1)} %get-tuple-element.32.q), channel_id=1, source_target_pairs={{8,0},{12,4},{16,8},{20,12},{24,16},{28,20},{32,24},{36,28},{40,32... | collective-permute-start | bytes 1622024 | tf_op jit(solution)/shard_map/ppermute | solution.py:355
  23.7 1.9 %copy-start.11 = (s32[128]{0:T(128)S(1)}, s32[128]{0:T(128)}, u32[]{:S(2)}) copy-start(s32[128]{0:T(128)} %docs.3) | copy-start | bytes 1540
  23.8 24.7 %collective-permute-start.2 = (bf16[768,512]{1,0:T(8,128)(2,1)S(1)}, bf16[768,512]{1,0:T(8,128)(2,1)S(1)}, u32[]{:S(2)}, u32[]{:S(2)}) collective-permute-start(bf16[768,512]{1,0:T(8,128)(2,1)S(1)} %get-tuple-element.34.tail), channel_id=1, source_target_pairs={{0,8},{4,12},{8,16},{12,20},{16,24},{20,28},{24,32},{28,36},{32,40... | collective-permute-start | bytes 2359304 | tf_op jit(solution)/shard_map/ppermute | solution.py:355
  28.2 0.7 copy-start.5
  28.9 0.7 copy-start.7
  29.6 0.7 copy-start.14
  31.4 0.7 copy-start.9
  32.1 22.0 %all-to-all-start.1 = ((bf16[64,16,128]{2,1,0:T(8,128)(2,1)}), bf16[64,16,128]{2,1,0:T(8,128)(2,1)}, u32[]{:S(2)}, u32[]{:S(2)}) async-start(bf16[64,16,128]{2,1,0:T(8,128)(2,1)} %copy-done.9), calls=%async_computation.1 | async-start | bytes 524288 | tf_op jit(solution)/shard_map/all_to_all | solution.py:436
  51.5 16.3 %collective-permute-start.3 = (bf16[560,512]{1,0:T(8,128)(2,1)}, bf16[560,512]{1,0:T(8,128)(2,1)S(1)}, u32[]{:S(2)}, u32[]{:S(2)}) collective-permute-start(bf16[560,512]{1,0:T(8,128)(2,1)} %shard_map.127), channel_id=1, source_target_pairs={{0,8},{4,12},{8,16},{12,20},{16,24},{20,28},{24,32},{28,36},{32,40... | collective-permute-start | bytes 1720328 | tf_op jit(solution)/shard_map/ppermute | solution.py:355
  54.2 13.7 %copy-start.6 = (f32[512,128]{1,0:T(8,128)S(1)}, f32[512,128]{1,0:T(8,128)}, u32[]{:S(2)}) copy-start(f32[512,128]{1,0:T(8,128)} %copy-done.5) | copy-start | bytes 786436
  54.2 13.6 %copy-start.8 = (f32[512,128]{1,0:T(8,128)S(1)}, f32[512,128]{1,0:T(8,128)}, u32[]{:S(2)}) copy-start(f32[512,128]{1,0:T(8,128)} %copy-done.7) | copy-start | bytes 786436
  57.2 11.3 %collective-permute-start.6 = (f32[8,256]{1,0:T(8,128)}, f32[8,256]{1,0:T(8,128)S(1)}, u32[]{:S(2)}, u32[]{:S(2)}) collective-permute-start(f32[8,256]{1,0:T(8,128)} %get-tuple-element.49.s0), channel_id=1, source_target_pairs={{0,3},{1,0},{2,1},{3,2},{4,7},{5,4},{6,5},{7,6},{8,11},{9,8},{10,9... | collective-permute-start | bytes 24584 | tf_op jit(solution)/shard_map/ppermute | solution.py:363
  57.4 11.1 %collective-permute-start.5 = (f32[8,256]{1,0:T(8,128)}, f32[8,256]{1,0:T(8,128)S(1)}, u32[]{:S(2)}, u32[]{:S(2)}) collective-permute-start(f32[8,256]{1,0:T(8,128)} %get-tuple-element.49.s0), channel_id=1, source_target_pairs={{0,2},{1,3},{2,0},{3,1},{4,6},{5,7},{6,4},{7,5},{8,10},{9,11},{10,... | collective-permute-start | bytes 24584 | tf_op jit(solution)/shard_map/ppermute | solution.py:363
  59.6 8.9 %collective-permute-start.4 = (f32[8,256]{1,0:T(8,128)}, f32[8,256]{1,0:T(8,128)S(1)}, u32[]{:S(2)}, u32[]{:S(2)}) collective-permute-start(f32[8,256]{1,0:T(8,128)} %get-tuple-element.49.s0), channel_id=1, source_target_pairs={{0,1},{1,2},{2,3},{3,0},{4,5},{5,6},{6,7},{7,4},{8,9},{9,10},{10,1... | collective-permute-start | bytes 24584 | tf_op jit(solution)/shard_map/ppermute | solution.py:363
  67.8 4.1 %copy-start.3 = (f32[256,1024]{1,0:T(8,128)S(1)}, f32[256,1024]{1,0:T(8,128)}, u32[]{:S(2)}) copy-start(f32[256,1024]{1,0:T(8,128)} %get-tuple-element.48.heads) | copy-start | bytes 3145732
  67.8 4.1 %copy-start.4 = (bf16[256,1024]{1,0:T(8,128)(2,1)S(1)}, bf16[256,1024]{1,0:T(8,128)(2,1)}, u32[]{:S(2)}) copy-start(bf16[256,1024]{1,0:T(8,128)(2,1)} %gate.1) | copy-start | bytes 1572868
  67.8 4.1 %copy-start.10 = (f32[8,256]{1,0:T(8,128)S(1)}, f32[8,256]{1,0:T(8,128)}, u32[]{:S(2)}) copy-start(f32[8,256]{1,0:T(8,128)} %get-tuple-element.49.s0) | copy-start | bytes 24580
  67.8 4.1 %copy-start.13 = (f32[1024]{0:T(1024)S(1)}, f32[1024]{0:T(1024)}, u32[]{:S(2)}) copy-start(f32[1024]{0:T(1024)} %param.15) | copy-start | bytes 12292
  68.5 4.8 %collective-permute-start.7 = (bf16[256,512]{1,0:T(8,128)(2,1)S(1)}, bf16[256,512]{1,0:T(8,128)(2,1)S(1)}, u32[]{:S(2)}, u32[]{:S(2)}) collective-permute-start(bf16[256,512]{1,0:T(8,128)(2,1)S(1)} %get-tuple-element.59), channel_id=1, source_target_pairs={{0,4},{4,0},{8,12},{12,8},{16,20},{20,16},{24,28},{28,24},{32,36},... | collective-permute-start | bytes 786440 | tf_op jit(solution)/shard_map/ppermute | solution.py:359

commit v6 on v5

--- a/solution.py
+++ b/solution.py
@@ -104,11 +104,10 @@
             state = step * state + parts[i].astype(f32)
 
 
-def inner_body(rate, q, k, v, out, q_out, first, rates):
+def inner_body(rate, q, k, v, out, first, rates):
     row = lax.broadcasted_iota(jnp.int32, (BLK, BLK), 0)
     col = lax.broadcasted_iota(jnp.int32, (BLK, BLK), 1)
     gap = jnp.maximum(row - col, 0).astype(f32)
-    q_out[...] = q[...]
     for h in range(LOCAL):
         rates[h : h + 1, :] = jnp.full((1, HD), rate[h], f32)
         first[cols(h), :] = block_state(rate, k, v, h, 0)
@@ -416,7 +415,46 @@
     tail = shifted(own_tail, 2)
     next_q = shifted(far_q, -2)
 
+    (prefix,) = call(
+        prefix_body,
+        [like((SHARDS, 16, HD), bf16)],
+        (index, decay_rate, parts),
+        [SMEM, SMEM, VMEM],
+        flops=PREFIX_COST,
+    )
+    prefix, doc_ids = lax.optimization_barrier((prefix, doc_ids))
+    entering = lax.all_to_all(prefix, "seq", 0, 0).reshape(WIDTH, HD)
+    inner, first, rates = call(
+        inner_body,
+        [wide, like((WIDTH, HD), f32), like((LOCAL, HD), f32)],
+        (decay_rate, lin_query, lin_key, lin_value),
+        [SMEM, VMEM, VMEM, VMEM],
+    )
     tables = [like((4 * BLK, HALF), f32), like((4 * BLK, HD), f32), like((4 * BLK, HD), f32)]
+    done, done_tops, done_sums = call(
+        next_body,
+        tables,
+        (index, doc_ids, next_q, own_head, own_tail),
+        [SMEM] * 2 + [VMEM] * 3,
+        [pltpu.VMEM((4 * BLK, 4 * BLK), f32)],
+    )
+    (far,) = call(
+        far_body,
+        [like((4 * BLK + 48, HALF), bf16)],
+        (index, doc_ids, next_q, tail, done, done_tops, done_sums),
+        [SMEM] * 2 + [VMEM] * 5,
+        [pltpu.VMEM((3 * BLK, 3 * BLK), f32)],
+    )
+    far = shifted(far, 2)
+    heads, squares = call(
+        carry_body,
+        [wide, like((8, ROWS), f32)],
+        (rates, inner, lin_query, first, entering),
+        [VMEM] * 5,
+        flops=CARRY_COST,
+    )
+    heads, own_head = lax.optimization_barrier((heads, own_head))
+    others = [turned(squares, d) for d in (1, 2, 3)]
     near, tops, sums = call(
         near_body,
         tables,
@@ -424,45 +462,6 @@
         [SMEM] * 2 + [VMEM] * 3,
         [pltpu.VMEM((4 * BLK, 4 * BLK), f32)],
     )
-    near, parts = lax.optimization_barrier((near, parts))
-    (prefix,) = call(
-        prefix_body,
-        [like((SHARDS, 16, HD), bf16)],
-        (index, decay_rate, parts),
-        [SMEM, SMEM, VMEM],
-        flops=PREFIX_COST,
-    )
-    prefix, doc_ids = lax.optimization_barrier((prefix, doc_ids))
-    entering = lax.all_to_all(prefix, "seq", 0, 0).reshape(WIDTH, HD)
-    inner, q_held, first, rates = call(
-        inner_body,
-        [wide, narrow, like((WIDTH, HD), f32), like((LOCAL, HD), f32)],
-        (decay_rate, lin_query, lin_key, lin_value),
-        [SMEM, VMEM, VMEM, VMEM],
-    )
-    done, done_tops, done_sums = call(
-        next_body,
-        tables,
-        (index, doc_ids, next_q, own_head, own_tail),
-        [SMEM] * 2 + [VMEM] * 3,
-        [pltpu.VMEM((4 * BLK, 4 * BLK), f32)],
-    )
-    (far,) = call(
-        far_body,
-        [like((4 * BLK + 48, HALF), bf16)],
-        (index, doc_ids, next_q, tail, done, done_tops, done_sums),
-        [SMEM] * 2 + [VMEM] * 5,
-        [pltpu.VMEM((3 * BLK, 3 * BLK), f32)],
-    )
-    far = shifted(far, 2)
-    heads, squares = call(
-        carry_body,
-        [wide, like((8, ROWS), f32)],
-        (rates, inner, q_held, first, entering),
-        [VMEM] * 5,
-        flops=CARRY_COST,
-    )
-    others = [turned(squares, d) for d in (1, 2, 3)]
     far, heads = lax.optimization_barrier((far, heads))
     mine, send = call(
         merge_body,

time: 74.6 us -> 75 us (level)
  waiting for transfers between devices: 7.25 us -> 12.8 us
  starting transfers between devices: 38.6 us -> 35.3 us
  local copies, waits for them, and re-layouts: 2.82 us -> 1.39 us
    all_to_all x1, waiting for transfers between devices: 0.01 us -> 3.13 us  [per_device(): parts = lax.all_to_all(state.reshape(SHARDS, 16, HD), 'seq', 0, 0)]
    all_to_all x1, starting transfers between devices: 9.25 us -> 6.75 us  [per_device(): entering = lax.all_to_all(prefix, 'seq', 0, 0).reshape(WIDTH, HD)]
    ppermute x3, waiting for transfers between devices: 7.23 us -> 9.65 us  [shifted(): lax.ppermute(x, 'seq', [(i, i + distance) for i in range(SHARDS) if 0 <=...]
    unnamed x30 -> x22, local copies, waits for them, and re-layouts: 2.82 us -> 1.39 us
  transfers between devices with their start and end apart: 10 -> 10, of which waited for: 2 -> 3; matrix products, arithmetic and copies ran while one was open for 0% -> 0% of each run, Pallas kernels for 27% -> 26%
where the time goes in v6:
time: 75 us; the launch traced here: 74.5 us
  starting transfers between devices  35.3 us (47%)
  Pallas kernels  24.2 us (32%)
  waiting for transfers between devices  12.8 us (17%)
  local copies, waits for them, and re-layouts  1.39 us (2%)
  between operations  0.85 us (1%)
    pallas_call x11, Pallas kernels, call(): pl.pallas_call(body, out_shape=outs, in_specs=specs, out_specs=outs_at or...  24.2 us
    all_to_all x1, starting transfers between devices, per_device(): parts = lax.all_to_all(state.reshape(SHARDS, 16, HD), 'seq', 0, 0)  12.2 us
    ppermute x3, waiting for transfers between devices, shifted(): lax.ppermute(x, 'seq', [(i, i + distance) for i in range(SHARDS) if 0 <=...  9.65 us
    ppermute x3, starting transfers between devices, shifted(): lax.ppermute(x, 'seq', [(i, i + distance) for i in range(SHARDS) if 0 <=...  8.42 us
    all_to_all x1, starting transfers between devices, per_device(): entering = lax.all_to_all(prefix, 'seq', 0, 0).reshape(WIDTH, HD)  6.75 us
    ppermute x2, starting transfers between devices, swapped(): return lax.ppermute(x, 'seq', [(i, i ^ 1) for i in range(SHARDS)])  4.09 us
    ppermute x3, starting transfers between devices, turned(): return lax.ppermute(x, 'head', [(i, (i + distance) % 4) for i in range(4)])  3.91 us
    all_to_all x1, waiting for transfers between devices, per_device(): parts = lax.all_to_all(state.reshape(SHARDS, 16, HD), 'seq', 0, 0)  3.13 us
  transfers between devices with their start and end apart: 10, of which 3 were waited for; matrix products, arithmetic and copies ran while one was open for 0% of the time, Pallas kernels for 26%

profile of v6, /device:TPU:27, one launch (start us, length us, event | category | flops | bytes accessed | tf_op | source)
XLA Modules:
  0.0 74.5 jit_solution(14587971129527578858)
XLA Ops:
  0.6 0.0 copy-start.1
  0.6 0.0 copy-start.2
  0.7 3.8 %shard_map.122 = (bf16[1024,128]{1,0:T(8,128)(2,1)}, bf16[784,512]{1,0:T(8,128)(2,1)}) custom-call(s32[1]{0:T(128)} %bitcast.index, f32[8]{0:T(128)} %rate.3, s32[2,128]{1,0:T(2,128)} %mask.3, bf16[256,1024]{1,0:T(8,128)(2,1)} %k.3, bf16[256,1024]{1,0:T(8,128)(2,1)} %v.3, bf16[256,1024]{1,0:T(8,128)(2,1)} %q.3, bf16[256,1024]{1,0:T(8,128)(2,1)} %k.2, ...), custom_call_target="tpu_custom_call" | custom-call | flops 1 | bytes 1 | tf_op jit(solution)/shard_map/pallas_call | solution.py:33
  4.5 0.0 copy-start
  4.5 0.8 %collective-permute-start = (bf16[784,512]{1,0:T(8,128)(2,1)}, bf16[784,512]{1,0:T(8,128)(2,1)S(1)}, u32[]{:S(2)}, u32[]{:S(2)}) collective-permute-start(bf16[784,512]{1,0:T(8,128)(2,1)} %get-tuple-element.32), channel_id=1, source_target_pairs={{0,4},{4,0},{8,12},{12,8},{16,20},{20,16},{24,28},{28,24},{32,36},... | collective-permute-start | bytes 2408456 | tf_op jit(solution)/shard_map/ppermute | solution.py:358
  5.2 0.0 copy-start.7
  5.2 12.2 %all-to-all-start = ((bf16[64,16,128]{2,1,0:T(8,128)(2,1)}), bf16[64,16,128]{2,1,0:T(8,128)(2,1)}, u32[]{:S(2)}, u32[]{:S(2)}) async-start(bf16[64,16,128]{2,1,0:T(8,128)(2,1)} %bitcast.6), calls=%async_computation | async-start | bytes 524288 | tf_op jit(solution)/shard_map/all_to_all | solution.py:399
  17.4 0.0 collective-permute-done.other
  17.4 0.0 copy-done.1
  17.4 0.0 copy-done.2
  17.4 0.0 copy-done
  17.4 0.0 copy-done.7
  17.4 1.7 %shard_map.124 = (bf16[528,512]{1,0:T(8,128)(2,1)}, bf16[256,512]{1,0:T(8,128)(2,1)S(1)}, bf16[768,512]{1,0:T(8,128)(2,1)S(1)}) custom-call(s32[1]{0:T(128)} %bitcast.index, s32[2,128]{1,0:T(2,128)S(1)} %copy-done.7, bf16[256,1024]{1,0:T(8,128)(2,1)S(1)} %copy-done, bf16[256,1024]{1,0:T(8,128)(2,1)S(1)} %copy-done.1, bf16[256,1024]{1,0:T(8,128)(2,1)S(1)} %copy-done.2, ...), custom_call_target="tpu_custom_call" | custom-call | flops 1 | bytes 1 | tf_op jit(solution)/shard_map/pallas_call | solution.py:33
  19.2 0.0 copy-start.9
  19.2 4.6 %collective-permute-start.1 = (bf16[528,512]{1,0:T(8,128)(2,1)}, bf16[528,512]{1,0:T(8,128)(2,1)S(1)}, u32[]{:S(2)}, u32[]{:S(2)}) collective-permute-start(bf16[528,512]{1,0:T(8,128)(2,1)} %get-tuple-element.33.q), channel_id=1, source_target_pairs={{8,0},{12,4},{16,8},{20,12},{24,16},{28,20},{32,24},{36,28},{40,32... | collective-permute-start | bytes 1622024 | tf_op jit(solution)/shard_map/ppermute | solution.py:354
  23.8 1.9 %collective-permute-start.2 = (bf16[768,512]{1,0:T(8,128)(2,1)S(1)}, bf16[768,512]{1,0:T(8,128)(2,1)S(1)}, u32[]{:S(2)}, u32[]{:S(2)}) collective-permute-start(bf16[768,512]{1,0:T(8,128)(2,1)S(1)} %get-tuple-element.34.tail), channel_id=1, source_target_pairs={{0,8},{4,12},{8,16},{12,20},{16,24},{20,28},{24,32},{28,36},{32,40... | collective-permute-start | bytes 2359304 | tf_op jit(solution)/shard_map/ppermute | solution.py:354
  25.7 3.1 %all-to-all-done.parts = bf16[64,16,128]{2,1,0:T(8,128)(2,1)} async-done(((bf16[64,16,128]{2,1,0:T(8,128)(2,1)}), bf16[64,16,128]{2,1,0:T(8,128)(2,1)}, u32[]{:S(2)}, u32[]{:S(2)}) %all-to-all-start) | async-done | bytes 262176 | tf_op jit(solution)/shard_map/all_to_all | solution.py:399
  28.9 0.0 copy-done.9
  28.9 1.8 %shard_map.123 = bf16[64,16,128]{2,1,0:T(8,128)(2,1)} custom-call(s32[1]{0:T(128)} %bitcast.index, f32[8]{0:T(128)S(1)} %copy-done.9, bf16[64,16,128]{2,1,0:T(8,128)(2,1)} %all-to-all-done.parts), custom_call_target="tpu_custom_call" | custom-call | flops 5000000000 | bytes 1 | tf_op jit(solution)/shard_map/pallas_call | solution.py:33
  30.7 6.7 %all-to-all-start.1 = ((bf16[64,16,128]{2,1,0:T(8,128)(2,1)}), bf16[64,16,128]{2,1,0:T(8,128)(2,1)S(1)}, u32[]{:S(2)}, u32[]{:S(2)}) async-start(bf16[64,16,128]{2,1,0:T(8,128)(2,1)} %shard_map.123), calls=%async_computation.1 | async-start | bytes 524288 | tf_op jit(solution)/shard_map/all_to_all | solution.py:426
  37.4 4.1 %shard_map.127 = (f32[256,1024]{1,0:T(8,128)}, f32[1024,128]{1,0:T(8,128)}, f32[8,128]{1,0:T(8,128)}) custom-call(f32[8]{0:T(128)} %rate.3, bf16[256,1024]{1,0:T(8,128)(2,1)} %q.5, bf16[256,1024]{1,0:T(8,128)(2,1)} %k.3, bf16[256,1024]{1,0:T(8,128)(2,1)} %v.3), custom_call_target="tpu_custom_call" | custom-call | flops 1 | bytes 1 | tf_op jit(solution)/shard_map/pallas_call | solution.py:33
  41.5 0.0 collective-permute-done.1.q
  41.5 0.6 copy-done.6
  42.2 2.2 %shard_map.125 = (f32[512,512]{1,0:T(8,128)S(1)}, f32[512,128]{1,0:T(8,128)S(1)}, f32[512,128]{1,0:T(8,128)S(1)}) custom-call(s32[1]{0:T(128)} %bitcast.index, s32[128]{0:T(128)S(1)} %copy-done.6, bf16[528,512]{1,0:T(8,128)(2,1)S(1)} %collective-permute-done.1.q, bf16[256,512]{1,0:T(8,128)(2,1)S(1)} %get-tuple-element.47.head, ...), custom_call_target="tpu_custom_call" | custom-call | flops 1 | bytes 1 | tf_op jit(solution)/shard_map/pallas_call | solution.py:33
  44.4 5.5 %collective-permute-done.2.tail = bf16[768,512]{1,0:T(8,128)(2,1)S(1)} collective-permute-done((bf16[768,512]{1,0:T(8,128)(2,1)S(1)}, bf16[768,512]{1,0:T(8,128)(2,1)S(1)}, u32[]{:S(2)}, u32[]{:S(2)}) %collective-permute-start.2) | collective-permute-done | bytes 786464 | tf_op jit(solution)/shard_map/ppermute | solution.py:354
  49.9 2.2 %shard_map.126 = bf16[560,512]{1,0:T(8,128)(2,1)S(1)} custom-call(s32[1]{0:T(128)} %bitcast.index, s32[128]{0:T(128)S(1)} %copy-done.6, bf16[528,512]{1,0:T(8,128)(2,1)S(1)} %collective-permute-done.1.q, bf16[768,512]{1,0:T(8,128)(2,1)S(1)} %collective-permute-done.2.tail, f32[512,512]{1,0:T(8,128)S(1)} %get-tuple-element.36.done, ...), custom_call_target="tpu_custom_call" | custom-call | flops 1 | bytes 1 | tf_op jit(solution)/shard_map/pallas_call | solution.py:33
  52.2 1.9 %collective-permute-start.3 = (bf16[560,512]{1,0:T(8,128)(2,1)S(1)}, bf16[560,512]{1,0:T(8,128)(2,1)S(1)}, u32[]{:S(2)}, u32[]{:S(2)}) collective-permute-start(bf16[560,512]{1,0:T(8,128)(2,1)S(1)} %shard_map.126), channel_id=1, source_target_pairs={{0,8},{4,12},{8,16},{12,20},{16,24},{20,28},{24,32},{28,36},{32,40... | collective-permute-start | bytes 1720328 | tf_op jit(solution)/shard_map/ppermute | solution.py:354
  54.1 0.0 all-to-all-done.1
  54.1 0.0 copy-start.10
  54.1 0.7 copy-done.10
  54.8 3.0 %shard_map.128 = (f32[256,1024]{1,0:T(8,128)}, f32[8,256]{1,0:T(8,128)}) custom-call(f32[8,128]{1,0:T(8,128)} %get-tuple-element.39.rates, f32[256,1024]{1,0:T(8,128)} %get-tuple-element.40.inner, bf16[256,1024]{1,0:T(8,128)(2,1)} %q.5, f32[1024,128]{1,0:T(8,128)} %get-tuple-element.41.first, bf16[1024,128]{1,0:T(8,128)(2,1)} %bitcast.5), custom_call_target="tpu_custom_call" | custom-call | flops 10000000000 | bytes 1 | tf_op jit(solution)/shard_map/pallas_call | solution.py:33
  57.8 0.2 collective-permute-start.6
  58.0 2.1 %collective-permute-start.5 = (f32[8,256]{1,0:T(8,128)}, f32[8,256]{1,0:T(8,128)S(1)}, u32[]{:S(2)}, u32[]{:S(2)}) collective-permute-start(f32[8,256]{1,0:T(8,128)} %get-tuple-element.46.s0), channel_id=1, source_target_pairs={{0,2},{1,3},{2,0},{3,1},{4,6},{5,7},{6,4},{7,5},{8,10},{9,11},{10,... | collective-permute-start | bytes 24584 | tf_op jit(solution)/shard_map/ppermute | solution.py:362
  60.2 1.5 %collective-permute-start.4 = (f32[8,256]{1,0:T(8,128)}, f32[8,256]{1,0:T(8,128)S(1)}, u32[]{:S(2)}, u32[]{:S(2)}) collective-permute-start(f32[8,256]{1,0:T(8,128)} %get-tuple-element.46.s0), channel_id=1, source_target_pairs={{0,1},{1,2},{2,3},{3,0},{4,5},{5,6},{6,7},{7,4},{8,9},{9,10},{10,1... | collective-permute-start | bytes 24584 | tf_op jit(solution)/shard_map/ppermute | solution.py:362
  61.7 2.5 %shard_map.129 = (f32[512,512]{1,0:T(8,128)S(1)}, f32[512,128]{1,0:T(8,128)S(1)}, f32[512,128]{1,0:T(8,128)S(1)}) custom-call(s32[1]{0:T(128)} %bitcast.index, s32[128]{0:T(128)S(1)} %copy-done.6, bf16[528,512]{1,0:T(8,128)(2,1)} %get-tuple-element.33.q, bf16[256,512]{1,0:T(8,128)(2,1)S(1)} %get-tuple-element.47.head, ...), custom_call_target="tpu_custom_call" | custom-call | flops 1 | bytes 1 | tf_op jit(solution)/shard_map/pallas_call | solution.py:33
  64.2 4.1 %collective-permute-done.3.far = bf16[560,512]{1,0:T(8,128)(2,1)S(1)} collective-permute-done((bf16[560,512]{1,0:T(8,128)(2,1)S(1)}, bf16[560,512]{1,0:T(8,128)(2,1)S(1)}, u32[]{:S(2)}, u32[]{:S(2)}) %collective-permute-start.3) | collective-permute-done | bytes 573472 | tf_op jit(solution)/shard_map/ppermute | solution.py:354
  68.3 0.7 shard_map.130
  69.0 0.0 collective-permute-done.6.s3
  69.0 0.0 collective-permute-done.5.s2
  69.0 0.0 collective-permute-done.4.s1
  69.0 3.3 %collective-permute-start.7 = (bf16[256,512]{1,0:T(8,128)(2,1)S(1)}, bf16[256,512]{1,0:T(8,128)(2,1)S(1)}, u32[]{:S(2)}, u32[]{:S(2)}) collective-permute-start(bf16[256,512]{1,0:T(8,128)(2,1)S(1)} %get-tuple-element.57), channel_id=1, source_target_pairs={{0,4},{4,0},{8,12},{12,8},{16,20},{20,16},{24,28},{28,24},{32,36},... | collective-permute-start | bytes 786440 | tf_op jit(solution)/shard_map/ppermute | solution.py:358
  72.4 0.0 copy-done.3
  72.4 0.0 copy-done.4
  72.4 0.0 copy-done.5
  72.4 0.0 copy-done.8
  72.4 1.3 %shard_map.131 = bf16[256,1024]{1,0:T(8,128)(2,1)} custom-call(f32[256,1024]{1,0:T(8,128)S(1)} %copy-done.3, bf16[256,1024]{1,0:T(8,128)(2,1)S(1)} %copy-done.4, f32[1,1024]{1,0:T(1,128)S(1)} %bitcast.4, f32[8,256]{1,0:T(8,128)S(1)} %copy-done.5, f32[8,256]{1,0:T(8,128)S(1)} %collective-permute-done.4.s1, f32[8,256]{1,0:T(8,128)S(1)} %collective-permute-done.5.s2, ...), custom_call_target="tpu_custom_call" | custom-call | flops 1 | bytes 1 | tf_op jit(solution)/shard_map/pallas_call | solution.py:33
  73.7 0.0 collective-permute-done.7.other
  73.7 0.8 %shard_map.132 = bf16[256,1024]{1,0:T(8,128)(2,1)} custom-call(s32[1]{0:T(128)} %bitcast.index, bf16[256,512]{1,0:T(8,128)(2,1)S(1)} %get-tuple-element.56.mine, bf16[256,512]{1,0:T(8,128)(2,1)S(1)} %collective-permute-done.7.other), custom_call_target="tpu_custom_call" | custom-call | flops 1 | bytes 1 | tf_op jit(solution)/shard_map/pallas_call | solution.py:33
  (5 shorter events, 0.0 us)
Async XLA Ops:
  0.6 16.8 %copy-start.1 = (bf16[256,1024]{1,0:T(8,128)(2,1)S(1)}, bf16[256,1024]{1,0:T(8,128)(2,1)}, u32[]{:S(2)}) copy-start(bf16[256,1024]{1,0:T(8,128)(2,1)} %k.2) | copy-start | bytes 1572868
  0.6 16.8 %copy-start.2 = (bf16[256,1024]{1,0:T(8,128)(2,1)S(1)}, bf16[256,1024]{1,0:T(8,128)(2,1)}, u32[]{:S(2)}) copy-start(bf16[256,1024]{1,0:T(8,128)(2,1)} %v.2) | copy-start | bytes 1572868
  4.5 13.0 %copy-start = (bf16[256,1024]{1,0:T(8,128)(2,1)S(1)}, bf16[256,1024]{1,0:T(8,128)(2,1)}, u32[]{:S(2)}) copy-start(bf16[256,1024]{1,0:T(8,128)(2,1)} %q.3) | copy-start | bytes 1572868
  4.5 12.9 %collective-permute-start = (bf16[784,512]{1,0:T(8,128)(2,1)}, bf16[784,512]{1,0:T(8,128)(2,1)S(1)}, u32[]{:S(2)}, u32[]{:S(2)}) collective-permute-start(bf16[784,512]{1,0:T(8,128)(2,1)} %get-tuple-element.32), channel_id=1, source_target_pairs={{0,4},{4,0},{8,12},{12,8},{16,20},{20,16},{24,28},{28,24},{32,36},... | collective-permute-start | bytes 2408456 | tf_op jit(solution)/shard_map/ppermute | solution.py:358
  5.2 12.2 %copy-start.7 = (s32[2,128]{1,0:T(2,128)S(1)}, s32[2,128]{1,0:T(2,128)}, u32[]{:S(2)}) copy-start(s32[2,128]{1,0:T(2,128)} %mask.3) | copy-start | bytes 3076
  5.2 23.6 %all-to-all-start = ((bf16[64,16,128]{2,1,0:T(8,128)(2,1)}), bf16[64,16,128]{2,1,0:T(8,128)(2,1)}, u32[]{:S(2)}, u32[]{:S(2)}) async-start(bf16[64,16,128]{2,1,0:T(8,128)(2,1)} %bitcast.6), calls=%async_computation | async-start | bytes 524288 | tf_op jit(solution)/shard_map/all_to_all | solution.py:399
  19.2 9.7 %copy-start.9 = (f32[8]{0:T(128)S(1)}, f32[8]{0:T(128)}, u32[]{:S(2)}) copy-start(f32[8]{0:T(128)} %rate.3) | copy-start | bytes 100
  19.2 22.3 %collective-permute-start.1 = (bf16[528,512]{1,0:T(8,128)(2,1)}, bf16[528,512]{1,0:T(8,128)(2,1)S(1)}, u32[]{:S(2)}, u32[]{:S(2)}) collective-permute-start(bf16[528,512]{1,0:T(8,128)(2,1)} %get-tuple-element.33.q), channel_id=1, source_target_pairs={{8,0},{12,4},{16,8},{20,12},{24,16},{28,20},{32,24},{36,28},{40,32... | collective-permute-start | bytes 1622024 | tf_op jit(solution)/shard_map/ppermute | solution.py:354
  23.8 26.1 %collective-permute-start.2 = (bf16[768,512]{1,0:T(8,128)(2,1)S(1)}, bf16[768,512]{1,0:T(8,128)(2,1)S(1)}, u32[]{:S(2)}, u32[]{:S(2)}) collective-permute-start(bf16[768,512]{1,0:T(8,128)(2,1)S(1)} %get-tuple-element.34.tail), channel_id=1, source_target_pairs={{0,8},{4,12},{8,16},{12,20},{16,24},{20,28},{24,32},{28,36},{32,40... | collective-permute-start | bytes 2359304 | tf_op jit(solution)/shard_map/ppermute | solution.py:354
  30.7 23.4 %all-to-all-start.1 = ((bf16[64,16,128]{2,1,0:T(8,128)(2,1)}), bf16[64,16,128]{2,1,0:T(8,128)(2,1)S(1)}, u32[]{:S(2)}, u32[]{:S(2)}) async-start(bf16[64,16,128]{2,1,0:T(8,128)(2,1)} %shard_map.123), calls=%async_computation.1 | async-start | bytes 524288 | tf_op jit(solution)/shard_map/all_to_all | solution.py:426
  41.5 0.7 copy-start.6
  52.2 16.2 %collective-permute-start.3 = (bf16[560,512]{1,0:T(8,128)(2,1)S(1)}, bf16[560,512]{1,0:T(8,128)(2,1)S(1)}, u32[]{:S(2)}, u32[]{:S(2)}) collective-permute-start(bf16[560,512]{1,0:T(8,128)(2,1)S(1)} %shard_map.126), channel_id=1, source_target_pairs={{0,8},{4,12},{8,16},{12,20},{16,24},{20,28},{24,32},{28,36},{32,40... | collective-permute-start | bytes 1720328 | tf_op jit(solution)/shard_map/ppermute | solution.py:354
  54.1 0.7 copy-start.10
  57.8 11.2 %collective-permute-start.6 = (f32[8,256]{1,0:T(8,128)}, f32[8,256]{1,0:T(8,128)S(1)}, u32[]{:S(2)}, u32[]{:S(2)}) collective-permute-start(f32[8,256]{1,0:T(8,128)} %get-tuple-element.46.s0), channel_id=1, source_target_pairs={{0,3},{1,0},{2,1},{3,2},{4,7},{5,4},{6,5},{7,6},{8,11},{9,8},{10,9... | collective-permute-start | bytes 24584 | tf_op jit(solution)/shard_map/ppermute | solution.py:362
  58.0 11.0 %collective-permute-start.5 = (f32[8,256]{1,0:T(8,128)}, f32[8,256]{1,0:T(8,128)S(1)}, u32[]{:S(2)}, u32[]{:S(2)}) collective-permute-start(f32[8,256]{1,0:T(8,128)} %get-tuple-element.46.s0), channel_id=1, source_target_pairs={{0,2},{1,3},{2,0},{3,1},{4,6},{5,7},{6,4},{7,5},{8,10},{9,11},{10,... | collective-permute-start | bytes 24584 | tf_op jit(solution)/shard_map/ppermute | solution.py:362
  60.2 8.8 %collective-permute-start.4 = (f32[8,256]{1,0:T(8,128)}, f32[8,256]{1,0:T(8,128)S(1)}, u32[]{:S(2)}, u32[]{:S(2)}) collective-permute-start(f32[8,256]{1,0:T(8,128)} %get-tuple-element.46.s0), channel_id=1, source_target_pairs={{0,1},{1,2},{2,3},{3,0},{4,5},{5,6},{6,7},{7,4},{8,9},{9,10},{10,1... | collective-permute-start | bytes 24584 | tf_op jit(solution)/shard_map/ppermute | solution.py:362
  68.3 4.0 %copy-start.3 = (f32[256,1024]{1,0:T(8,128)S(1)}, f32[256,1024]{1,0:T(8,128)}, u32[]{:S(2)}) copy-start(f32[256,1024]{1,0:T(8,128)} %get-tuple-element.45.heads) | copy-start | bytes 3145732
  68.3 4.0 %copy-start.4 = (bf16[256,1024]{1,0:T(8,128)(2,1)S(1)}, bf16[256,1024]{1,0:T(8,128)(2,1)}, u32[]{:S(2)}) copy-start(bf16[256,1024]{1,0:T(8,128)(2,1)} %gate.1) | copy-start | bytes 1572868
  68.3 4.0 %copy-start.5 = (f32[8,256]{1,0:T(8,128)S(1)}, f32[8,256]{1,0:T(8,128)}, u32[]{:S(2)}) copy-start(f32[8,256]{1,0:T(8,128)} %get-tuple-element.46.s0) | copy-start | bytes 24580
  68.3 4.0 %copy-start.8 = (f32[1024]{0:T(1024)S(1)}, f32[1024]{0:T(1024)}, u32[]{:S(2)}) copy-start(f32[1024]{0:T(1024)} %param.15) | copy-start | bytes 12292
  69.0 4.6 %collective-permute-start.7 = (bf16[256,512]{1,0:T(8,128)(2,1)S(1)}, bf16[256,512]{1,0:T(8,128)(2,1)S(1)}, u32[]{:S(2)}, u32[]{:S(2)}) collective-permute-start(bf16[256,512]{1,0:T(8,128)(2,1)S(1)} %get-tuple-element.57), channel_id=1, source_target_pairs={{0,4},{4,0},{8,12},{12,8},{16,20},{20,16},{24,28},{28,24},{32,36},... | collective-permute-start | bytes 786440 | tf_op jit(solution)/shard_map/ppermute | solution.py:358

commit v7 on v6

--- a/solution.py
+++ b/solution.py
@@ -18,7 +18,7 @@
 D = 4096
 SHARDS = 64
 FILL = -1e30
-PREFIX_COST = 5_000_000_000
+PREFIX_COST = 1_500_000_000
 CARRY_COST = 10_000_000_000
 EXP2_SCALE = HD ** (-0.5) * math.log2(math.e)
 

time: 75 us -> 69.9 us (0.932)
  the two profiles are of different devices: /device:TPU:27 before, /device:TPU:15 now
where the time goes in v7:
time: 69.9 us; the launch traced here: 69.4 us
  starting transfers between devices  34.8 us (50%)
  Pallas kernels  24.2 us (35%)
  waiting for transfers between devices  8.28 us (12%)
  local copies, waits for them, and re-layouts  1.39 us (2%)
  between operations  0.85 us (1%)
    pallas_call x11, Pallas kernels, call(): pl.pallas_call(body, out_shape=outs, in_specs=specs, out_specs=outs_at or...  24.2 us
    all_to_all x1, starting transfers between devices, per_device(): parts = lax.all_to_all(state.reshape(SHARDS, 16, HD), 'seq', 0, 0)  12.2 us
    ppermute x3, starting transfers between devices, shifted(): lax.ppermute(x, 'seq', [(i, i + distance) for i in range(SHARDS) if 0 <=...  10.5 us
    all_to_all x1, starting transfers between devices, per_device(): entering = lax.all_to_all(prefix, 'seq', 0, 0).reshape(WIDTH, HD)  6.85 us
    ppermute x3, waiting for transfers between devices, shifted(): lax.ppermute(x, 'seq', [(i, i + distance) for i in range(SHARDS) if 0 <=...  5.72 us
    ppermute x3, starting transfers between devices, turned(): return lax.ppermute(x, 'head', [(i, (i + distance) % 4) for i in range(4)])  3.2 us
    all_to_all x1, waiting for transfers between devices, per_device(): parts = lax.all_to_all(state.reshape(SHARDS, 16, HD), 'seq', 0, 0)  2.55 us
    ppermute x2, starting transfers between devices, swapped(): return lax.ppermute(x, 'seq', [(i, i ^ 1) for i in range(SHARDS)])  2.04 us
  transfers between devices with their start and end apart: 10, of which 2 were waited for; matrix products, arithmetic and copies ran while one was open for 0% of the time, Pallas kernels for 28%

profile of v7, /device:TPU:15, one launch (start us, length us, event | category | flops | bytes accessed | tf_op | source)
XLA Modules:
  0.0 69.4 jit_solution(280156872820692001)
XLA Ops:
  0.6 0.0 copy-start.1
  0.6 0.0 copy-start.2
  0.7 3.8 %shard_map.122 = (bf16[1024,128]{1,0:T(8,128)(2,1)}, bf16[784,512]{1,0:T(8,128)(2,1)}) custom-call(s32[1]{0:T(128)} %bitcast.index, f32[8]{0:T(128)} %rate.3, s32[2,128]{1,0:T(2,128)} %mask.3, bf16[256,1024]{1,0:T(8,128)(2,1)} %k.3, bf16[256,1024]{1,0:T(8,128)(2,1)} %v.3, bf16[256,1024]{1,0:T(8,128)(2,1)} %q.3, bf16[256,1024]{1,0:T(8,128)(2,1)} %k.2, ...), custom_call_target="tpu_custom_call" | custom-call | flops 1 | bytes 1 | tf_op jit(solution)/shard_map/pallas_call | solution.py:33
  4.5 0.0 copy-start
  4.5 0.8 %collective-permute-start = (bf16[784,512]{1,0:T(8,128)(2,1)}, bf16[784,512]{1,0:T(8,128)(2,1)S(1)}, u32[]{:S(2)}, u32[]{:S(2)}) collective-permute-start(bf16[784,512]{1,0:T(8,128)(2,1)} %get-tuple-element.32), channel_id=1, source_target_pairs={{0,4},{4,0},{8,12},{12,8},{16,20},{20,16},{24,28},{28,24},{32,36},... | collective-permute-start | bytes 2408456 | tf_op jit(solution)/shard_map/ppermute | solution.py:358
  5.2 0.0 copy-start.7
  5.2 12.2 %all-to-all-start = ((bf16[64,16,128]{2,1,0:T(8,128)(2,1)}), bf16[64,16,128]{2,1,0:T(8,128)(2,1)}, u32[]{:S(2)}, u32[]{:S(2)}) async-start(bf16[64,16,128]{2,1,0:T(8,128)(2,1)} %bitcast.6), calls=%async_computation | async-start | bytes 524288 | tf_op jit(solution)/shard_map/all_to_all | solution.py:399
  17.4 0.0 collective-permute-done.other
  17.4 0.0 copy-done.1
  17.4 0.0 copy-done.2
  17.4 0.0 copy-done
  17.5 0.0 copy-done.7
  17.5 1.7 %shard_map.124 = (bf16[528,512]{1,0:T(8,128)(2,1)}, bf16[256,512]{1,0:T(8,128)(2,1)S(1)}, bf16[768,512]{1,0:T(8,128)(2,1)S(1)}) custom-call(s32[1]{0:T(128)} %bitcast.index, s32[2,128]{1,0:T(2,128)S(1)} %copy-done.7, bf16[256,1024]{1,0:T(8,128)(2,1)S(1)} %copy-done, bf16[256,1024]{1,0:T(8,128)(2,1)S(1)} %copy-done.1, bf16[256,1024]{1,0:T(8,128)(2,1)S(1)} %copy-done.2, ...), custom_call_target="tpu_custom_call" | custom-call | flops 1 | bytes 1 | tf_op jit(solution)/shard_map/pallas_call | solution.py:33
  19.2 0.0 copy-start.9
  19.2 3.1 %collective-permute-start.2 = (bf16[768,512]{1,0:T(8,128)(2,1)S(1)}, bf16[768,512]{1,0:T(8,128)(2,1)S(1)}, u32[]{:S(2)}, u32[]{:S(2)}) collective-permute-start(bf16[768,512]{1,0:T(8,128)(2,1)S(1)} %get-tuple-element.34.tail), channel_id=1, source_target_pairs={{0,8},{4,12},{8,16},{12,20},{16,24},{20,28},{24,32},{28,36},{32,40... | collective-permute-start | bytes 2359304 | tf_op jit(solution)/shard_map/ppermute | solution.py:354
  22.3 4.3 %collective-permute-start.1 = (bf16[528,512]{1,0:T(8,128)(2,1)}, bf16[528,512]{1,0:T(8,128)(2,1)S(1)}, u32[]{:S(2)}, u32[]{:S(2)}) collective-permute-start(bf16[528,512]{1,0:T(8,128)(2,1)} %get-tuple-element.33.q), channel_id=1, source_target_pairs={{8,0},{12,4},{16,8},{20,12},{24,16},{28,20},{32,24},{36,28},{40,32... | collective-permute-start | bytes 1622024 | tf_op jit(solution)/shard_map/ppermute | solution.py:354
  26.6 2.6 %all-to-all-done.parts = bf16[64,16,128]{2,1,0:T(8,128)(2,1)} async-done(((bf16[64,16,128]{2,1,0:T(8,128)(2,1)}), bf16[64,16,128]{2,1,0:T(8,128)(2,1)}, u32[]{:S(2)}, u32[]{:S(2)}) %all-to-all-start) | async-done | bytes 262176 | tf_op jit(solution)/shard_map/all_to_all | solution.py:399
  29.2 0.0 copy-done.9
  29.2 1.8 %shard_map.123 = bf16[64,16,128]{2,1,0:T(8,128)(2,1)} custom-call(s32[1]{0:T(128)} %bitcast.index, f32[8]{0:T(128)S(1)} %copy-done.9, bf16[64,16,128]{2,1,0:T(8,128)(2,1)} %all-to-all-done.parts), custom_call_target="tpu_custom_call" | custom-call | flops 1500000000 | bytes 1 | tf_op jit(solution)/shard_map/pallas_call | solution.py:33
  31.0 6.8 %all-to-all-start.1 = ((bf16[64,16,128]{2,1,0:T(8,128)(2,1)}), bf16[64,16,128]{2,1,0:T(8,128)(2,1)S(1)}, u32[]{:S(2)}, u32[]{:S(2)}) async-start(bf16[64,16,128]{2,1,0:T(8,128)(2,1)} %shard_map.123), calls=%async_computation.1 | async-start | bytes 524288 | tf_op jit(solution)/shard_map/all_to_all | solution.py:426
  37.9 4.1 %shard_map.127 = (f32[256,1024]{1,0:T(8,128)}, f32[1024,128]{1,0:T(8,128)}, f32[8,128]{1,0:T(8,128)}) custom-call(f32[8]{0:T(128)} %rate.3, bf16[256,1024]{1,0:T(8,128)(2,1)} %q.5, bf16[256,1024]{1,0:T(8,128)(2,1)} %k.3, bf16[256,1024]{1,0:T(8,128)(2,1)} %v.3), custom_call_target="tpu_custom_call" | custom-call | flops 1 | bytes 1 | tf_op jit(solution)/shard_map/pallas_call | solution.py:33
  42.0 0.0 collective-permute-done.1.q
  42.0 0.6 copy-done.6
  42.6 2.2 %shard_map.125 = (f32[512,512]{1,0:T(8,128)S(1)}, f32[512,128]{1,0:T(8,128)S(1)}, f32[512,128]{1,0:T(8,128)S(1)}) custom-call(s32[1]{0:T(128)} %bitcast.index, s32[128]{0:T(128)S(1)} %copy-done.6, bf16[528,512]{1,0:T(8,128)(2,1)S(1)} %collective-permute-done.1.q, bf16[256,512]{1,0:T(8,128)(2,1)S(1)} %get-tuple-element.47.head, ...), custom_call_target="tpu_custom_call" | custom-call | flops 1 | bytes 1 | tf_op jit(solution)/shard_map/pallas_call | solution.py:33
  44.9 0.0 collective-permute-done.2.tail
  44.9 2.2 %shard_map.126 = bf16[560,512]{1,0:T(8,128)(2,1)S(1)} custom-call(s32[1]{0:T(128)} %bitcast.index, s32[128]{0:T(128)S(1)} %copy-done.6, bf16[528,512]{1,0:T(8,128)(2,1)S(1)} %collective-permute-done.1.q, bf16[768,512]{1,0:T(8,128)(2,1)S(1)} %collective-permute-done.2.tail, f32[512,512]{1,0:T(8,128)S(1)} %get-tuple-element.36.done, ...), custom_call_target="tpu_custom_call" | custom-call | flops 1 | bytes 1 | tf_op jit(solution)/shard_map/pallas_call | solution.py:33
  47.1 3.1 %collective-permute-start.3 = (bf16[560,512]{1,0:T(8,128)(2,1)S(1)}, bf16[560,512]{1,0:T(8,128)(2,1)S(1)}, u32[]{:S(2)}, u32[]{:S(2)}) collective-permute-start(bf16[560,512]{1,0:T(8,128)(2,1)S(1)} %shard_map.126), channel_id=1, source_target_pairs={{0,8},{4,12},{8,16},{12,20},{16,24},{20,28},{24,32},{28,36},{32,40... | collective-permute-start | bytes 1720328 | tf_op jit(solution)/shard_map/ppermute | solution.py:354
  50.2 0.0 all-to-all-done.1
  50.2 0.0 copy-start.10
  50.2 0.7 copy-done.10
  50.9 3.0 %shard_map.128 = (f32[256,1024]{1,0:T(8,128)}, f32[8,256]{1,0:T(8,128)}) custom-call(f32[8,128]{1,0:T(8,128)} %get-tuple-element.39.rates, f32[256,1024]{1,0:T(8,128)} %get-tuple-element.40.inner, bf16[256,1024]{1,0:T(8,128)(2,1)} %q.5, f32[1024,128]{1,0:T(8,128)} %get-tuple-element.41.first, bf16[1024,128]{1,0:T(8,128)(2,1)} %bitcast.5), custom_call_target="tpu_custom_call" | custom-call | flops 10000000000 | bytes 1 | tf_op jit(solution)/shard_map/pallas_call | solution.py:33
  53.9 0.6 collective-permute-start.6
  54.4 0.8 %collective-permute-start.5 = (f32[8,256]{1,0:T(8,128)}, f32[8,256]{1,0:T(8,128)S(1)}, u32[]{:S(2)}, u32[]{:S(2)}) collective-permute-start(f32[8,256]{1,0:T(8,128)} %get-tuple-element.46.s0), channel_id=1, source_target_pairs={{0,2},{1,3},{2,0},{3,1},{4,6},{5,7},{6,4},{7,5},{8,10},{9,11},{10,... | collective-permute-start | bytes 24584 | tf_op jit(solution)/shard_map/ppermute | solution.py:362
  55.3 1.8 %collective-permute-start.4 = (f32[8,256]{1,0:T(8,128)}, f32[8,256]{1,0:T(8,128)S(1)}, u32[]{:S(2)}, u32[]{:S(2)}) collective-permute-start(f32[8,256]{1,0:T(8,128)} %get-tuple-element.46.s0), channel_id=1, source_target_pairs={{0,1},{1,2},{2,3},{3,0},{4,5},{5,6},{6,7},{7,4},{8,9},{9,10},{10,1... | collective-permute-start | bytes 24584 | tf_op jit(solution)/shard_map/ppermute | solution.py:362
  57.1 2.5 %shard_map.129 = (f32[512,512]{1,0:T(8,128)S(1)}, f32[512,128]{1,0:T(8,128)S(1)}, f32[512,128]{1,0:T(8,128)S(1)}) custom-call(s32[1]{0:T(128)} %bitcast.index, s32[128]{0:T(128)S(1)} %copy-done.6, bf16[528,512]{1,0:T(8,128)(2,1)} %get-tuple-element.33.q, bf16[256,512]{1,0:T(8,128)(2,1)S(1)} %get-tuple-element.47.head, ...), custom_call_target="tpu_custom_call" | custom-call | flops 1 | bytes 1 | tf_op jit(solution)/shard_map/pallas_call | solution.py:33
  59.6 5.7 %collective-permute-done.3.far = bf16[560,512]{1,0:T(8,128)(2,1)S(1)} collective-permute-done((bf16[560,512]{1,0:T(8,128)(2,1)S(1)}, bf16[560,512]{1,0:T(8,128)(2,1)S(1)}, u32[]{:S(2)}, u32[]{:S(2)}) %collective-permute-start.3) | collective-permute-done | bytes 573472 | tf_op jit(solution)/shard_map/ppermute | solution.py:354
  65.3 0.7 shard_map.130
  66.0 0.0 collective-permute-done.6.s3
  66.0 0.0 collective-permute-done.5.s2
  66.0 0.0 collective-permute-done.4.s1
  66.0 1.3 %collective-permute-start.7 = (bf16[256,512]{1,0:T(8,128)(2,1)S(1)}, bf16[256,512]{1,0:T(8,128)(2,1)S(1)}, u32[]{:S(2)}, u32[]{:S(2)}) collective-permute-start(bf16[256,512]{1,0:T(8,128)(2,1)S(1)} %get-tuple-element.57), channel_id=1, source_target_pairs={{0,4},{4,0},{8,12},{12,8},{16,20},{20,16},{24,28},{28,24},{32,36},... | collective-permute-start | bytes 786440 | tf_op jit(solution)/shard_map/ppermute | solution.py:358
  67.3 0.0 copy-done.3
  67.3 0.0 copy-done.4
  67.3 0.0 copy-done.5
  67.3 0.0 copy-done.8
  67.3 1.3 %shard_map.131 = bf16[256,1024]{1,0:T(8,128)(2,1)} custom-call(f32[256,1024]{1,0:T(8,128)S(1)} %copy-done.3, bf16[256,1024]{1,0:T(8,128)(2,1)S(1)} %copy-done.4, f32[1,1024]{1,0:T(1,128)S(1)} %bitcast.4, f32[8,256]{1,0:T(8,128)S(1)} %copy-done.5, f32[8,256]{1,0:T(8,128)S(1)} %collective-permute-done.4.s1, f32[8,256]{1,0:T(8,128)S(1)} %collective-permute-done.5.s2, ...), custom_call_target="tpu_custom_call" | custom-call | flops 1 | bytes 1 | tf_op jit(solution)/shard_map/pallas_call | solution.py:33
  68.6 0.0 collective-permute-done.7.other
  68.6 0.8 %shard_map.132 = bf16[256,1024]{1,0:T(8,128)(2,1)} custom-call(s32[1]{0:T(128)} %bitcast.index, bf16[256,512]{1,0:T(8,128)(2,1)S(1)} %get-tuple-element.56.mine, bf16[256,512]{1,0:T(8,128)(2,1)S(1)} %collective-permute-done.7.other), custom_call_target="tpu_custom_call" | custom-call | flops 1 | bytes 1 | tf_op jit(solution)/shard_map/pallas_call | solution.py:33
  (5 shorter events, 0.0 us)
Async XLA Ops:
  0.6 16.8 %copy-start.1 = (bf16[256,1024]{1,0:T(8,128)(2,1)S(1)}, bf16[256,1024]{1,0:T(8,128)(2,1)}, u32[]{:S(2)}) copy-start(bf16[256,1024]{1,0:T(8,128)(2,1)} %k.2) | copy-start | bytes 1572868
  0.6 16.8 %copy-start.2 = (bf16[256,1024]{1,0:T(8,128)(2,1)S(1)}, bf16[256,1024]{1,0:T(8,128)(2,1)}, u32[]{:S(2)}) copy-start(bf16[256,1024]{1,0:T(8,128)(2,1)} %v.2) | copy-start | bytes 1572868
  4.5 13.0 %copy-start = (bf16[256,1024]{1,0:T(8,128)(2,1)S(1)}, bf16[256,1024]{1,0:T(8,128)(2,1)}, u32[]{:S(2)}) copy-start(bf16[256,1024]{1,0:T(8,128)(2,1)} %q.3) | copy-start | bytes 1572868
  4.5 13.0 %collective-permute-start = (bf16[784,512]{1,0:T(8,128)(2,1)}, bf16[784,512]{1,0:T(8,128)(2,1)S(1)}, u32[]{:S(2)}, u32[]{:S(2)}) collective-permute-start(bf16[784,512]{1,0:T(8,128)(2,1)} %get-tuple-element.32), channel_id=1, source_target_pairs={{0,4},{4,0},{8,12},{12,8},{16,20},{20,16},{24,28},{28,24},{32,36},... | collective-permute-start | bytes 2408456 | tf_op jit(solution)/shard_map/ppermute | solution.py:358
  5.2 12.2 %copy-start.7 = (s32[2,128]{1,0:T(2,128)S(1)}, s32[2,128]{1,0:T(2,128)}, u32[]{:S(2)}) copy-start(s32[2,128]{1,0:T(2,128)} %mask.3) | copy-start | bytes 3076
  5.2 24.0 %all-to-all-start = ((bf16[64,16,128]{2,1,0:T(8,128)(2,1)}), bf16[64,16,128]{2,1,0:T(8,128)(2,1)}, u32[]{:S(2)}, u32[]{:S(2)}) async-start(bf16[64,16,128]{2,1,0:T(8,128)(2,1)} %bitcast.6), calls=%async_computation | async-start | bytes 524288 | tf_op jit(solution)/shard_map/all_to_all | solution.py:399
  19.2 10.0 %copy-start.9 = (f32[8]{0:T(128)S(1)}, f32[8]{0:T(128)}, u32[]{:S(2)}) copy-start(f32[8]{0:T(128)} %rate.3) | copy-start | bytes 100
  19.2 25.6 %collective-permute-start.2 = (bf16[768,512]{1,0:T(8,128)(2,1)S(1)}, bf16[768,512]{1,0:T(8,128)(2,1)S(1)}, u32[]{:S(2)}, u32[]{:S(2)}) collective-permute-start(bf16[768,512]{1,0:T(8,128)(2,1)S(1)} %get-tuple-element.34.tail), channel_id=1, source_target_pairs={{0,8},{4,12},{8,16},{12,20},{16,24},{20,28},{24,32},{28,36},{32,40... | collective-permute-start | bytes 2359304 | tf_op jit(solution)/shard_map/ppermute | solution.py:354
  22.3 19.6 %collective-permute-start.1 = (bf16[528,512]{1,0:T(8,128)(2,1)}, bf16[528,512]{1,0:T(8,128)(2,1)S(1)}, u32[]{:S(2)}, u32[]{:S(2)}) collective-permute-start(bf16[528,512]{1,0:T(8,128)(2,1)} %get-tuple-element.33.q), channel_id=1, source_target_pairs={{8,0},{12,4},{16,8},{20,12},{24,16},{28,20},{32,24},{36,28},{40,32... | collective-permute-start | bytes 1622024 | tf_op jit(solution)/shard_map/ppermute | solution.py:354
  31.0 19.2 %all-to-all-start.1 = ((bf16[64,16,128]{2,1,0:T(8,128)(2,1)}), bf16[64,16,128]{2,1,0:T(8,128)(2,1)S(1)}, u32[]{:S(2)}, u32[]{:S(2)}) async-start(bf16[64,16,128]{2,1,0:T(8,128)(2,1)} %shard_map.123), calls=%async_computation.1 | async-start | bytes 524288 | tf_op jit(solution)/shard_map/all_to_all | solution.py:426
  42.0 0.7 copy-start.6
  47.1 18.2 %collective-permute-start.3 = (bf16[560,512]{1,0:T(8,128)(2,1)S(1)}, bf16[560,512]{1,0:T(8,128)(2,1)S(1)}, u32[]{:S(2)}, u32[]{:S(2)}) collective-permute-start(bf16[560,512]{1,0:T(8,128)(2,1)S(1)} %shard_map.126), channel_id=1, source_target_pairs={{0,8},{4,12},{8,16},{12,20},{16,24},{20,28},{24,32},{28,36},{32,40... | collective-permute-start | bytes 1720328 | tf_op jit(solution)/shard_map/ppermute | solution.py:354
  50.2 0.7 %copy-start.10 = (bf16[64,16,128]{2,1,0:T(8,128)(2,1)}, bf16[64,16,128]{2,1,0:T(8,128)(2,1)S(1)}, u32[]{:S(2)}) copy-start(bf16[64,16,128]{2,1,0:T(8,128)(2,1)S(1)} %all-to-all-done.1) | copy-start | bytes 786436
  53.9 12.1 %collective-permute-start.6 = (f32[8,256]{1,0:T(8,128)}, f32[8,256]{1,0:T(8,128)S(1)}, u32[]{:S(2)}, u32[]{:S(2)}) collective-permute-start(f32[8,256]{1,0:T(8,128)} %get-tuple-element.46.s0), channel_id=1, source_target_pairs={{0,3},{1,0},{2,1},{3,2},{4,7},{5,4},{6,5},{7,6},{8,11},{9,8},{10,9... | collective-permute-start | bytes 24584 | tf_op jit(solution)/shard_map/ppermute | solution.py:362
  54.4 11.6 %collective-permute-start.5 = (f32[8,256]{1,0:T(8,128)}, f32[8,256]{1,0:T(8,128)S(1)}, u32[]{:S(2)}, u32[]{:S(2)}) collective-permute-start(f32[8,256]{1,0:T(8,128)} %get-tuple-element.46.s0), channel_id=1, source_target_pairs={{0,2},{1,3},{2,0},{3,1},{4,6},{5,7},{6,4},{7,5},{8,10},{9,11},{10,... | collective-permute-start | bytes 24584 | tf_op jit(solution)/shard_map/ppermute | solution.py:362
  55.3 10.7 %collective-permute-start.4 = (f32[8,256]{1,0:T(8,128)}, f32[8,256]{1,0:T(8,128)S(1)}, u32[]{:S(2)}, u32[]{:S(2)}) collective-permute-start(f32[8,256]{1,0:T(8,128)} %get-tuple-element.46.s0), channel_id=1, source_target_pairs={{0,1},{1,2},{2,3},{3,0},{4,5},{5,6},{6,7},{7,4},{8,9},{9,10},{10,1... | collective-permute-start | bytes 24584 | tf_op jit(solution)/shard_map/ppermute | solution.py:362
  65.3 2.0 %copy-start.3 = (f32[256,1024]{1,0:T(8,128)S(1)}, f32[256,1024]{1,0:T(8,128)}, u32[]{:S(2)}) copy-start(f32[256,1024]{1,0:T(8,128)} %get-tuple-element.45.heads) | copy-start | bytes 3145732
  65.3 2.0 %copy-start.4 = (bf16[256,1024]{1,0:T(8,128)(2,1)S(1)}, bf16[256,1024]{1,0:T(8,128)(2,1)}, u32[]{:S(2)}) copy-start(bf16[256,1024]{1,0:T(8,128)(2,1)} %gate.1) | copy-start | bytes 1572868
  65.3 2.0 %copy-start.5 = (f32[8,256]{1,0:T(8,128)S(1)}, f32[8,256]{1,0:T(8,128)}, u32[]{:S(2)}) copy-start(f32[8,256]{1,0:T(8,128)} %get-tuple-element.46.s0) | copy-start | bytes 24580
  65.3 2.0 %copy-start.8 = (f32[1024]{0:T(1024)S(1)}, f32[1024]{0:T(1024)}, u32[]{:S(2)}) copy-start(f32[1024]{0:T(1024)} %param.15) | copy-start | bytes 12292
  66.0 2.6 %collective-permute-start.7 = (bf16[256,512]{1,0:T(8,128)(2,1)S(1)}, bf16[256,512]{1,0:T(8,128)(2,1)S(1)}, u32[]{:S(2)}, u32[]{:S(2)}) collective-permute-start(bf16[256,512]{1,0:T(8,128)(2,1)S(1)} %get-tuple-element.57), channel_id=1, source_target_pairs={{0,4},{4,0},{8,12},{12,8},{16,20},{20,16},{24,28},{28,24},{32,36},... | collective-permute-start | bytes 786440 | tf_op jit(solution)/shard_map/ppermute | solution.py:358

commit v8 on v7

--- a/solution.py
+++ b/solution.py
@@ -29,10 +29,11 @@
 VMEM = pl.BlockSpec(memory_space=pltpu.VMEM)
 
 
-def call(body, outs, ins, specs, scratch=(), flops=1, outs_at=None):
+def call(body, outs, ins, specs, scratch=(), flops=1, outs_at=None, grid=()):
     return pl.pallas_call(
         body,
         out_shape=outs,
+        grid=grid,
         in_specs=specs,
         out_specs=outs_at or [VMEM] * len(outs),
         scratch_shapes=list(scratch),
@@ -58,7 +59,7 @@
 def block_state(rate, k, v, h, b):
     rows = slice(b * BLK, (b + 1) * BLK)
     back = (BLK - 1.0) - lax.broadcasted_iota(jnp.int32, (BLK, HD), 0).astype(f32)
-    decayed = (k[rows, cols(h)].astype(f32) * jnp.exp(-rate[h] * back)).astype(bf16)
+    decayed = (k[rows, cols(h)].astype(f32) * jnp.exp(-rate * back)).astype(bf16)
     return dot(decayed, v[rows, cols(h)], ((0,), (0,)))
 
 
@@ -89,7 +90,8 @@
         copies[2 * g + 2].wait()
         for h in (2 * g, 2 * g + 1):
             step = jnp.exp(jnp.full((HD, HD), -rate[h] * BLK, f32))
-            state = step * block_state(rate, k, v, h, 0) + block_state(rate, k, v, h, 1)
+            state = step * block_state(rate[h], k, v, h, 0)
+            state = state + block_state(rate[h], k, v, h, 1)
             out[cols(h), :] = state.astype(bf16)
     for copy in copies[LOCAL + 1 :]:
         copy.wait()
@@ -110,8 +112,10 @@
     gap = jnp.maximum(row - col, 0).astype(f32)
     for h in range(LOCAL):
         rates[h : h + 1, :] = jnp.full((1, HD), rate[h], f32)
-        first[cols(h), :] = block_state(rate, k, v, h, 0)
-        decay = jnp.where(row >= col, jnp.exp(-rate[h] * gap), 0.0)
+    for h in range(2):
+        own = rate[2 * pl.program_id(0) + h]
+        first[cols(h), :] = block_state(own, k, v, h, 0)
+        decay = jnp.where(row >= col, jnp.exp(-own * gap), 0.0)
         for b in range(2):
             rows = slice(b * BLK, (b + 1) * BLK)
             scores = dot(q[rows, cols(h)], k[rows, cols(h)], ((1,), (1,)))
@@ -120,11 +124,12 @@
             )
 
 
-def carry_body(rates, inner, q, first, state, heads, squares):
+def carry_body(rates, inner, q, first, state, heads, squares, total):
+    step = pl.program_id(0)
     ahead = lax.broadcasted_iota(jnp.int32, (BLK, HD), 0).astype(f32) + 1.0
-    totals = [jnp.zeros((BLK, HD), f32)] * 2
-    for h in range(LOCAL):
-        rate = rates[h : h + 1, :]
+    added = [jnp.zeros((BLK, HD), f32)] * 2
+    for h in range(2):
+        rate = rates[pl.ds(2 * step + h, 1), :]
         decay = jnp.exp(-rate * ahead)
         entering = state[cols(h), :]
         middle = (jnp.exp(-rate * BLK) * entering.astype(f32) + first[cols(h), :]).astype(bf16)
@@ -133,9 +138,20 @@
             carried = dot(q[rows, cols(h)], block_start, ((1,), (0,)))
             value = inner[rows, cols(h)] + carried * decay
             heads[rows, cols(h)] = value
-            totals[b] = totals[b] + value * value
-    total = jnp.concatenate(totals, axis=0)
-    squares[...] = exact_dot(jnp.ones((8, HD), f32), total, ((1,), (1,)))
+            added[b] = added[b] + value * value
+    both = jnp.concatenate(added, axis=0)
+
+    @pl.when(step == 0)
+    def _():
+        total[...] = both
+
+    @pl.when(step > 0)
+    def _():
+        total[...] = total[...] + both
+
+    @pl.when(step == LOCAL // 2 - 1)
+    def _():
+        squares[...] = exact_dot(jnp.ones((8, HD), f32), total[...], ((1,), (1,)))
 
 
 def norm_body(heads, gate, gain, s0, s1, s2, s3, out):
@@ -152,7 +168,7 @@
     return pl.ds(pl.multiple_of(c * HALF, HALF), HALF)
 
 
-def gather_body(index, mask, q, k, v, other, far_q, head, tail, theirs, packed, sems):
+def gather_body(index, docs, doc_row, mask, q, k, v, other, far_q, head, tail, theirs, packed, sems):
     core = index[0] % 2
 
     def put(source, target, at):
@@ -194,6 +210,14 @@
     first = jnp.where(core == 0, own, arrived)
     second = jnp.where(core == 0, arrived, own)
     rows = jnp.concatenate([first, second, jnp.zeros((12, NBLK), f32)], axis=0)
+    line = lax.broadcasted_iota(jnp.int32, (16, NBLK), 0)
+    lane = lax.broadcasted_iota(jnp.int32, (16, NBLK), 1)
+    query = 4 * (index[0] // 2)
+    document = jnp.full((16, NBLK), -1, jnp.int32)
+    for i in range(4):
+        document = jnp.where(line == i, docs[query + i], document)
+    reach = (doc_row[...] == document) & (lane < query + line)
+    rows = jnp.where(reach, rows, 0.0)
     packed[...] = jnp.concatenate([rows.astype(bf16)] * 4, axis=1)
     flags = put(packed, far_q.at[4 * BLK :, :], 9)
     flags.start()
@@ -207,13 +231,9 @@
     flags.wait()
 
 
-def allowed(docs, flags, i, query, key):
-    q_at = jnp.clip(query, 0, NBLK - 1)
-    k_at = jnp.clip(key, 0, NBLK - 1)
-    inside = (key >= 0) & (key < query) & (query < NBLK) & (docs[k_at] == docs[q_at])
+def allowed(flags, i, key):
     lane = lax.broadcasted_iota(jnp.int32, (1, NBLK), 1)
-    wanted = jnp.where(inside, k_at, -1)
-    ok = jnp.sum(jnp.where(lane == wanted, flags[i : i + 1, :], 0.0), axis=1, keepdims=True)
+    ok = jnp.sum(jnp.where(lane == key, flags[i : i + 1, :], 0.0), axis=1, keepdims=True)
     return jnp.broadcast_to(jnp.where(ok > 0.5, 0.0, FILL), (BLK, BLK))
 
 
@@ -230,7 +250,7 @@
     return both[:, :HD], top, both[:, HD:]
 
 
-def attend_chip(index, docs, ahead, q, head, tail, out, tops, sums, bias):
+def attend_chip(index, ahead, q, head, tail, out, tops, sums, bias):
     chip = index[0] // 2
     rows = q[4 * BLK :, :NBLK].astype(f32)
     for i in range(4):
@@ -242,9 +262,7 @@
             elif ahead == 0 and j > i:
                 bias[block(i), block(j)] = jnp.full((BLK, BLK), FILL, f32)
             else:
-                bias[block(i), block(j)] = allowed(
-                    docs, rows, i, 4 * (chip + ahead) + i, 4 * chip + j
-                )
+                bias[block(i), block(j)] = allowed(rows, i, 4 * chip + j)
     lane = lax.broadcasted_iota(jnp.int32, (2 * BLK, HD), 1)
     for r in range(2):
         part = slice(r * 2 * BLK, (r + 1) * 2 * BLK)
@@ -267,12 +285,12 @@
         sums[part, :] = sum_table
 
 
-def near_body(index, docs, q, head, tail, out, tops, sums, bias):
-    attend_chip(index, docs, 0, q, head, tail, out, tops, sums, bias)
-
-
-def next_body(index, docs, q, head, tail, out, tops, sums, bias):
-    attend_chip(index, docs, 1, q, head, tail, out, tops, sums, bias)
+def near_body(index, q, head, tail, out, tops, sums, bias):
+    attend_chip(index, 0, q, head, tail, out, tops, sums, bias)
+
+
+def next_body(index, q, head, tail, out, tops, sums, bias):
+    attend_chip(index, 1, q, head, tail, out, tops, sums, bias)
 
 
 def weighed(top1, sum1, top2, sum2):
@@ -282,14 +300,12 @@
     return top, part1 + part2, part2 / (part1 + part2)
 
 
-def far_body(index, docs, q, tail, done, tops, sums, out, bias):
+def far_body(index, q, tail, done, tops, sums, out, bias):
     chip = index[0] // 2
     flags = q[4 * BLK :, :NBLK].astype(f32)
     for i in range(3):
         for j in range(3):
-            bias[block(i), block(j)] = allowed(
-                docs, flags, i, 4 * (chip + 1) + i, 4 * (chip - 1) + 1 + j
-            )
+            bias[block(i), block(j)] = allowed(flags, i, 4 * (chip - 1) + 1 + j)
     rows = slice(0, 3 * BLK)
     rest = slice(3 * BLK, 4 * BLK)
     lane = lax.broadcasted_iota(jnp.int32, (3 * BLK, HD), 1)
@@ -404,8 +420,11 @@
             like((2 * BLK, HALF), bf16),
             like((6 * BLK, HALF), bf16),
         ],
-        (index, block_mask, soft_query, soft_key, soft_value, other),
-        [SMEM, VMEM] + [anywhere] * 4,
+        (
+            index, doc_ids, doc_ids.reshape(1, NBLK), block_mask,
+            soft_query, soft_key, soft_value, other,
+        ),
+        [SMEM, SMEM, VMEM, VMEM] + [anywhere] * 4,
         [
             pltpu.VMEM((16, NBLK), bf16),
             pltpu.VMEM((16, HALF), bf16),
@@ -422,27 +441,32 @@
         [SMEM, SMEM, VMEM],
         flops=PREFIX_COST,
     )
-    prefix, doc_ids = lax.optimization_barrier((prefix, doc_ids))
+    prefix, own_head = lax.optimization_barrier((prefix, own_head))
     entering = lax.all_to_all(prefix, "seq", 0, 0).reshape(WIDTH, HD)
+    pair_columns = pl.BlockSpec((ROWS, 2 * HD), lambda g: (0, g))
+    pair_rows = pl.BlockSpec((2 * HD, HD), lambda g: (g, 0))
+    whole_rates = pl.BlockSpec((LOCAL, HD), lambda g: (0, 0))
     inner, first, rates = call(
         inner_body,
         [wide, like((WIDTH, HD), f32), like((LOCAL, HD), f32)],
         (decay_rate, lin_query, lin_key, lin_value),
-        [SMEM, VMEM, VMEM, VMEM],
+        [SMEM] + [pair_columns] * 3,
+        outs_at=[pair_columns, pair_rows, whole_rates],
+        grid=(LOCAL // 2,),
     )
     tables = [like((4 * BLK, HALF), f32), like((4 * BLK, HD), f32), like((4 * BLK, HD), f32)]
     done, done_tops, done_sums = call(
         next_body,
         tables,
-        (index, doc_ids, next_q, own_head, own_tail),
-        [SMEM] * 2 + [VMEM] * 3,
+        (index, next_q, own_head, own_tail),
+        [SMEM] + [VMEM] * 3,
         [pltpu.VMEM((4 * BLK, 4 * BLK), f32)],
     )
     (far,) = call(
         far_body,
         [like((4 * BLK + 48, HALF), bf16)],
-        (index, doc_ids, next_q, tail, done, done_tops, done_sums),
-        [SMEM] * 2 + [VMEM] * 5,
+        (index, next_q, tail, done, done_tops, done_sums),
+        [SMEM] + [VMEM] * 5,
         [pltpu.VMEM((3 * BLK, 3 * BLK), f32)],
     )
     far = shifted(far, 2)
@@ -450,7 +474,10 @@
         carry_body,
         [wide, like((8, ROWS), f32)],
         (rates, inner, lin_query, first, entering),
-        [VMEM] * 5,
+        [whole_rates, pair_columns, pair_columns, pair_rows, pair_rows],
+        [pltpu.VMEM((ROWS, HD), f32)],
+        outs_at=[pair_columns, pl.BlockSpec((8, ROWS), lambda g: (0, 0))],
+        grid=(LOCAL // 2,),
         flops=CARRY_COST,
     )
     heads, own_head = lax.optimization_barrier((heads, own_head))
@@ -458,8 +485,8 @@
     near, tops, sums = call(
         near_body,
         tables,
-        (index, doc_ids, far_q, own_head, own_tail),
-        [SMEM] * 2 + [VMEM] * 3,
+        (index, far_q, own_head, own_tail),
+        [SMEM] + [VMEM] * 3,
         [pltpu.VMEM((4 * BLK, 4 * BLK), f32)],
     )
     far, heads = lax.optimization_barrier((far, heads))

time: 69.9 us -> 70.1 us (level)
  the two profiles are of different devices: /device:TPU:15 before, /device:TPU:1 now
where the time goes in v8:
time: 70.1 us; the launch traced here: 69.5 us
  starting transfers between devices  35.4 us (50%)
  Pallas kernels  25.6 us (37%)
  waiting for transfers between devices  6.32 us (9%)
  local copies, waits for them, and re-layouts  1.37 us (2%)
  between operations  0.87 us (1%)
    pallas_call x11, Pallas kernels, call(): pl.pallas_call(body, out_shape=outs, grid=grid, in_specs=specs, out_specs...  25.6 us
    all_to_all x1, starting transfers between devices, per_device(): parts = lax.all_to_all(state.reshape(SHARDS, 16, HD), 'seq', 0, 0)  10.3 us
    ppermute x3, starting transfers between devices, shifted(): lax.ppermute(x, 'seq', [(i, i + distance) for i in range(SHARDS) if 0 <=...  7.96 us
    all_to_all x1, starting transfers between devices, per_device(): entering = lax.all_to_all(prefix, 'seq', 0, 0).reshape(WIDTH, HD)  7.85 us
    ppermute x2, starting transfers between devices, swapped(): return lax.ppermute(x, 'seq', [(i, i ^ 1) for i in range(SHARDS)])  5.71 us
    all_to_all x1, waiting for transfers between devices, per_device(): parts = lax.all_to_all(state.reshape(SHARDS, 16, HD), 'seq', 0, 0)  4.31 us
    ppermute x3, starting transfers between devices, turned(): return lax.ppermute(x, 'head', [(i, (i + distance) % 4) for i in range(4)])  3.6 us
    all_to_all x1, waiting for transfers between devices, per_device(): entering = lax.all_to_all(prefix, 'seq', 0, 0).reshape(WIDTH, HD)  1.9 us
  transfers between devices with their start and end apart: 10, of which 3 were waited for; matrix products, arithmetic and copies ran while one was open for 0% of the time, Pallas kernels for 30%

profile of v8, /device:TPU:1, one launch (start us, length us, event | category | flops | bytes accessed | tf_op | source)
XLA Modules:
  0.0 69.5 jit_solution(14414867546486596147)
XLA Ops:
  0.6 0.0 copy-start.1
  0.6 0.0 copy-start.2
  0.7 3.8 %shard_map.122 = (bf16[1024,128]{1,0:T(8,128)(2,1)}, bf16[784,512]{1,0:T(8,128)(2,1)}) custom-call(s32[1]{0:T(128)} %bitcast.index, f32[8]{0:T(128)} %rate.3, s32[2,128]{1,0:T(2,128)} %mask.3, bf16[256,1024]{1,0:T(8,128)(2,1)} %k.3, bf16[256,1024]{1,0:T(8,128)(2,1)} %v.3, bf16[256,1024]{1,0:T(8,128)(2,1)} %q.3, bf16[256,1024]{1,0:T(8,128)(2,1)} %k.2, ...), custom_call_target="tpu_custom_call" | custom-call | flops 1 | bytes 1 | tf_op jit(solution)/shard_map/pallas_call | solution.py:33
  4.5 0.0 copy-start
  4.5 3.3 %collective-permute-start = (bf16[784,512]{1,0:T(8,128)(2,1)}, bf16[784,512]{1,0:T(8,128)(2,1)S(1)}, u32[]{:S(2)}, u32[]{:S(2)}) collective-permute-start(bf16[784,512]{1,0:T(8,128)(2,1)} %get-tuple-element.30), channel_id=1, source_target_pairs={{0,4},{4,0},{8,12},{12,8},{16,20},{20,16},{24,28},{28,24},{32,36},... | collective-permute-start | bytes 2408456 | tf_op jit(solution)/shard_map/ppermute | solution.py:374
  7.8 10.3 %all-to-all-start = ((bf16[64,16,128]{2,1,0:T(8,128)(2,1)}), bf16[64,16,128]{2,1,0:T(8,128)(2,1)}, u32[]{:S(2)}, u32[]{:S(2)}) async-start(bf16[64,16,128]{2,1,0:T(8,128)(2,1)} %bitcast.8), calls=%async_computation | async-start | bytes 524288 | tf_op jit(solution)/shard_map/all_to_all | solution.py:415
  18.1 0.0 copy-start.7
  18.1 0.0 copy-start.8
  18.1 0.0 collective-permute-done.other
  18.1 0.0 copy-done.1
  18.1 0.0 copy-done.2
  18.1 0.0 copy-done
  18.1 0.6 copy-done.7
  18.7 0.0 copy-done.8
  18.7 2.3 %shard_map.123 = (bf16[528,512]{1,0:T(8,128)(2,1)}, bf16[256,512]{1,0:T(8,128)(2,1)S(1)}, bf16[768,512]{1,0:T(8,128)(2,1)S(1)}) custom-call(s32[1]{0:T(128)} %bitcast.index, s32[128]{0:T(128)S(1)} %copy-done.8, s32[1,128]{1,0:T(1,128)S(1)} %bitcast.6, s32[2,128]{1,0:T(2,128)S(1)} %copy-done.7, bf16[256,1024]{1,0:T(8,128)(2,1)S(1)} %copy-done, ...), custom_call_target="tpu_custom_call" | custom-call | flops 1 | bytes 1 | tf_op jit(solution)/shard_map/pallas_call | solution.py:33
  21.0 0.0 copy-start.9
  21.1 3.3 %collective-permute-start.2 = (bf16[768,512]{1,0:T(8,128)(2,1)S(1)}, bf16[768,512]{1,0:T(8,128)(2,1)S(1)}, u32[]{:S(2)}, u32[]{:S(2)}) collective-permute-start(bf16[768,512]{1,0:T(8,128)(2,1)S(1)} %get-tuple-element.32.tail), channel_id=1, source_target_pairs={{0,8},{4,12},{8,16},{12,20},{16,24},{20,28},{24,32},{28,36},{32,40... | collective-permute-start | bytes 2359304 | tf_op jit(solution)/shard_map/ppermute | solution.py:370
  24.4 1.3 %collective-permute-start.1 = (bf16[528,512]{1,0:T(8,128)(2,1)}, bf16[528,512]{1,0:T(8,128)(2,1)S(1)}, u32[]{:S(2)}, u32[]{:S(2)}) collective-permute-start(bf16[528,512]{1,0:T(8,128)(2,1)} %get-tuple-element.31.q), channel_id=1, source_target_pairs={{8,0},{12,4},{16,8},{20,12},{24,16},{28,20},{32,24},{36,28},{40,32... | collective-permute-start | bytes 1622024 | tf_op jit(solution)/shard_map/ppermute | solution.py:370
  25.7 4.3 %all-to-all-done.parts = bf16[64,16,128]{2,1,0:T(8,128)(2,1)} async-done(((bf16[64,16,128]{2,1,0:T(8,128)(2,1)}), bf16[64,16,128]{2,1,0:T(8,128)(2,1)}, u32[]{:S(2)}, u32[]{:S(2)}) %all-to-all-start) | async-done | bytes 262176 | tf_op jit(solution)/shard_map/all_to_all | solution.py:415
  30.0 0.0 copy-done.9
  30.0 1.8 %shard_map.124 = bf16[64,16,128]{2,1,0:T(8,128)(2,1)} custom-call(s32[1]{0:T(128)} %bitcast.index, f32[8]{0:T(128)S(1)} %copy-done.9, bf16[64,16,128]{2,1,0:T(8,128)(2,1)} %all-to-all-done.parts), custom_call_target="tpu_custom_call" | custom-call | flops 1500000000 | bytes 1 | tf_op jit(solution)/shard_map/pallas_call | solution.py:33
  31.8 7.8 %all-to-all-start.1 = ((bf16[64,16,128]{2,1,0:T(8,128)(2,1)}), bf16[64,16,128]{2,1,0:T(8,128)(2,1)S(1)}, u32[]{:S(2)}, u32[]{:S(2)}) async-start(bf16[64,16,128]{2,1,0:T(8,128)(2,1)} %shard_map.124), calls=%async_computation.1 | async-start | bytes 524288 | tf_op jit(solution)/shard_map/all_to_all | solution.py:445
  39.7 4.9 %shard_map.127 = (f32[256,1024]{1,0:T(8,128)}, f32[1024,128]{1,0:T(8,128)}, f32[8,128]{1,0:T(8,128)}) custom-call(f32[8]{0:T(128)} %rate.3, bf16[256,1024]{1,0:T(8,128)(2,1)} %q.5, bf16[256,1024]{1,0:T(8,128)(2,1)} %k.3, bf16[256,1024]{1,0:T(8,128)(2,1)} %v.3), custom_call_target="tpu_custom_call" | custom-call | flops 1 | bytes 1 | tf_op jit(solution)/shard_map/pallas_call | solution.py:33
  44.6 0.0 collective-permute-done.1.q
  44.6 1.6 %shard_map.125 = (f32[512,512]{1,0:T(8,128)S(1)}, f32[512,128]{1,0:T(8,128)S(1)}, f32[512,128]{1,0:T(8,128)S(1)}) custom-call(s32[1]{0:T(128)} %bitcast.index, bf16[528,512]{1,0:T(8,128)(2,1)S(1)} %collective-permute-done.1.q, bf16[256,512]{1,0:T(8,128)(2,1)S(1)} %get-tuple-element.47.head, bf16[768,512]{1,0:T(8,128)(2,1)S(1)} %get-tuple-element.32.tail), custom_call_target="tpu_custom_call" | custom-call | flops 1 | bytes 1 | tf_op jit(solution)/shard_map/pallas_call | solution.py:33
  46.2 0.0 collective-permute-done.2.tail
  46.2 1.7 %shard_map.126 = bf16[560,512]{1,0:T(8,128)(2,1)S(1)} custom-call(s32[1]{0:T(128)} %bitcast.index, bf16[528,512]{1,0:T(8,128)(2,1)S(1)} %collective-permute-done.1.q, bf16[768,512]{1,0:T(8,128)(2,1)S(1)} %collective-permute-done.2.tail, f32[512,512]{1,0:T(8,128)S(1)} %get-tuple-element.36.done, f32[512,128]{1,0:T(8,128)S(1)} %get-tuple-element.37.tops, ...), custom_call_target="tpu_custom_call" | custom-call | flops 1 | bytes 1 | tf_op jit(solution)/shard_map/pallas_call | solution.py:33
  47.9 3.3 %collective-permute-start.3 = (bf16[560,512]{1,0:T(8,128)(2,1)S(1)}, bf16[560,512]{1,0:T(8,128)(2,1)S(1)}, u32[]{:S(2)}, u32[]{:S(2)}) collective-permute-start(bf16[560,512]{1,0:T(8,128)(2,1)S(1)} %shard_map.126), channel_id=1, source_target_pairs={{0,8},{4,12},{8,16},{12,20},{16,24},{20,28},{24,32},{28,36},{32,40... | collective-permute-start | bytes 1720328 | tf_op jit(solution)/shard_map/ppermute | solution.py:370
  51.2 1.9 %all-to-all-done.1 = bf16[64,16,128]{2,1,0:T(8,128)(2,1)S(1)} async-done(((bf16[64,16,128]{2,1,0:T(8,128)(2,1)}), bf16[64,16,128]{2,1,0:T(8,128)(2,1)S(1)}, u32[]{:S(2)}, u32[]{:S(2)}) %all-to-all-start.1) | async-done | bytes 262176 | tf_op jit(solution)/shard_map/all_to_all | solution.py:445
  53.1 0.7 %copy-done.10 = bf16[64,16,128]{2,1,0:T(8,128)(2,1)} copy-done((bf16[64,16,128]{2,1,0:T(8,128)(2,1)}, bf16[64,16,128]{2,1,0:T(8,128)(2,1)S(1)}, u32[]{:S(2)}) %copy-start.10) | copy-done | bytes 262168
  53.8 4.2 %shard_map.128 = (f32[256,1024]{1,0:T(8,128)}, f32[8,256]{1,0:T(8,128)}) custom-call(f32[8,128]{1,0:T(8,128)} %get-tuple-element.39.rates, f32[256,1024]{1,0:T(8,128)} %get-tuple-element.40.inner, bf16[256,1024]{1,0:T(8,128)(2,1)} %q.5, f32[1024,128]{1,0:T(8,128)} %get-tuple-element.41.first, bf16[1024,128]{1,0:T(8,128)(2,1)} %bitcast.7), custom_call_target="tpu_custom_call" | custom-call | flops 10000000000 | bytes 1 | tf_op jit(solution)/shard_map/pallas_call | solution.py:33
  58.0 2.5 %collective-permute-start.6 = (f32[8,256]{1,0:T(8,128)}, f32[8,256]{1,0:T(8,128)S(1)}, u32[]{:S(2)}, u32[]{:S(2)}) collective-permute-start(f32[8,256]{1,0:T(8,128)} %get-tuple-element.46.s0), channel_id=1, source_target_pairs={{0,3},{1,0},{2,1},{3,2},{4,7},{5,4},{6,5},{7,6},{8,11},{9,8},{10,9... | collective-permute-start | bytes 24584 | tf_op jit(solution)/shard_map/ppermute | solution.py:378
  60.5 0.5 collective-permute-start.5
  61.0 0.6 collective-permute-start.4
  61.7 2.5 %shard_map.129 = (f32[512,512]{1,0:T(8,128)S(1)}, f32[512,128]{1,0:T(8,128)S(1)}, f32[512,128]{1,0:T(8,128)S(1)}) custom-call(s32[1]{0:T(128)} %bitcast.index, bf16[528,512]{1,0:T(8,128)(2,1)} %get-tuple-element.31.q, bf16[256,512]{1,0:T(8,128)(2,1)S(1)} %get-tuple-element.47.head, bf16[768,512]{1,0:T(8,128)(2,1)S(1)} %get-tuple-element.32.tail), custom_call_target="tpu_custom_call" | custom-call | flops 1 | bytes 1 | tf_op jit(solution)/shard_map/pallas_call | solution.py:33
  64.2 0.0 collective-permute-done.3.far
  64.2 0.0 copy-start.3
  64.2 0.0 copy-start.4
  64.2 0.0 copy-start.6
  64.2 0.6 shard_map.130
  64.9 0.0 collective-permute-done.6.s3
  64.9 0.0 collective-permute-done.5.s2
  64.9 0.1 collective-permute-done.4.s1
  65.0 2.4 %collective-permute-start.7 = (bf16[256,512]{1,0:T(8,128)(2,1)S(1)}, bf16[256,512]{1,0:T(8,128)(2,1)S(1)}, u32[]{:S(2)}, u32[]{:S(2)}) collective-permute-start(bf16[256,512]{1,0:T(8,128)(2,1)S(1)} %get-tuple-element.57), channel_id=1, source_target_pairs={{0,4},{4,0},{8,12},{12,8},{16,20},{20,16},{24,28},{28,24},{32,36},... | collective-permute-start | bytes 786440 | tf_op jit(solution)/shard_map/ppermute | solution.py:374
  67.4 0.0 copy-done.5
  67.4 1.3 %shard_map.131 = bf16[256,1024]{1,0:T(8,128)(2,1)} custom-call(f32[256,1024]{1,0:T(8,128)S(1)} %copy-done.3, bf16[256,1024]{1,0:T(8,128)(2,1)S(1)} %copy-done.4, f32[1,1024]{1,0:T(1,128)S(1)} %bitcast.5, f32[8,256]{1,0:T(8,128)S(1)} %copy-done.5, f32[8,256]{1,0:T(8,128)S(1)} %collective-permute-done.4.s1, f32[8,256]{1,0:T(8,128)S(1)} %collective-permute-done.5.s2, ...), custom_call_target="tpu_custom_call" | custom-call | flops 1 | bytes 1 | tf_op jit(solution)/shard_map/pallas_call | solution.py:33
  68.7 0.0 collective-permute-done.7.other
  68.7 0.8 %shard_map.132 = bf16[256,1024]{1,0:T(8,128)(2,1)} custom-call(s32[1]{0:T(128)} %bitcast.index, bf16[256,512]{1,0:T(8,128)(2,1)S(1)} %get-tuple-element.56.mine, bf16[256,512]{1,0:T(8,128)(2,1)S(1)} %collective-permute-done.7.other), custom_call_target="tpu_custom_call" | custom-call | flops 1 | bytes 1 | tf_op jit(solution)/shard_map/pallas_call | solution.py:33
  (5 shorter events, 0.0 us)
Async XLA Ops:
  0.6 17.5 %copy-start.1 = (bf16[256,1024]{1,0:T(8,128)(2,1)S(1)}, bf16[256,1024]{1,0:T(8,128)(2,1)}, u32[]{:S(2)}) copy-start(bf16[256,1024]{1,0:T(8,128)(2,1)} %k.2) | copy-start | bytes 1572868
  0.6 17.5 %copy-start.2 = (bf16[256,1024]{1,0:T(8,128)(2,1)S(1)}, bf16[256,1024]{1,0:T(8,128)(2,1)}, u32[]{:S(2)}) copy-start(bf16[256,1024]{1,0:T(8,128)(2,1)} %v.2) | copy-start | bytes 1572868
  4.5 13.7 %copy-start = (bf16[256,1024]{1,0:T(8,128)(2,1)S(1)}, bf16[256,1024]{1,0:T(8,128)(2,1)}, u32[]{:S(2)}) copy-start(bf16[256,1024]{1,0:T(8,128)(2,1)} %q.3) | copy-start | bytes 1572868
  4.5 13.6 %collective-permute-start = (bf16[784,512]{1,0:T(8,128)(2,1)}, bf16[784,512]{1,0:T(8,128)(2,1)S(1)}, u32[]{:S(2)}, u32[]{:S(2)}) collective-permute-start(bf16[784,512]{1,0:T(8,128)(2,1)} %get-tuple-element.30), channel_id=1, source_target_pairs={{0,4},{4,0},{8,12},{12,8},{16,20},{20,16},{24,28},{28,24},{32,36},... | collective-permute-start | bytes 2408456 | tf_op jit(solution)/shard_map/ppermute | solution.py:374
  7.8 22.2 %all-to-all-start = ((bf16[64,16,128]{2,1,0:T(8,128)(2,1)}), bf16[64,16,128]{2,1,0:T(8,128)(2,1)}, u32[]{:S(2)}, u32[]{:S(2)}) async-start(bf16[64,16,128]{2,1,0:T(8,128)(2,1)} %bitcast.8), calls=%async_computation | async-start | bytes 524288 | tf_op jit(solution)/shard_map/all_to_all | solution.py:415
  18.1 0.7 copy-start.7
  18.1 0.7 copy-start.8
  21.0 9.0 %copy-start.9 = (f32[8]{0:T(128)S(1)}, f32[8]{0:T(128)}, u32[]{:S(2)}) copy-start(f32[8]{0:T(128)} %rate.3) | copy-start | bytes 100
  21.1 25.2 %collective-permute-start.2 = (bf16[768,512]{1,0:T(8,128)(2,1)S(1)}, bf16[768,512]{1,0:T(8,128)(2,1)S(1)}, u32[]{:S(2)}, u32[]{:S(2)}) collective-permute-start(bf16[768,512]{1,0:T(8,128)(2,1)S(1)} %get-tuple-element.32.tail), channel_id=1, source_target_pairs={{0,8},{4,12},{8,16},{12,20},{16,24},{20,28},{24,32},{28,36},{32,40... | collective-permute-start | bytes 2359304 | tf_op jit(solution)/shard_map/ppermute | solution.py:370
  24.4 20.2 %collective-permute-start.1 = (bf16[528,512]{1,0:T(8,128)(2,1)}, bf16[528,512]{1,0:T(8,128)(2,1)S(1)}, u32[]{:S(2)}, u32[]{:S(2)}) collective-permute-start(bf16[528,512]{1,0:T(8,128)(2,1)} %get-tuple-element.31.q), channel_id=1, source_target_pairs={{8,0},{12,4},{16,8},{20,12},{24,16},{28,20},{32,24},{36,28},{40,32... | collective-permute-start | bytes 1622024 | tf_op jit(solution)/shard_map/ppermute | solution.py:370
  31.8 21.3 %all-to-all-start.1 = ((bf16[64,16,128]{2,1,0:T(8,128)(2,1)}), bf16[64,16,128]{2,1,0:T(8,128)(2,1)S(1)}, u32[]{:S(2)}, u32[]{:S(2)}) async-start(bf16[64,16,128]{2,1,0:T(8,128)(2,1)} %shard_map.124), calls=%async_computation.1 | async-start | bytes 524288 | tf_op jit(solution)/shard_map/all_to_all | solution.py:445
  47.9 16.3 %collective-permute-start.3 = (bf16[560,512]{1,0:T(8,128)(2,1)S(1)}, bf16[560,512]{1,0:T(8,128)(2,1)S(1)}, u32[]{:S(2)}, u32[]{:S(2)}) collective-permute-start(bf16[560,512]{1,0:T(8,128)(2,1)S(1)} %shard_map.126), channel_id=1, source_target_pairs={{0,8},{4,12},{8,16},{12,20},{16,24},{20,28},{24,32},{28,36},{32,40... | collective-permute-start | bytes 1720328 | tf_op jit(solution)/shard_map/ppermute | solution.py:370
  53.1 0.7 %copy-start.10 = (bf16[64,16,128]{2,1,0:T(8,128)(2,1)}, bf16[64,16,128]{2,1,0:T(8,128)(2,1)S(1)}, u32[]{:S(2)}) copy-start(bf16[64,16,128]{2,1,0:T(8,128)(2,1)S(1)} %all-to-all-done.1) | copy-start | bytes 786436
  58.0 6.8 %collective-permute-start.6 = (f32[8,256]{1,0:T(8,128)}, f32[8,256]{1,0:T(8,128)S(1)}, u32[]{:S(2)}, u32[]{:S(2)}) collective-permute-start(f32[8,256]{1,0:T(8,128)} %get-tuple-element.46.s0), channel_id=1, source_target_pairs={{0,3},{1,0},{2,1},{3,2},{4,7},{5,4},{6,5},{7,6},{8,11},{9,8},{10,9... | collective-permute-start | bytes 24584 | tf_op jit(solution)/shard_map/ppermute | solution.py:378
  60.5 4.3 %collective-permute-start.5 = (f32[8,256]{1,0:T(8,128)}, f32[8,256]{1,0:T(8,128)S(1)}, u32[]{:S(2)}, u32[]{:S(2)}) collective-permute-start(f32[8,256]{1,0:T(8,128)} %get-tuple-element.46.s0), channel_id=1, source_target_pairs={{0,2},{1,3},{2,0},{3,1},{4,6},{5,7},{6,4},{7,5},{8,10},{9,11},{10,... | collective-permute-start | bytes 24584 | tf_op jit(solution)/shard_map/ppermute | solution.py:378
  61.0 3.9 %collective-permute-start.4 = (f32[8,256]{1,0:T(8,128)}, f32[8,256]{1,0:T(8,128)S(1)}, u32[]{:S(2)}, u32[]{:S(2)}) collective-permute-start(f32[8,256]{1,0:T(8,128)} %get-tuple-element.46.s0), channel_id=1, source_target_pairs={{0,1},{1,2},{2,3},{3,0},{4,5},{5,6},{6,7},{7,4},{8,9},{9,10},{10,1... | collective-permute-start | bytes 24584 | tf_op jit(solution)/shard_map/ppermute | solution.py:378
  64.2 3.2 %copy-start.3 = (f32[256,1024]{1,0:T(8,128)S(1)}, f32[256,1024]{1,0:T(8,128)}, u32[]{:S(2)}) copy-start(f32[256,1024]{1,0:T(8,128)} %get-tuple-element.45.heads) | copy-start | bytes 3145732
  64.2 3.2 %copy-start.4 = (bf16[256,1024]{1,0:T(8,128)(2,1)S(1)}, bf16[256,1024]{1,0:T(8,128)(2,1)}, u32[]{:S(2)}) copy-start(bf16[256,1024]{1,0:T(8,128)(2,1)} %gate.1) | copy-start | bytes 1572868
  64.2 3.2 %copy-start.5 = (f32[8,256]{1,0:T(8,128)S(1)}, f32[8,256]{1,0:T(8,128)}, u32[]{:S(2)}) copy-start(f32[8,256]{1,0:T(8,128)} %get-tuple-element.46.s0) | copy-start | bytes 24580
  64.2 3.2 %copy-start.6 = (f32[1024]{0:T(1024)S(1)}, f32[1024]{0:T(1024)}, u32[]{:S(2)}) copy-start(f32[1024]{0:T(1024)} %param.15) | copy-start | bytes 12292
  65.0 3.7 %collective-permute-start.7 = (bf16[256,512]{1,0:T(8,128)(2,1)S(1)}, bf16[256,512]{1,0:T(8,128)(2,1)S(1)}, u32[]{:S(2)}, u32[]{:S(2)}) collective-permute-start(bf16[256,512]{1,0:T(8,128)(2,1)S(1)} %get-tuple-element.57), channel_id=1, source_target_pairs={{0,4},{4,0},{8,12},{12,8},{16,20},{20,16},{24,28},{28,24},{32,36},... | collective-permute-start | bytes 786440 | tf_op jit(solution)/shard_map/ppermute | solution.py:374

commit v9 on v7

--- a/solution.py
+++ b/solution.py
@@ -29,12 +29,12 @@
 VMEM = pl.BlockSpec(memory_space=pltpu.VMEM)
 
 
-def call(body, outs, ins, specs, scratch=(), flops=1, outs_at=None):
+def call(body, outs, ins, specs, scratch=(), flops=1):
     return pl.pallas_call(
         body,
         out_shape=outs,
         in_specs=specs,
-        out_specs=outs_at or [VMEM] * len(outs),
+        out_specs=[VMEM] * len(outs),
         scratch_shapes=list(scratch),
         compiler_params=pltpu.CompilerParams(vmem_limit_bytes=(16 if body in SMALL else 60) * 1024 * 1024),
         cost_estimate=pl.CostEstimate(flops=flops, bytes_accessed=1, transcendentals=0),
@@ -58,12 +58,12 @@
 def block_state(rate, k, v, h, b):
     rows = slice(b * BLK, (b + 1) * BLK)
     back = (BLK - 1.0) - lax.broadcasted_iota(jnp.int32, (BLK, HD), 0).astype(f32)
-    decayed = (k[rows, cols(h)].astype(f32) * jnp.exp(-rate[h] * back)).astype(bf16)
+    decayed = (k[rows, cols(h)].astype(f32) * jnp.exp(-rate * back)).astype(bf16)
     return dot(decayed, v[rows, cols(h)], ((0,), (0,)))
 
 
 def start_body(
-    index, rate_hbm, mask, k_hbm, v_hbm, sq, sk, sv, out, sent, rate, k, v, packed, rate_sem, sems
+    index, docs, doc_row, rate_hbm, mask, k_hbm, v_hbm, sq, sk, sv, out, sent, own, rate, k, v, packed, rate_sem, sems
 ):
     other = 1 - index[0] % 2
     copies = [pltpu.make_async_copy(rate_hbm, rate, rate_sem)]
@@ -78,8 +78,15 @@
         )
     for copy in copies:
         copy.start()
-    flags = mask[...].astype(f32)
-    flags = jnp.concatenate([flags, jnp.zeros((14, NBLK), f32)], axis=0).astype(bf16)
+    line = lax.broadcasted_iota(jnp.int32, (2, NBLK), 0)
+    lane = lax.broadcasted_iota(jnp.int32, (2, NBLK), 1)
+    query = 2 * index[0]
+    document = jnp.where(line == 0, docs[query], docs[query + 1])
+    reach = (doc_row[...] == document) & (lane < query + line) & (mask[...] == 1)
+    flags = jnp.where(reach, 1.0, 0.0)
+    flags = jnp.concatenate([flags, jnp.zeros((14, NBLK), f32)], axis=0)
+    own[...] = flags
+    flags = flags.astype(bf16)
     packed[...] = jnp.concatenate([flags] * 4, axis=1)
     copies.append(pltpu.make_async_copy(packed, sent.at[3 * ROWS :, :], sems.at[LOCAL + 3]))
     copies[-1].start()
@@ -89,7 +96,8 @@
         copies[2 * g + 2].wait()
         for h in (2 * g, 2 * g + 1):
             step = jnp.exp(jnp.full((HD, HD), -rate[h] * BLK, f32))
-            state = step * block_state(rate, k, v, h, 0) + block_state(rate, k, v, h, 1)
+            state = step * block_state(rate[h], k, v, h, 0)
+            state = state + block_state(rate[h], k, v, h, 1)
             out[cols(h), :] = state.astype(bf16)
     for copy in copies[LOCAL + 1 :]:
         copy.wait()
@@ -110,7 +118,7 @@
     gap = jnp.maximum(row - col, 0).astype(f32)
     for h in range(LOCAL):
         rates[h : h + 1, :] = jnp.full((1, HD), rate[h], f32)
-        first[cols(h), :] = block_state(rate, k, v, h, 0)
+        first[cols(h), :] = block_state(rate[h], k, v, h, 0)
         decay = jnp.where(row >= col, jnp.exp(-rate[h] * gap), 0.0)
         for b in range(2):
             rows = slice(b * BLK, (b + 1) * BLK)
@@ -152,7 +160,7 @@
     return pl.ds(pl.multiple_of(c * HALF, HALF), HALF)
 
 
-def gather_body(index, mask, q, k, v, other, far_q, head, tail, theirs, packed, sems):
+def gather_body(index, flags_own, q, k, v, other, far_q, head, tail, theirs, packed, sems):
     core = index[0] % 2
 
     def put(source, target, at):
@@ -189,7 +197,7 @@
     fetch = put(other.at[3 * ROWS :, :NBLK], theirs, 8)
     fetch.start()
     fetch.wait()
-    own = mask[...].astype(f32)
+    own = flags_own[:2, :]
     arrived = theirs[...].astype(f32)[:2]
     first = jnp.where(core == 0, own, arrived)
     second = jnp.where(core == 0, arrived, own)
@@ -207,13 +215,9 @@
     flags.wait()
 
 
-def allowed(docs, flags, i, query, key):
-    q_at = jnp.clip(query, 0, NBLK - 1)
-    k_at = jnp.clip(key, 0, NBLK - 1)
-    inside = (key >= 0) & (key < query) & (query < NBLK) & (docs[k_at] == docs[q_at])
+def allowed(flags, i, key):
     lane = lax.broadcasted_iota(jnp.int32, (1, NBLK), 1)
-    wanted = jnp.where(inside, k_at, -1)
-    ok = jnp.sum(jnp.where(lane == wanted, flags[i : i + 1, :], 0.0), axis=1, keepdims=True)
+    ok = jnp.sum(jnp.where(lane == key, flags[i : i + 1, :], 0.0), axis=1, keepdims=True)
     return jnp.broadcast_to(jnp.where(ok > 0.5, 0.0, FILL), (BLK, BLK))
 
 
@@ -230,7 +234,7 @@
     return both[:, :HD], top, both[:, HD:]
 
 
-def attend_chip(index, docs, ahead, q, head, tail, out, tops, sums, bias):
+def attend_chip(index, ahead, q, head, tail, out, tops, sums, bias):
     chip = index[0] // 2
     rows = q[4 * BLK :, :NBLK].astype(f32)
     for i in range(4):
@@ -242,9 +246,7 @@
             elif ahead == 0 and j > i:
                 bias[block(i), block(j)] = jnp.full((BLK, BLK), FILL, f32)
             else:
-                bias[block(i), block(j)] = allowed(
-                    docs, rows, i, 4 * (chip + ahead) + i, 4 * chip + j
-                )
+                bias[block(i), block(j)] = allowed(rows, i, 4 * chip + j)
     lane = lax.broadcasted_iota(jnp.int32, (2 * BLK, HD), 1)
     for r in range(2):
         part = slice(r * 2 * BLK, (r + 1) * 2 * BLK)
@@ -267,12 +269,12 @@
         sums[part, :] = sum_table
 
 
-def near_body(index, docs, q, head, tail, out, tops, sums, bias):
-    attend_chip(index, docs, 0, q, head, tail, out, tops, sums, bias)
-
-
-def next_body(index, docs, q, head, tail, out, tops, sums, bias):
-    attend_chip(index, docs, 1, q, head, tail, out, tops, sums, bias)
+def near_body(index, q, head, tail, out, tops, sums, bias):
+    attend_chip(index, 0, q, head, tail, out, tops, sums, bias)
+
+
+def next_body(index, q, head, tail, out, tops, sums, bias):
+    attend_chip(index, 1, q, head, tail, out, tops, sums, bias)
 
 
 def weighed(top1, sum1, top2, sum2):
@@ -282,14 +284,12 @@
     return top, part1 + part2, part2 / (part1 + part2)
 
 
-def far_body(index, docs, q, tail, done, tops, sums, out, bias):
+def far_body(index, q, tail, done, tops, sums, out, bias):
     chip = index[0] // 2
     flags = q[4 * BLK :, :NBLK].astype(f32)
     for i in range(3):
         for j in range(3):
-            bias[block(i), block(j)] = allowed(
-                docs, flags, i, 4 * (chip + 1) + i, 4 * (chip - 1) + 1 + j
-            )
+            bias[block(i), block(j)] = allowed(flags, i, 4 * (chip - 1) + 1 + j)
     rows = slice(0, 3 * BLK)
     rest = slice(3 * BLK, 4 * BLK)
     lane = lax.broadcasted_iota(jnp.int32, (3 * BLK, HD), 1)
@@ -381,11 +381,14 @@
     narrow = like((ROWS, WIDTH), bf16)
 
     anywhere = pl.BlockSpec(memory_space=pl.ANY)
-    state, sent = call(
+    state, sent, own_flags = call(
         start_body,
-        [like((WIDTH, HD), bf16), like((3 * ROWS + 16, HALF), bf16)],
-        (index, decay_rate, block_mask, lin_key, lin_value, soft_query, soft_key, soft_value),
-        [SMEM, anywhere, VMEM] + [anywhere] * 5,
+        [like((WIDTH, HD), bf16), like((3 * ROWS + 16, HALF), bf16), like((16, NBLK), f32)],
+        (
+            index, doc_ids, doc_ids.reshape(1, NBLK), decay_rate, block_mask,
+            lin_key, lin_value, soft_query, soft_key, soft_value,
+        ),
+        [SMEM, SMEM, VMEM, anywhere, VMEM] + [anywhere] * 5,
         [
             pltpu.SMEM((LOCAL,), f32),
             pltpu.VMEM((ROWS, WIDTH), bf16),
@@ -404,7 +407,7 @@
             like((2 * BLK, HALF), bf16),
             like((6 * BLK, HALF), bf16),
         ],
-        (index, block_mask, soft_query, soft_key, soft_value, other),
+        (index, own_flags, soft_query, soft_key, soft_value, other),
         [SMEM, VMEM] + [anywhere] * 4,
         [
             pltpu.VMEM((16, NBLK), bf16),
@@ -422,30 +425,31 @@
         [SMEM, SMEM, VMEM],
         flops=PREFIX_COST,
     )
-    prefix, doc_ids = lax.optimization_barrier((prefix, doc_ids))
+    prefix, own_head = lax.optimization_barrier((prefix, own_head))
     entering = lax.all_to_all(prefix, "seq", 0, 0).reshape(WIDTH, HD)
+    tables = [like((4 * BLK, HALF), f32), like((4 * BLK, HD), f32), like((4 * BLK, HD), f32)]
+    done, done_tops, done_sums = call(
+        next_body,
+        tables,
+        (index, next_q, own_head, own_tail),
+        [SMEM] + [VMEM] * 3,
+        [pltpu.VMEM((4 * BLK, 4 * BLK), f32)],
+    )
+    (far,) = call(
+        far_body,
+        [like((4 * BLK + 48, HALF), bf16)],
+        (index, next_q, tail, done, done_tops, done_sums),
+        [SMEM] + [VMEM] * 5,
+        [pltpu.VMEM((3 * BLK, 3 * BLK), f32)],
+    )
+    far, lin_query = lax.optimization_barrier((far, lin_query))
+    far = shifted(far, 2)
     inner, first, rates = call(
         inner_body,
         [wide, like((WIDTH, HD), f32), like((LOCAL, HD), f32)],
         (decay_rate, lin_query, lin_key, lin_value),
-        [SMEM, VMEM, VMEM, VMEM],
-    )
-    tables = [like((4 * BLK, HALF), f32), like((4 * BLK, HD), f32), like((4 * BLK, HD), f32)]
-    done, done_tops, done_sums = call(
-        next_body,
-        tables,
-        (index, doc_ids, next_q, own_head, own_tail),
-        [SMEM] * 2 + [VMEM] * 3,
-        [pltpu.VMEM((4 * BLK, 4 * BLK), f32)],
-    )
-    (far,) = call(
-        far_body,
-        [like((4 * BLK + 48, HALF), bf16)],
-        (index, doc_ids, next_q, tail, done, done_tops, done_sums),
-        [SMEM] * 2 + [VMEM] * 5,
-        [pltpu.VMEM((3 * BLK, 3 * BLK), f32)],
-    )
-    far = shifted(far, 2)
+        [SMEM] + [VMEM] * 3,
+    )
     heads, squares = call(
         carry_body,
         [wide, like((8, ROWS), f32)],
@@ -458,8 +462,8 @@
     near, tops, sums = call(
         near_body,
         tables,
-        (index, doc_ids, far_q, own_head, own_tail),
-        [SMEM] * 2 + [VMEM] * 3,
+        (index, far_q, own_head, own_tail),
+        [SMEM] + [VMEM] * 3,
         [pltpu.VMEM((4 * BLK, 4 * BLK), f32)],
     )
     far, heads = lax.optimization_barrier((far, heads))

time: 69.9 us -> 69.6 us (level)
  the two profiles are of different devices: /device:TPU:15 before, /device:TPU:1 now
where the time goes in v9:
time: 69.6 us; the launch traced here: 68.2 us
  starting transfers between devices  36 us (52%)
  Pallas kernels  23 us (33%)
  waiting for transfers between devices  6.99 us (10%)
  local copies, waits for them, and re-layouts  1.44 us (2%)
  between operations  0.86 us (1%)
    pallas_call x11, Pallas kernels, call(): pl.pallas_call(body, out_shape=outs, in_specs=specs, out_specs=[VMEM] * l...  23 us
    all_to_all x1, starting transfers between devices, per_device(): parts = lax.all_to_all(state.reshape(SHARDS, 16, HD), 'seq', 0, 0)  10.3 us
    ppermute x3, starting transfers between devices, shifted(): lax.ppermute(x, 'seq', [(i, i + distance) for i in range(SHARDS) if 0 <=...  8.78 us
    all_to_all x1, starting transfers between devices, per_device(): entering = lax.all_to_all(prefix, 'seq', 0, 0).reshape(WIDTH, HD)  7.3 us
    ppermute x2, starting transfers between devices, swapped(): return lax.ppermute(x, 'seq', [(i, i ^ 1) for i in range(SHARDS)])  6.02 us
    all_to_all x1, waiting for transfers between devices, per_device(): parts = lax.all_to_all(state.reshape(SHARDS, 16, HD), 'seq', 0, 0)  4.86 us
    ppermute x3, starting transfers between devices, turned(): return lax.ppermute(x, 'head', [(i, (i + distance) % 4) for i in range(4)])  3.61 us
    unnamed x20, local copies, waits for them, and re-layouts  1.44 us
  transfers between devices with their start and end apart: 10, of which 5 were waited for; matrix products, arithmetic and copies ran while one was open for 0% of the time, Pallas kernels for 27%

profile of v9, /device:TPU:1, one launch (start us, length us, event | category | flops | bytes accessed | tf_op | source)
XLA Modules:
  0.0 68.2 jit_solution(5796614824782031074)
XLA Ops:
  0.6 0.0 copy-start.1
  0.6 0.0 copy-start.2
  0.7 3.8 %shard_map.122 = (bf16[1024,128]{1,0:T(8,128)(2,1)}, bf16[784,512]{1,0:T(8,128)(2,1)}, f32[16,128]{1,0:T(8,128)}) custom-call(s32[1]{0:T(128)} %bitcast.index, s32[128]{0:T(128)} %docs.1, s32[1,128]{1,0:T(1,128)} %bitcast.8, f32[8]{0:T(128)} %rate.3, s32[2,128]{1,0:T(2,128)} %mask.1, bf16[256,1024]{1,0:T(8,128)(2,1)} %k.3, bf16[256,1024]{1,0:T(8,128)(2,1)} %v.3, ...), custom_call_target="tpu_custom_call" | custom-call | flops 1 | bytes 1 | tf_op jit(solution)/shard_map/pallas_call | solution.py:33
  4.5 0.0 copy-start
  4.5 3.3 %collective-permute-start = (bf16[784,512]{1,0:T(8,128)(2,1)}, bf16[784,512]{1,0:T(8,128)(2,1)S(1)}, u32[]{:S(2)}, u32[]{:S(2)}) collective-permute-start(bf16[784,512]{1,0:T(8,128)(2,1)} %get-tuple-element.34), channel_id=1, source_target_pairs={{0,4},{4,0},{8,12},{12,8},{16,20},{20,16},{24,28},{28,24},{32,36},... | collective-permute-start | bytes 2408456 | tf_op jit(solution)/shard_map/ppermute | solution.py:358
  7.8 10.3 %all-to-all-start = ((bf16[64,16,128]{2,1,0:T(8,128)(2,1)}), bf16[64,16,128]{2,1,0:T(8,128)(2,1)}, u32[]{:S(2)}, u32[]{:S(2)}) async-start(bf16[64,16,128]{2,1,0:T(8,128)(2,1)} %bitcast.7), calls=%async_computation | async-start | bytes 524288 | tf_op jit(solution)/shard_map/all_to_all | solution.py:402
  18.1 0.0 collective-permute-done.other
  18.1 0.0 copy-done.1
  18.1 0.0 copy-done.2
  18.1 0.0 copy-done
  18.1 0.0 copy-start.6
  18.1 0.7 %copy-done.6 = f32[16,128]{1,0:T(8,128)S(1)} copy-done((f32[16,128]{1,0:T(8,128)S(1)}, f32[16,128]{1,0:T(8,128)}, u32[]{:S(2)}) %copy-start.6) | copy-done | bytes 8216
  18.8 1.7 %shard_map.123 = (bf16[528,512]{1,0:T(8,128)(2,1)}, bf16[256,512]{1,0:T(8,128)(2,1)S(1)}, bf16[768,512]{1,0:T(8,128)(2,1)S(1)}) custom-call(s32[1]{0:T(128)} %bitcast.index, f32[16,128]{1,0:T(8,128)S(1)} %copy-done.6, bf16[256,1024]{1,0:T(8,128)(2,1)S(1)} %copy-done, bf16[256,1024]{1,0:T(8,128)(2,1)S(1)} %copy-done.1, bf16[256,1024]{1,0:T(8,128)(2,1)S(1)} %copy-done.2, ...), custom_call_target="tpu_custom_call" | custom-call | flops 1 | bytes 1 | tf_op jit(solution)/shard_map/pallas_call | solution.py:33
  20.5 0.0 copy-start.8
  20.5 3.3 %collective-permute-start.2 = (bf16[768,512]{1,0:T(8,128)(2,1)S(1)}, bf16[768,512]{1,0:T(8,128)(2,1)S(1)}, u32[]{:S(2)}, u32[]{:S(2)}) collective-permute-start(bf16[768,512]{1,0:T(8,128)(2,1)S(1)} %get-tuple-element.36.tail), channel_id=1, source_target_pairs={{0,8},{4,12},{8,16},{12,20},{16,24},{20,28},{24,32},{28,36},{32,40... | collective-permute-start | bytes 2359304 | tf_op jit(solution)/shard_map/ppermute | solution.py:354
  23.9 1.3 %collective-permute-start.1 = (bf16[528,512]{1,0:T(8,128)(2,1)}, bf16[528,512]{1,0:T(8,128)(2,1)S(1)}, u32[]{:S(2)}, u32[]{:S(2)}) collective-permute-start(bf16[528,512]{1,0:T(8,128)(2,1)} %get-tuple-element.35.q), channel_id=1, source_target_pairs={{8,0},{12,4},{16,8},{20,12},{24,16},{28,20},{32,24},{36,28},{40,32... | collective-permute-start | bytes 1622024 | tf_op jit(solution)/shard_map/ppermute | solution.py:354
  25.2 4.9 %all-to-all-done.parts = bf16[64,16,128]{2,1,0:T(8,128)(2,1)} async-done(((bf16[64,16,128]{2,1,0:T(8,128)(2,1)}), bf16[64,16,128]{2,1,0:T(8,128)(2,1)}, u32[]{:S(2)}, u32[]{:S(2)}) %all-to-all-start) | async-done | bytes 262176 | tf_op jit(solution)/shard_map/all_to_all | solution.py:402
  30.0 0.0 copy-done.8
  30.0 1.8 %shard_map.124 = bf16[64,16,128]{2,1,0:T(8,128)(2,1)} custom-call(s32[1]{0:T(128)} %bitcast.index, f32[8]{0:T(128)S(1)} %copy-done.8, bf16[64,16,128]{2,1,0:T(8,128)(2,1)} %all-to-all-done.parts), custom_call_target="tpu_custom_call" | custom-call | flops 1500000000 | bytes 1 | tf_op jit(solution)/shard_map/pallas_call | solution.py:33
  31.9 7.3 %all-to-all-start.1 = ((bf16[64,16,128]{2,1,0:T(8,128)(2,1)}), bf16[64,16,128]{2,1,0:T(8,128)(2,1)S(1)}, u32[]{:S(2)}, u32[]{:S(2)}) async-start(bf16[64,16,128]{2,1,0:T(8,128)(2,1)} %shard_map.124), calls=%async_computation.1 | async-start | bytes 524288 | tf_op jit(solution)/shard_map/all_to_all | solution.py:429
  39.2 0.7 collective-permute-done.1.q
  39.8 1.6 %shard_map.125 = (f32[512,512]{1,0:T(8,128)S(1)}, f32[512,128]{1,0:T(8,128)S(1)}, f32[512,128]{1,0:T(8,128)S(1)}) custom-call(s32[1]{0:T(128)} %bitcast.index, bf16[528,512]{1,0:T(8,128)(2,1)S(1)} %collective-permute-done.1.q, bf16[256,512]{1,0:T(8,128)(2,1)S(1)} %get-tuple-element.53.head, bf16[768,512]{1,0:T(8,128)(2,1)S(1)} %get-tuple-element.36.tail), custom_call_target="tpu_custom_call" | custom-call | flops 1 | bytes 1 | tf_op jit(solution)/shard_map/pallas_call | solution.py:33
  41.5 0.3 collective-permute-done.2.tail
  41.8 1.7 %shard_map.126 = bf16[560,512]{1,0:T(8,128)(2,1)S(1)} custom-call(s32[1]{0:T(128)} %bitcast.index, bf16[528,512]{1,0:T(8,128)(2,1)S(1)} %collective-permute-done.1.q, bf16[768,512]{1,0:T(8,128)(2,1)S(1)} %collective-permute-done.2.tail, f32[512,512]{1,0:T(8,128)S(1)} %get-tuple-element.40.done, f32[512,128]{1,0:T(8,128)S(1)} %get-tuple-element.41.tops, ...), custom_call_target="tpu_custom_call" | custom-call | flops 1 | bytes 1 | tf_op jit(solution)/shard_map/pallas_call | solution.py:33
  43.4 4.1 %collective-permute-start.3 = (bf16[560,512]{1,0:T(8,128)(2,1)S(1)}, bf16[560,512]{1,0:T(8,128)(2,1)S(1)}, u32[]{:S(2)}, u32[]{:S(2)}) collective-permute-start(bf16[560,512]{1,0:T(8,128)(2,1)S(1)} %shard_map.126), channel_id=1, source_target_pairs={{0,8},{4,12},{8,16},{12,20},{16,24},{20,28},{24,32},{28,36},{32,40... | collective-permute-start | bytes 1720328 | tf_op jit(solution)/shard_map/ppermute | solution.py:354
  47.6 4.1 %shard_map.127 = (f32[256,1024]{1,0:T(8,128)}, f32[1024,128]{1,0:T(8,128)}, f32[8,128]{1,0:T(8,128)}) custom-call(f32[8]{0:T(128)} %rate.3, bf16[256,1024]{1,0:T(8,128)(2,1)} %q.3, bf16[256,1024]{1,0:T(8,128)(2,1)} %k.3, bf16[256,1024]{1,0:T(8,128)(2,1)} %v.3), custom_call_target="tpu_custom_call" | custom-call | flops 1 | bytes 1 | tf_op jit(solution)/shard_map/pallas_call | solution.py:33
  51.7 1.1 %all-to-all-done.1 = bf16[64,16,128]{2,1,0:T(8,128)(2,1)S(1)} async-done(((bf16[64,16,128]{2,1,0:T(8,128)(2,1)}), bf16[64,16,128]{2,1,0:T(8,128)(2,1)S(1)}, u32[]{:S(2)}, u32[]{:S(2)}) %all-to-all-start.1) | async-done | bytes 262176 | tf_op jit(solution)/shard_map/all_to_all | solution.py:429
  52.8 0.7 %copy-done.9 = bf16[64,16,128]{2,1,0:T(8,128)(2,1)} copy-done((bf16[64,16,128]{2,1,0:T(8,128)(2,1)}, bf16[64,16,128]{2,1,0:T(8,128)(2,1)S(1)}, u32[]{:S(2)}) %copy-start.9) | copy-done | bytes 262168
  53.5 3.0 %shard_map.128 = (f32[256,1024]{1,0:T(8,128)}, f32[8,256]{1,0:T(8,128)}) custom-call(f32[8,128]{1,0:T(8,128)} %get-tuple-element.45.rates, f32[256,1024]{1,0:T(8,128)} %get-tuple-element.46.inner, bf16[256,1024]{1,0:T(8,128)(2,1)} %q.3, f32[1024,128]{1,0:T(8,128)} %get-tuple-element.47.first, bf16[1024,128]{1,0:T(8,128)(2,1)} %bitcast.6), custom_call_target="tpu_custom_call" | custom-call | flops 10000000000 | bytes 1 | tf_op jit(solution)/shard_map/pallas_call | solution.py:33
  56.5 2.5 %collective-permute-start.6 = (f32[8,256]{1,0:T(8,128)}, f32[8,256]{1,0:T(8,128)S(1)}, u32[]{:S(2)}, u32[]{:S(2)}) collective-permute-start(f32[8,256]{1,0:T(8,128)} %get-tuple-element.52.s0), channel_id=1, source_target_pairs={{0,3},{1,0},{2,1},{3,2},{4,7},{5,4},{6,5},{7,6},{8,11},{9,8},{10,9... | collective-permute-start | bytes 24584 | tf_op jit(solution)/shard_map/ppermute | solution.py:362
  58.9 0.5 collective-permute-start.5
  59.5 0.6 collective-permute-start.4
  60.1 2.5 %shard_map.129 = (f32[512,512]{1,0:T(8,128)S(1)}, f32[512,128]{1,0:T(8,128)S(1)}, f32[512,128]{1,0:T(8,128)S(1)}) custom-call(s32[1]{0:T(128)} %bitcast.index, bf16[528,512]{1,0:T(8,128)(2,1)} %get-tuple-element.35.q, bf16[256,512]{1,0:T(8,128)(2,1)S(1)} %get-tuple-element.53.head, bf16[768,512]{1,0:T(8,128)(2,1)S(1)} %get-tuple-element.36.tail), custom_call_target="tpu_custom_call" | custom-call | flops 1 | bytes 1 | tf_op jit(solution)/shard_map/pallas_call | solution.py:33
  62.6 0.0 collective-permute-done.3.far
  62.6 0.0 copy-start.3
  62.6 0.0 copy-start.4
  62.6 0.0 copy-start.5
  62.6 0.0 copy-start.7
  62.6 0.6 shard_map.130
  63.3 0.0 collective-permute-done.6.s3
  63.3 0.0 collective-permute-done.5.s2
  63.3 0.1 collective-permute-done.4.s1
  63.4 2.7 %collective-permute-start.7 = (bf16[256,512]{1,0:T(8,128)(2,1)S(1)}, bf16[256,512]{1,0:T(8,128)(2,1)S(1)}, u32[]{:S(2)}, u32[]{:S(2)}) collective-permute-start(bf16[256,512]{1,0:T(8,128)(2,1)S(1)} %get-tuple-element.63), channel_id=1, source_target_pairs={{0,4},{4,0},{8,12},{12,8},{16,20},{20,16},{24,28},{28,24},{32,36},... | collective-permute-start | bytes 786440 | tf_op jit(solution)/shard_map/ppermute | solution.py:358
  66.1 0.0 copy-done.3
  66.1 0.0 copy-done.5
  66.1 1.3 %shard_map.131 = bf16[256,1024]{1,0:T(8,128)(2,1)} custom-call(f32[256,1024]{1,0:T(8,128)S(1)} %copy-done.3, bf16[256,1024]{1,0:T(8,128)(2,1)S(1)} %copy-done.4, f32[1,1024]{1,0:T(1,128)S(1)} %bitcast.5, f32[8,256]{1,0:T(8,128)S(1)} %copy-done.5, f32[8,256]{1,0:T(8,128)S(1)} %collective-permute-done.4.s1, f32[8,256]{1,0:T(8,128)S(1)} %collective-permute-done.5.s2, ...), custom_call_target="tpu_custom_call" | custom-call | flops 1 | bytes 1 | tf_op jit(solution)/shard_map/pallas_call | solution.py:33
  67.4 0.0 collective-permute-done.7.other
  67.4 0.8 %shard_map.132 = bf16[256,1024]{1,0:T(8,128)(2,1)} custom-call(s32[1]{0:T(128)} %bitcast.index, bf16[256,512]{1,0:T(8,128)(2,1)S(1)} %get-tuple-element.62.mine, bf16[256,512]{1,0:T(8,128)(2,1)S(1)} %collective-permute-done.7.other), custom_call_target="tpu_custom_call" | custom-call | flops 1 | bytes 1 | tf_op jit(solution)/shard_map/pallas_call | solution.py:33
  (3 shorter events, 0.0 us)
Async XLA Ops:
  0.6 17.4 %copy-start.1 = (bf16[256,1024]{1,0:T(8,128)(2,1)S(1)}, bf16[256,1024]{1,0:T(8,128)(2,1)}, u32[]{:S(2)}) copy-start(bf16[256,1024]{1,0:T(8,128)(2,1)} %k.2) | copy-start | bytes 1572868
  0.6 17.4 %copy-start.2 = (bf16[256,1024]{1,0:T(8,128)(2,1)S(1)}, bf16[256,1024]{1,0:T(8,128)(2,1)}, u32[]{:S(2)}) copy-start(bf16[256,1024]{1,0:T(8,128)(2,1)} %v.2) | copy-start | bytes 1572868
  4.5 13.6 %copy-start = (bf16[256,1024]{1,0:T(8,128)(2,1)S(1)}, bf16[256,1024]{1,0:T(8,128)(2,1)}, u32[]{:S(2)}) copy-start(bf16[256,1024]{1,0:T(8,128)(2,1)} %q.1) | copy-start | bytes 1572868
  4.5 13.6 %collective-permute-start = (bf16[784,512]{1,0:T(8,128)(2,1)}, bf16[784,512]{1,0:T(8,128)(2,1)S(1)}, u32[]{:S(2)}, u32[]{:S(2)}) collective-permute-start(bf16[784,512]{1,0:T(8,128)(2,1)} %get-tuple-element.34), channel_id=1, source_target_pairs={{0,4},{4,0},{8,12},{12,8},{16,20},{20,16},{24,28},{28,24},{32,36},... | collective-permute-start | bytes 2408456 | tf_op jit(solution)/shard_map/ppermute | solution.py:358
  7.8 22.2 %all-to-all-start = ((bf16[64,16,128]{2,1,0:T(8,128)(2,1)}), bf16[64,16,128]{2,1,0:T(8,128)(2,1)}, u32[]{:S(2)}, u32[]{:S(2)}) async-start(bf16[64,16,128]{2,1,0:T(8,128)(2,1)} %bitcast.7), calls=%async_computation | async-start | bytes 524288 | tf_op jit(solution)/shard_map/all_to_all | solution.py:402
  18.1 0.7 %copy-start.6 = (f32[16,128]{1,0:T(8,128)S(1)}, f32[16,128]{1,0:T(8,128)}, u32[]{:S(2)}) copy-start(f32[16,128]{1,0:T(8,128)} %get-tuple-element.33.flags_own) | copy-start | bytes 24580
  20.5 9.5 %copy-start.8 = (f32[8]{0:T(128)S(1)}, f32[8]{0:T(128)}, u32[]{:S(2)}) copy-start(f32[8]{0:T(128)} %rate.3) | copy-start | bytes 100
  20.5 21.2 %collective-permute-start.2 = (bf16[768,512]{1,0:T(8,128)(2,1)S(1)}, bf16[768,512]{1,0:T(8,128)(2,1)S(1)}, u32[]{:S(2)}, u32[]{:S(2)}) collective-permute-start(bf16[768,512]{1,0:T(8,128)(2,1)S(1)} %get-tuple-element.36.tail), channel_id=1, source_target_pairs={{0,8},{4,12},{8,16},{12,20},{16,24},{20,28},{24,32},{28,36},{32,40... | collective-permute-start | bytes 2359304 | tf_op jit(solution)/shard_map/ppermute | solution.py:354
  23.9 16.0 %collective-permute-start.1 = (bf16[528,512]{1,0:T(8,128)(2,1)}, bf16[528,512]{1,0:T(8,128)(2,1)S(1)}, u32[]{:S(2)}, u32[]{:S(2)}) collective-permute-start(bf16[528,512]{1,0:T(8,128)(2,1)} %get-tuple-element.35.q), channel_id=1, source_target_pairs={{8,0},{12,4},{16,8},{20,12},{24,16},{28,20},{32,24},{36,28},{40,32... | collective-permute-start | bytes 1622024 | tf_op jit(solution)/shard_map/ppermute | solution.py:354
  31.9 20.9 %all-to-all-start.1 = ((bf16[64,16,128]{2,1,0:T(8,128)(2,1)}), bf16[64,16,128]{2,1,0:T(8,128)(2,1)S(1)}, u32[]{:S(2)}, u32[]{:S(2)}) async-start(bf16[64,16,128]{2,1,0:T(8,128)(2,1)} %shard_map.124), calls=%async_computation.1 | async-start | bytes 524288 | tf_op jit(solution)/shard_map/all_to_all | solution.py:429
  43.4 19.1 %collective-permute-start.3 = (bf16[560,512]{1,0:T(8,128)(2,1)S(1)}, bf16[560,512]{1,0:T(8,128)(2,1)S(1)}, u32[]{:S(2)}, u32[]{:S(2)}) collective-permute-start(bf16[560,512]{1,0:T(8,128)(2,1)S(1)} %shard_map.126), channel_id=1, source_target_pairs={{0,8},{4,12},{8,16},{12,20},{16,24},{20,28},{24,32},{28,36},{32,40... | collective-permute-start | bytes 1720328 | tf_op jit(solution)/shard_map/ppermute | solution.py:354
  52.8 0.7 %copy-start.9 = (bf16[64,16,128]{2,1,0:T(8,128)(2,1)}, bf16[64,16,128]{2,1,0:T(8,128)(2,1)S(1)}, u32[]{:S(2)}) copy-start(bf16[64,16,128]{2,1,0:T(8,128)(2,1)S(1)} %all-to-all-done.1) | copy-start | bytes 786436
  56.5 6.8 %collective-permute-start.6 = (f32[8,256]{1,0:T(8,128)}, f32[8,256]{1,0:T(8,128)S(1)}, u32[]{:S(2)}, u32[]{:S(2)}) collective-permute-start(f32[8,256]{1,0:T(8,128)} %get-tuple-element.52.s0), channel_id=1, source_target_pairs={{0,3},{1,0},{2,1},{3,2},{4,7},{5,4},{6,5},{7,6},{8,11},{9,8},{10,9... | collective-permute-start | bytes 24584 | tf_op jit(solution)/shard_map/ppermute | solution.py:362
  58.9 4.4 %collective-permute-start.5 = (f32[8,256]{1,0:T(8,128)}, f32[8,256]{1,0:T(8,128)S(1)}, u32[]{:S(2)}, u32[]{:S(2)}) collective-permute-start(f32[8,256]{1,0:T(8,128)} %get-tuple-element.52.s0), channel_id=1, source_target_pairs={{0,2},{1,3},{2,0},{3,1},{4,6},{5,7},{6,4},{7,5},{8,10},{9,11},{10,... | collective-permute-start | bytes 24584 | tf_op jit(solution)/shard_map/ppermute | solution.py:362
  59.5 3.9 %collective-permute-start.4 = (f32[8,256]{1,0:T(8,128)}, f32[8,256]{1,0:T(8,128)S(1)}, u32[]{:S(2)}, u32[]{:S(2)}) collective-permute-start(f32[8,256]{1,0:T(8,128)} %get-tuple-element.52.s0), channel_id=1, source_target_pairs={{0,1},{1,2},{2,3},{3,0},{4,5},{5,6},{6,7},{7,4},{8,9},{9,10},{10,1... | collective-permute-start | bytes 24584 | tf_op jit(solution)/shard_map/ppermute | solution.py:362
  62.6 3.5 %copy-start.3 = (f32[256,1024]{1,0:T(8,128)S(1)}, f32[256,1024]{1,0:T(8,128)}, u32[]{:S(2)}) copy-start(f32[256,1024]{1,0:T(8,128)} %get-tuple-element.51.heads) | copy-start | bytes 3145732
  62.6 3.5 %copy-start.4 = (bf16[256,1024]{1,0:T(8,128)(2,1)S(1)}, bf16[256,1024]{1,0:T(8,128)(2,1)}, u32[]{:S(2)}) copy-start(bf16[256,1024]{1,0:T(8,128)(2,1)} %gate.1) | copy-start | bytes 1572868
  62.6 3.5 %copy-start.5 = (f32[8,256]{1,0:T(8,128)S(1)}, f32[8,256]{1,0:T(8,128)}, u32[]{:S(2)}) copy-start(f32[8,256]{1,0:T(8,128)} %get-tuple-element.52.s0) | copy-start | bytes 24580
  62.6 3.5 %copy-start.7 = (f32[1024]{0:T(1024)S(1)}, f32[1024]{0:T(1024)}, u32[]{:S(2)}) copy-start(f32[1024]{0:T(1024)} %param.15) | copy-start | bytes 12292
  63.4 4.0 %collective-permute-start.7 = (bf16[256,512]{1,0:T(8,128)(2,1)S(1)}, bf16[256,512]{1,0:T(8,128)(2,1)S(1)}, u32[]{:S(2)}, u32[]{:S(2)}) collective-permute-start(bf16[256,512]{1,0:T(8,128)(2,1)S(1)} %get-tuple-element.63), channel_id=1, source_target_pairs={{0,4},{4,0},{8,12},{12,8},{16,20},{20,16},{24,28},{28,24},{32,36},... | collective-permute-start | bytes 786440 | tf_op jit(solution)/shard_map/ppermute | solution.py:358

commit v10 on v9

--- a/solution.py
+++ b/solution.py
@@ -63,7 +63,7 @@
 
 
 def start_body(
-    index, docs, doc_row, rate_hbm, mask, k_hbm, v_hbm, sq, sk, sv, out, sent, own, rate, k, v, packed, rate_sem, sems
+    index, docs, doc_row, rate_hbm, mask, k_hbm, v_hbm, sq, sk, sv, first, out, sent, own, rate, k, v, packed, rate_sem, sems
 ):
     other = 1 - index[0] % 2
     copies = [pltpu.make_async_copy(rate_hbm, rate, rate_sem)]
@@ -96,9 +96,9 @@
         copies[2 * g + 2].wait()
         for h in (2 * g, 2 * g + 1):
             step = jnp.exp(jnp.full((HD, HD), -rate[h] * BLK, f32))
-            state = step * block_state(rate[h], k, v, h, 0)
-            state = state + block_state(rate[h], k, v, h, 1)
-            out[cols(h), :] = state.astype(bf16)
+            early = block_state(rate[h], k, v, h, 0)
+            first[cols(h), :] = early
+            out[cols(h), :] = (step * early + block_state(rate[h], k, v, h, 1)).astype(bf16)
     for copy in copies[LOCAL + 1 :]:
         copy.wait()
 
@@ -112,20 +112,16 @@
             state = step * state + parts[i].astype(f32)
 
 
-def inner_body(rate, q, k, v, out, first, rates):
-    row = lax.broadcasted_iota(jnp.int32, (BLK, BLK), 0)
-    col = lax.broadcasted_iota(jnp.int32, (BLK, BLK), 1)
+def inner_body(rate, q, k, v, out, rates):
+    row = lax.broadcasted_iota(jnp.int32, (ROWS, ROWS), 0)
+    col = lax.broadcasted_iota(jnp.int32, (ROWS, ROWS), 1)
     gap = jnp.maximum(row - col, 0).astype(f32)
+    inside = (row >= col) & ((row >= BLK) == (col >= BLK))
     for h in range(LOCAL):
         rates[h : h + 1, :] = jnp.full((1, HD), rate[h], f32)
-        first[cols(h), :] = block_state(rate[h], k, v, h, 0)
-        decay = jnp.where(row >= col, jnp.exp(-rate[h] * gap), 0.0)
-        for b in range(2):
-            rows = slice(b * BLK, (b + 1) * BLK)
-            scores = dot(q[rows, cols(h)], k[rows, cols(h)], ((1,), (1,)))
-            out[rows, cols(h)] = dot(
-                (scores * decay).astype(bf16), v[rows, cols(h)], ((1,), (0,))
-            )
+        decay = jnp.where(inside, jnp.exp(-rate[h] * gap), 0.0)
+        scores = dot(q[:, cols(h)], k[:, cols(h)], ((1,), (1,)))
+        out[:, cols(h)] = dot((scores * decay).astype(bf16), v[:, cols(h)], ((1,), (0,)))
 
 
 def carry_body(rates, inner, q, first, state, heads, squares):
@@ -381,9 +377,9 @@
     narrow = like((ROWS, WIDTH), bf16)
 
     anywhere = pl.BlockSpec(memory_space=pl.ANY)
-    state, sent, own_flags = call(
+    first, state, sent, own_flags = call(
         start_body,
-        [like((WIDTH, HD), bf16), like((3 * ROWS + 16, HALF), bf16), like((16, NBLK), f32)],
+        [like((WIDTH, HD), f32), like((WIDTH, HD), bf16), like((3 * ROWS + 16, HALF), bf16), like((16, NBLK), f32)],
         (
             index, doc_ids, doc_ids.reshape(1, NBLK), decay_rate, block_mask,
             lin_key, lin_value, soft_query, soft_key, soft_value,
@@ -444,9 +440,9 @@
     )
     far, lin_query = lax.optimization_barrier((far, lin_query))
     far = shifted(far, 2)
-    inner, first, rates = call(
+    inner, rates = call(
         inner_body,
-        [wide, like((WIDTH, HD), f32), like((LOCAL, HD), f32)],
+        [wide, like((LOCAL, HD), f32)],
         (decay_rate, lin_query, lin_key, lin_value),
         [SMEM] + [VMEM] * 3,
     )

time: 69.6 us -> 69 us (level); the launches traced: 68.2 us -> 68.4 us
  waiting for transfers between devices: 6.99 us -> 7.85 us
  Pallas kernels: 23 us -> 22.3 us
    all_to_all x1, waiting for transfers between devices: 1.07 us -> 1.92 us  [per_device(): entering = lax.all_to_all(prefix, 'seq', 0, 0).reshape(WIDTH, HD)]
  transfers between devices with their start and end apart: 10 -> 10, of which waited for: 5 -> 5; matrix products, arithmetic and copies ran while one was open for 0% -> 0% of each run, Pallas kernels for 27% -> 26%
where the time goes in v10:
time: 69 us; the launch traced here: 68.4 us
  starting transfers between devices  36 us (52%)
  Pallas kernels  22.3 us (32%)
  waiting for transfers between devices  7.85 us (11%)
  local copies, waits for them, and re-layouts  1.43 us (2%)
  between operations  0.86 us (1%)
    pallas_call x11, Pallas kernels, call(): pl.pallas_call(body, out_shape=outs, in_specs=specs, out_specs=[VMEM] * l...  22.3 us
    all_to_all x1, starting transfers between devices, per_device(): parts = lax.all_to_all(state.reshape(SHARDS, 16, HD), 'seq', 0, 0)  10.3 us
    ppermute x3, starting transfers between devices, shifted(): lax.ppermute(x, 'seq', [(i, i + distance) for i in range(SHARDS) if 0 <=...  8.77 us
    all_to_all x1, starting transfers between devices, per_device(): entering = lax.all_to_all(prefix, 'seq', 0, 0).reshape(WIDTH, HD)  7.3 us
    ppermute x2, starting transfers between devices, swapped(): return lax.ppermute(x, 'seq', [(i, i ^ 1) for i in range(SHARDS)])  6.02 us
    all_to_all x1, waiting for transfers between devices, per_device(): parts = lax.all_to_all(state.reshape(SHARDS, 16, HD), 'seq', 0, 0)  4.86 us
    ppermute x3, starting transfers between devices, turned(): return lax.ppermute(x, 'head', [(i, (i + distance) % 4) for i in range(4)])  3.61 us
    all_to_all x1, waiting for transfers between devices, per_device(): entering = lax.all_to_all(prefix, 'seq', 0, 0).reshape(WIDTH, HD)  1.92 us
  transfers between devices with their start and end apart: 10, of which 5 were waited for; matrix products, arithmetic and copies ran while one was open for 0% of the time, Pallas kernels for 26%

profile of v10, /device:TPU:1, one launch (start us, length us, event | category | flops | bytes accessed | tf_op | source)
XLA Modules:
  0.0 68.4 jit_solution(5380014034996221291)
XLA Ops:
  0.6 0.0 copy-start.1
  0.6 0.0 copy-start.2
  0.7 4.0 %shard_map.122 = (f32[1024,128]{1,0:T(8,128)}, bf16[1024,128]{1,0:T(8,128)(2,1)}, bf16[784,512]{1,0:T(8,128)(2,1)}, f32[16,128]{1,0:T(8,128)}) custom-call(s32[1]{0:T(128)} %bitcast.index, s32[128]{0:T(128)} %docs.1, s32[1,128]{1,0:T(1,128)} %bitcast.8, f32[8]{0:T(128)} %rate.3, s32[2,128]{1,0:T(2,128)} %mask.1, bf16[256,1024]{1,0:T(8,128)(2,1)} %k.3, ...), custom_call_target="tpu_custom_call" | custom-call | flops 1 | bytes 1 | tf_op jit(solution)/shard_map/pallas_call | solution.py:33
  4.7 0.0 copy-start
  4.7 3.3 %collective-permute-start = (bf16[784,512]{1,0:T(8,128)(2,1)}, bf16[784,512]{1,0:T(8,128)(2,1)S(1)}, u32[]{:S(2)}, u32[]{:S(2)}) collective-permute-start(bf16[784,512]{1,0:T(8,128)(2,1)} %get-tuple-element.34), channel_id=1, source_target_pairs={{0,4},{4,0},{8,12},{12,8},{16,20},{20,16},{24,28},{28,24},{32,36},... | collective-permute-start | bytes 2408456 | tf_op jit(solution)/shard_map/ppermute | solution.py:354
  8.0 10.3 %all-to-all-start = ((bf16[64,16,128]{2,1,0:T(8,128)(2,1)}), bf16[64,16,128]{2,1,0:T(8,128)(2,1)}, u32[]{:S(2)}, u32[]{:S(2)}) async-start(bf16[64,16,128]{2,1,0:T(8,128)(2,1)} %bitcast.7), calls=%async_computation | async-start | bytes 524288 | tf_op jit(solution)/shard_map/all_to_all | solution.py:398
  18.3 0.0 collective-permute-done.other
  18.3 0.0 copy-done.1
  18.3 0.0 copy-done.2
  18.3 0.0 copy-done
  18.3 0.0 copy-start.6
  18.3 0.7 %copy-done.6 = f32[16,128]{1,0:T(8,128)S(1)} copy-done((f32[16,128]{1,0:T(8,128)S(1)}, f32[16,128]{1,0:T(8,128)}, u32[]{:S(2)}) %copy-start.6) | copy-done | bytes 8216
  19.0 1.7 %shard_map.123 = (bf16[528,512]{1,0:T(8,128)(2,1)}, bf16[256,512]{1,0:T(8,128)(2,1)S(1)}, bf16[768,512]{1,0:T(8,128)(2,1)S(1)}) custom-call(s32[1]{0:T(128)} %bitcast.index, f32[16,128]{1,0:T(8,128)S(1)} %copy-done.6, bf16[256,1024]{1,0:T(8,128)(2,1)S(1)} %copy-done, bf16[256,1024]{1,0:T(8,128)(2,1)S(1)} %copy-done.1, bf16[256,1024]{1,0:T(8,128)(2,1)S(1)} %copy-done.2, ...), custom_call_target="tpu_custom_call" | custom-call | flops 1 | bytes 1 | tf_op jit(solution)/shard_map/pallas_call | solution.py:33
  20.7 0.0 copy-start.8
  20.7 3.3 %collective-permute-start.2 = (bf16[768,512]{1,0:T(8,128)(2,1)S(1)}, bf16[768,512]{1,0:T(8,128)(2,1)S(1)}, u32[]{:S(2)}, u32[]{:S(2)}) collective-permute-start(bf16[768,512]{1,0:T(8,128)(2,1)S(1)} %get-tuple-element.36.tail), channel_id=1, source_target_pairs={{0,8},{4,12},{8,16},{12,20},{16,24},{20,28},{24,32},{28,36},{32,40... | collective-permute-start | bytes 2359304 | tf_op jit(solution)/shard_map/ppermute | solution.py:350
  24.1 1.3 %collective-permute-start.1 = (bf16[528,512]{1,0:T(8,128)(2,1)}, bf16[528,512]{1,0:T(8,128)(2,1)S(1)}, u32[]{:S(2)}, u32[]{:S(2)}) collective-permute-start(bf16[528,512]{1,0:T(8,128)(2,1)} %get-tuple-element.35.q), channel_id=1, source_target_pairs={{8,0},{12,4},{16,8},{20,12},{24,16},{28,20},{32,24},{36,28},{40,32... | collective-permute-start | bytes 1622024 | tf_op jit(solution)/shard_map/ppermute | solution.py:350
  25.4 4.9 %all-to-all-done.parts = bf16[64,16,128]{2,1,0:T(8,128)(2,1)} async-done(((bf16[64,16,128]{2,1,0:T(8,128)(2,1)}), bf16[64,16,128]{2,1,0:T(8,128)(2,1)}, u32[]{:S(2)}, u32[]{:S(2)}) %all-to-all-start) | async-done | bytes 262176 | tf_op jit(solution)/shard_map/all_to_all | solution.py:398
  30.2 0.0 copy-done.8
  30.2 1.8 %shard_map.124 = bf16[64,16,128]{2,1,0:T(8,128)(2,1)} custom-call(s32[1]{0:T(128)} %bitcast.index, f32[8]{0:T(128)S(1)} %copy-done.8, bf16[64,16,128]{2,1,0:T(8,128)(2,1)} %all-to-all-done.parts), custom_call_target="tpu_custom_call" | custom-call | flops 1500000000 | bytes 1 | tf_op jit(solution)/shard_map/pallas_call | solution.py:33
  32.0 7.3 %all-to-all-start.1 = ((bf16[64,16,128]{2,1,0:T(8,128)(2,1)}), bf16[64,16,128]{2,1,0:T(8,128)(2,1)S(1)}, u32[]{:S(2)}, u32[]{:S(2)}) async-start(bf16[64,16,128]{2,1,0:T(8,128)(2,1)} %shard_map.124), calls=%async_computation.1 | async-start | bytes 524288 | tf_op jit(solution)/shard_map/all_to_all | solution.py:425
  39.4 0.7 collective-permute-done.1.q
  40.0 1.6 %shard_map.125 = (f32[512,512]{1,0:T(8,128)S(1)}, f32[512,128]{1,0:T(8,128)S(1)}, f32[512,128]{1,0:T(8,128)S(1)}) custom-call(s32[1]{0:T(128)} %bitcast.index, bf16[528,512]{1,0:T(8,128)(2,1)S(1)} %collective-permute-done.1.q, bf16[256,512]{1,0:T(8,128)(2,1)S(1)} %get-tuple-element.53.head, bf16[768,512]{1,0:T(8,128)(2,1)S(1)} %get-tuple-element.36.tail), custom_call_target="tpu_custom_call" | custom-call | flops 1 | bytes 1 | tf_op jit(solution)/shard_map/pallas_call | solution.py:33
  41.7 0.3 collective-permute-done.2.tail
  42.0 1.7 %shard_map.126 = bf16[560,512]{1,0:T(8,128)(2,1)S(1)} custom-call(s32[1]{0:T(128)} %bitcast.index, bf16[528,512]{1,0:T(8,128)(2,1)S(1)} %collective-permute-done.1.q, bf16[768,512]{1,0:T(8,128)(2,1)S(1)} %collective-permute-done.2.tail, f32[512,512]{1,0:T(8,128)S(1)} %get-tuple-element.40.done, f32[512,128]{1,0:T(8,128)S(1)} %get-tuple-element.41.tops, ...), custom_call_target="tpu_custom_call" | custom-call | flops 1 | bytes 1 | tf_op jit(solution)/shard_map/pallas_call | solution.py:33
  43.6 4.1 %collective-permute-start.3 = (bf16[560,512]{1,0:T(8,128)(2,1)S(1)}, bf16[560,512]{1,0:T(8,128)(2,1)S(1)}, u32[]{:S(2)}, u32[]{:S(2)}) collective-permute-start(bf16[560,512]{1,0:T(8,128)(2,1)S(1)} %shard_map.126), channel_id=1, source_target_pairs={{0,8},{4,12},{8,16},{12,20},{16,24},{20,28},{24,32},{28,36},{32,40... | collective-permute-start | bytes 1720328 | tf_op jit(solution)/shard_map/ppermute | solution.py:350
  47.8 3.3 %shard_map.127 = (f32[256,1024]{1,0:T(8,128)}, f32[8,128]{1,0:T(8,128)}) custom-call(f32[8]{0:T(128)} %rate.3, bf16[256,1024]{1,0:T(8,128)(2,1)} %q.3, bf16[256,1024]{1,0:T(8,128)(2,1)} %k.3, bf16[256,1024]{1,0:T(8,128)(2,1)} %v.3), custom_call_target="tpu_custom_call" | custom-call | flops 1 | bytes 1 | tf_op jit(solution)/shard_map/pallas_call | solution.py:33
  51.0 1.9 %all-to-all-done.1 = bf16[64,16,128]{2,1,0:T(8,128)(2,1)S(1)} async-done(((bf16[64,16,128]{2,1,0:T(8,128)(2,1)}), bf16[64,16,128]{2,1,0:T(8,128)(2,1)S(1)}, u32[]{:S(2)}, u32[]{:S(2)}) %all-to-all-start.1) | async-done | bytes 262176 | tf_op jit(solution)/shard_map/all_to_all | solution.py:425
  53.0 0.7 %copy-done.9 = bf16[64,16,128]{2,1,0:T(8,128)(2,1)} copy-done((bf16[64,16,128]{2,1,0:T(8,128)(2,1)}, bf16[64,16,128]{2,1,0:T(8,128)(2,1)S(1)}, u32[]{:S(2)}) %copy-start.9) | copy-done | bytes 262168
  53.7 3.0 %shard_map.128 = (f32[256,1024]{1,0:T(8,128)}, f32[8,256]{1,0:T(8,128)}) custom-call(f32[8,128]{1,0:T(8,128)} %get-tuple-element.45.rates, f32[256,1024]{1,0:T(8,128)} %get-tuple-element.46.inner, bf16[256,1024]{1,0:T(8,128)(2,1)} %q.3, f32[1024,128]{1,0:T(8,128)} %get-tuple-element.47.first, bf16[1024,128]{1,0:T(8,128)(2,1)} %bitcast.6), custom_call_target="tpu_custom_call" | custom-call | flops 10000000000 | bytes 1 | tf_op jit(solution)/shard_map/pallas_call | solution.py:33
  56.7 2.5 %collective-permute-start.6 = (f32[8,256]{1,0:T(8,128)}, f32[8,256]{1,0:T(8,128)S(1)}, u32[]{:S(2)}, u32[]{:S(2)}) collective-permute-start(f32[8,256]{1,0:T(8,128)} %get-tuple-element.52.s0), channel_id=1, source_target_pairs={{0,3},{1,0},{2,1},{3,2},{4,7},{5,4},{6,5},{7,6},{8,11},{9,8},{10,9... | collective-permute-start | bytes 24584 | tf_op jit(solution)/shard_map/ppermute | solution.py:358
  59.1 0.5 collective-permute-start.5
  59.7 0.6 collective-permute-start.4
  60.3 2.5 %shard_map.129 = (f32[512,512]{1,0:T(8,128)S(1)}, f32[512,128]{1,0:T(8,128)S(1)}, f32[512,128]{1,0:T(8,128)S(1)}) custom-call(s32[1]{0:T(128)} %bitcast.index, bf16[528,512]{1,0:T(8,128)(2,1)} %get-tuple-element.35.q, bf16[256,512]{1,0:T(8,128)(2,1)S(1)} %get-tuple-element.53.head, bf16[768,512]{1,0:T(8,128)(2,1)S(1)} %get-tuple-element.36.tail), custom_call_target="tpu_custom_call" | custom-call | flops 1 | bytes 1 | tf_op jit(solution)/shard_map/pallas_call | solution.py:33
  62.8 0.0 collective-permute-done.3.far
  62.8 0.0 copy-start.3
  62.8 0.0 copy-start.4
  62.8 0.0 copy-start.5
  62.8 0.0 copy-start.7
  62.8 0.6 shard_map.130
  63.5 0.0 collective-permute-done.6.s3
  63.5 0.0 collective-permute-done.5.s2
  63.5 0.1 collective-permute-done.4.s1
  63.6 2.7 %collective-permute-start.7 = (bf16[256,512]{1,0:T(8,128)(2,1)S(1)}, bf16[256,512]{1,0:T(8,128)(2,1)S(1)}, u32[]{:S(2)}, u32[]{:S(2)}) collective-permute-start(bf16[256,512]{1,0:T(8,128)(2,1)S(1)} %get-tuple-element.63), channel_id=1, source_target_pairs={{0,4},{4,0},{8,12},{12,8},{16,20},{20,16},{24,28},{28,24},{32,36},... | collective-permute-start | bytes 786440 | tf_op jit(solution)/shard_map/ppermute | solution.py:354
  66.3 0.0 copy-done.3
  66.3 0.0 copy-done.4
  66.3 1.3 %shard_map.131 = bf16[256,1024]{1,0:T(8,128)(2,1)} custom-call(f32[256,1024]{1,0:T(8,128)S(1)} %copy-done.3, bf16[256,1024]{1,0:T(8,128)(2,1)S(1)} %copy-done.4, f32[1,1024]{1,0:T(1,128)S(1)} %bitcast.5, f32[8,256]{1,0:T(8,128)S(1)} %copy-done.5, f32[8,256]{1,0:T(8,128)S(1)} %collective-permute-done.4.s1, f32[8,256]{1,0:T(8,128)S(1)} %collective-permute-done.5.s2, ...), custom_call_target="tpu_custom_call" | custom-call | flops 1 | bytes 1 | tf_op jit(solution)/shard_map/pallas_call | solution.py:33
  67.6 0.0 collective-permute-done.7.other
  67.6 0.8 %shard_map.132 = bf16[256,1024]{1,0:T(8,128)(2,1)} custom-call(s32[1]{0:T(128)} %bitcast.index, bf16[256,512]{1,0:T(8,128)(2,1)S(1)} %get-tuple-element.62.mine, bf16[256,512]{1,0:T(8,128)(2,1)S(1)} %collective-permute-done.7.other), custom_call_target="tpu_custom_call" | custom-call | flops 1 | bytes 1 | tf_op jit(solution)/shard_map/pallas_call | solution.py:33
  (3 shorter events, 0.0 us)
Async XLA Ops:
  0.6 17.6 %copy-start.1 = (bf16[256,1024]{1,0:T(8,128)(2,1)S(1)}, bf16[256,1024]{1,0:T(8,128)(2,1)}, u32[]{:S(2)}) copy-start(bf16[256,1024]{1,0:T(8,128)(2,1)} %k.2) | copy-start | bytes 1572868
  0.6 17.6 %copy-start.2 = (bf16[256,1024]{1,0:T(8,128)(2,1)S(1)}, bf16[256,1024]{1,0:T(8,128)(2,1)}, u32[]{:S(2)}) copy-start(bf16[256,1024]{1,0:T(8,128)(2,1)} %v.2) | copy-start | bytes 1572868
  4.7 13.6 %copy-start = (bf16[256,1024]{1,0:T(8,128)(2,1)S(1)}, bf16[256,1024]{1,0:T(8,128)(2,1)}, u32[]{:S(2)}) copy-start(bf16[256,1024]{1,0:T(8,128)(2,1)} %q.1) | copy-start | bytes 1572868
  4.7 13.6 %collective-permute-start = (bf16[784,512]{1,0:T(8,128)(2,1)}, bf16[784,512]{1,0:T(8,128)(2,1)S(1)}, u32[]{:S(2)}, u32[]{:S(2)}) collective-permute-start(bf16[784,512]{1,0:T(8,128)(2,1)} %get-tuple-element.34), channel_id=1, source_target_pairs={{0,4},{4,0},{8,12},{12,8},{16,20},{20,16},{24,28},{28,24},{32,36},... | collective-permute-start | bytes 2408456 | tf_op jit(solution)/shard_map/ppermute | solution.py:354
  8.0 22.2 %all-to-all-start = ((bf16[64,16,128]{2,1,0:T(8,128)(2,1)}), bf16[64,16,128]{2,1,0:T(8,128)(2,1)}, u32[]{:S(2)}, u32[]{:S(2)}) async-start(bf16[64,16,128]{2,1,0:T(8,128)(2,1)} %bitcast.7), calls=%async_computation | async-start | bytes 524288 | tf_op jit(solution)/shard_map/all_to_all | solution.py:398
  18.3 0.7 %copy-start.6 = (f32[16,128]{1,0:T(8,128)S(1)}, f32[16,128]{1,0:T(8,128)}, u32[]{:S(2)}) copy-start(f32[16,128]{1,0:T(8,128)} %get-tuple-element.33.flags_own) | copy-start | bytes 24580
  20.7 9.5 %copy-start.8 = (f32[8]{0:T(128)S(1)}, f32[8]{0:T(128)}, u32[]{:S(2)}) copy-start(f32[8]{0:T(128)} %rate.3) | copy-start | bytes 100
  20.7 21.2 %collective-permute-start.2 = (bf16[768,512]{1,0:T(8,128)(2,1)S(1)}, bf16[768,512]{1,0:T(8,128)(2,1)S(1)}, u32[]{:S(2)}, u32[]{:S(2)}) collective-permute-start(bf16[768,512]{1,0:T(8,128)(2,1)S(1)} %get-tuple-element.36.tail), channel_id=1, source_target_pairs={{0,8},{4,12},{8,16},{12,20},{16,24},{20,28},{24,32},{28,36},{32,40... | collective-permute-start | bytes 2359304 | tf_op jit(solution)/shard_map/ppermute | solution.py:350
  24.1 16.0 %collective-permute-start.1 = (bf16[528,512]{1,0:T(8,128)(2,1)}, bf16[528,512]{1,0:T(8,128)(2,1)S(1)}, u32[]{:S(2)}, u32[]{:S(2)}) collective-permute-start(bf16[528,512]{1,0:T(8,128)(2,1)} %get-tuple-element.35.q), channel_id=1, source_target_pairs={{8,0},{12,4},{16,8},{20,12},{24,16},{28,20},{32,24},{36,28},{40,32... | collective-permute-start | bytes 1622024 | tf_op jit(solution)/shard_map/ppermute | solution.py:350
  32.0 20.9 %all-to-all-start.1 = ((bf16[64,16,128]{2,1,0:T(8,128)(2,1)}), bf16[64,16,128]{2,1,0:T(8,128)(2,1)S(1)}, u32[]{:S(2)}, u32[]{:S(2)}) async-start(bf16[64,16,128]{2,1,0:T(8,128)(2,1)} %shard_map.124), calls=%async_computation.1 | async-start | bytes 524288 | tf_op jit(solution)/shard_map/all_to_all | solution.py:425
  43.6 19.1 %collective-permute-start.3 = (bf16[560,512]{1,0:T(8,128)(2,1)S(1)}, bf16[560,512]{1,0:T(8,128)(2,1)S(1)}, u32[]{:S(2)}, u32[]{:S(2)}) collective-permute-start(bf16[560,512]{1,0:T(8,128)(2,1)S(1)} %shard_map.126), channel_id=1, source_target_pairs={{0,8},{4,12},{8,16},{12,20},{16,24},{20,28},{24,32},{28,36},{32,40... | collective-permute-start | bytes 1720328 | tf_op jit(solution)/shard_map/ppermute | solution.py:350
  53.0 0.7 %copy-start.9 = (bf16[64,16,128]{2,1,0:T(8,128)(2,1)}, bf16[64,16,128]{2,1,0:T(8,128)(2,1)S(1)}, u32[]{:S(2)}) copy-start(bf16[64,16,128]{2,1,0:T(8,128)(2,1)S(1)} %all-to-all-done.1) | copy-start | bytes 786436
  56.7 6.8 %collective-permute-start.6 = (f32[8,256]{1,0:T(8,128)}, f32[8,256]{1,0:T(8,128)S(1)}, u32[]{:S(2)}, u32[]{:S(2)}) collective-permute-start(f32[8,256]{1,0:T(8,128)} %get-tuple-element.52.s0), channel_id=1, source_target_pairs={{0,3},{1,0},{2,1},{3,2},{4,7},{5,4},{6,5},{7,6},{8,11},{9,8},{10,9... | collective-permute-start | bytes 24584 | tf_op jit(solution)/shard_map/ppermute | solution.py:358
  59.1 4.3 %collective-permute-start.5 = (f32[8,256]{1,0:T(8,128)}, f32[8,256]{1,0:T(8,128)S(1)}, u32[]{:S(2)}, u32[]{:S(2)}) collective-permute-start(f32[8,256]{1,0:T(8,128)} %get-tuple-element.52.s0), channel_id=1, source_target_pairs={{0,2},{1,3},{2,0},{3,1},{4,6},{5,7},{6,4},{7,5},{8,10},{9,11},{10,... | collective-permute-start | bytes 24584 | tf_op jit(solution)/shard_map/ppermute | solution.py:358
  59.7 3.9 %collective-permute-start.4 = (f32[8,256]{1,0:T(8,128)}, f32[8,256]{1,0:T(8,128)S(1)}, u32[]{:S(2)}, u32[]{:S(2)}) collective-permute-start(f32[8,256]{1,0:T(8,128)} %get-tuple-element.52.s0), channel_id=1, source_target_pairs={{0,1},{1,2},{2,3},{3,0},{4,5},{5,6},{6,7},{7,4},{8,9},{9,10},{10,1... | collective-permute-start | bytes 24584 | tf_op jit(solution)/shard_map/ppermute | solution.py:358
  62.8 3.5 %copy-start.3 = (f32[256,1024]{1,0:T(8,128)S(1)}, f32[256,1024]{1,0:T(8,128)}, u32[]{:S(2)}) copy-start(f32[256,1024]{1,0:T(8,128)} %get-tuple-element.51.heads) | copy-start | bytes 3145732
  62.8 3.5 %copy-start.4 = (bf16[256,1024]{1,0:T(8,128)(2,1)S(1)}, bf16[256,1024]{1,0:T(8,128)(2,1)}, u32[]{:S(2)}) copy-start(bf16[256,1024]{1,0:T(8,128)(2,1)} %gate.1) | copy-start | bytes 1572868
  62.8 3.5 %copy-start.5 = (f32[8,256]{1,0:T(8,128)S(1)}, f32[8,256]{1,0:T(8,128)}, u32[]{:S(2)}) copy-start(f32[8,256]{1,0:T(8,128)} %get-tuple-element.52.s0) | copy-start | bytes 24580
  62.8 3.5 %copy-start.7 = (f32[1024]{0:T(1024)S(1)}, f32[1024]{0:T(1024)}, u32[]{:S(2)}) copy-start(f32[1024]{0:T(1024)} %param.15) | copy-start | bytes 12292
  63.6 4.0 %collective-permute-start.7 = (bf16[256,512]{1,0:T(8,128)(2,1)S(1)}, bf16[256,512]{1,0:T(8,128)(2,1)S(1)}, u32[]{:S(2)}, u32[]{:S(2)}) collective-permute-start(bf16[256,512]{1,0:T(8,128)(2,1)S(1)} %get-tuple-element.63), channel_id=1, source_target_pairs={{0,4},{4,0},{8,12},{12,8},{16,20},{20,16},{24,28},{28,24},{32,36},... | collective-permute-start | bytes 786440 | tf_op jit(solution)/shard_map/ppermute | solution.py:354

commit v11 on v10

--- a/solution.py
+++ b/solution.py
@@ -63,7 +63,7 @@
 
 
 def start_body(
-    index, docs, doc_row, rate_hbm, mask, k_hbm, v_hbm, sq, sk, sv, first, out, sent, own, rate, k, v, packed, rate_sem, sems
+    index, docs, doc_row, rate_hbm, mask, k_hbm, v_hbm, sq, sk, sv, first, out, sent, rate, k, v, packed, rate_sem, sems
 ):
     other = 1 - index[0] % 2
     copies = [pltpu.make_async_copy(rate_hbm, rate, rate_sem)]
@@ -85,7 +85,6 @@
     reach = (doc_row[...] == document) & (lane < query + line) & (mask[...] == 1)
     flags = jnp.where(reach, 1.0, 0.0)
     flags = jnp.concatenate([flags, jnp.zeros((14, NBLK), f32)], axis=0)
-    own[...] = flags
     flags = flags.astype(bf16)
     packed[...] = jnp.concatenate([flags] * 4, axis=1)
     copies.append(pltpu.make_async_copy(packed, sent.at[3 * ROWS :, :], sems.at[LOCAL + 3]))
@@ -156,7 +155,7 @@
     return pl.ds(pl.multiple_of(c * HALF, HALF), HALF)
 
 
-def gather_body(index, flags_own, q, k, v, other, far_q, head, tail, theirs, packed, sems):
+def gather_body(index, sent, q, k, v, other, far_q, head, tail, ours, theirs, packed, sems):
     core = index[0] % 2
 
     def put(source, target, at):
@@ -192,8 +191,11 @@
 
     fetch = put(other.at[3 * ROWS :, :NBLK], theirs, 8)
     fetch.start()
+    fetch_own = put(sent.at[3 * ROWS :, :NBLK], ours, 10)
+    fetch_own.start()
     fetch.wait()
-    own = flags_own[:2, :]
+    fetch_own.wait()
+    own = ours[...].astype(f32)[:2]
     arrived = theirs[...].astype(f32)[:2]
     first = jnp.where(core == 0, own, arrived)
     second = jnp.where(core == 0, arrived, own)
@@ -377,9 +379,9 @@
     narrow = like((ROWS, WIDTH), bf16)
 
     anywhere = pl.BlockSpec(memory_space=pl.ANY)
-    first, state, sent, own_flags = call(
+    first, state, sent = call(
         start_body,
-        [like((WIDTH, HD), f32), like((WIDTH, HD), bf16), like((3 * ROWS + 16, HALF), bf16), like((16, NBLK), f32)],
+        [like((WIDTH, HD), f32), like((WIDTH, HD), bf16), like((3 * ROWS + 16, HALF), bf16)],
         (
             index, doc_ids, doc_ids.reshape(1, NBLK), decay_rate, block_mask,
             lin_key, lin_value, soft_query, soft_key, soft_value,
@@ -403,12 +405,13 @@
             like((2 * BLK, HALF), bf16),
             like((6 * BLK, HALF), bf16),
         ],
-        (index, own_flags, soft_query, soft_key, soft_value, other),
-        [SMEM, VMEM] + [anywhere] * 4,
+        (index, sent, soft_query, soft_key, soft_value, other),
+        [SMEM] + [anywhere] * 5,
         [
             pltpu.VMEM((16, NBLK), bf16),
+            pltpu.VMEM((16, NBLK), bf16),
             pltpu.VMEM((16, HALF), bf16),
-            pltpu.SemaphoreType.DMA((10,)),
+            pltpu.SemaphoreType.DMA((11,)),
         ],
     )
     tail = shifted(own_tail, 2)

time: 69 us -> 69.3 us (level)
  waiting for transfers between devices: 7.85 us -> 7.14 us
  transfers between devices with their start and end apart: 10 -> 10, of which waited for: 5 -> 4; matrix products, arithmetic and copies ran while one was open for 0% -> 0% of each run, Pallas kernels for 26% -> 26%
where the time goes in v11:
time: 69.3 us; the launch traced here: 68.4 us
  starting transfers between devices  36.2 us (52%)
  Pallas kernels  22.3 us (32%)
  waiting for transfers between devices  7.14 us (10%)
  local copies, waits for them, and re-layouts  1.88 us (3%)
  between operations  0.86 us (1%)
    pallas_call x11, Pallas kernels, call(): pl.pallas_call(body, out_shape=outs, in_specs=specs, out_specs=[VMEM] * l...  22.3 us
    all_to_all x1, starting transfers between devices, per_device(): parts = lax.all_to_all(state.reshape(SHARDS, 16, HD), 'seq', 0, 0)  10.3 us
    ppermute x3, starting transfers between devices, shifted(): lax.ppermute(x, 'seq', [(i, i + distance) for i in range(SHARDS) if 0 <=...  8.76 us
    all_to_all x1, starting transfers between devices, per_device(): entering = lax.all_to_all(prefix, 'seq', 0, 0).reshape(WIDTH, HD)  7.75 us
    ppermute x2, starting transfers between devices, swapped(): return lax.ppermute(x, 'seq', [(i, i ^ 1) for i in range(SHARDS)])  5.82 us
    all_to_all x1, waiting for transfers between devices, per_device(): parts = lax.all_to_all(state.reshape(SHARDS, 16, HD), 'seq', 0, 0)  4.41 us
    ppermute x3, starting transfers between devices, turned(): return lax.ppermute(x, 'head', [(i, (i + distance) % 4) for i in range(4)])  3.61 us
    all_to_all x1, waiting for transfers between devices, per_device(): entering = lax.all_to_all(prefix, 'seq', 0, 0).reshape(WIDTH, HD)  1.95 us
  transfers between devices with their start and end apart: 10, of which 4 were waited for; matrix products, arithmetic and copies ran while one was open for 0% of the time, Pallas kernels for 26%

profile of v11, /device:TPU:1, one launch (start us, length us, event | category | flops | bytes accessed | tf_op | source)
XLA Modules:
  0.0 68.4 jit_solution(2767893575358603973)
XLA Ops:
  0.6 0.0 copy-start.1
  0.6 0.0 copy-start.2
  0.7 4.0 %shard_map.122 = (f32[1024,128]{1,0:T(8,128)}, bf16[1024,128]{1,0:T(8,128)(2,1)}, bf16[784,512]{1,0:T(8,128)(2,1)}) custom-call(s32[1]{0:T(128)} %bitcast.index, s32[128]{0:T(128)} %docs.1, s32[1,128]{1,0:T(1,128)} %bitcast.8, f32[8]{0:T(128)} %rate.3, s32[2,128]{1,0:T(2,128)} %mask.1, bf16[256,1024]{1,0:T(8,128)(2,1)} %k.3, bf16[256,1024]{1,0:T(8,128)(2,1)} %v.3, ...), custom_call_target="tpu_custom_call" | custom-call | flops 1 | bytes 1 | tf_op jit(solution)/shard_map/pallas_call | solution.py:33
  4.7 0.0 copy-start
  4.7 3.3 %collective-permute-start = (bf16[784,512]{1,0:T(8,128)(2,1)}, bf16[784,512]{1,0:T(8,128)(2,1)S(1)}, u32[]{:S(2)}, u32[]{:S(2)}) collective-permute-start(bf16[784,512]{1,0:T(8,128)(2,1)} %get-tuple-element.32.sent), channel_id=1, source_target_pairs={{0,4},{4,0},{8,12},{12,8},{16,20},{20,16},{24,28},{28,24},{32,36},... | collective-permute-start | bytes 2408456 | tf_op jit(solution)/shard_map/ppermute | solution.py:356
  8.0 10.3 %all-to-all-start = ((bf16[64,16,128]{2,1,0:T(8,128)(2,1)}), bf16[64,16,128]{2,1,0:T(8,128)(2,1)}, u32[]{:S(2)}, u32[]{:S(2)}) async-start(bf16[64,16,128]{2,1,0:T(8,128)(2,1)} %bitcast.7), calls=%async_computation | async-start | bytes 524288 | tf_op jit(solution)/shard_map/all_to_all | solution.py:400
  18.3 0.0 collective-permute-done.other
  18.3 0.0 copy-done.1
  18.3 0.0 copy-done.2
  18.3 0.0 copy-done
  18.3 0.0 copy-start.4
  18.3 1.1 %copy-done.4 = bf16[784,512]{1,0:T(8,128)(2,1)S(1)} copy-done((bf16[784,512]{1,0:T(8,128)(2,1)S(1)}, bf16[784,512]{1,0:T(8,128)(2,1)}, u32[]{:S(2)}) %copy-start.4) | copy-done | bytes 802840
  19.4 1.7 %shard_map.123 = (bf16[528,512]{1,0:T(8,128)(2,1)}, bf16[256,512]{1,0:T(8,128)(2,1)S(1)}, bf16[768,512]{1,0:T(8,128)(2,1)S(1)}) custom-call(s32[1]{0:T(128)} %bitcast.index, bf16[784,512]{1,0:T(8,128)(2,1)S(1)} %copy-done.4, bf16[256,1024]{1,0:T(8,128)(2,1)S(1)} %copy-done, bf16[256,1024]{1,0:T(8,128)(2,1)S(1)} %copy-done.1, ...), custom_call_target="tpu_custom_call" | custom-call | flops 1 | bytes 1 | tf_op jit(solution)/shard_map/pallas_call | solution.py:33
  21.2 0.0 copy-start.8
  21.2 3.3 %collective-permute-start.2 = (bf16[768,512]{1,0:T(8,128)(2,1)S(1)}, bf16[768,512]{1,0:T(8,128)(2,1)S(1)}, u32[]{:S(2)}, u32[]{:S(2)}) collective-permute-start(bf16[768,512]{1,0:T(8,128)(2,1)S(1)} %get-tuple-element.34.tail), channel_id=1, source_target_pairs={{0,8},{4,12},{8,16},{12,20},{16,24},{20,28},{24,32},{28,36},{32,40... | collective-permute-start | bytes 2359304 | tf_op jit(solution)/shard_map/ppermute | solution.py:352
  24.5 1.3 %collective-permute-start.1 = (bf16[528,512]{1,0:T(8,128)(2,1)}, bf16[528,512]{1,0:T(8,128)(2,1)S(1)}, u32[]{:S(2)}, u32[]{:S(2)}) collective-permute-start(bf16[528,512]{1,0:T(8,128)(2,1)} %get-tuple-element.33.q), channel_id=1, source_target_pairs={{8,0},{12,4},{16,8},{20,12},{24,16},{28,20},{32,24},{36,28},{40,32... | collective-permute-start | bytes 1622024 | tf_op jit(solution)/shard_map/ppermute | solution.py:352
  25.8 4.4 %all-to-all-done.parts = bf16[64,16,128]{2,1,0:T(8,128)(2,1)} async-done(((bf16[64,16,128]{2,1,0:T(8,128)(2,1)}), bf16[64,16,128]{2,1,0:T(8,128)(2,1)}, u32[]{:S(2)}, u32[]{:S(2)}) %all-to-all-start) | async-done | bytes 262176 | tf_op jit(solution)/shard_map/all_to_all | solution.py:400
  30.2 0.0 copy-done.8
  30.2 1.8 %shard_map.124 = bf16[64,16,128]{2,1,0:T(8,128)(2,1)} custom-call(s32[1]{0:T(128)} %bitcast.index, f32[8]{0:T(128)S(1)} %copy-done.8, bf16[64,16,128]{2,1,0:T(8,128)(2,1)} %all-to-all-done.parts), custom_call_target="tpu_custom_call" | custom-call | flops 1500000000 | bytes 1 | tf_op jit(solution)/shard_map/pallas_call | solution.py:33
  32.0 7.8 %all-to-all-start.1 = ((bf16[64,16,128]{2,1,0:T(8,128)(2,1)}), bf16[64,16,128]{2,1,0:T(8,128)(2,1)S(1)}, u32[]{:S(2)}, u32[]{:S(2)}) async-start(bf16[64,16,128]{2,1,0:T(8,128)(2,1)} %shard_map.124), calls=%async_computation.1 | async-start | bytes 524288 | tf_op jit(solution)/shard_map/all_to_all | solution.py:428
  39.8 0.7 collective-permute-done.1.q
  40.5 1.6 %shard_map.125 = (f32[512,512]{1,0:T(8,128)S(1)}, f32[512,128]{1,0:T(8,128)S(1)}, f32[512,128]{1,0:T(8,128)S(1)}) custom-call(s32[1]{0:T(128)} %bitcast.index, bf16[528,512]{1,0:T(8,128)(2,1)S(1)} %collective-permute-done.1.q, bf16[256,512]{1,0:T(8,128)(2,1)S(1)} %get-tuple-element.51.head, bf16[768,512]{1,0:T(8,128)(2,1)S(1)} %get-tuple-element.34.tail), custom_call_target="tpu_custom_call" | custom-call | flops 1 | bytes 1 | tf_op jit(solution)/shard_map/pallas_call | solution.py:33
  42.1 0.0 collective-permute-done.2.tail
  42.1 1.7 %shard_map.126 = bf16[560,512]{1,0:T(8,128)(2,1)S(1)} custom-call(s32[1]{0:T(128)} %bitcast.index, bf16[528,512]{1,0:T(8,128)(2,1)S(1)} %collective-permute-done.1.q, bf16[768,512]{1,0:T(8,128)(2,1)S(1)} %collective-permute-done.2.tail, f32[512,512]{1,0:T(8,128)S(1)} %get-tuple-element.38.done, f32[512,128]{1,0:T(8,128)S(1)} %get-tuple-element.39.tops, ...), custom_call_target="tpu_custom_call" | custom-call | flops 1 | bytes 1 | tf_op jit(solution)/shard_map/pallas_call | solution.py:33
  43.8 4.1 %collective-permute-start.3 = (bf16[560,512]{1,0:T(8,128)(2,1)S(1)}, bf16[560,512]{1,0:T(8,128)(2,1)S(1)}, u32[]{:S(2)}, u32[]{:S(2)}) collective-permute-start(bf16[560,512]{1,0:T(8,128)(2,1)S(1)} %shard_map.126), channel_id=1, source_target_pairs={{0,8},{4,12},{8,16},{12,20},{16,24},{20,28},{24,32},{28,36},{32,40... | collective-permute-start | bytes 1720328 | tf_op jit(solution)/shard_map/ppermute | solution.py:352
  47.9 3.3 %shard_map.127 = (f32[256,1024]{1,0:T(8,128)}, f32[8,128]{1,0:T(8,128)}) custom-call(f32[8]{0:T(128)} %rate.3, bf16[256,1024]{1,0:T(8,128)(2,1)} %q.3, bf16[256,1024]{1,0:T(8,128)(2,1)} %k.3, bf16[256,1024]{1,0:T(8,128)(2,1)} %v.3), custom_call_target="tpu_custom_call" | custom-call | flops 1 | bytes 1 | tf_op jit(solution)/shard_map/pallas_call | solution.py:33
  51.2 1.9 %all-to-all-done.1 = bf16[64,16,128]{2,1,0:T(8,128)(2,1)S(1)} async-done(((bf16[64,16,128]{2,1,0:T(8,128)(2,1)}), bf16[64,16,128]{2,1,0:T(8,128)(2,1)S(1)}, u32[]{:S(2)}, u32[]{:S(2)}) %all-to-all-start.1) | async-done | bytes 262176 | tf_op jit(solution)/shard_map/all_to_all | solution.py:428
  53.2 0.7 %copy-done.9 = bf16[64,16,128]{2,1,0:T(8,128)(2,1)} copy-done((bf16[64,16,128]{2,1,0:T(8,128)(2,1)}, bf16[64,16,128]{2,1,0:T(8,128)(2,1)S(1)}, u32[]{:S(2)}) %copy-start.9) | copy-done | bytes 262168
  53.9 3.0 %shard_map.128 = (f32[256,1024]{1,0:T(8,128)}, f32[8,256]{1,0:T(8,128)}) custom-call(f32[8,128]{1,0:T(8,128)} %get-tuple-element.43.rates, f32[256,1024]{1,0:T(8,128)} %get-tuple-element.44.inner, bf16[256,1024]{1,0:T(8,128)(2,1)} %q.3, f32[1024,128]{1,0:T(8,128)} %get-tuple-element.45.first, bf16[1024,128]{1,0:T(8,128)(2,1)} %bitcast.6), custom_call_target="tpu_custom_call" | custom-call | flops 10000000000 | bytes 1 | tf_op jit(solution)/shard_map/pallas_call | solution.py:33
  56.8 2.5 %collective-permute-start.6 = (f32[8,256]{1,0:T(8,128)}, f32[8,256]{1,0:T(8,128)S(1)}, u32[]{:S(2)}, u32[]{:S(2)}) collective-permute-start(f32[8,256]{1,0:T(8,128)} %get-tuple-element.50.s0), channel_id=1, source_target_pairs={{0,3},{1,0},{2,1},{3,2},{4,7},{5,4},{6,5},{7,6},{8,11},{9,8},{10,9... | collective-permute-start | bytes 24584 | tf_op jit(solution)/shard_map/ppermute | solution.py:360
  59.3 0.5 collective-permute-start.5
  59.8 0.6 collective-permute-start.4
  60.5 2.5 %shard_map.129 = (f32[512,512]{1,0:T(8,128)S(1)}, f32[512,128]{1,0:T(8,128)S(1)}, f32[512,128]{1,0:T(8,128)S(1)}) custom-call(s32[1]{0:T(128)} %bitcast.index, bf16[528,512]{1,0:T(8,128)(2,1)} %get-tuple-element.33.q, bf16[256,512]{1,0:T(8,128)(2,1)S(1)} %get-tuple-element.51.head, bf16[768,512]{1,0:T(8,128)(2,1)S(1)} %get-tuple-element.34.tail), custom_call_target="tpu_custom_call" | custom-call | flops 1 | bytes 1 | tf_op jit(solution)/shard_map/pallas_call | solution.py:33
  63.0 0.0 collective-permute-done.3.far
  63.0 0.0 copy-start.3
  63.0 0.0 copy-start.5
  63.0 0.0 copy-start.6
  63.0 0.0 copy-start.7
  63.0 0.6 shard_map.130
  63.7 0.0 collective-permute-done.6.s3
  63.7 0.0 collective-permute-done.5.s2
  63.7 0.1 collective-permute-done.4.s1
  63.8 2.5 %collective-permute-start.7 = (bf16[256,512]{1,0:T(8,128)(2,1)S(1)}, bf16[256,512]{1,0:T(8,128)(2,1)S(1)}, u32[]{:S(2)}, u32[]{:S(2)}) collective-permute-start(bf16[256,512]{1,0:T(8,128)(2,1)S(1)} %get-tuple-element.61), channel_id=1, source_target_pairs={{0,4},{4,0},{8,12},{12,8},{16,20},{20,16},{24,28},{28,24},{32,36},... | collective-permute-start | bytes 786440 | tf_op jit(solution)/shard_map/ppermute | solution.py:356
  66.3 0.0 copy-done.3
  66.3 0.0 copy-done.6
  66.3 1.3 %shard_map.131 = bf16[256,1024]{1,0:T(8,128)(2,1)} custom-call(f32[256,1024]{1,0:T(8,128)S(1)} %copy-done.3, bf16[256,1024]{1,0:T(8,128)(2,1)S(1)} %copy-done.5, f32[1,1024]{1,0:T(1,128)S(1)} %bitcast.5, f32[8,256]{1,0:T(8,128)S(1)} %copy-done.6, f32[8,256]{1,0:T(8,128)S(1)} %collective-permute-done.4.s1, f32[8,256]{1,0:T(8,128)S(1)} %collective-permute-done.5.s2, ...), custom_call_target="tpu_custom_call" | custom-call | flops 1 | bytes 1 | tf_op jit(solution)/shard_map/pallas_call | solution.py:33
  67.6 0.0 collective-permute-done.7.other
  67.6 0.8 %shard_map.132 = bf16[256,1024]{1,0:T(8,128)(2,1)} custom-call(s32[1]{0:T(128)} %bitcast.index, bf16[256,512]{1,0:T(8,128)(2,1)S(1)} %get-tuple-element.60.mine, bf16[256,512]{1,0:T(8,128)(2,1)S(1)} %collective-permute-done.7.other), custom_call_target="tpu_custom_call" | custom-call | flops 1 | bytes 1 | tf_op jit(solution)/shard_map/pallas_call | solution.py:33
  (3 shorter events, 0.0 us)
Async XLA Ops:
  0.6 17.6 %copy-start.1 = (bf16[256,1024]{1,0:T(8,128)(2,1)S(1)}, bf16[256,1024]{1,0:T(8,128)(2,1)}, u32[]{:S(2)}) copy-start(bf16[256,1024]{1,0:T(8,128)(2,1)} %k.2) | copy-start | bytes 1572868
  0.6 17.6 %copy-start.2 = (bf16[256,1024]{1,0:T(8,128)(2,1)S(1)}, bf16[256,1024]{1,0:T(8,128)(2,1)}, u32[]{:S(2)}) copy-start(bf16[256,1024]{1,0:T(8,128)(2,1)} %v.2) | copy-start | bytes 1572868
  4.7 13.6 %copy-start = (bf16[256,1024]{1,0:T(8,128)(2,1)S(1)}, bf16[256,1024]{1,0:T(8,128)(2,1)}, u32[]{:S(2)}) copy-start(bf16[256,1024]{1,0:T(8,128)(2,1)} %q.1) | copy-start | bytes 1572868
  4.7 13.6 %collective-permute-start = (bf16[784,512]{1,0:T(8,128)(2,1)}, bf16[784,512]{1,0:T(8,128)(2,1)S(1)}, u32[]{:S(2)}, u32[]{:S(2)}) collective-permute-start(bf16[784,512]{1,0:T(8,128)(2,1)} %get-tuple-element.32.sent), channel_id=1, source_target_pairs={{0,4},{4,0},{8,12},{12,8},{16,20},{20,16},{24,28},{28,24},{32,36},... | collective-permute-start | bytes 2408456 | tf_op jit(solution)/shard_map/ppermute | solution.py:356
  8.0 22.2 %all-to-all-start = ((bf16[64,16,128]{2,1,0:T(8,128)(2,1)}), bf16[64,16,128]{2,1,0:T(8,128)(2,1)}, u32[]{:S(2)}, u32[]{:S(2)}) async-start(bf16[64,16,128]{2,1,0:T(8,128)(2,1)} %bitcast.7), calls=%async_computation | async-start | bytes 524288 | tf_op jit(solution)/shard_map/all_to_all | solution.py:400
  18.3 1.1 %copy-start.4 = (bf16[784,512]{1,0:T(8,128)(2,1)S(1)}, bf16[784,512]{1,0:T(8,128)(2,1)}, u32[]{:S(2)}) copy-start(bf16[784,512]{1,0:T(8,128)(2,1)} %get-tuple-element.32.sent) | copy-start | bytes 2408452
  21.2 9.1 %copy-start.8 = (f32[8]{0:T(128)S(1)}, f32[8]{0:T(128)}, u32[]{:S(2)}) copy-start(f32[8]{0:T(128)} %rate.3) | copy-start | bytes 100
  21.2 21.0 %collective-permute-start.2 = (bf16[768,512]{1,0:T(8,128)(2,1)S(1)}, bf16[768,512]{1,0:T(8,128)(2,1)S(1)}, u32[]{:S(2)}, u32[]{:S(2)}) collective-permute-start(bf16[768,512]{1,0:T(8,128)(2,1)S(1)} %get-tuple-element.34.tail), channel_id=1, source_target_pairs={{0,8},{4,12},{8,16},{12,20},{16,24},{20,28},{24,32},{28,36},{32,40... | collective-permute-start | bytes 2359304 | tf_op jit(solution)/shard_map/ppermute | solution.py:352
  24.5 16.0 %collective-permute-start.1 = (bf16[528,512]{1,0:T(8,128)(2,1)}, bf16[528,512]{1,0:T(8,128)(2,1)S(1)}, u32[]{:S(2)}, u32[]{:S(2)}) collective-permute-start(bf16[528,512]{1,0:T(8,128)(2,1)} %get-tuple-element.33.q), channel_id=1, source_target_pairs={{8,0},{12,4},{16,8},{20,12},{24,16},{28,20},{32,24},{36,28},{40,32... | collective-permute-start | bytes 1622024 | tf_op jit(solution)/shard_map/ppermute | solution.py:352
  32.0 21.1 %all-to-all-start.1 = ((bf16[64,16,128]{2,1,0:T(8,128)(2,1)}), bf16[64,16,128]{2,1,0:T(8,128)(2,1)S(1)}, u32[]{:S(2)}, u32[]{:S(2)}) async-start(bf16[64,16,128]{2,1,0:T(8,128)(2,1)} %shard_map.124), calls=%async_computation.1 | async-start | bytes 524288 | tf_op jit(solution)/shard_map/all_to_all | solution.py:428
  43.8 19.2 %collective-permute-start.3 = (bf16[560,512]{1,0:T(8,128)(2,1)S(1)}, bf16[560,512]{1,0:T(8,128)(2,1)S(1)}, u32[]{:S(2)}, u32[]{:S(2)}) collective-permute-start(bf16[560,512]{1,0:T(8,128)(2,1)S(1)} %shard_map.126), channel_id=1, source_target_pairs={{0,8},{4,12},{8,16},{12,20},{16,24},{20,28},{24,32},{28,36},{32,40... | collective-permute-start | bytes 1720328 | tf_op jit(solution)/shard_map/ppermute | solution.py:352
  53.2 0.7 %copy-start.9 = (bf16[64,16,128]{2,1,0:T(8,128)(2,1)}, bf16[64,16,128]{2,1,0:T(8,128)(2,1)S(1)}, u32[]{:S(2)}) copy-start(bf16[64,16,128]{2,1,0:T(8,128)(2,1)S(1)} %all-to-all-done.1) | copy-start | bytes 786436
  56.8 6.8 %collective-permute-start.6 = (f32[8,256]{1,0:T(8,128)}, f32[8,256]{1,0:T(8,128)S(1)}, u32[]{:S(2)}, u32[]{:S(2)}) collective-permute-start(f32[8,256]{1,0:T(8,128)} %get-tuple-element.50.s0), channel_id=1, source_target_pairs={{0,3},{1,0},{2,1},{3,2},{4,7},{5,4},{6,5},{7,6},{8,11},{9,8},{10,9... | collective-permute-start | bytes 24584 | tf_op jit(solution)/shard_map/ppermute | solution.py:360
  59.3 4.3 %collective-permute-start.5 = (f32[8,256]{1,0:T(8,128)}, f32[8,256]{1,0:T(8,128)S(1)}, u32[]{:S(2)}, u32[]{:S(2)}) collective-permute-start(f32[8,256]{1,0:T(8,128)} %get-tuple-element.50.s0), channel_id=1, source_target_pairs={{0,2},{1,3},{2,0},{3,1},{4,6},{5,7},{6,4},{7,5},{8,10},{9,11},{10,... | collective-permute-start | bytes 24584 | tf_op jit(solution)/shard_map/ppermute | solution.py:360
  59.8 3.9 %collective-permute-start.4 = (f32[8,256]{1,0:T(8,128)}, f32[8,256]{1,0:T(8,128)S(1)}, u32[]{:S(2)}, u32[]{:S(2)}) collective-permute-start(f32[8,256]{1,0:T(8,128)} %get-tuple-element.50.s0), channel_id=1, source_target_pairs={{0,1},{1,2},{2,3},{3,0},{4,5},{5,6},{6,7},{7,4},{8,9},{9,10},{10,1... | collective-permute-start | bytes 24584 | tf_op jit(solution)/shard_map/ppermute | solution.py:360
  63.0 3.3 %copy-start.3 = (f32[256,1024]{1,0:T(8,128)S(1)}, f32[256,1024]{1,0:T(8,128)}, u32[]{:S(2)}) copy-start(f32[256,1024]{1,0:T(8,128)} %get-tuple-element.49.heads) | copy-start | bytes 3145732
  63.0 3.3 %copy-start.5 = (bf16[256,1024]{1,0:T(8,128)(2,1)S(1)}, bf16[256,1024]{1,0:T(8,128)(2,1)}, u32[]{:S(2)}) copy-start(bf16[256,1024]{1,0:T(8,128)(2,1)} %gate.1) | copy-start | bytes 1572868
  63.0 3.3 %copy-start.6 = (f32[8,256]{1,0:T(8,128)S(1)}, f32[8,256]{1,0:T(8,128)}, u32[]{:S(2)}) copy-start(f32[8,256]{1,0:T(8,128)} %get-tuple-element.50.s0) | copy-start | bytes 24580
  63.0 3.3 %copy-start.7 = (f32[1024]{0:T(1024)S(1)}, f32[1024]{0:T(1024)}, u32[]{:S(2)}) copy-start(f32[1024]{0:T(1024)} %param.15) | copy-start | bytes 12292
  63.8 3.8 %collective-permute-start.7 = (bf16[256,512]{1,0:T(8,128)(2,1)S(1)}, bf16[256,512]{1,0:T(8,128)(2,1)S(1)}, u32[]{:S(2)}, u32[]{:S(2)}) collective-permute-start(bf16[256,512]{1,0:T(8,128)(2,1)S(1)} %get-tuple-element.61), channel_id=1, source_target_pairs={{0,4},{4,0},{8,12},{12,8},{16,20},{20,16},{24,28},{28,24},{32,36},... | collective-permute-start | bytes 786440 | tf_op jit(solution)/shard_map/ppermute | solution.py:356

commit v12 on v10

--- a/solution.py
+++ b/solution.py
@@ -63,7 +63,7 @@
 
 
 def start_body(
-    index, docs, doc_row, rate_hbm, mask, k_hbm, v_hbm, sq, sk, sv, first, out, sent, own, rate, k, v, packed, rate_sem, sems
+    index, docs, doc_row, rate_hbm, mask, k_hbm, v_hbm, sq, sk, sv, first, out, sent, rate, k, v, packed, rate_sem, sems
 ):
     other = 1 - index[0] % 2
     copies = [pltpu.make_async_copy(rate_hbm, rate, rate_sem)]
@@ -84,9 +84,8 @@
     document = jnp.where(line == 0, docs[query], docs[query + 1])
     reach = (doc_row[...] == document) & (lane < query + line) & (mask[...] == 1)
     flags = jnp.where(reach, 1.0, 0.0)
-    flags = jnp.concatenate([flags, jnp.zeros((14, NBLK), f32)], axis=0)
-    own[...] = flags
-    flags = flags.astype(bf16)
+    ids = doc_row[...].astype(f32)
+    flags = jnp.concatenate([flags, ids, jnp.zeros((13, NBLK), f32)], axis=0).astype(bf16)
     packed[...] = jnp.concatenate([flags] * 4, axis=1)
     copies.append(pltpu.make_async_copy(packed, sent.at[3 * ROWS :, :], sems.at[LOCAL + 3]))
     copies[-1].start()
@@ -156,7 +155,7 @@
     return pl.ds(pl.multiple_of(c * HALF, HALF), HALF)
 
 
-def gather_body(index, flags_own, q, k, v, other, far_q, head, tail, theirs, packed, sems):
+def gather_body(index, mask, q, k, v, other, far_q, head, tail, theirs, packed, sems):
     core = index[0] % 2
 
     def put(source, target, at):
@@ -193,8 +192,15 @@
     fetch = put(other.at[3 * ROWS :, :NBLK], theirs, 8)
     fetch.start()
     fetch.wait()
-    own = flags_own[:2, :]
-    arrived = theirs[...].astype(f32)[:2]
+    arrived = theirs[...].astype(f32)
+    ids = arrived[2:3, :]
+    line = lax.broadcasted_iota(jnp.int32, (2, NBLK), 0)
+    lane = lax.broadcasted_iota(jnp.int32, (2, NBLK), 1)
+    query = 2 * index[0] + line
+    document = jnp.sum(jnp.where(lane == query, ids, 0.0), axis=1, keepdims=True)
+    reach = (ids == document) & (lane < query) & (mask[...] == 1)
+    own = jnp.where(reach, 1.0, 0.0)
+    arrived = arrived[:2, :]
     first = jnp.where(core == 0, own, arrived)
     second = jnp.where(core == 0, arrived, own)
     rows = jnp.concatenate([first, second, jnp.zeros((12, NBLK), f32)], axis=0)
@@ -377,9 +383,9 @@
     narrow = like((ROWS, WIDTH), bf16)
 
     anywhere = pl.BlockSpec(memory_space=pl.ANY)
-    first, state, sent, own_flags = call(
+    first, state, sent = call(
         start_body,
-        [like((WIDTH, HD), f32), like((WIDTH, HD), bf16), like((3 * ROWS + 16, HALF), bf16), like((16, NBLK), f32)],
+        [like((WIDTH, HD), f32), like((WIDTH, HD), bf16), like((3 * ROWS + 16, HALF), bf16)],
         (
             index, doc_ids, doc_ids.reshape(1, NBLK), decay_rate, block_mask,
             lin_key, lin_value, soft_query, soft_key, soft_value,
@@ -403,7 +409,7 @@
             like((2 * BLK, HALF), bf16),
             like((6 * BLK, HALF), bf16),
         ],
-        (index, own_flags, soft_query, soft_key, soft_value, other),
+        (index, block_mask, soft_query, soft_key, soft_value, other),
         [SMEM, VMEM] + [anywhere] * 4,
         [
             pltpu.VMEM((16, NBLK), bf16),

time: 69 us -> 68.7 us (level)
  starting transfers between devices: 36 us -> 35.1 us
  waiting for transfers between devices: 7.85 us -> 8.57 us
where the time goes in v12:
time: 68.7 us; the launch traced here: 67.7 us
  starting transfers between devices  35.1 us (51%)
  Pallas kernels  22.4 us (33%)
  waiting for transfers between devices  8.57 us (12%)
  between operations  0.86 us (1%)
  local copies, waits for them, and re-layouts  0.75 us (1%)
    pallas_call x11, Pallas kernels, call(): pl.pallas_call(body, out_shape=outs, in_specs=specs, out_specs=[VMEM] * l...  22.4 us
    all_to_all x1, starting transfers between devices, per_device(): parts = lax.all_to_all(state.reshape(SHARDS, 16, HD), 'seq', 0, 0)  10.4 us
    ppermute x3, starting transfers between devices, shifted(): lax.ppermute(x, 'seq', [(i, i + distance) for i in range(SHARDS) if 0 <=...  8.77 us
    all_to_all x1, starting transfers between devices, per_device(): entering = lax.all_to_all(prefix, 'seq', 0, 0).reshape(WIDTH, HD)  6.7 us
    ppermute x2, starting transfers between devices, swapped(): return lax.ppermute(x, 'seq', [(i, i ^ 1) for i in range(SHARDS)])  5.71 us
    all_to_all x1, waiting for transfers between devices, per_device(): parts = lax.all_to_all(state.reshape(SHARDS, 16, HD), 'seq', 0, 0)  5.46 us
    ppermute x3, starting transfers between devices, turned(): return lax.ppermute(x, 'head', [(i, (i + distance) % 4) for i in range(4)])  3.61 us
    all_to_all x1, waiting for transfers between devices, per_device(): entering = lax.all_to_all(prefix, 'seq', 0, 0).reshape(WIDTH, HD)  1.85 us
  transfers between devices with their start and end apart: 10, of which 5 were waited for; matrix products, arithmetic and copies ran while one was open for 0% of the time, Pallas kernels for 26%

profile of v12, /device:TPU:1, one launch (start us, length us, event | category | flops | bytes accessed | tf_op | source)
XLA Modules:
  0.0 67.7 jit_solution(1778247581962565544)
XLA Ops:
  0.6 0.0 copy-start.1
  0.6 0.0 copy-start.2
  0.7 4.0 %shard_map.122 = (f32[1024,128]{1,0:T(8,128)}, bf16[1024,128]{1,0:T(8,128)(2,1)}, bf16[784,512]{1,0:T(8,128)(2,1)}) custom-call(s32[1]{0:T(128)} %bitcast.index, s32[128]{0:T(128)} %docs.1, s32[1,128]{1,0:T(1,128)} %bitcast.8, f32[8]{0:T(128)} %rate.3, s32[2,128]{1,0:T(2,128)} %mask.3, bf16[256,1024]{1,0:T(8,128)(2,1)} %k.3, bf16[256,1024]{1,0:T(8,128)(2,1)} %v.3, ...), custom_call_target="tpu_custom_call" | custom-call | flops 1 | bytes 1 | tf_op jit(solution)/shard_map/pallas_call | solution.py:33
  4.7 0.0 copy-start
  4.7 3.3 %collective-permute-start = (bf16[784,512]{1,0:T(8,128)(2,1)}, bf16[784,512]{1,0:T(8,128)(2,1)S(1)}, u32[]{:S(2)}, u32[]{:S(2)}) collective-permute-start(bf16[784,512]{1,0:T(8,128)(2,1)} %get-tuple-element.32), channel_id=1, source_target_pairs={{0,4},{4,0},{8,12},{12,8},{16,20},{20,16},{24,28},{28,24},{32,36},... | collective-permute-start | bytes 2408456 | tf_op jit(solution)/shard_map/ppermute | solution.py:360
  8.0 10.4 %all-to-all-start = ((bf16[64,16,128]{2,1,0:T(8,128)(2,1)}), bf16[64,16,128]{2,1,0:T(8,128)(2,1)}, u32[]{:S(2)}, u32[]{:S(2)}) async-start(bf16[64,16,128]{2,1,0:T(8,128)(2,1)} %bitcast.7), calls=%async_computation | async-start | bytes 524288 | tf_op jit(solution)/shard_map/all_to_all | solution.py:404
  18.4 0.0 collective-permute-done.other
  18.4 0.0 copy-done.1
  18.4 0.0 copy-done.2
  18.4 0.0 copy-done
  18.4 0.0 copy-done.6
  18.4 1.8 %shard_map.123 = (bf16[528,512]{1,0:T(8,128)(2,1)}, bf16[256,512]{1,0:T(8,128)(2,1)S(1)}, bf16[768,512]{1,0:T(8,128)(2,1)S(1)}) custom-call(s32[1]{0:T(128)} %bitcast.index, s32[2,128]{1,0:T(2,128)S(1)} %copy-done.6, bf16[256,1024]{1,0:T(8,128)(2,1)S(1)} %copy-done, bf16[256,1024]{1,0:T(8,128)(2,1)S(1)} %copy-done.1, bf16[256,1024]{1,0:T(8,128)(2,1)S(1)} %copy-done.2, ...), custom_call_target="tpu_custom_call" | custom-call | flops 1 | bytes 1 | tf_op jit(solution)/shard_map/pallas_call | solution.py:33
  20.2 0.0 copy-start.8
  20.2 3.3 %collective-permute-start.2 = (bf16[768,512]{1,0:T(8,128)(2,1)S(1)}, bf16[768,512]{1,0:T(8,128)(2,1)S(1)}, u32[]{:S(2)}, u32[]{:S(2)}) collective-permute-start(bf16[768,512]{1,0:T(8,128)(2,1)S(1)} %get-tuple-element.34.tail), channel_id=1, source_target_pairs={{0,8},{4,12},{8,16},{12,20},{16,24},{20,28},{24,32},{28,36},{32,40... | collective-permute-start | bytes 2359304 | tf_op jit(solution)/shard_map/ppermute | solution.py:356
  23.6 1.3 %collective-permute-start.1 = (bf16[528,512]{1,0:T(8,128)(2,1)}, bf16[528,512]{1,0:T(8,128)(2,1)S(1)}, u32[]{:S(2)}, u32[]{:S(2)}) collective-permute-start(bf16[528,512]{1,0:T(8,128)(2,1)} %get-tuple-element.33.q), channel_id=1, source_target_pairs={{8,0},{12,4},{16,8},{20,12},{24,16},{28,20},{32,24},{36,28},{40,32... | collective-permute-start | bytes 1622024 | tf_op jit(solution)/shard_map/ppermute | solution.py:356
  24.9 5.5 %all-to-all-done.parts = bf16[64,16,128]{2,1,0:T(8,128)(2,1)} async-done(((bf16[64,16,128]{2,1,0:T(8,128)(2,1)}), bf16[64,16,128]{2,1,0:T(8,128)(2,1)}, u32[]{:S(2)}, u32[]{:S(2)}) %all-to-all-start) | async-done | bytes 262176 | tf_op jit(solution)/shard_map/all_to_all | solution.py:404
  30.3 0.0 copy-done.8
  30.3 1.8 %shard_map.124 = bf16[64,16,128]{2,1,0:T(8,128)(2,1)} custom-call(s32[1]{0:T(128)} %bitcast.index, f32[8]{0:T(128)S(1)} %copy-done.8, bf16[64,16,128]{2,1,0:T(8,128)(2,1)} %all-to-all-done.parts), custom_call_target="tpu_custom_call" | custom-call | flops 1500000000 | bytes 1 | tf_op jit(solution)/shard_map/pallas_call | solution.py:33
  32.1 6.7 %all-to-all-start.1 = ((bf16[64,16,128]{2,1,0:T(8,128)(2,1)}), bf16[64,16,128]{2,1,0:T(8,128)(2,1)S(1)}, u32[]{:S(2)}, u32[]{:S(2)}) async-start(bf16[64,16,128]{2,1,0:T(8,128)(2,1)} %shard_map.124), calls=%async_computation.1 | async-start | bytes 524288 | tf_op jit(solution)/shard_map/all_to_all | solution.py:431
  38.8 0.7 collective-permute-done.1.q
  39.5 1.6 %shard_map.125 = (f32[512,512]{1,0:T(8,128)S(1)}, f32[512,128]{1,0:T(8,128)S(1)}, f32[512,128]{1,0:T(8,128)S(1)}) custom-call(s32[1]{0:T(128)} %bitcast.index, bf16[528,512]{1,0:T(8,128)(2,1)S(1)} %collective-permute-done.1.q, bf16[256,512]{1,0:T(8,128)(2,1)S(1)} %get-tuple-element.51.head, bf16[768,512]{1,0:T(8,128)(2,1)S(1)} %get-tuple-element.34.tail), custom_call_target="tpu_custom_call" | custom-call | flops 1 | bytes 1 | tf_op jit(solution)/shard_map/pallas_call | solution.py:33
  41.2 0.5 collective-permute-done.2.tail
  41.7 1.7 %shard_map.126 = bf16[560,512]{1,0:T(8,128)(2,1)S(1)} custom-call(s32[1]{0:T(128)} %bitcast.index, bf16[528,512]{1,0:T(8,128)(2,1)S(1)} %collective-permute-done.1.q, bf16[768,512]{1,0:T(8,128)(2,1)S(1)} %collective-permute-done.2.tail, f32[512,512]{1,0:T(8,128)S(1)} %get-tuple-element.38.done, f32[512,128]{1,0:T(8,128)S(1)} %get-tuple-element.39.tops, ...), custom_call_target="tpu_custom_call" | custom-call | flops 1 | bytes 1 | tf_op jit(solution)/shard_map/pallas_call | solution.py:33
  43.3 4.1 %collective-permute-start.3 = (bf16[560,512]{1,0:T(8,128)(2,1)S(1)}, bf16[560,512]{1,0:T(8,128)(2,1)S(1)}, u32[]{:S(2)}, u32[]{:S(2)}) collective-permute-start(bf16[560,512]{1,0:T(8,128)(2,1)S(1)} %shard_map.126), channel_id=1, source_target_pairs={{0,8},{4,12},{8,16},{12,20},{16,24},{20,28},{24,32},{28,36},{32,40... | collective-permute-start | bytes 1720328 | tf_op jit(solution)/shard_map/ppermute | solution.py:356
  47.5 3.3 %shard_map.127 = (f32[256,1024]{1,0:T(8,128)}, f32[8,128]{1,0:T(8,128)}) custom-call(f32[8]{0:T(128)} %rate.3, bf16[256,1024]{1,0:T(8,128)(2,1)} %q.3, bf16[256,1024]{1,0:T(8,128)(2,1)} %k.3, bf16[256,1024]{1,0:T(8,128)(2,1)} %v.3), custom_call_target="tpu_custom_call" | custom-call | flops 1 | bytes 1 | tf_op jit(solution)/shard_map/pallas_call | solution.py:33
  50.7 1.9 %all-to-all-done.1 = bf16[64,16,128]{2,1,0:T(8,128)(2,1)S(1)} async-done(((bf16[64,16,128]{2,1,0:T(8,128)(2,1)}), bf16[64,16,128]{2,1,0:T(8,128)(2,1)S(1)}, u32[]{:S(2)}, u32[]{:S(2)}) %all-to-all-start.1) | async-done | bytes 262176 | tf_op jit(solution)/shard_map/all_to_all | solution.py:431
  52.6 0.7 %copy-done.9 = bf16[64,16,128]{2,1,0:T(8,128)(2,1)} copy-done((bf16[64,16,128]{2,1,0:T(8,128)(2,1)}, bf16[64,16,128]{2,1,0:T(8,128)(2,1)S(1)}, u32[]{:S(2)}) %copy-start.9) | copy-done | bytes 262168
  53.3 3.0 %shard_map.128 = (f32[256,1024]{1,0:T(8,128)}, f32[8,256]{1,0:T(8,128)}) custom-call(f32[8,128]{1,0:T(8,128)} %get-tuple-element.43.rates, f32[256,1024]{1,0:T(8,128)} %get-tuple-element.44.inner, bf16[256,1024]{1,0:T(8,128)(2,1)} %q.3, f32[1024,128]{1,0:T(8,128)} %get-tuple-element.45.first, bf16[1024,128]{1,0:T(8,128)(2,1)} %bitcast.6), custom_call_target="tpu_custom_call" | custom-call | flops 10000000000 | bytes 1 | tf_op jit(solution)/shard_map/pallas_call | solution.py:33
  56.3 2.5 %collective-permute-start.6 = (f32[8,256]{1,0:T(8,128)}, f32[8,256]{1,0:T(8,128)S(1)}, u32[]{:S(2)}, u32[]{:S(2)}) collective-permute-start(f32[8,256]{1,0:T(8,128)} %get-tuple-element.50.s0), channel_id=1, source_target_pairs={{0,3},{1,0},{2,1},{3,2},{4,7},{5,4},{6,5},{7,6},{8,11},{9,8},{10,9... | collective-permute-start | bytes 24584 | tf_op jit(solution)/shard_map/ppermute | solution.py:364
  58.8 0.5 collective-permute-start.5
  59.3 0.6 collective-permute-start.4
  59.9 2.5 %shard_map.129 = (f32[512,512]{1,0:T(8,128)S(1)}, f32[512,128]{1,0:T(8,128)S(1)}, f32[512,128]{1,0:T(8,128)S(1)}) custom-call(s32[1]{0:T(128)} %bitcast.index, bf16[528,512]{1,0:T(8,128)(2,1)} %get-tuple-element.33.q, bf16[256,512]{1,0:T(8,128)(2,1)S(1)} %get-tuple-element.51.head, bf16[768,512]{1,0:T(8,128)(2,1)S(1)} %get-tuple-element.34.tail), custom_call_target="tpu_custom_call" | custom-call | flops 1 | bytes 1 | tf_op jit(solution)/shard_map/pallas_call | solution.py:33
  62.4 0.0 collective-permute-done.3.far
  62.4 0.0 copy-start.3
  62.4 0.0 copy-start.4
  62.4 0.0 copy-start.5
  62.4 0.0 copy-start.7
  62.4 0.6 shard_map.130
  63.1 0.0 collective-permute-done.6.s3
  63.1 0.0 collective-permute-done.5.s2
  63.1 0.1 collective-permute-done.4.s1
  63.2 2.4 %collective-permute-start.7 = (bf16[256,512]{1,0:T(8,128)(2,1)S(1)}, bf16[256,512]{1,0:T(8,128)(2,1)S(1)}, u32[]{:S(2)}, u32[]{:S(2)}) collective-permute-start(bf16[256,512]{1,0:T(8,128)(2,1)S(1)} %get-tuple-element.61), channel_id=1, source_target_pairs={{0,4},{4,0},{8,12},{12,8},{16,20},{20,16},{24,28},{28,24},{32,36},... | collective-permute-start | bytes 786440 | tf_op jit(solution)/shard_map/ppermute | solution.py:360
  65.6 0.0 copy-done.3
  65.6 0.0 copy-done.4
  65.6 0.0 copy-done.5
  65.6 1.3 %shard_map.131 = bf16[256,1024]{1,0:T(8,128)(2,1)} custom-call(f32[256,1024]{1,0:T(8,128)S(1)} %copy-done.3, bf16[256,1024]{1,0:T(8,128)(2,1)S(1)} %copy-done.4, f32[1,1024]{1,0:T(1,128)S(1)} %bitcast.5, f32[8,256]{1,0:T(8,128)S(1)} %copy-done.5, f32[8,256]{1,0:T(8,128)S(1)} %collective-permute-done.4.s1, f32[8,256]{1,0:T(8,128)S(1)} %collective-permute-done.5.s2, ...), custom_call_target="tpu_custom_call" | custom-call | flops 1 | bytes 1 | tf_op jit(solution)/shard_map/pallas_call | solution.py:33
  66.9 0.0 collective-permute-done.7.other
  66.9 0.8 %shard_map.132 = bf16[256,1024]{1,0:T(8,128)(2,1)} custom-call(s32[1]{0:T(128)} %bitcast.index, bf16[256,512]{1,0:T(8,128)(2,1)S(1)} %get-tuple-element.60.mine, bf16[256,512]{1,0:T(8,128)(2,1)S(1)} %collective-permute-done.7.other), custom_call_target="tpu_custom_call" | custom-call | flops 1 | bytes 1 | tf_op jit(solution)/shard_map/pallas_call | solution.py:33
  (3 shorter events, 0.0 us)
Async XLA Ops:
  0.6 17.7 %copy-start.1 = (bf16[256,1024]{1,0:T(8,128)(2,1)S(1)}, bf16[256,1024]{1,0:T(8,128)(2,1)}, u32[]{:S(2)}) copy-start(bf16[256,1024]{1,0:T(8,128)(2,1)} %k.2) | copy-start | bytes 1572868
  0.6 17.7 %copy-start.2 = (bf16[256,1024]{1,0:T(8,128)(2,1)S(1)}, bf16[256,1024]{1,0:T(8,128)(2,1)}, u32[]{:S(2)}) copy-start(bf16[256,1024]{1,0:T(8,128)(2,1)} %v.2) | copy-start | bytes 1572868
  4.7 13.7 %copy-start = (bf16[256,1024]{1,0:T(8,128)(2,1)S(1)}, bf16[256,1024]{1,0:T(8,128)(2,1)}, u32[]{:S(2)}) copy-start(bf16[256,1024]{1,0:T(8,128)(2,1)} %q.1) | copy-start | bytes 1572868
  4.7 13.7 %collective-permute-start = (bf16[784,512]{1,0:T(8,128)(2,1)}, bf16[784,512]{1,0:T(8,128)(2,1)S(1)}, u32[]{:S(2)}, u32[]{:S(2)}) collective-permute-start(bf16[784,512]{1,0:T(8,128)(2,1)} %get-tuple-element.32), channel_id=1, source_target_pairs={{0,4},{4,0},{8,12},{12,8},{16,20},{20,16},{24,28},{28,24},{32,36},... | collective-permute-start | bytes 2408456 | tf_op jit(solution)/shard_map/ppermute | solution.py:360
  8.0 10.4 %copy-start.6 = (s32[2,128]{1,0:T(2,128)S(1)}, s32[2,128]{1,0:T(2,128)}, u32[]{:S(2)}) copy-start(s32[2,128]{1,0:T(2,128)} %mask.3) | copy-start | bytes 3076
  8.0 22.3 %all-to-all-start = ((bf16[64,16,128]{2,1,0:T(8,128)(2,1)}), bf16[64,16,128]{2,1,0:T(8,128)(2,1)}, u32[]{:S(2)}, u32[]{:S(2)}) async-start(bf16[64,16,128]{2,1,0:T(8,128)(2,1)} %bitcast.7), calls=%async_computation | async-start | bytes 524288 | tf_op jit(solution)/shard_map/all_to_all | solution.py:404
  20.2 10.1 %copy-start.8 = (f32[8]{0:T(128)S(1)}, f32[8]{0:T(128)}, u32[]{:S(2)}) copy-start(f32[8]{0:T(128)} %rate.3) | copy-start | bytes 100
  20.2 21.4 %collective-permute-start.2 = (bf16[768,512]{1,0:T(8,128)(2,1)S(1)}, bf16[768,512]{1,0:T(8,128)(2,1)S(1)}, u32[]{:S(2)}, u32[]{:S(2)}) collective-permute-start(bf16[768,512]{1,0:T(8,128)(2,1)S(1)} %get-tuple-element.34.tail), channel_id=1, source_target_pairs={{0,8},{4,12},{8,16},{12,20},{16,24},{20,28},{24,32},{28,36},{32,40... | collective-permute-start | bytes 2359304 | tf_op jit(solution)/shard_map/ppermute | solution.py:356
  23.6 16.0 %collective-permute-start.1 = (bf16[528,512]{1,0:T(8,128)(2,1)}, bf16[528,512]{1,0:T(8,128)(2,1)S(1)}, u32[]{:S(2)}, u32[]{:S(2)}) collective-permute-start(bf16[528,512]{1,0:T(8,128)(2,1)} %get-tuple-element.33.q), channel_id=1, source_target_pairs={{8,0},{12,4},{16,8},{20,12},{24,16},{28,20},{32,24},{36,28},{40,32... | collective-permute-start | bytes 1622024 | tf_op jit(solution)/shard_map/ppermute | solution.py:356
  32.1 20.4 %all-to-all-start.1 = ((bf16[64,16,128]{2,1,0:T(8,128)(2,1)}), bf16[64,16,128]{2,1,0:T(8,128)(2,1)S(1)}, u32[]{:S(2)}, u32[]{:S(2)}) async-start(bf16[64,16,128]{2,1,0:T(8,128)(2,1)} %shard_map.124), calls=%async_computation.1 | async-start | bytes 524288 | tf_op jit(solution)/shard_map/all_to_all | solution.py:431
  43.3 19.1 %collective-permute-start.3 = (bf16[560,512]{1,0:T(8,128)(2,1)S(1)}, bf16[560,512]{1,0:T(8,128)(2,1)S(1)}, u32[]{:S(2)}, u32[]{:S(2)}) collective-permute-start(bf16[560,512]{1,0:T(8,128)(2,1)S(1)} %shard_map.126), channel_id=1, source_target_pairs={{0,8},{4,12},{8,16},{12,20},{16,24},{20,28},{24,32},{28,36},{32,40... | collective-permute-start | bytes 1720328 | tf_op jit(solution)/shard_map/ppermute | solution.py:356
  52.6 0.7 %copy-start.9 = (bf16[64,16,128]{2,1,0:T(8,128)(2,1)}, bf16[64,16,128]{2,1,0:T(8,128)(2,1)S(1)}, u32[]{:S(2)}) copy-start(bf16[64,16,128]{2,1,0:T(8,128)(2,1)S(1)} %all-to-all-done.1) | copy-start | bytes 786436
  56.3 6.8 %collective-permute-start.6 = (f32[8,256]{1,0:T(8,128)}, f32[8,256]{1,0:T(8,128)S(1)}, u32[]{:S(2)}, u32[]{:S(2)}) collective-permute-start(f32[8,256]{1,0:T(8,128)} %get-tuple-element.50.s0), channel_id=1, source_target_pairs={{0,3},{1,0},{2,1},{3,2},{4,7},{5,4},{6,5},{7,6},{8,11},{9,8},{10,9... | collective-permute-start | bytes 24584 | tf_op jit(solution)/shard_map/ppermute | solution.py:364
  58.8 4.4 %collective-permute-start.5 = (f32[8,256]{1,0:T(8,128)}, f32[8,256]{1,0:T(8,128)S(1)}, u32[]{:S(2)}, u32[]{:S(2)}) collective-permute-start(f32[8,256]{1,0:T(8,128)} %get-tuple-element.50.s0), channel_id=1, source_target_pairs={{0,2},{1,3},{2,0},{3,1},{4,6},{5,7},{6,4},{7,5},{8,10},{9,11},{10,... | collective-permute-start | bytes 24584 | tf_op jit(solution)/shard_map/ppermute | solution.py:364
  59.3 3.9 %collective-permute-start.4 = (f32[8,256]{1,0:T(8,128)}, f32[8,256]{1,0:T(8,128)S(1)}, u32[]{:S(2)}, u32[]{:S(2)}) collective-permute-start(f32[8,256]{1,0:T(8,128)} %get-tuple-element.50.s0), channel_id=1, source_target_pairs={{0,1},{1,2},{2,3},{3,0},{4,5},{5,6},{6,7},{7,4},{8,9},{9,10},{10,1... | collective-permute-start | bytes 24584 | tf_op jit(solution)/shard_map/ppermute | solution.py:364
  62.4 3.2 %copy-start.3 = (f32[256,1024]{1,0:T(8,128)S(1)}, f32[256,1024]{1,0:T(8,128)}, u32[]{:S(2)}) copy-start(f32[256,1024]{1,0:T(8,128)} %get-tuple-element.49.heads) | copy-start | bytes 3145732
  62.4 3.2 %copy-start.4 = (bf16[256,1024]{1,0:T(8,128)(2,1)S(1)}, bf16[256,1024]{1,0:T(8,128)(2,1)}, u32[]{:S(2)}) copy-start(bf16[256,1024]{1,0:T(8,128)(2,1)} %gate.1) | copy-start | bytes 1572868
  62.4 3.2 %copy-start.5 = (f32[8,256]{1,0:T(8,128)S(1)}, f32[8,256]{1,0:T(8,128)}, u32[]{:S(2)}) copy-start(f32[8,256]{1,0:T(8,128)} %get-tuple-element.50.s0) | copy-start | bytes 24580
  62.4 3.2 %copy-start.7 = (f32[1024]{0:T(1024)S(1)}, f32[1024]{0:T(1024)}, u32[]{:S(2)}) copy-start(f32[1024]{0:T(1024)} %param.15) | copy-start | bytes 12292
  63.2 3.7 %collective-permute-start.7 = (bf16[256,512]{1,0:T(8,128)(2,1)S(1)}, bf16[256,512]{1,0:T(8,128)(2,1)S(1)}, u32[]{:S(2)}, u32[]{:S(2)}) collective-permute-start(bf16[256,512]{1,0:T(8,128)(2,1)S(1)} %get-tuple-element.61), channel_id=1, source_target_pairs={{0,4},{4,0},{8,12},{12,8},{16,20},{20,16},{24,28},{28,24},{32,36},... | collective-permute-start | bytes 786440 | tf_op jit(solution)/shard_map/ppermute | solution.py:360

commit v13 on v12

--- a/solution.py
+++ b/solution.py
@@ -19,7 +19,7 @@
 SHARDS = 64
 FILL = -1e30
 PREFIX_COST = 1_500_000_000
-CARRY_COST = 10_000_000_000
+CARRY_COST = 2000000000
 EXP2_SCALE = HD ** (-0.5) * math.log2(math.e)
 
 f32 = jnp.float32
@@ -437,6 +437,14 @@
         [SMEM] + [VMEM] * 3,
         [pltpu.VMEM((4 * BLK, 4 * BLK), f32)],
     )
+    near, tops, sums = call(
+        near_body,
+        tables,
+        (index, far_q, own_head, own_tail),
+        [SMEM] + [VMEM] * 3,
+        [pltpu.VMEM((4 * BLK, 4 * BLK), f32)],
+    )
+    near, tail = lax.optimization_barrier((near, tail))
     (far,) = call(
         far_body,
         [like((4 * BLK + 48, HALF), bf16)],
@@ -459,15 +467,7 @@
         [VMEM] * 5,
         flops=CARRY_COST,
     )
-    heads, own_head = lax.optimization_barrier((heads, own_head))
     others = [turned(squares, d) for d in (1, 2, 3)]
-    near, tops, sums = call(
-        near_body,
-        tables,
-        (index, far_q, own_head, own_tail),
-        [SMEM] + [VMEM] * 3,
-        [pltpu.VMEM((4 * BLK, 4 * BLK), f32)],
-    )
     far, heads = lax.optimization_barrier((far, heads))
     mine, send = call(
         merge_body,

time: 68.7 us -> 69.7 us (1.015)
  the two profiles are of different devices: /device:TPU:1 before, /device:TPU:31 now
where the time goes in v13:
time: 69.7 us; the launch traced here: 69.2 us
  starting transfers between devices  34.3 us (49%)
  Pallas kernels  23.3 us (33%)
  waiting for transfers between devices  9.35 us (13%)
  local copies, waits for them, and re-layouts  1.46 us (2%)
  between operations  0.86 us (1%)
    pallas_call x11, Pallas kernels, call(): pl.pallas_call(body, out_shape=outs, in_specs=specs, out_specs=[VMEM] * l...  23.3 us
    all_to_all x1, starting transfers between devices, per_device(): parts = lax.all_to_all(state.reshape(SHARDS, 16, HD), 'seq', 0, 0)  12.2 us
    ppermute x3, starting transfers between devices, shifted(): lax.ppermute(x, 'seq', [(i, i + distance) for i in range(SHARDS) if 0 <=...  10.2 us
    all_to_all x1, starting transfers between devices, per_device(): entering = lax.all_to_all(prefix, 'seq', 0, 0).reshape(WIDTH, HD)  7.1 us
    ppermute x3, waiting for transfers between devices, shifted(): lax.ppermute(x, 'seq', [(i, i + distance) for i in range(SHARDS) if 0 <=...  6.84 us
    ppermute x2, starting transfers between devices, swapped(): return lax.ppermute(x, 'seq', [(i, i ^ 1) for i in range(SHARDS)])  2.5 us
    all_to_all x1, waiting for transfers between devices, per_device(): parts = lax.all_to_all(state.reshape(SHARDS, 16, HD), 'seq', 0, 0)  2.5 us
    ppermute x3, starting transfers between devices, turned(): return lax.ppermute(x, 'head', [(i, (i + distance) % 4) for i in range(4)])  2.33 us
  transfers between devices with their start and end apart: 10, of which 3 were waited for; matrix products, arithmetic and copies ran while one was open for 0% of the time, Pallas kernels for 27%

profile of v13, /device:TPU:31, one launch (start us, length us, event | category | flops | bytes accessed | tf_op | source)
XLA Modules:
  0.0 69.2 jit_solution(5504717046853847429)
XLA Ops:
  0.6 0.0 copy-start.1
  0.6 0.0 copy-start.2
  0.7 4.0 %shard_map.122 = (f32[1024,128]{1,0:T(8,128)}, bf16[1024,128]{1,0:T(8,128)(2,1)}, bf16[784,512]{1,0:T(8,128)(2,1)}) custom-call(s32[1]{0:T(128)} %bitcast.index, s32[128]{0:T(128)} %docs.1, s32[1,128]{1,0:T(1,128)} %bitcast.7, f32[8]{0:T(128)} %rate.3, s32[2,128]{1,0:T(2,128)} %mask.3, bf16[256,1024]{1,0:T(8,128)(2,1)} %k.3, bf16[256,1024]{1,0:T(8,128)(2,1)} %v.3, ...), custom_call_target="tpu_custom_call" | custom-call | flops 1 | bytes 1 | tf_op jit(solution)/shard_map/pallas_call | solution.py:33
  4.6 0.0 copy-start
  4.7 0.8 %collective-permute-start = (bf16[784,512]{1,0:T(8,128)(2,1)}, bf16[784,512]{1,0:T(8,128)(2,1)S(1)}, u32[]{:S(2)}, u32[]{:S(2)}) collective-permute-start(bf16[784,512]{1,0:T(8,128)(2,1)} %get-tuple-element.32), channel_id=1, source_target_pairs={{0,4},{4,0},{8,12},{12,8},{16,20},{20,16},{24,28},{28,24},{32,36},... | collective-permute-start | bytes 2408456 | tf_op jit(solution)/shard_map/ppermute | solution.py:360
  5.4 12.2 %all-to-all-start = ((bf16[64,16,128]{2,1,0:T(8,128)(2,1)}), bf16[64,16,128]{2,1,0:T(8,128)(2,1)}, u32[]{:S(2)}, u32[]{:S(2)}) async-start(bf16[64,16,128]{2,1,0:T(8,128)(2,1)} %bitcast.6), calls=%async_computation | async-start | bytes 524288 | tf_op jit(solution)/shard_map/all_to_all | solution.py:404
  17.6 0.0 collective-permute-done.other
  17.6 0.0 copy-done.1
  17.6 0.0 copy-done.2
  17.6 0.0 copy-done
  17.6 0.0 copy-done.10
  17.6 1.8 %shard_map.123 = (bf16[528,512]{1,0:T(8,128)(2,1)}, bf16[256,512]{1,0:T(8,128)(2,1)S(1)}, bf16[768,512]{1,0:T(8,128)(2,1)S(1)}) custom-call(s32[1]{0:T(128)} %bitcast.index, s32[2,128]{1,0:T(2,128)S(1)} %copy-done.10, bf16[256,1024]{1,0:T(8,128)(2,1)S(1)} %copy-done, bf16[256,1024]{1,0:T(8,128)(2,1)S(1)} %copy-done.1, bf16[256,1024]{1,0:T(8,128)(2,1)S(1)} %copy-done.2, ...), custom_call_target="tpu_custom_call" | custom-call | flops 1 | bytes 1 | tf_op jit(solution)/shard_map/pallas_call | solution.py:33
  19.4 0.0 copy-start.12
  19.4 3.1 %collective-permute-start.2 = (bf16[768,512]{1,0:T(8,128)(2,1)S(1)}, bf16[768,512]{1,0:T(8,128)(2,1)S(1)}, u32[]{:S(2)}, u32[]{:S(2)}) collective-permute-start(bf16[768,512]{1,0:T(8,128)(2,1)S(1)} %get-tuple-element.37.tail), channel_id=1, source_target_pairs={{0,8},{4,12},{8,16},{12,20},{16,24},{20,28},{24,32},{28,36},{32,40... | collective-permute-start | bytes 2359304 | tf_op jit(solution)/shard_map/ppermute | solution.py:356
  22.6 4.3 %collective-permute-start.1 = (bf16[528,512]{1,0:T(8,128)(2,1)}, bf16[528,512]{1,0:T(8,128)(2,1)S(1)}, u32[]{:S(2)}, u32[]{:S(2)}) collective-permute-start(bf16[528,512]{1,0:T(8,128)(2,1)} %get-tuple-element.33.q), channel_id=1, source_target_pairs={{8,0},{12,4},{16,8},{20,12},{24,16},{28,20},{32,24},{36,28},{40,32... | collective-permute-start | bytes 1622024 | tf_op jit(solution)/shard_map/ppermute | solution.py:356
  26.9 2.5 %all-to-all-done.parts = bf16[64,16,128]{2,1,0:T(8,128)(2,1)} async-done(((bf16[64,16,128]{2,1,0:T(8,128)(2,1)}), bf16[64,16,128]{2,1,0:T(8,128)(2,1)}, u32[]{:S(2)}, u32[]{:S(2)}) %all-to-all-start) | async-done | bytes 262176 | tf_op jit(solution)/shard_map/all_to_all | solution.py:404
  29.4 0.0 copy-done.12
  29.4 1.8 %shard_map.124 = bf16[64,16,128]{2,1,0:T(8,128)(2,1)} custom-call(s32[1]{0:T(128)} %bitcast.index, f32[8]{0:T(128)S(1)} %copy-done.12, bf16[64,16,128]{2,1,0:T(8,128)(2,1)} %all-to-all-done.parts), custom_call_target="tpu_custom_call" | custom-call | flops 1500000000 | bytes 1 | tf_op jit(solution)/shard_map/pallas_call | solution.py:33
  31.2 7.1 %all-to-all-start.1 = ((bf16[64,16,128]{2,1,0:T(8,128)(2,1)}), bf16[64,16,128]{2,1,0:T(8,128)(2,1)}, u32[]{:S(2)}, u32[]{:S(2)}) async-start(bf16[64,16,128]{2,1,0:T(8,128)(2,1)} %shard_map.124), calls=%async_computation.1 | async-start | bytes 524288 | tf_op jit(solution)/shard_map/all_to_all | solution.py:431
  38.3 2.5 %shard_map.125 = (f32[512,512]{1,0:T(8,128)S(1)}, f32[512,128]{1,0:T(8,128)S(1)}, f32[512,128]{1,0:T(8,128)S(1)}) custom-call(s32[1]{0:T(128)} %bitcast.index, bf16[528,512]{1,0:T(8,128)(2,1)} %get-tuple-element.33.q, bf16[256,512]{1,0:T(8,128)(2,1)S(1)} %get-tuple-element.36.head, bf16[768,512]{1,0:T(8,128)(2,1)S(1)} %get-tuple-element.37.tail), custom_call_target="tpu_custom_call" | custom-call | flops 1 | bytes 1 | tf_op jit(solution)/shard_map/pallas_call | solution.py:33
  40.8 0.0 copy-start.5
  40.8 0.7 copy-done.5
  41.5 0.7 %copy-done.7 = f32[512,128]{1,0:T(8,128)} copy-done((f32[512,128]{1,0:T(8,128)}, f32[512,128]{1,0:T(8,128)S(1)}, u32[]{:S(2)}) %copy-start.7) | copy-done | bytes 262168
  42.2 0.0 collective-permute-done.1.q
  42.2 1.6 %shard_map.126 = (f32[512,512]{1,0:T(8,128)S(1)}, f32[512,128]{1,0:T(8,128)S(1)}, f32[512,128]{1,0:T(8,128)S(1)}) custom-call(s32[1]{0:T(128)} %bitcast.index, bf16[528,512]{1,0:T(8,128)(2,1)S(1)} %collective-permute-done.1.q, bf16[256,512]{1,0:T(8,128)(2,1)S(1)} %get-tuple-element.36.head, bf16[768,512]{1,0:T(8,128)(2,1)S(1)} %get-tuple-element.37.tail), custom_call_target="tpu_custom_call" | custom-call | flops 1 | bytes 1 | tf_op jit(solution)/shard_map/pallas_call | solution.py:33
  43.9 0.3 collective-permute-done.2.tail
  44.2 2.5 %shard_map.127 = bf16[560,512]{1,0:T(8,128)(2,1)} custom-call(s32[1]{0:T(128)} %bitcast.index, bf16[528,512]{1,0:T(8,128)(2,1)S(1)} %collective-permute-done.1.q, bf16[768,512]{1,0:T(8,128)(2,1)S(1)} %collective-permute-done.2.tail, f32[512,512]{1,0:T(8,128)S(1)} %get-tuple-element.40.done, f32[512,128]{1,0:T(8,128)S(1)} %get-tuple-element.41.tops, ...), custom_call_target="tpu_custom_call" | custom-call | flops 1 | bytes 1 | tf_op jit(solution)/shard_map/pallas_call | solution.py:33
  46.7 2.8 %collective-permute-start.3 = (bf16[560,512]{1,0:T(8,128)(2,1)}, bf16[560,512]{1,0:T(8,128)(2,1)S(1)}, u32[]{:S(2)}, u32[]{:S(2)}) collective-permute-start(bf16[560,512]{1,0:T(8,128)(2,1)} %shard_map.127), channel_id=1, source_target_pairs={{0,8},{4,12},{8,16},{12,20},{16,24},{20,28},{24,32},{28,36},{32,40... | collective-permute-start | bytes 1720328 | tf_op jit(solution)/shard_map/ppermute | solution.py:356
  49.4 3.3 %shard_map.128 = (f32[256,1024]{1,0:T(8,128)}, f32[8,128]{1,0:T(8,128)}) custom-call(f32[8]{0:T(128)} %rate.3, bf16[256,1024]{1,0:T(8,128)(2,1)} %q.3, bf16[256,1024]{1,0:T(8,128)(2,1)} %k.3, bf16[256,1024]{1,0:T(8,128)(2,1)} %v.3), custom_call_target="tpu_custom_call" | custom-call | flops 1 | bytes 1 | tf_op jit(solution)/shard_map/pallas_call | solution.py:33
  52.7 0.0 all-to-all-done.1
  52.7 0.0 copy-start.8
  52.7 3.0 %shard_map.129 = (f32[256,1024]{1,0:T(8,128)}, f32[8,256]{1,0:T(8,128)}) custom-call(f32[8,128]{1,0:T(8,128)} %get-tuple-element.45.rates, f32[256,1024]{1,0:T(8,128)} %get-tuple-element.46.inner, bf16[256,1024]{1,0:T(8,128)(2,1)} %q.3, f32[1024,128]{1,0:T(8,128)} %get-tuple-element.47.first, bf16[1024,128]{1,0:T(8,128)(2,1)} %bitcast.3.state), custom_call_target="tpu_custom_call" | custom-call | flops 2000000000 | bytes 1 | tf_op jit(solution)/shard_map/pallas_call | solution.py:33
  55.7 0.2 collective-permute-start.4
  55.9 2.1 %collective-permute-start.5 = (f32[8,256]{1,0:T(8,128)}, f32[8,256]{1,0:T(8,128)S(1)}, u32[]{:S(2)}, u32[]{:S(2)}) collective-permute-start(f32[8,256]{1,0:T(8,128)} %get-tuple-element.51.s0), channel_id=1, source_target_pairs={{0,2},{1,3},{2,0},{3,1},{4,6},{5,7},{6,4},{7,5},{8,10},{9,11},{10,... | collective-permute-start | bytes 24584 | tf_op jit(solution)/shard_map/ppermute | solution.py:364
  58.1 0.0 collective-permute-start.6
  58.1 6.5 %collective-permute-done.3.far = bf16[560,512]{1,0:T(8,128)(2,1)S(1)} collective-permute-done((bf16[560,512]{1,0:T(8,128)(2,1)}, bf16[560,512]{1,0:T(8,128)(2,1)S(1)}, u32[]{:S(2)}, u32[]{:S(2)}) %collective-permute-start.3) | collective-permute-done | bytes 573472 | tf_op jit(solution)/shard_map/ppermute | solution.py:356
  64.6 0.0 copy-done.6
  64.6 0.0 copy-start.9
  64.6 0.0 copy-start.11
  64.6 0.6 shard_map.130
  65.3 0.0 collective-permute-done.4.s1
  65.3 0.0 collective-permute-done.5.s2
  65.3 0.0 collective-permute-done.6.s3
  65.3 1.7 %collective-permute-start.7 = (bf16[256,512]{1,0:T(8,128)(2,1)S(1)}, bf16[256,512]{1,0:T(8,128)(2,1)S(1)}, u32[]{:S(2)}, u32[]{:S(2)}) collective-permute-start(bf16[256,512]{1,0:T(8,128)(2,1)S(1)} %get-tuple-element.61), channel_id=1, source_target_pairs={{0,4},{4,0},{8,12},{12,8},{16,20},{20,16},{24,28},{28,24},{32,36},... | collective-permute-start | bytes 786440 | tf_op jit(solution)/shard_map/ppermute | solution.py:360
  67.0 0.0 copy-done.9
  67.0 1.3 %shard_map.131 = bf16[256,1024]{1,0:T(8,128)(2,1)} custom-call(f32[256,1024]{1,0:T(8,128)S(1)} %copy-done.3, bf16[256,1024]{1,0:T(8,128)(2,1)S(1)} %copy-done.4, f32[1,1024]{1,0:T(1,128)S(1)} %bitcast.5, f32[8,256]{1,0:T(8,128)S(1)} %copy-done.9, f32[8,256]{1,0:T(8,128)S(1)} %collective-permute-done.4.s1, f32[8,256]{1,0:T(8,128)S(1)} %collective-permute-done.5.s2, ...), custom_call_target="tpu_custom_call" | custom-call | flops 1 | bytes 1 | tf_op jit(solution)/shard_map/pallas_call | solution.py:33
  68.4 0.0 collective-permute-done.7.other
  68.4 0.8 %shard_map.132 = bf16[256,1024]{1,0:T(8,128)(2,1)} custom-call(s32[1]{0:T(128)} %bitcast.index, bf16[256,512]{1,0:T(8,128)(2,1)S(1)} %get-tuple-element.60.mine, bf16[256,512]{1,0:T(8,128)(2,1)S(1)} %collective-permute-done.7.other), custom_call_target="tpu_custom_call" | custom-call | flops 1 | bytes 1 | tf_op jit(solution)/shard_map/pallas_call | solution.py:33
  (9 shorter events, 0.0 us)
Async XLA Ops:
  0.6 17.0 %copy-start.1 = (bf16[256,1024]{1,0:T(8,128)(2,1)S(1)}, bf16[256,1024]{1,0:T(8,128)(2,1)}, u32[]{:S(2)}) copy-start(bf16[256,1024]{1,0:T(8,128)(2,1)} %k.2) | copy-start | bytes 1572868
  0.6 17.0 %copy-start.2 = (bf16[256,1024]{1,0:T(8,128)(2,1)S(1)}, bf16[256,1024]{1,0:T(8,128)(2,1)}, u32[]{:S(2)}) copy-start(bf16[256,1024]{1,0:T(8,128)(2,1)} %v.2) | copy-start | bytes 1572868
  4.6 13.0 %copy-start = (bf16[256,1024]{1,0:T(8,128)(2,1)S(1)}, bf16[256,1024]{1,0:T(8,128)(2,1)}, u32[]{:S(2)}) copy-start(bf16[256,1024]{1,0:T(8,128)(2,1)} %q.1) | copy-start | bytes 1572868
  4.7 12.9 %collective-permute-start = (bf16[784,512]{1,0:T(8,128)(2,1)}, bf16[784,512]{1,0:T(8,128)(2,1)S(1)}, u32[]{:S(2)}, u32[]{:S(2)}) collective-permute-start(bf16[784,512]{1,0:T(8,128)(2,1)} %get-tuple-element.32), channel_id=1, source_target_pairs={{0,4},{4,0},{8,12},{12,8},{16,20},{20,16},{24,28},{28,24},{32,36},... | collective-permute-start | bytes 2408456 | tf_op jit(solution)/shard_map/ppermute | solution.py:360
  5.4 12.2 %copy-start.10 = (s32[2,128]{1,0:T(2,128)S(1)}, s32[2,128]{1,0:T(2,128)}, u32[]{:S(2)}) copy-start(s32[2,128]{1,0:T(2,128)} %mask.3) | copy-start | bytes 3076
  5.4 23.9 %all-to-all-start = ((bf16[64,16,128]{2,1,0:T(8,128)(2,1)}), bf16[64,16,128]{2,1,0:T(8,128)(2,1)}, u32[]{:S(2)}, u32[]{:S(2)}) async-start(bf16[64,16,128]{2,1,0:T(8,128)(2,1)} %bitcast.6), calls=%async_computation | async-start | bytes 524288 | tf_op jit(solution)/shard_map/all_to_all | solution.py:404
  19.4 9.9 %copy-start.12 = (f32[8]{0:T(128)S(1)}, f32[8]{0:T(128)}, u32[]{:S(2)}) copy-start(f32[8]{0:T(128)} %rate.3) | copy-start | bytes 100
  19.4 24.7 %collective-permute-start.2 = (bf16[768,512]{1,0:T(8,128)(2,1)S(1)}, bf16[768,512]{1,0:T(8,128)(2,1)S(1)}, u32[]{:S(2)}, u32[]{:S(2)}) collective-permute-start(bf16[768,512]{1,0:T(8,128)(2,1)S(1)} %get-tuple-element.37.tail), channel_id=1, source_target_pairs={{0,8},{4,12},{8,16},{12,20},{16,24},{20,28},{24,32},{28,36},{32,40... | collective-permute-start | bytes 2359304 | tf_op jit(solution)/shard_map/ppermute | solution.py:356
  22.6 19.6 %collective-permute-start.1 = (bf16[528,512]{1,0:T(8,128)(2,1)}, bf16[528,512]{1,0:T(8,128)(2,1)S(1)}, u32[]{:S(2)}, u32[]{:S(2)}) collective-permute-start(bf16[528,512]{1,0:T(8,128)(2,1)} %get-tuple-element.33.q), channel_id=1, source_target_pairs={{8,0},{12,4},{16,8},{20,12},{24,16},{28,20},{32,24},{36,28},{40,32... | collective-permute-start | bytes 1622024 | tf_op jit(solution)/shard_map/ppermute | solution.py:356
  31.2 21.5 %all-to-all-start.1 = ((bf16[64,16,128]{2,1,0:T(8,128)(2,1)}), bf16[64,16,128]{2,1,0:T(8,128)(2,1)}, u32[]{:S(2)}, u32[]{:S(2)}) async-start(bf16[64,16,128]{2,1,0:T(8,128)(2,1)} %shard_map.124), calls=%async_computation.1 | async-start | bytes 524288 | tf_op jit(solution)/shard_map/all_to_all | solution.py:431
  40.8 0.7 %copy-start.5 = (f32[512,128]{1,0:T(8,128)}, f32[512,128]{1,0:T(8,128)S(1)}, u32[]{:S(2)}) copy-start(f32[512,128]{1,0:T(8,128)S(1)} %get-tuple-element.53.tops) | copy-start | bytes 786436
  41.5 0.7 %copy-start.7 = (f32[512,128]{1,0:T(8,128)}, f32[512,128]{1,0:T(8,128)S(1)}, u32[]{:S(2)}) copy-start(f32[512,128]{1,0:T(8,128)S(1)} %get-tuple-element.54.sums) | copy-start | bytes 786436
  46.7 17.9 %collective-permute-start.3 = (bf16[560,512]{1,0:T(8,128)(2,1)}, bf16[560,512]{1,0:T(8,128)(2,1)S(1)}, u32[]{:S(2)}, u32[]{:S(2)}) collective-permute-start(bf16[560,512]{1,0:T(8,128)(2,1)} %shard_map.127), channel_id=1, source_target_pairs={{0,8},{4,12},{8,16},{12,20},{16,24},{20,28},{24,32},{28,36},{32,40... | collective-permute-start | bytes 1720328 | tf_op jit(solution)/shard_map/ppermute | solution.py:356
  52.7 11.9 %copy-start.6 = (f32[512,128]{1,0:T(8,128)S(1)}, f32[512,128]{1,0:T(8,128)}, u32[]{:S(2)}) copy-start(f32[512,128]{1,0:T(8,128)} %copy-done.5) | copy-start | bytes 786436
  52.7 11.9 %copy-start.8 = (f32[512,128]{1,0:T(8,128)S(1)}, f32[512,128]{1,0:T(8,128)}, u32[]{:S(2)}) copy-start(f32[512,128]{1,0:T(8,128)} %copy-done.7) | copy-start | bytes 786436
  55.7 9.5 %collective-permute-start.4 = (f32[8,256]{1,0:T(8,128)}, f32[8,256]{1,0:T(8,128)S(1)}, u32[]{:S(2)}, u32[]{:S(2)}) collective-permute-start(f32[8,256]{1,0:T(8,128)} %get-tuple-element.51.s0), channel_id=1, source_target_pairs={{0,1},{1,2},{2,3},{3,0},{4,5},{5,6},{6,7},{7,4},{8,9},{9,10},{10,1... | collective-permute-start | bytes 24584 | tf_op jit(solution)/shard_map/ppermute | solution.py:364
  55.9 9.3 %collective-permute-start.5 = (f32[8,256]{1,0:T(8,128)}, f32[8,256]{1,0:T(8,128)S(1)}, u32[]{:S(2)}, u32[]{:S(2)}) collective-permute-start(f32[8,256]{1,0:T(8,128)} %get-tuple-element.51.s0), channel_id=1, source_target_pairs={{0,2},{1,3},{2,0},{3,1},{4,6},{5,7},{6,4},{7,5},{8,10},{9,11},{10,... | collective-permute-start | bytes 24584 | tf_op jit(solution)/shard_map/ppermute | solution.py:364
  58.1 7.2 %collective-permute-start.6 = (f32[8,256]{1,0:T(8,128)}, f32[8,256]{1,0:T(8,128)S(1)}, u32[]{:S(2)}, u32[]{:S(2)}) collective-permute-start(f32[8,256]{1,0:T(8,128)} %get-tuple-element.51.s0), channel_id=1, source_target_pairs={{0,3},{1,0},{2,1},{3,2},{4,7},{5,4},{6,5},{7,6},{8,11},{9,8},{10,9... | collective-permute-start | bytes 24584 | tf_op jit(solution)/shard_map/ppermute | solution.py:364
  64.6 2.4 %copy-start.3 = (f32[256,1024]{1,0:T(8,128)S(1)}, f32[256,1024]{1,0:T(8,128)}, u32[]{:S(2)}) copy-start(f32[256,1024]{1,0:T(8,128)} %get-tuple-element.50.heads) | copy-start | bytes 3145732
  64.6 2.4 %copy-start.4 = (bf16[256,1024]{1,0:T(8,128)(2,1)S(1)}, bf16[256,1024]{1,0:T(8,128)(2,1)}, u32[]{:S(2)}) copy-start(bf16[256,1024]{1,0:T(8,128)(2,1)} %gate.1) | copy-start | bytes 1572868
  64.6 2.4 %copy-start.9 = (f32[8,256]{1,0:T(8,128)S(1)}, f32[8,256]{1,0:T(8,128)}, u32[]{:S(2)}) copy-start(f32[8,256]{1,0:T(8,128)} %get-tuple-element.51.s0) | copy-start | bytes 24580
  64.6 2.4 %copy-start.11 = (f32[1024]{0:T(1024)S(1)}, f32[1024]{0:T(1024)}, u32[]{:S(2)}) copy-start(f32[1024]{0:T(1024)} %param.15) | copy-start | bytes 12292
  65.3 3.1 %collective-permute-start.7 = (bf16[256,512]{1,0:T(8,128)(2,1)S(1)}, bf16[256,512]{1,0:T(8,128)(2,1)S(1)}, u32[]{:S(2)}, u32[]{:S(2)}) collective-permute-start(bf16[256,512]{1,0:T(8,128)(2,1)S(1)} %get-tuple-element.61), channel_id=1, source_target_pairs={{0,4},{4,0},{8,12},{12,8},{16,20},{20,16},{24,28},{28,24},{32,36},... | collective-permute-start | bytes 786440 | tf_op jit(solution)/shard_map/ppermute | solution.py:360
